TPU v7x, 128 devices: a whole 4x4x4 slice. The times are simulated.
128 devices in a mesh: ctx: 8 (over z_lo, y), fsdp: 4 (over x), head: 4 (over z_hi, core).
Axes of the slice: x: 4, y: 4, z: 4 (z_hi: 2, z_lo: 2; z = z_hi * 2 + z_lo), core: 2. Of those that a mesh axis runs over, the one named last changes fastest.
Arguments:
- tokens: bfloat16 [4, 1024, 1024], P('fsdp', 'ctx'), may hold values from -6 to 6
- positions: int32 [4, 1024], P('fsdp'), may hold values from 0 to 1023, as said below
- attn_gain: float32 [1024], replicated, may hold values from 0.5 to 1.5
- ffn_gain: float32 [1024], replicated, may hold values from 0.5 to 1.5
- query_gain: float32 [64], replicated, may hold values from 0.5 to 1.5
- key_gain: float32 [64], replicated, may hold values from 0.5 to 1.5
- w_query: bfloat16 [1024, 1024], P(('ctx', 'fsdp'), 'head'), may hold values from -0.1875 to 0.1875
- w_key: bfloat16 [1024, 512], P(('ctx', 'fsdp'), 'head'), may hold values from -0.1875 to 0.1875
- w_value: bfloat16 [1024, 512], P(('ctx', 'fsdp'), 'head'), may hold values from -0.1875 to 0.1875
- w_out: bfloat16 [1024, 1024], P(('ctx', 'fsdp'), 'head'), may hold values from -1.5 to 1.5
- w_gate: bfloat16 [1024, 4608], P(('ctx', 'fsdp'), 'head'), may hold values from -0.1875 to 0.1875
- w_up: bfloat16 [1024, 4608], P(('ctx', 'fsdp'), 'head'), may hold values from -0.1875 to 0.1875
- w_down: bfloat16 [1024, 4608], P(('ctx', 'fsdp'), 'head'), may hold values from -0.09375 to 0.09375
- cotangent: bfloat16 [4, 1024, 1024], P('fsdp', 'ctx'), may hold values from -6 to 6
Outputs:
- block_out: bfloat16 [4, 1024, 1024], P('fsdp', 'ctx')
- tokens_grad: bfloat16 [4, 1024, 1024], P('fsdp', 'ctx')
- attn_gain_grad: float32 [1024], replicated
- ffn_gain_grad: float32 [1024], replicated
- query_gain_grad: float32 [64], replicated
- key_gain_grad: float32 [64], replicated
- w_query_grad: float32 [1024, 1024], P(('ctx', 'fsdp'), 'head')
- w_key_grad: float32 [1024, 512], P(('ctx', 'fsdp'), 'head')
- w_value_grad: float32 [1024, 512], P(('ctx', 'fsdp'), 'head')
- w_out_grad: float32 [1024, 1024], P(('ctx', 'fsdp'), 'head')
- w_gate_grad: float32 [1024, 4608], P(('ctx', 'fsdp'), 'head')
- w_up_grad: float32 [1024, 4608], P(('ctx', 'fsdp'), 'head')
- w_down_grad: float32 [1024, 4608], P(('ctx', 'fsdp'), 'head')
Inputs may be any that keep to these rules, and one draw needn't show every extreme that they name: Each row of positions names every position of its sequence once; it is made of 16 aligned blocks of 64 consecutive rising positions, in an order drawn for each sequence.
All inputs are finite; a program needn't handle non-finite values.
Results may differ from a plain program's by a relative error of at most 0.03.
Values may be sent and summed in bfloat16 or wider, within the bound.
No kernel may reach another device: no remote copies, remote signals or barrier semaphores. Data moves between devices by JAX's collectives and lax.ppermute only.
A program may use at most 64 MiB of HBM per device.

v0:
```python
import jax
import jax.numpy as jnp
from jax import lax
from jax.sharding import PartitionSpec as P

HEAD_DIM = 64


EPSILON = 1e-05
ROPE_BASE = 1000000.0


def rms_scale(values):
    return lax.rsqrt(jnp.mean(values * values, axis=-1, keepdims=True) + EPSILON)


def norm_grad(grad_norm, normal, scale_rows):
    return scale_rows * (grad_norm - normal * jnp.mean(grad_norm * normal, axis=-1, keepdims=True))


def rope_tables(places, head_dim):
    half_dim = head_dim // 2
    frequency = ROPE_BASE ** (-(jnp.arange(half_dim).astype(jnp.float32) * 2.0 / head_dim))
    angles = places.astype(jnp.float32)[..., None] * frequency
    return (jnp.cos(angles), jnp.sin(angles))


def rotate(values, cosine_table, sine_table):
    half_dim = values.shape[-1] // 2
    lower_half = values[..., :half_dim]
    upper_half = values[..., half_dim:]
    cosine_b = cosine_table[..., None, :]
    sine_b = sine_table[..., None, :]
    return jnp.concatenate(
        [lower_half * cosine_b - upper_half * sine_b, upper_half * cosine_b + lower_half * sine_b],
        axis=-1,
    )


def rotate_back(grads, cosine_table, sine_table):
    half_dim = grads.shape[-1] // 2
    lower_half = grads[..., :half_dim]
    upper_half = grads[..., half_dim:]
    cosine_b = cosine_table[..., None, :]
    sine_b = sine_table[..., None, :]
    return jnp.concatenate(
        [lower_half * cosine_b + upper_half * sine_b, upper_half * cosine_b - lower_half * sine_b],
        axis=-1,
    )


def left_product(left, right):
    return lax.dot_general(
        left, right, (((0,), (0,)), ((), ())), preferred_element_type=jnp.float32
    )


def right_product(left, right):
    return lax.dot_general(
        left, right, (((1,), (1,)), ((), ())), preferred_element_type=jnp.float32
    )


def score_weights(q_heads, key_rows, own_places, key_places, scale):
    scores = (
        jnp.einsum("tkgd,skd->kgts", q_heads, key_rows, preferred_element_type=jnp.float32) * scale
    )
    return jnp.where(key_places[None, :] <= own_places[:, None], jnp.exp(scores), 0.0)


def local(
    tokens,
    positions,
    attn_gain,
    ffn_gain,
    query_gain,
    key_gain,
    w_query,
    w_key,
    w_value,
    w_out,
    w_gate,
    w_up,
    w_down,
    cotangent,
):
    query_full, key_full, value_full, out_full, gate_full, up_full, down_full = (
        lax.all_gather(w_query, ("ctx", "fsdp"), axis=0, tiled=True),
        lax.all_gather(w_key, ("ctx", "fsdp"), axis=0, tiled=True),
        lax.all_gather(w_value, ("ctx", "fsdp"), axis=0, tiled=True),
        lax.all_gather(w_out, ("ctx", "fsdp"), axis=0, tiled=True),
        lax.all_gather(w_gate, ("ctx", "fsdp"), axis=0, tiled=True),
        lax.all_gather(w_up, ("ctx", "fsdp"), axis=0, tiled=True),
        lax.all_gather(w_down, ("ctx", "fsdp"), axis=0, tiled=True),
    )
    local_rows = tokens.shape[1]
    seq_places = positions[0]
    own_places = lax.dynamic_slice_in_dim(
        seq_places, lax.axis_index("ctx") * local_rows, local_rows
    )
    head_count = query_full.shape[1] // HEAD_DIM
    kv_count = key_full.shape[1] // HEAD_DIM
    group_size = head_count // kv_count
    scale = HEAD_DIM ** (-0.5)
    x_rows = tokens[0].astype(jnp.float32)
    x_scale = rms_scale(x_rows)
    x_hat = x_rows * x_scale
    normed = (x_hat * attn_gain).astype(jnp.bfloat16)
    query_proj = jnp.dot(normed, query_full, preferred_element_type=jnp.float32).reshape(
        local_rows, head_count, HEAD_DIM
    )
    key_proj = jnp.dot(normed, key_full, preferred_element_type=jnp.float32).reshape(
        local_rows, kv_count, HEAD_DIM
    )
    v_heads = (
        jnp.dot(normed, value_full, preferred_element_type=jnp.float32)
        .astype(jnp.bfloat16)
        .reshape(local_rows, kv_count, HEAD_DIM)
    )
    query_scale = rms_scale(query_proj)
    query_hat = query_proj * query_scale
    key_scale = rms_scale(key_proj)
    key_hat = key_proj * key_scale
    cosine_table, sine_table = rope_tables(own_places, HEAD_DIM)
    q_heads = (
        rotate(query_hat * query_gain, cosine_table, sine_table)
        .astype(jnp.bfloat16)
        .reshape(local_rows, kv_count, group_size, HEAD_DIM)
    )
    k_heads = rotate(key_hat * key_gain, cosine_table, sine_table).astype(jnp.bfloat16)
    key_piece = lax.all_gather(k_heads, "ctx", axis=0, tiled=True)
    value_piece = lax.all_gather(v_heads, "ctx", axis=0, tiled=True)
    weights = score_weights(q_heads, key_piece, own_places, seq_places, scale)
    inner_sum = jnp.einsum(
        "kgts,skd->tkgd",
        weights.astype(jnp.bfloat16),
        value_piece,
        preferred_element_type=jnp.float32,
    )
    inner_sum, row_total = (inner_sum, jnp.sum(weights, axis=-1))
    denom = jnp.transpose(row_total, (2, 0, 1))[..., None]
    attn_heads = inner_sum / denom
    attn_low = attn_heads.astype(jnp.bfloat16).reshape(local_rows, head_count * HEAD_DIM)
    attn_out = lax.psum(right_product(attn_low, out_full), "head")
    hidden = x_rows + attn_out
    h_scale = rms_scale(hidden)
    h_hat = hidden * h_scale
    h_normed = (h_hat * ffn_gain).astype(jnp.bfloat16)
    gate_proj = jnp.dot(h_normed, gate_full, preferred_element_type=jnp.float32)
    up_proj = jnp.dot(h_normed, up_full, preferred_element_type=jnp.float32)
    silu_gate = jax.nn.silu(gate_proj)
    active = (silu_gate * up_proj).astype(jnp.bfloat16)
    branch = lax.psum(right_product(active, down_full).astype(jnp.bfloat16), "head").astype(
        jnp.float32
    )
    block_out = (hidden + branch).astype(jnp.bfloat16)[None]
    grad_out = cotangent[0]
    grad_wdown = left_product(grad_out, active)
    grad_active = jnp.dot(grad_out, down_full, preferred_element_type=jnp.float32)
    sigmoid_gate = jax.nn.sigmoid(gate_proj)
    grad_gate = (
        grad_active * up_proj * sigmoid_gate * (1.0 + gate_proj * (1.0 - sigmoid_gate))
    ).astype(jnp.bfloat16)
    grad_up = (grad_active * silu_gate).astype(jnp.bfloat16)
    grad_wgate = left_product(h_normed, grad_gate)
    grad_wup = left_product(h_normed, grad_up)
    grad_hnorm_part = right_product(grad_gate, gate_full) + right_product(grad_up, up_full)
    ffn_gain_part = jnp.sum(grad_hnorm_part * h_hat, axis=0)
    grad_hnorm = lax.psum(grad_hnorm_part.astype(jnp.bfloat16), "head").astype(jnp.float32)
    grad_hidden = grad_out.astype(jnp.float32) + norm_grad(grad_hnorm * ffn_gain, h_hat, h_scale)
    grad_attn = grad_hidden.astype(jnp.bfloat16)
    grad_wout = left_product(grad_attn, attn_low)
    grad_heads = jnp.dot(grad_attn, out_full, preferred_element_type=jnp.float32).reshape(
        local_rows, kv_count, group_size, HEAD_DIM
    )
    grad_inner = (grad_heads / denom).astype(jnp.bfloat16)
    delta_rows = jnp.transpose(jnp.sum(grad_heads * attn_heads, axis=-1) / denom[..., 0], (1, 2, 0))
    key_all, value_all = (
        lax.all_gather(k_heads, "ctx", axis=0, tiled=True),
        lax.all_gather(v_heads, "ctx", axis=0, tiled=True),
    )
    weights = score_weights(q_heads, key_all, own_places, seq_places, scale)
    grad_probs = jnp.einsum(
        "tkgd,skd->kgts", grad_inner, value_all, preferred_element_type=jnp.float32
    )
    grad_scores = (weights * (grad_probs - delta_rows[..., None])).astype(jnp.bfloat16)
    grad_qheads = (
        jnp.einsum("kgts,skd->tkgd", grad_scores, key_all, preferred_element_type=jnp.float32)
        * scale
    )
    grad_key_all = (
        jnp.einsum("kgts,tkgd->skd", grad_scores, q_heads, preferred_element_type=jnp.float32)
        * scale
    )
    grad_value_all = jnp.einsum(
        "kgts,tkgd->skd",
        weights.astype(jnp.bfloat16),
        grad_inner,
        preferred_element_type=jnp.float32,
    )
    grad_kheads, grad_vheads = (
        lax.psum_scatter(
            grad_key_all.astype(jnp.bfloat16), "ctx", scatter_dimension=0, tiled=True
        ).astype(jnp.float32),
        lax.psum_scatter(
            grad_value_all.astype(jnp.bfloat16), "ctx", scatter_dimension=0, tiled=True
        ).astype(jnp.float32),
    )
    grad_qnorm = rotate_back(
        grad_qheads.reshape(local_rows, head_count, HEAD_DIM), cosine_table, sine_table
    )
    grad_knorm = rotate_back(grad_kheads, cosine_table, sine_table)
    query_gain_part = jnp.sum(grad_qnorm * query_hat, axis=(0, 1))
    key_gain_part = jnp.sum(grad_knorm * key_hat, axis=(0, 1))
    grad_query = (
        norm_grad(grad_qnorm * query_gain, query_hat, query_scale)
        .astype(jnp.bfloat16)
        .reshape(local_rows, head_count * HEAD_DIM)
    )
    grad_key = (
        norm_grad(grad_knorm * key_gain, key_hat, key_scale)
        .astype(jnp.bfloat16)
        .reshape(local_rows, kv_count * HEAD_DIM)
    )
    grad_value = grad_vheads.astype(jnp.bfloat16).reshape(local_rows, kv_count * HEAD_DIM)
    grad_wquery = left_product(normed, grad_query)
    grad_wkey = left_product(normed, grad_key)
    grad_wvalue = left_product(normed, grad_value)
    grad_norm_part = (
        right_product(grad_query, query_full)
        + right_product(grad_key, key_full)
        + right_product(grad_value, value_full)
    )
    attn_gain_part = jnp.sum(grad_norm_part * x_hat, axis=0)
    grad_normed = lax.psum(grad_norm_part.astype(jnp.bfloat16), "head").astype(jnp.float32)
    tokens_grad = (grad_hidden + norm_grad(grad_normed * attn_gain, x_hat, x_scale)).astype(
        jnp.bfloat16
    )[None]
    attn_gain_grad, ffn_gain_grad, query_gain_grad, key_gain_grad = lax.psum(
        (attn_gain_part, ffn_gain_part, query_gain_part, key_gain_part), ("ctx", "fsdp", "head")
    )
    query_grad, key_grad, value_grad, out_grad, gate_grad, up_grad, down_grad = (
        lax.psum_scatter(
            grad_wquery.astype(jnp.bfloat16), ("ctx", "fsdp"), scatter_dimension=0, tiled=True
        ).astype(jnp.float32),
        lax.psum_scatter(
            grad_wkey.astype(jnp.bfloat16), ("ctx", "fsdp"), scatter_dimension=0, tiled=True
        ).astype(jnp.float32),
        lax.psum_scatter(
            grad_wvalue.astype(jnp.bfloat16), ("ctx", "fsdp"), scatter_dimension=0, tiled=True
        ).astype(jnp.float32),
        lax.psum_scatter(
            grad_wout.astype(jnp.bfloat16), ("ctx", "fsdp"), scatter_dimension=0, tiled=True
        ).astype(jnp.float32),
        lax.psum_scatter(
            grad_wgate.astype(jnp.bfloat16), ("ctx", "fsdp"), scatter_dimension=0, tiled=True
        ).astype(jnp.float32),
        lax.psum_scatter(
            grad_wup.astype(jnp.bfloat16), ("ctx", "fsdp"), scatter_dimension=0, tiled=True
        ).astype(jnp.float32),
        lax.psum_scatter(
            grad_wdown.astype(jnp.bfloat16), ("ctx", "fsdp"), scatter_dimension=0, tiled=True
        ).astype(jnp.float32),
    )
    return (
        block_out,
        tokens_grad,
        attn_gain_grad,
        ffn_gain_grad,
        query_gain_grad,
        key_gain_grad,
        query_grad,
        key_grad,
        value_grad,
        out_grad,
        gate_grad,
        up_grad,
        down_grad,
    )


def solution(mesh):
    placed = (
        P("fsdp", "ctx", None),
        P("fsdp", None),
        P(),
        P(),
        P(),
        P(),
        P(("ctx", "fsdp"), "head"),
        P(("ctx", "fsdp"), "head"),
        P(("ctx", "fsdp"), "head"),
        P(("ctx", "fsdp"), "head"),
        P(("ctx", "fsdp"), "head"),
        P(("ctx", "fsdp"), "head"),
        P(("ctx", "fsdp"), "head"),
        P("fsdp", "ctx", None),
    )
    return jax.shard_map(
        local,
        mesh=mesh,
        in_specs=placed,
        out_specs=(
            P("fsdp", "ctx", None),
            P("fsdp", "ctx", None),
            P(),
            P(),
            P(),
            P(),
            P(("ctx", "fsdp"), "head"),
            P(("ctx", "fsdp"), "head"),
            P(("ctx", "fsdp"), "head"),
            P(("ctx", "fsdp"), "head"),
            P(("ctx", "fsdp"), "head"),
            P(("ctx", "fsdp"), "head"),
            P(("ctx", "fsdp"), "head"),
        ),
        check_vma=False,
    )
```

profile of v0, /device:TPU:0, one launch (start us, length us, event | category | flops | bytes accessed | tf_op | source)
XLA Modules:
  0.0 2117.6 jit_solution(12707381013572017532)
XLA Ops:
  9.2 83.5 %all_gather.31 = bf16[1024,128]{1,0:T(8,128)(2,1)S(1)} all-gather(bf16[32,128]{1,0:T(8,128)(2,1)} %param.21), channel_id=1, replica_groups=mesh['ctx'=8,'fsdp'=4,'head'=4] {'ctx','fsdp'}, dimensions={0}, use_global_device_ids=true | all-gather | bytes 270336 | tf_op jit(solution)/shard_map/all_gather | solution.py:89
  92.7 76.9 %all_gather.29 = bf16[1024,128]{1,0:T(8,128)(2,1)S(1)} all-gather(bf16[32,128]{1,0:T(8,128)(2,1)} %param.22), channel_id=1, replica_groups=mesh['ctx'=8,'fsdp'=4,'head'=4] {'ctx','fsdp'}, dimensions={0}, use_global_device_ids=true | all-gather | bytes 270336 | tf_op jit(solution)/shard_map/all_gather | solution.py:90
  171.0 24.1 %all_gather.30 = bf16[1024,2,64]{0,2,1:T(8,128)(2,1)S(1)} all-gather(bf16[128,2,64]{0,2,1:T(8,128)(2,1)S(1)} %bitcast.197), channel_id=1, replica_groups=mesh['ctx'=8,'fsdp'=4,'head'=4] {'ctx'}, dimensions={0}, use_global_device_ids=true | all-gather | bytes 294912 | tf_op jit(solution)/shard_map/all_gather | solution.py:132
  197.2 24.1 %all_gather.32 = bf16[1024,2,64]{0,2,1:T(8,128)(2,1)S(1)} all-gather(bf16[128,2,64]{0,2,1:T(8,128)(2,1)S(1)} %pad_maximum_fusion.5), channel_id=1, replica_groups=mesh['ctx'=8,'fsdp'=4,'head'=4] {'ctx'}, dimensions={0}, use_global_device_ids=true | all-gather | bytes 294912 | tf_op jit(solution)/shard_map/all_gather | solution.py:131
  221.3 80.3 %all_gather.33 = bf16[1024,256]{1,0:T(8,128)(2,1)S(1)} all-gather(bf16[32,256]{1,0:T(8,128)(2,1)S(1)} %copy-done.47), channel_id=1, replica_groups=mesh['ctx'=8,'fsdp'=4,'head'=4] {'ctx','fsdp'}, dimensions={0}, use_global_device_ids=true | all-gather | bytes 540672 | tf_op jit(solution)/shard_map/all_gather | solution.py:88
  301.6 78.0 %all_gather.34 = bf16[1024,256]{1,0:T(8,128)(2,1)S(1)} all-gather(bf16[32,256]{1,0:T(8,128)(2,1)S(1)} %copy-done.48), channel_id=1, replica_groups=mesh['ctx'=8,'fsdp'=4,'head'=4] {'ctx','fsdp'}, dimensions={0}, use_global_device_ids=true | all-gather | bytes 540672 | tf_op jit(solution)/shard_map/all_gather | solution.py:91
  386.5 39.5 %all-reduce.6.cloned.1.call-done = f32[128,1024]{1,0:T(8,128)} async-done(((f32[128,1024]{1,0:T(8,128)}), f32[128,1024]{1,0:T(8,128)}) %all-reduce.6.cloned.1.call-update) | async-done | bytes 524304 | tf_op jit(solution)/shard_map/psum | solution.py:144
  427.3 112.3 %all-gather.6.cloned.1.call-done = bf16[1024,1152]{1,0:T(8,128)(2,1)} async-done(((bf16[32,1152]{1,0:T(8,128)(2,1)}), bf16[1024,1152]{1,0:T(8,128)(2,1)}) %all-gather.6.cloned.1.call-update) | async-done | bytes 2359312 | tf_op jit(solution)/shard_map/all_gather | solution.py:93
  539.7 3.0 fusion.64
  542.7 153.3 %all-gather.4.cloned.1.call-done = bf16[1024,1152]{1,0:T(8,128)(2,1)} async-done(((bf16[32,1152]{1,0:T(8,128)(2,1)}), bf16[1024,1152]{1,0:T(8,128)(2,1)}) %all-gather.4.cloned.1.call-update) | async-done | bytes 2359312 | tf_op jit(solution)/shard_map/all_gather | solution.py:92
  696.0 3.0 fusion.63
  699.0 153.2 %all-gather.8.cloned.1.call-done = bf16[1024,1152]{1,0:T(8,128)(2,1)} async-done(((bf16[32,1152]{1,0:T(8,128)(2,1)}), bf16[1024,1152]{1,0:T(8,128)(2,1)}) %all-gather.8.cloned.1.call-update) | async-done | bytes 2359312 | tf_op jit(solution)/shard_map/all_gather | solution.py:94
  852.2 3.5 multiply_convert_fusion
  859.2 3.4 convolution_convert_fusion.7
  862.6 37.6 %all-reduce.8.cloned.1.call-done = bf16[128,1024]{1,0:T(8,128)(2,1)} async-done(((bf16[128,1024]{1,0:T(8,128)(2,1)}), bf16[128,1024]{1,0:T(8,128)(2,1)}) %all-reduce.8.cloned.1.call-update) | async-done | bytes 262160 | tf_op jit(solution)/shard_map/psum | solution.py:169
  900.2 1.8 multiply_reduce_fusion
  911.3 1.9 copy.60
  916.5 29.5 %reduce-scatter.28.cloned.1.call-done = bf16[128,128]{1,0:T(8,128)(2,1)} async-done(((bf16[1024,128]{1,0:T(8,128)(2,1)}), bf16[128,128]{1,0:T(8,128)(2,1)}) %reduce-scatter.28.cloned.1.call-update) | async-done | bytes 32784
  946.9 37.3 %reduce-scatter.30.cloned.1.call-done = bf16[128,128]{1,0:T(8,128)(2,1)} async-done(((bf16[1024,128]{1,0:T(8,128)(2,1)}), bf16[128,128]{1,0:T(8,128)(2,1)}) %reduce-scatter.30.cloned.1.call-update) | async-done | bytes 32784 | tf_op jit(solution)/shard_map/reshape | solution.py:225
  992.8 1.8 fusion
  994.6 2.5 copy.56
  998.2 2.3 convolution_convert_fusion.1
  1000.6 2.2 convolution_convert_fusion.2
  1002.8 141.8 %reduce-scatter.20.cloned.1.call-done = bf16[32,128]{1,0:T(8,128)(2,1)} async-done(((bf16[1024,128]{1,0:T(8,128)(2,1)}), bf16[32,128]{1,0:T(8,128)(2,1)}) %reduce-scatter.20.cloned.1.call-update) | async-done | bytes 8208 | tf_op jit(solution)/shard_map/reduce_scatter | solution.py:249
  1145.9 157.2 %reduce-scatter.18.cloned.1.call-done = bf16[32,128]{1,0:T(8,128)(2,1)} async-done(((bf16[1024,128]{1,0:T(8,128)(2,1)}), bf16[32,128]{1,0:T(8,128)(2,1)}) %reduce-scatter.18.cloned.1.call-update) | async-done | bytes 8208 | tf_op jit(solution)/shard_map/reduce_scatter | solution.py:246
  1305.7 63.3 %all-reduce = (f32[1024]{0:T(1024)}, f32[1024]{0:T(1024)}, f32[64]{0:T(128)}, f32[64]{0:T(128)}) all-reduce(f32[1024]{0:T(1024)S(1)} %get-tuple-element.43, f32[1024]{0:T(1024)S(1)} %copy-done.46, f32[64]{0:T(128)S(1)} %copy-done.59, f32[64]{0:T(128)S(1)} %get-tuple-element.45), channel_id=1, replica_groups=mesh['ctx'=8,'fsdp'=4,'head'=4] {'ctx','fsdp','head'}, use_global_device_ids=true, to_apply=%region_17.18 | all-reduce | flops 2176 | bytes 17408 | tf_op jit(solution)/shard_map/psum | solution.py:239
  1369.0 2.1 fusion.27
  1371.0 91.0 %reduce-scatter.22.cloned.1.call-done = bf16[32,256]{1,0:T(8,128)(2,1)} async-done(((bf16[1024,256]{1,0:T(8,128)(2,1)}), bf16[32,256]{1,0:T(8,128)(2,1)}) %reduce-scatter.22.cloned.1.call-update) | async-done | bytes 16400 | tf_op jit(solution)/shard_map/reduce_scatter | solution.py:252
  1463.3 157.1 %reduce-scatter.16.cloned.1.call-done = bf16[32,256]{1,0:T(8,128)(2,1)} async-done(((bf16[1024,256]{1,0:T(8,128)(2,1)}), bf16[32,256]{1,0:T(8,128)(2,1)}) %reduce-scatter.16.cloned.1.call-update) | async-done | bytes 16400 | tf_op jit(solution)/shard_map/reduce_scatter | solution.py:243
  1621.7 161.3 %reduce-scatter.32.cloned.1.call-done = bf16[32,1152]{1,0:T(8,128)(2,1)} async-done(((bf16[1024,1152]{1,0:T(8,128)(2,1)}), bf16[32,1152]{1,0:T(8,128)(2,1)}) %reduce-scatter.32.cloned.1.call-update) | async-done | bytes 73744
  1784.9 160.9 %reduce-scatter.26.cloned.1.call-done = bf16[32,1152]{1,0:T(8,128)(2,1)} async-done(((bf16[1024,1152]{1,0:T(8,128)(2,1)}), bf16[32,1152]{1,0:T(8,128)(2,1)}) %reduce-scatter.26.cloned.1.call-update) | async-done | bytes 73744 | tf_op jit(solution)/shard_map/reduce_scatter | solution.py:258
  1947.4 161.5 %reduce-scatter.24.cloned.1.call-done = bf16[32,1152]{1,0:T(8,128)(2,1)} async-done(((bf16[1024,1152]{1,0:T(8,128)(2,1)}), bf16[32,1152]{1,0:T(8,128)(2,1)}) %reduce-scatter.24.cloned.1.call-update) | async-done | bytes 73744 | tf_op jit(solution)/shard_map/reduce_scatter | solution.py:255
  (213 shorter events, 50.3 us)
Async XLA Ops:
  8.0 188.6 %copy-start.54 = (s32[1,1024]{1,0:T(1,128)S(1)}, s32[1,1024]{1,0:T(1,128)}, u32[]{:S(2)}) copy-start(s32[1,1024]{1,0:T(1,128)} %param.15) | copy-start | bytes 12292
  8.0 188.8 %copy-start.57 = (f32[64]{0:T(128)S(1)}, f32[64]{0:T(128)}, u32[]{:S(2)}) copy-start(f32[64]{0:T(128)} %param.19) | copy-start | bytes 772
  8.0 213.3 %copy-start.47 = (bf16[32,256]{1,0:T(8,128)(2,1)S(1)}, bf16[32,256]{1,0:T(8,128)(2,1)}, u32[]{:S(2)}) copy-start(bf16[32,256]{1,0:T(8,128)(2,1)} %param.20) | copy-start | bytes 49156
  8.0 293.6 %copy-start.48 = (bf16[32,256]{1,0:T(8,128)(2,1)S(1)}, bf16[32,256]{1,0:T(8,128)(2,1)}, u32[]{:S(2)}) copy-start(bf16[32,256]{1,0:T(8,128)(2,1)} %param.23) | copy-start | bytes 49156
  8.1 417.9 %all-reduce.6.cloned.1.call-start = ((), (), s32[]{:S(2)}) async-start(), calls=%async_computation.9 | async-start | bytes 1048576 | tf_op jit(solution)/shard_map/psum | solution.py:144
  9.2 370.6 %copy-start.51 = (f32[128]{0:T(128)}, f32[128]{0:T(128)S(1)}, u32[]{:S(2)}) copy-start(f32[128]{0:T(128)S(1)} %add_rsqrt_fusion.3) | copy-start | bytes 1540
  169.7 210.2 %copy-start = (bf16[1,128,1024]{2,1,0:T(8,128)(2,1)S(1)}, bf16[1,128,1024]{2,1,0:T(8,128)(2,1)}, u32[]{:S(2)}) copy-start(bf16[1,128,1024]{2,1,0:T(8,128)(2,1)} %param.14) | copy-start | bytes 786436
  169.7 210.2 %copy-start.38 = (f32[1024]{0:T(1024)S(1)}, f32[1024]{0:T(1024)}, u32[]{:S(2)}) copy-start(f32[1024]{0:T(1024)} %param.16) | copy-start | bytes 12292
  195.1 186.9 %copy-start.13 = (bf16[1024,2,64]{0,2,1:T(8,128)(2,1)}, bf16[1024,2,64]{0,2,1:T(8,128)(2,1)S(1)}, u32[]{:S(2)}) copy-start(bf16[1024,2,64]{0,2,1:T(8,128)(2,1)S(1)} %all_gather.30) | copy-start | bytes 786436
  195.3 185.6 %copy-start.55 = (f32[64]{0:T(128)S(1)}, f32[64]{0:T(128)}, u32[]{:S(2)}) copy-start(f32[64]{0:T(128)} %param.18) | copy-start | bytes 772
  196.8 185.2 %copy-start.30 = (f32[128,32]{0,1:T(8,128)}, f32[128,32]{0,1:T(8,128)S(1)}, u32[]{:S(2)}) copy-start(f32[128,32]{0,1:T(8,128)S(1)} %get-tuple-element.69) | copy-start | bytes 49156
  221.3 160.7 %copy-start.25 = (bf16[1024,2,64]{0,2,1:T(8,128)(2,1)}, bf16[1024,2,64]{0,2,1:T(8,128)(2,1)S(1)}, u32[]{:S(2)}) copy-start(bf16[1024,2,64]{0,2,1:T(8,128)(2,1)S(1)} %all_gather.32) | copy-start | bytes 786436
  384.7 155.0 %all-gather.6.cloned.1.call-start = ((), (), s32[]{:S(2)}) async-start(), calls=%async_computation.11 | async-start | bytes 2433024 | tf_op jit(solution)/shard_map/all_gather | solution.py:93
  385.3 310.7 %all-gather.4.cloned.1.call-start = ((), (), s32[]{:S(2)}) async-start(), calls=%async_computation.10 | async-start | bytes 2433024 | tf_op jit(solution)/shard_map/all_gather | solution.py:92
  385.9 466.3 %all-gather.8.cloned.1.call-start = ((), (), s32[]{:S(2)}) async-start(), calls=%async_computation.12 | async-start | bytes 2433024 | tf_op jit(solution)/shard_map/all_gather | solution.py:94
  386.4 513.7 %all-reduce.8.cloned.1.call-start = ((), (), s32[]{:S(2)}) async-start(), calls=%async_computation.13 | async-start | bytes 524288 | tf_op jit(solution)/shard_map/psum | solution.py:169
  427.3 271.7 %copy-start.6 = (bf16[128,1024]{1,0:T(8,128)(2,1)}, bf16[128,1024]{1,0:T(8,128)(2,1)S(1)}, u32[]{:S(2)}) copy-start(bf16[128,1024]{1,0:T(8,128)(2,1)S(1)} %multiply_convert_fusion.3) | copy-start | bytes 786436
  542.7 309.5 %copy-start.24 = (bf16[1,128,1024]{2,1,0:T(8,128)(2,1)S(1)}, bf16[1,128,1024]{2,1,0:T(8,128)(2,1)}, u32[]{:S(2)}) copy-start(bf16[1,128,1024]{2,1,0:T(8,128)(2,1)} %param.27) | copy-start | bytes 786436
  859.2 86.8 %reduce-scatter.28.cloned.1.call-start = ((), (), s32[]{:S(2)}) async-start(), calls=%async_computation.20 | async-start | bytes 294912
  909.4 74.8 %reduce-scatter.30.cloned.1.call-start = ((), (), s32[]{:S(2)}) async-start(), calls=%async_computation.21 | async-start | bytes 294912 | tf_op jit(solution)/shard_map/reshape | solution.py:225
  915.7 228.9 %reduce-scatter.20.cloned.1.call-start = ((), (), s32[]{:S(2)}) async-start(), calls=%async_computation.16 | async-start | bytes 270336 | tf_op jit(solution)/shard_map/reduce_scatter | solution.py:249
  986.0 317.1 %reduce-scatter.18.cloned.1.call-start = ((), (), s32[]{:S(2)}) async-start(), calls=%async_computation.15 | async-start | bytes 270336 | tf_op jit(solution)/shard_map/reduce_scatter | solution.py:246
  987.4 317.0 %all-reduce.10.cloned.1.call-start = ((), (), s32[]{:S(2)}) async-start(), calls=%async_computation.23 | async-start | bytes 1048576 | tf_op jit(solution)/shard_map/psum | solution.py:153
  990.0 472.0 %reduce-scatter.22.cloned.1.call-start = ((), (), s32[]{:S(2)}) async-start(), calls=%async_computation.17 | async-start | bytes 540672 | tf_op jit(solution)/shard_map/reduce_scatter | solution.py:252
  991.3 629.1 %reduce-scatter.16.cloned.1.call-start = ((), (), s32[]{:S(2)}) async-start(), calls=%async_computation.14 | async-start | bytes 540672 | tf_op jit(solution)/shard_map/reduce_scatter | solution.py:243
  992.5 790.5 %reduce-scatter.32.cloned.1.call-start = ((), (), s32[]{:S(2)}) async-start(), calls=%async_computation.22 | async-start | bytes 2433024
  997.2 948.7 %reduce-scatter.26.cloned.1.call-start = ((), (), s32[]{:S(2)}) async-start(), calls=%async_computation.19 | async-start | bytes 2433024 | tf_op jit(solution)/shard_map/reduce_scatter | solution.py:258
  1000.5 303.9 %copy-start.15 = (f32[128,1024]{1,0:T(8,128)S(1)}, f32[128,1024]{1,0:T(8,128)}, u32[]{:S(2)}) copy-start(f32[128,1024]{1,0:T(8,128)} %get-tuple-element.83) | copy-start | bytes 1572868
  1000.5 1108.4 %reduce-scatter.24.cloned.1.call-start = ((), (), s32[]{:S(2)}) async-start(), calls=%async_computation.18 | async-start | bytes 2433024 | tf_op jit(solution)/shard_map/reduce_scatter | solution.py:255
  1002.8 302.9 %copy-start.46 = (f32[1024]{0:T(1024)S(1)}, f32[1024]{0:T(1024)}, u32[]{:S(2)}) copy-start(f32[1024]{0:T(1024)} %get-tuple-element.39) | copy-start | bytes 12292
  1002.8 302.9 %copy-start.59 = (f32[64]{0:T(128)S(1)}, f32[64]{0:T(128)}, u32[]{:S(2)}) copy-start(f32[64]{0:T(128)} %get-tuple-element.41) | copy-start | bytes 772
  1002.8 366.2 %copy-start.5 = (f32[128,1024]{1,0:T(8,128)S(1)}, f32[128,1024]{1,0:T(8,128)}, u32[]{:S(2)}) copy-start(f32[128,1024]{1,0:T(8,128)} %copy-done.4) | copy-start | bytes 1572868
  (43 other events, 1103.0 us)
Sparse Core Ops, SparseCore 0:
  384.8 41.1 all-reduce.5
  859.3 40.8 all-reduce.7
  909.5 36.4 reduce-scatter.27
  948.2 35.9 reduce-scatter.29
  991.3 41.5 all-reduce.9
Sparse Core Ops, SparseCore 1:
  386.8 152.8 all-gather.5
  541.2 154.8 all-gather.3
  697.5 154.6 all-gather.7
  986.1 158.5 reduce-scatter.19
  1147.0 156.1 reduce-scatter.17
  1305.6 156.3 reduce-scatter.21
  1464.2 156.1 reduce-scatter.15
  1622.8 160.2 reduce-scatter.31
  1785.4 160.4 reduce-scatter.25
  1948.4 160.4 reduce-scatter.23
where the time goes:
time: 2120 us
  waiting for transfers between devices  1600 us (75%)
  blocking collectives  430 us (20%)
  matrix products  41.7 us (2%)
    unnamed x17, waiting for transfers between devices  193 us
    reduce_scatter x1, waiting for transfers between devices, local(): lax.psum_scatter(grad_wgate.astype(jnp.bfloat16), ('ctx', 'fsdp'), scatte...  161 us
    reduce_scatter x1, waiting for transfers between devices, local(): lax.psum_scatter(grad_wup.astype(jnp.bfloat16), ('ctx', 'fsdp'), scatter_...  161 us
    reduce_scatter x1, waiting for transfers between devices, local(): lax.psum_scatter(grad_wkey.astype(jnp.bfloat16), ('ctx', 'fsdp'), scatter...  157 us
    reduce_scatter x1, waiting for transfers between devices, local(): lax.psum_scatter(grad_wquery.astype(jnp.bfloat16), ('ctx', 'fsdp'), scatt...  157 us
    all_gather x1, waiting for transfers between devices, local(): lax.all_gather(w_gate, ('ctx', 'fsdp'), axis=0, tiled=True)  153 us
    all_gather x1, waiting for transfers between devices, local(): lax.all_gather(w_down, ('ctx', 'fsdp'), axis=0, tiled=True)  153 us
    reduce_scatter x1, waiting for transfers between devices, local(): lax.psum_scatter(grad_wvalue.astype(jnp.bfloat16), ('ctx', 'fsdp'), scatt...  142 us
  transfers between devices with their start and end apart: 15, of which 14 were waited for; matrix products, arithmetic and copies ran while one was open for 2% of the time, Pallas kernels for 0%

commit v1 on v0

v1 whole, which is shorter than its diff:
```python
import jax
import jax.numpy as jnp
from jax import lax
from jax.sharding import Mesh, PartitionSpec as P

HEAD_DIM = 64
EPSILON = 1e-05
ROPE_BASE = 1000000.0
AXES = ("zl", "y", "x", "zh", "c")
BF = jnp.bfloat16
F32 = jnp.float32


def rms_scale(values):
    return lax.rsqrt(jnp.mean(values * values, axis=-1, keepdims=True) + EPSILON)


def norm_grad(grad_norm, normal, scale_rows):
    return scale_rows * (grad_norm - normal * jnp.mean(grad_norm * normal, axis=-1, keepdims=True))


def rope_tables(places, head_dim):
    half_dim = head_dim // 2
    frequency = ROPE_BASE ** (-(jnp.arange(half_dim).astype(F32) * 2.0 / head_dim))
    angles = places.astype(F32)[..., None] * frequency
    return (jnp.cos(angles), jnp.sin(angles))


def rotate(values, cosine, sine):
    half = values.shape[-1] // 2
    low, high = values[..., :half], values[..., half:]
    cosine, sine = cosine[..., None, :], sine[..., None, :]
    return jnp.concatenate([low * cosine - high * sine, high * cosine + low * sine], axis=-1)


def rotate_back(values, cosine, sine):
    return rotate(values, cosine, -sine)


def dot(left, right):
    return jnp.dot(left, right, preferred_element_type=F32)


def left_product(left, right):
    return lax.dot_general(left, right, (((0,), (0,)), ((), ())), preferred_element_type=F32)


def right_product(left, right):
    return lax.dot_general(left, right, (((1,), (1,)), ((), ())), preferred_element_type=F32)


def swap(value, axes, size, mask):
    return lax.ppermute(value, axes, [(i, i ^ mask) for i in range(size)])


def fan(pieces, axes):
    return [swap(pieces[k], axes, 4, k) for k in (1, 2, 3)]


def spread(piece, axes):
    return jnp.stack([piece] + fan([piece] * 4, axes))


Z = ("zl", "zh")


def sum_scatter(partial):
    blocks = partial.reshape(4, 2, 32, partial.shape[-1])
    other = swap(blocks[:, 1].astype(BF), "c", 2, 1)
    pair = blocks[:, 0] + other.astype(F32)
    low = pair.astype(BF)
    total = pair[0]
    for got in fan([None] + [low[k] for k in (1, 2, 3)], Z):
        total = total + got.astype(F32)
    return total


def gather_rows(rows):
    column = spread(rows, Z)
    other = swap(column, "c", 2, 1)
    return jnp.stack([column, other], axis=1).reshape(256, rows.shape[-1])


def gather_head(rows, head):
    pair = jnp.stack([rows, swap(rows, "c", 2, 1)])
    quad = jnp.concatenate([pair, swap(pair, "zh", 2, 1)])
    return quad[head ^ jnp.arange(4)].reshape(128, rows.shape[-1])


def halves(parts, zl):
    low = jnp.concatenate([p[:, : p.shape[1] // 2] for p in parts], axis=1)
    high = jnp.concatenate([p[:, p.shape[1] // 2 :] for p in parts], axis=1)
    return jnp.where(zl == 0, low, high), jnp.where(zl == 0, high, low)


def in_order(own, other, zl, axis=0):
    return jnp.where(
        zl == 0, jnp.stack([own, other], axis=axis), jnp.stack([other, own], axis=axis)
    )


def local(
    tokens, positions, attn_gain, ffn_gain, query_gain, key_gain,
    w_query, w_key, w_value, w_out, w_gate, w_up, w_down, cotangent,
):
    zl, y, head = lax.axis_index("zl"), lax.axis_index("y"), lax.axis_index(("zh", "c"))
    scale = HEAD_DIM ** (-0.5)

    keep_a, send_a = halves([w_query, w_key, w_value, w_out], zl)
    keep_f, send_f = halves([w_gate, w_up, w_down], zl)
    got_a = swap(send_a, "zl", 2, 1)
    own_tokens = tokens[0].reshape(4, 32, 1024)[head ^ jnp.arange(4)].reshape(128, 1024)
    x_low = jnp.concatenate([own_tokens, swap(own_tokens, "zl", 2, 1)])
    got_f = swap(send_f, "zl", 2, 1)
    own_dy = cotangent[0].reshape(4, 32, 1024)[head ^ jnp.arange(4)].reshape(128, 1024)
    dy = jnp.concatenate([own_dy, swap(own_dy, "zl", 2, 1)])

    rows_f = in_order(keep_f, got_f, zl)
    full_f = lax.all_gather(rows_f, ("y", "x"), axis=0)
    full_f = jnp.transpose(full_f, (1, 0, 2, 3)).reshape(1024, -1)
    rows_a = in_order(keep_a, got_a, zl)
    full_a = lax.all_to_all(
        jnp.broadcast_to(rows_a[None], (16,) + rows_a.shape), ("y", "x"), 0, 0, tiled=True
    )
    full_a = jnp.transpose(full_a, (1, 0, 2, 3)).reshape(1024, -1)
    w_qkv, w_o = full_a[:, :256], full_a[:, 256:]
    gate_w, up_w, down_w = full_f[:, :576], full_f[:, 576:1152], full_f[:, 1152:]

    steps = jnp.array([dl * 16 + ky * 4 + d for ky in range(4) for dl in range(2) for d in range(4)])
    places = positions[0].reshape(32, 32)[steps ^ (zl * 16 + y * 4 + head)].reshape(1024)
    own_places = places[:256]

    x = x_low.astype(F32)
    x_scale = rms_scale(x)
    x_hat = x * x_scale
    normed = (x_hat * attn_gain).astype(BF)
    qkv = dot(normed, w_qkv)
    q = qkv[:, :128].reshape(256, 2, 64)
    k = qkv[:, 128:192].reshape(256, 1, 64)
    v = qkv[:, 192:].astype(BF)
    q_scale, k_scale = rms_scale(q), rms_scale(k)
    q_hat, k_hat = q * q_scale, k * k_scale
    cosine, sine = rope_tables(own_places, HEAD_DIM)
    qh = rotate(q_hat * query_gain, cosine, sine).astype(BF)
    kh = rotate(k_hat * key_gain, cosine, sine).astype(BF)
    kv = spread(jnp.concatenate([kh[:, 0], v], axis=1), "y").reshape(1024, 128)
    k_all, v_all = kv[:, :64], kv[:, 64:]
    visible = places[None, :] <= own_places[:, None]
    scores = jnp.einsum("tgd,sd->gts", qh, k_all, preferred_element_type=F32) * scale
    u = jnp.where(visible[None], jnp.exp(scores), 0.0)
    u_low = u.astype(BF)
    denom = jnp.sum(u, axis=-1).T[..., None]
    o = jnp.einsum("gts,sd->tgd", u_low, v_all, preferred_element_type=F32) / denom
    o_low = o.astype(BF).reshape(256, 128)

    own_x = x[:32]
    h = own_x + sum_scatter(right_product(o_low, w_o))
    h_scale = rms_scale(h)
    h_hat = h * h_scale
    hn = gather_rows((h_hat * ffn_gain).astype(BF))
    gate, up = dot(hn, gate_w), dot(hn, up_w)
    sig = jax.nn.sigmoid(gate)
    silu = gate * sig
    active = (silu * up).astype(BF)
    d_act = dot(dy, down_w)
    d_gate = (d_act * up * sig * (1.0 + gate * (1.0 - sig))).astype(BF)
    d_up = (d_act * silu).astype(BF)
    d_hn = right_product(d_gate, gate_w) + right_product(d_up, up_w)
    d_hn = sum_scatter(d_hn)

    branch = sum_scatter(right_product(active, down_w))
    block_out = gather_head((h + branch).astype(BF), head)[None]

    dw_f = jnp.concatenate(
        [left_product(hn, d_gate), left_product(hn, d_up), left_product(dy, active)], axis=1
    ).astype(BF)
    dw_f = jnp.transpose(dw_f.reshape(2, 16, 32, -1), (1, 0, 2, 3))
    dw_f = lax.psum_scatter(dw_f, ("y", "x"), scatter_dimension=0, tiled=True)[0]

    ffn_gain_part = jnp.sum(d_hn * h_hat, axis=0)
    dh = dy[:32].astype(F32) + norm_grad(d_hn * ffn_gain, h_hat, h_scale)
    d_attn = gather_rows(dh.astype(BF))
    d_o = dot(d_attn, w_o).reshape(256, 2, 64)
    d_inner = (d_o / denom).astype(BF)
    delta = (jnp.sum(d_o * o, axis=-1) / denom[..., 0]).T
    dp = jnp.einsum("tgd,sd->gts", d_inner, v_all, preferred_element_type=F32)
    ds = (u * (dp - delta[..., None])).astype(BF)
    d_kall = jnp.einsum("gts,tgd->sd", ds, qh, preferred_element_type=F32) * scale
    d_vall = jnp.einsum("gts,tgd->sd", u_low, d_inner, preferred_element_type=F32)
    d_kv = jnp.concatenate([d_kall, d_vall], axis=1).reshape(4, 256, 128)
    d_kv_low = d_kv.astype(BF)
    d_kv_sum = d_kv[0]
    for got in fan([d_kv_low[i] for i in range(4)], "y"):
        d_kv_sum = d_kv_sum + got.astype(F32)
    d_qh = jnp.einsum("gts,sd->tgd", ds, k_all, preferred_element_type=F32) * scale
    d_qn = rotate_back(d_qh, cosine, sine)
    d_kn = rotate_back(d_kv_sum[:, None, :64], cosine, sine)
    query_gain_part = jnp.sum(d_qn * q_hat, axis=(0, 1))
    key_gain_part = jnp.sum(d_kn * k_hat, axis=(0, 1))
    d_q = norm_grad(d_qn * query_gain, q_hat, q_scale).astype(BF).reshape(256, 128)
    d_k = norm_grad(d_kn * key_gain, k_hat, k_scale).astype(BF).reshape(256, 64)
    d_qkv = jnp.concatenate([d_q, d_k, d_kv_sum[:, 64:].astype(BF)], axis=1)
    d_xn_part = right_product(d_qkv, w_qkv)
    d_xn = sum_scatter(d_xn_part)

    dw_a = jnp.concatenate([left_product(normed, d_qkv), left_product(d_attn, o_low)], axis=1)
    dw_a = jnp.transpose(dw_a.astype(BF).reshape(2, 16, 32, -1), (1, 0, 2, 3))
    dw_a = lax.all_to_all(dw_a, ("y", "x"), 0, 0, tiled=True)
    dw_a = jnp.sum(dw_a.astype(F32), axis=0).astype(BF)

    def finish(total, widths):
        other = swap(jnp.where(zl == 0, total[1], total[0]), "zl", 2, 1)
        own = jnp.where(zl == 0, total[0], total[1])
        low, high = jnp.where(zl == 0, own, other), jnp.where(zl == 0, other, own)
        outs, at = [], 0
        for width in widths:
            pair = [low[:, at : at + width], high[:, at : at + width]]
            outs.append(jnp.concatenate(pair, axis=1).astype(F32))
            at += width
        return outs

    grad_wg, grad_wu, grad_wd = finish(dw_f, (576, 576, 576))
    grad_wq, grad_wk, grad_wv, grad_wo = finish(dw_a, (128, 64, 64, 128))

    own_hat = x_hat[:32]
    attn_gain_part = jnp.sum(d_xn * own_hat, axis=0)
    d_x = dh + norm_grad(d_xn * attn_gain, own_hat, x_scale[:32])
    tokens_grad = gather_head(d_x.astype(BF), head)[None]

    gains = jnp.concatenate([attn_gain_part, ffn_gain_part, query_gain_part, key_gain_part])
    gains = gains.reshape(17, 128)
    gains = gains + swap(gains, "c", 2, 1)
    for axes in (Z, "y", "x"):
        one, two, three = fan([gains] * 4, axes)
        gains = (gains + one) + (two + three)
    gains = gains.reshape(-1)
    return (
        block_out, tokens_grad, gains[:1024], gains[1024:2048], gains[2048:2112], gains[2112:],
        grad_wq, grad_wk, grad_wv, grad_wo, grad_wg, grad_wu, grad_wd,
    )


def solution(mesh):
    cube = Mesh(mesh.devices.reshape(2, 4, 4, 2, 2), AXES)
    rows = P("x", ("zl", "y"), None)
    weight = P(("zl", "y", "x"), ("zh", "c"))
    return jax.shard_map(
        local,
        mesh=cube,
        in_specs=(rows, P("x", None)) + (P(),) * 4 + (weight,) * 7 + (rows,),
        out_specs=(rows, rows) + (P(),) * 4 + (weight,) * 7,
        check_vma=False,
    )
```

time: 2120 us -> 247 us (0.12)
  waiting for transfers between devices: 1600 us -> 71.4 us
  blocking collectives: 430 us -> 0 us
  starting transfers between devices: 0.82 us -> 75.2 us
  local copies, waits for them, and re-layouts: 14 us -> 40.5 us
  matrix products: 41.7 us -> 19.3 us
    reduce_scatter x6 -> x0, waiting for transfers between devices: 869 us -> none  [the longest x1 161 us: local(): lax.psum_scatter(grad_wgate.astype(jnp.bfloat16), ('ctx', 'fsdp'), scatte...]
    all_gather x3 -> x1, waiting for transfers between devices: 419 us -> 0.02 us  [local(): full_f = lax.all_gather(rows_f, ('y', 'x'), axis=0)]
    all_gather x6 -> x0, blocking collectives: 367 us -> none  [the longest x1 83.5 us: local(): lax.all_gather(w_key, ('ctx', 'fsdp'), axis=0, tiled=True)]
    unnamed x17 -> x3, waiting for transfers between devices: 193 us -> 20.8 us
    psum x3 -> x0, waiting for transfers between devices: 77.1 us -> none  [the longest x1 39.5 us: local(): attn_out = lax.psum(right_product(attn_low, out_full), 'head')]
    ppermute x0 -> x50, starting transfers between devices: none -> 64.4 us  [swap(): return lax.ppermute(value, axes, [(i, i ^ mask) for i in range(size)])]
    psum x1 -> x0, blocking collectives: 63.3 us -> none  [local(): lax.psum((attn_gain_part, ffn_gain_part, query_gain_part, key_gain_part),...]
    ppermute x0 -> x50, waiting for transfers between devices: none -> 38.6 us  [swap(): return lax.ppermute(value, axes, [(i, i ^ mask) for i in range(size)])]
  transfers between devices with their start and end apart: 15 -> 54, of which waited for: 14 -> 22; matrix products, arithmetic and copies ran while one was open for 2% -> 29% of each run, Pallas kernels for 0% -> 0%
where the time goes in v1:
time: 247 us; the launch traced here: 245 us
  starting transfers between devices  75.2 us (30%)
  waiting for transfers between devices  71.4 us (29%)
  local copies, waits for them, and re-layouts  40.5 us (16%)
  other arithmetic  23.5 us (10%)
  matrix products  19.3 us (8%)
  between operations  15.4 us (6%)
    ppermute x50, starting transfers between devices, swap(): return lax.ppermute(value, axes, [(i, i ^ mask) for i in range(size)])  64.4 us
    ppermute x50, waiting for transfers between devices, swap(): return lax.ppermute(value, axes, [(i, i ^ mask) for i in range(size)])  38.6 us
    unnamed x3, waiting for transfers between devices  20.8 us
    all_to_all x1, waiting for transfers between devices, local(): lax.all_to_all(jnp.broadcast_to(rows_a[None], (16,) + rows_a.shape), ('y'...  12 us
    dot_general x5, matrix products, left_product(): lax.dot_general(left, right, (((0,), (0,)), ((), ())), preferred_element_...  7.56 us
    all_to_all x1, starting transfers between devices, local(): lax.all_to_all(jnp.broadcast_to(rows_a[None], (16,) + rows_a.shape), ('y'...  7.17 us
    concatenate x1, local copies, waits for them, and re-layouts, local(): jnp.concatenate([left_product(hn, d_gate), left_product(hn, d_up), left_p...  7.04 us
    unnamed x122, local copies, waits for them, and re-layouts  5.02 us
  transfers between devices with their start and end apart: 54, of which 22 were waited for; matrix products, arithmetic and copies ran while one was open for 29% of the time, Pallas kernels for 0%

profile of v1, /device:TPU:0, one launch (start us, length us, event | category | flops | bytes accessed | tf_op | source)
XLA Modules:
  0.0 245.3 jit_solution(5433622415289235833)
XLA Ops:
  8.7 2.1 collective-permute-start
  14.8 2.1 collective-permute-start.13
  17.2 2.9 %collective-permute-done.13 = bf16[32,1728]{1,0:T(8,128)(2,1)S(1)} collective-permute-done((bf16[32,1728]{1,0:T(8,128)(2,1)S(1)}, bf16[32,1728]{1,0:T(8,128)(2,1)S(1)}, u32[]{:S(2)}, u32[]{:S(2)}) %collective-permute-start.13) | collective-permute-done | bytes 110624 | tf_op jit(solution)/shard_map/ppermute | solution.py:53
  21.9 7.2 %all-to-all-start = ((bf16[16,2,32,384]{3,2,1,0:T(8,128)(2,1)}), bf16[16,2,32,384]{3,2,1,0:T(8,128)(2,1)S(1)}, u32[]{:S(2)}, u32[]{:S(2)}) async-start(bf16[16,2,32,384]{3,2,1,0:T(8,128)(2,1)} %broadcast_in_dim.14), calls=%async_computation | async-start | bytes 1572864 | tf_op jit(solution)/shard_map/all_to_all | solution.py:122
  33.1 12.0 %all-to-all-done = bf16[16,2,32,384]{3,2,1,0:T(8,128)(2,1)S(1)} async-done(((bf16[16,2,32,384]{3,2,1,0:T(8,128)(2,1)}), bf16[16,2,32,384]{3,2,1,0:T(8,128)(2,1)S(1)}, u32[]{:S(2)}, u32[]{:S(2)}) %all-to-all-start) | async-done | bytes 786464 | tf_op jit(solution)/shard_map/all_to_all | solution.py:122
  47.2 3.1 %collective-permute-start.2 = (bf16[256,128]{0,1:T(8,128)(2,1)S(1)}, bf16[256,128]{0,1:T(8,128)(2,1)S(1)}, u32[]{:S(2)}, u32[]{:S(2)}) collective-permute-start(bf16[256,128]{0,1:T(8,128)(2,1)S(1)} %get-tuple-element.90), channel_id=1, source_target_pairs={{0,16},{16,0},{32,48},{48,32},{1,17},{17,1},{33,49},{49,33},{2,18}... | collective-permute-start | bytes 196616 | tf_op jit(solution)/shard_map/ppermute | solution.py:53
  60.7 2.4 gather_fusion.3
  68.5 2.7 %collective-permute-start.8 = (bf16[32,1024]{1,0:T(8,128)(2,1)S(1)}, bf16[32,1024]{1,0:T(8,128)(2,1)S(1)}, u32[]{:S(2)}, u32[]{:S(2)}) collective-permute-start(bf16[32,1024]{1,0:T(8,128)(2,1)S(1)} %get-tuple-element.55), channel_id=1, source_target_pairs={{0,66},{2,64},{64,2},{66,0},{1,67},{3,65},{65,3},{67,1},{4,70},{6,... | collective-permute-start | bytes 196616 | tf_op jit(solution)/shard_map/ppermute | solution.py:53
  74.1 1.9 collective-permute-done.7
  75.9 2.2 collective-permute-done.6
  79.7 3.6 %collective-permute-start.9 = (bf16[32,1024]{1,0:T(8,128)(2,1)S(1)}, bf16[32,1024]{1,0:T(8,128)(2,1)S(1)}, u32[]{:S(2)}, u32[]{:S(2)}) collective-permute-start(bf16[32,1024]{1,0:T(8,128)(2,1)S(1)} %multiply_convert_fusion.6), channel_id=1, source_target_pairs={{0,2},{2,0},{64,66},{66,64},{1,3},{3,1},{65,67},{67,65},{4,6},{6,4... | collective-permute-start | bytes 196616 | tf_op jit(solution)/shard_map/ppermute | solution.py:53
  90.4 2.5 %copy.77 = bf16[2,16,32,1728]{3,2,1,0:T(8,128)(2,1)S(1)} copy(bf16[2,16,32,1728]{3,2,0,1:T(8,128)(2,1)} %bitcast.358) | data formatting | bytes 7077888 | tf_op jit(solution)/shard_map/transpose | solution.py:120
  103.4 1.9 collective-permute-start.22
  107.0 2.1 collective-permute-done.22
  112.4 2.8 %collective-permute-start.25 = (bf16[32,1024]{1,0:T(8,128)(2,1)}, bf16[32,1024]{1,0:T(8,128)(2,1)}, u32[]{:S(2)}, u32[]{:S(2)}) collective-permute-start(bf16[32,1024]{1,0:T(8,128)(2,1)} %fusion.87), channel_id=1, source_target_pairs={{0,2},{2,0},{64,66},{66,64},{1,3},{3,1},{65,67},{67,65},{4,6},{6,4... | collective-permute-start | bytes 196616 | tf_op jit(solution)/shard_map/ppermute | solution.py:53
  119.6 2.9 %convolution_convert_fusion = bf16[2,16,32,576]{3,2,1,0:T(8,128)(2,1)} fusion(bf16[2,16,32,256]{3,2,1,0:T(8,128)(2,1)} %bitcast.343, bf16[256,576]{0,1:T(8,128)(2,1)} %copy-done.19), kind=kOutput, calls=%fused_computation.9 | convolution fusion | flops 302579712 | bytes 1998848 | tf_op jit(solution)/shard_map/dot_general | solution.py:45
  122.5 7.0 %concatenate.256 = bf16[2,16,32,1728]{3,2,1,0:T(8,128)(2,1)} concatenate(bf16[2,16,32,576]{3,2,1,0:T(8,128)(2,1)} %convolution_convert_fusion.1, bf16[2,16,32,576]{3,2,1,0:T(8,128)(2,1)} %convolution_convert_fusion, bf16[2,16,32,576]{3,2,1,0:T(8,128)(2,1)} %bitcast.339), dimensions={3} | concatenate | bytes 7077888 | tf_op jit(solution)/shard_map/concatenate | solution.py:174
  133.0 2.0 collective-permute-start.31
  139.3 3.3 %collective-permute-done.30 = bf16[256,128]{0,1:T(8,128)(2,1)S(1)} collective-permute-done((bf16[256,128]{0,1:T(8,128)(2,1)S(1)}, bf16[256,128]{0,1:T(8,128)(2,1)S(1)}, u32[]{:S(2)}, u32[]{:S(2)}) %collective-permute-start.30) | collective-permute-done | bytes 65568 | tf_op jit(solution)/shard_map/ppermute | solution.py:53
  153.7 2.8 %collective-permute-start.33 = (bf16[32,1024]{1,0:T(8,128)(2,1)S(1)}, bf16[32,1024]{1,0:T(8,128)(2,1)S(1)}, u32[]{:S(2)}, u32[]{:S(2)}) collective-permute-start(bf16[32,1024]{1,0:T(8,128)(2,1)S(1)} %get-tuple-element.38), channel_id=1, source_target_pairs={{0,2},{2,0},{64,66},{66,64},{1,3},{3,1},{65,67},{67,65},{4,6},{6,4... | collective-permute-start | bytes 196616 | tf_op jit(solution)/shard_map/ppermute | solution.py:53
  157.6 1.9 collective-permute-done.33
  164.2 1.9 collective-permute-start.41
  167.8 3.6 %all-to-all-start.1 = ((bf16[16,2,32,384]{3,2,1,0:T(8,128)(2,1)}), bf16[16,2,32,384]{3,2,1,0:T(8,128)(2,1)S(1)}, u32[]{:S(2)}, u32[]{:S(2)}) async-start(bf16[16,2,32,384]{3,2,1,0:T(8,128)(2,1)} %copy_bitcast_fusion), calls=%async_computation.1 | async-start | bytes 1572864 | tf_op jit(solution)/shard_map/all_to_all | solution.py:208
  171.5 3.4 %collective-permute-start.43 = (f32[17,128]{1,0:T(8,128)S(1)}, f32[17,128]{1,0:T(8,128)S(1)}, u32[]{:S(2)}, u32[]{:S(2)}) collective-permute-start(f32[17,128]{1,0:T(8,128)S(1)} %add_add_fusion.2), channel_id=1, source_target_pairs={{0,32},{16,48},{32,0},{48,16},{1,33},{17,49},{33,1},{49,17},{2,34}... | collective-permute-start | bytes 26120 | tf_op jit(solution)/shard_map/ppermute | solution.py:53
  176.1 6.9 %collective-permute-done.43 = f32[17,128]{1,0:T(8,128)S(1)} collective-permute-done((f32[17,128]{1,0:T(8,128)S(1)}, f32[17,128]{1,0:T(8,128)S(1)}, u32[]{:S(2)}, u32[]{:S(2)}) %collective-permute-start.43) | collective-permute-done | bytes 8736 | tf_op jit(solution)/shard_map/ppermute | solution.py:53
  183.0 3.0 %collective-permute-start.15 = (bf16[32,1024]{1,0:T(8,128)(2,1)S(1)}, bf16[32,1024]{1,0:T(8,128)(2,1)S(1)}, u32[]{:S(2)}, u32[]{:S(2)}) collective-permute-start(bf16[32,1024]{1,0:T(8,128)(2,1)S(1)} %copy-done.36), channel_id=1, source_target_pairs={{0,2},{2,0},{64,66},{66,64},{1,3},{3,1},{65,67},{67,65},{4,6},{6,4... | collective-permute-start | bytes 196616 | tf_op jit(solution)/shard_map/ppermute | solution.py:53
  185.9 3.9 %collective-permute-start.46 = (f32[17,128]{1,0:T(8,128)S(1)}, f32[17,128]{1,0:T(8,128)S(1)}, u32[]{:S(2)}, u32[]{:S(2)}) collective-permute-start(f32[17,128]{1,0:T(8,128)S(1)} %add_add_fusion.1), channel_id=1, source_target_pairs={{0,8},{4,12},{8,0},{12,4},{1,9},{5,13},{9,1},{13,5},{2,10},{6,14},... | collective-permute-start | bytes 26120 | tf_op jit(solution)/shard_map/ppermute | solution.py:53
  192.2 2.6 %collective-permute-done.47 = f32[17,128]{1,0:T(8,128)S(1)} collective-permute-done((f32[17,128]{1,0:T(8,128)S(1)}, f32[17,128]{1,0:T(8,128)S(1)}, u32[]{:S(2)}, u32[]{:S(2)}) %collective-permute-start.47) | collective-permute-done | bytes 8736 | tf_op jit(solution)/shard_map/ppermute | solution.py:53
  197.0 2.7 %collective-permute-start.37 = (bf16[2,32,1024]{2,1,0:T(8,128)(2,1)S(1)}, bf16[2,32,1024]{2,1,0:T(8,128)(2,1)S(1)}, u32[]{:S(2)}, u32[]{:S(2)}) collective-permute-start(bf16[2,32,1024]{2,1,0:T(8,128)(2,1)S(1)} %pad_maximum_fusion.15), channel_id=1, source_target_pairs={{0,2},{2,0},{1,3},{3,1},{4,6},{6,4},{5,7},{7,5},{8,10},{10,8},{9,1... | collective-permute-start | bytes 393224 | tf_op jit(solution)/shard_map/ppermute | solution.py:53
  199.7 2.5 %collective-permute-done.19 = bf16[2,32,1024]{2,1,0:T(8,128)(2,1)S(1)} collective-permute-done((bf16[2,32,1024]{2,1,0:T(8,128)(2,1)S(1)}, bf16[2,32,1024]{2,1,0:T(8,128)(2,1)S(1)}, u32[]{:S(2)}, u32[]{:S(2)}) %collective-permute-start.19) | collective-permute-done | bytes 131104 | tf_op jit(solution)/shard_map/ppermute | solution.py:53
  208.8 20.8 %all-reduce.3.cloned.1.call-done = bf16[16,2,32,1728]{3,2,0,1:T(8,128)(2,1)} async-done(((bf16[16,2,32,1728]{3,2,0,1:T(8,128)(2,1)}), bf16[16,2,32,1728]{3,2,0,1:T(8,128)(2,1)}) %all-reduce.3.cloned.1.call-update) | async-done | bytes 3538960
  233.5 2.6 %collective-permute-done.49 = bf16[32,1728]{1,0:T(8,128)(2,1)S(1)} collective-permute-done((bf16[32,1728]{1,0:T(8,128)(2,1)S(1)}, bf16[32,1728]{1,0:T(8,128)(2,1)S(1)}, u32[]{:S(2)}, u32[]{:S(2)}) %collective-permute-start.49) | collective-permute-done | bytes 110624 | tf_op jit(solution)/shard_map/ppermute | solution.py:53
  (359 shorter events, 105.0 us)
Async XLA Ops:
  7.2 83.2 %all-gather.2.cloned.1.call-start = ((), (), s32[]{:S(2)}) async-start(), calls=%async_computation.2 | async-start | bytes 3899392 | tf_op jit(solution)/shard_map/all_gather | solution.py:119
  8.7 24.2 %collective-permute-start = (bf16[128,1024]{1,0:T(8,128)(2,1)S(1)}, bf16[128,1024]{1,0:T(8,128)(2,1)S(1)}, u32[]{:S(2)}, u32[]{:S(2)}) collective-permute-start(bf16[128,1024]{1,0:T(8,128)(2,1)S(1)} %bitcast.348), channel_id=1, source_target_pairs={{0,64},{64,0},{1,65},{65,1},{2,66},{66,2},{3,67},{67,3},{4,68},{68... | collective-permute-start | bytes 786440 | tf_op jit(solution)/shard_map/ppermute | solution.py:53
  12.5 8.4 %collective-permute-start.1 = (bf16[32,384]{1,0:T(8,128)(2,1)S(1)}, bf16[32,384]{1,0:T(8,128)(2,1)S(1)}, u32[]{:S(2)}, u32[]{:S(2)}) collective-permute-start(bf16[32,384]{1,0:T(8,128)(2,1)S(1)} %maximum_select_fusion.3), channel_id=1, source_target_pairs={{0,64},{64,0},{1,65},{65,1},{2,66},{66,2},{3,67},{67,3},{4,68},{68... | collective-permute-start | bytes 73736 | tf_op jit(solution)/shard_map/ppermute | solution.py:53
  21.9 23.2 %all-to-all-start = ((bf16[16,2,32,384]{3,2,1,0:T(8,128)(2,1)}), bf16[16,2,32,384]{3,2,1,0:T(8,128)(2,1)S(1)}, u32[]{:S(2)}, u32[]{:S(2)}) async-start(bf16[16,2,32,384]{3,2,1,0:T(8,128)(2,1)} %broadcast_in_dim.14), calls=%async_computation | async-start | bytes 1572864 | tf_op jit(solution)/shard_map/all_to_all | solution.py:122
  29.1 200.5 %all-reduce.3.cloned.1.call-start = ((), (), s32[]{:S(2)}) async-start(), calls=%async_computation.3 | async-start | bytes 7340032
  47.2 6.0 %collective-permute-start.2 = (bf16[256,128]{0,1:T(8,128)(2,1)S(1)}, bf16[256,128]{0,1:T(8,128)(2,1)S(1)}, u32[]{:S(2)}, u32[]{:S(2)}) collective-permute-start(bf16[256,128]{0,1:T(8,128)(2,1)S(1)} %get-tuple-element.90), channel_id=1, source_target_pairs={{0,16},{16,0},{32,48},{48,32},{1,17},{17,1},{33,49},{49,33},{2,18}... | collective-permute-start | bytes 196616 | tf_op jit(solution)/shard_map/ppermute | solution.py:53
  60.7 6.6 %collective-permute-start.5 = (bf16[4,32,1024]{2,1,0:T(8,128)(2,1)}, bf16[4,32,1024]{2,1,0:T(8,128)(2,1)}, u32[]{:S(2)}, u32[]{:S(2)}) collective-permute-start(bf16[4,32,1024]{2,1,0:T(8,128)(2,1)} %fusion.30), channel_id=1, source_target_pairs={{0,1},{1,0},{2,3},{3,2},{4,5},{5,4},{6,7},{7,6},{8,9},{9,8},{10,11... | collective-permute-start | bytes 786440 | tf_op jit(solution)/shard_map/ppermute | solution.py:53
  63.1 31.8 %collective-permute-start.20 = (bf16[128,1024]{1,0:T(8,128)(2,1)}, bf16[128,1024]{1,0:T(8,128)(2,1)}, u32[]{:S(2)}, u32[]{:S(2)}) collective-permute-start(bf16[128,1024]{1,0:T(8,128)(2,1)} %bitcast.370), channel_id=1, source_target_pairs={{0,64},{64,0},{1,65},{65,1},{2,66},{66,2},{3,67},{67,3},{4,68},{68... | collective-permute-start | bytes 786440 | tf_op jit(solution)/shard_map/ppermute | solution.py:53
  78.5 6.3 %collective-permute-start.11 = (bf16[32,1024]{1,0:T(8,128)(2,1)S(1)}, bf16[32,1024]{1,0:T(8,128)(2,1)S(1)}, u32[]{:S(2)}, u32[]{:S(2)}) collective-permute-start(bf16[32,1024]{1,0:T(8,128)(2,1)S(1)} %multiply_convert_fusion.6), channel_id=1, source_target_pairs={{0,66},{2,64},{64,2},{66,0},{1,67},{3,65},{65,3},{67,1},{4,70},{6,... | collective-permute-start | bytes 196616 | tf_op jit(solution)/shard_map/ppermute | solution.py:53
  79.7 6.5 %collective-permute-start.9 = (bf16[32,1024]{1,0:T(8,128)(2,1)S(1)}, bf16[32,1024]{1,0:T(8,128)(2,1)S(1)}, u32[]{:S(2)}, u32[]{:S(2)}) collective-permute-start(bf16[32,1024]{1,0:T(8,128)(2,1)S(1)} %multiply_convert_fusion.6), channel_id=1, source_target_pairs={{0,2},{2,0},{64,66},{66,64},{1,3},{3,1},{65,67},{67,65},{4,6},{6,4... | collective-permute-start | bytes 196616 | tf_op jit(solution)/shard_map/ppermute | solution.py:53
  100.4 45.5 %collective-permute-start.14 = (bf16[4,32,1024]{2,1,0:T(8,128)(2,1)}, bf16[4,32,1024]{2,1,0:T(8,128)(2,1)}, u32[]{:S(2)}, u32[]{:S(2)}) collective-permute-start(bf16[4,32,1024]{2,1,0:T(8,128)(2,1)} %fusion.31), channel_id=1, source_target_pairs={{0,1},{1,0},{2,3},{3,2},{4,5},{5,4},{6,7},{7,6},{8,9},{9,8},{10,11... | collective-permute-start | bytes 786440 | tf_op jit(solution)/shard_map/ppermute | solution.py:53
  100.5 6.5 %collective-permute-start.24 = (bf16[32,1024]{1,0:T(8,128)(2,1)S(1)}, bf16[32,1024]{1,0:T(8,128)(2,1)S(1)}, u32[]{:S(2)}, u32[]{:S(2)}) collective-permute-start(bf16[32,1024]{1,0:T(8,128)(2,1)S(1)} %get-tuple-element.47), channel_id=1, source_target_pairs={{0,66},{2,64},{64,2},{66,0},{1,67},{3,65},{65,3},{67,1},{4,70},{6,... | collective-permute-start | bytes 196616 | tf_op jit(solution)/shard_map/ppermute | solution.py:53
  110.6 7.6 %collective-permute-start.27 = (bf16[32,1024]{1,0:T(8,128)(2,1)}, bf16[32,1024]{1,0:T(8,128)(2,1)}, u32[]{:S(2)}, u32[]{:S(2)}) collective-permute-start(bf16[32,1024]{1,0:T(8,128)(2,1)} %fusion.87), channel_id=1, source_target_pairs={{0,66},{2,64},{64,2},{66,0},{1,67},{3,65},{65,3},{67,1},{4,70},{6,... | collective-permute-start | bytes 196616 | tf_op jit(solution)/shard_map/ppermute | solution.py:53
  111.9 6.2 %collective-permute-start.26 = (bf16[32,1024]{1,0:T(8,128)(2,1)}, bf16[32,1024]{1,0:T(8,128)(2,1)}, u32[]{:S(2)}, u32[]{:S(2)}) collective-permute-start(bf16[32,1024]{1,0:T(8,128)(2,1)} %fusion.87), channel_id=1, source_target_pairs={{0,64},{2,66},{64,0},{66,2},{1,65},{3,67},{65,1},{67,3},{4,68},{6,... | collective-permute-start | bytes 196616 | tf_op jit(solution)/shard_map/ppermute | solution.py:53
  112.4 6.1 %collective-permute-start.25 = (bf16[32,1024]{1,0:T(8,128)(2,1)}, bf16[32,1024]{1,0:T(8,128)(2,1)}, u32[]{:S(2)}, u32[]{:S(2)}) collective-permute-start(bf16[32,1024]{1,0:T(8,128)(2,1)} %fusion.87), channel_id=1, source_target_pairs={{0,2},{2,0},{64,66},{66,64},{1,3},{3,1},{65,67},{67,65},{4,6},{6,4... | collective-permute-start | bytes 196616 | tf_op jit(solution)/shard_map/ppermute | solution.py:53
  119.5 10.0 %collective-permute-start.28 = (bf16[4,32,1024]{2,1,0:T(8,128)(2,1)S(1)}, bf16[4,32,1024]{2,1,0:T(8,128)(2,1)S(1)}, u32[]{:S(2)}, u32[]{:S(2)}) collective-permute-start(bf16[4,32,1024]{2,1,0:T(8,128)(2,1)S(1)} %get-tuple-element.45), channel_id=1, source_target_pairs={{0,1},{1,0},{2,3},{3,2},{4,5},{5,4},{6,7},{7,6},{8,9},{9,8},{10,11... | collective-permute-start | bytes 786440 | tf_op jit(solution)/shard_map/ppermute | solution.py:53
  133.0 6.3 %collective-permute-start.31 = (bf16[256,128]{0,1:T(8,128)(2,1)S(1)}, bf16[256,128]{0,1:T(8,128)(2,1)S(1)}, u32[]{:S(2)}, u32[]{:S(2)}) collective-permute-start(bf16[256,128]{0,1:T(8,128)(2,1)S(1)} %get-tuple-element.42), channel_id=1, source_target_pairs={{0,48},{16,32},{32,16},{48,0},{1,49},{17,33},{33,17},{49,1},{2,50}... | collective-permute-start | bytes 196616 | tf_op jit(solution)/shard_map/ppermute | solution.py:53
  135.0 7.5 %collective-permute-start.30 = (bf16[256,128]{0,1:T(8,128)(2,1)S(1)}, bf16[256,128]{0,1:T(8,128)(2,1)S(1)}, u32[]{:S(2)}, u32[]{:S(2)}) collective-permute-start(bf16[256,128]{0,1:T(8,128)(2,1)S(1)} %get-tuple-element.43), channel_id=1, source_target_pairs={{0,32},{16,48},{32,0},{48,16},{1,33},{17,49},{33,1},{49,17},{2,34}... | collective-permute-start | bytes 196616 | tf_op jit(solution)/shard_map/ppermute | solution.py:53
  136.5 7.3 %collective-permute-start.29 = (bf16[256,128]{0,1:T(8,128)(2,1)S(1)}, bf16[256,128]{0,1:T(8,128)(2,1)S(1)}, u32[]{:S(2)}, u32[]{:S(2)}) collective-permute-start(bf16[256,128]{0,1:T(8,128)(2,1)S(1)} %get-tuple-element.41), channel_id=1, source_target_pairs={{0,16},{16,0},{32,48},{48,32},{1,17},{17,1},{33,49},{49,33},{2,18}... | collective-permute-start | bytes 196616 | tf_op jit(solution)/shard_map/ppermute | solution.py:53
  147.7 42.6 %collective-permute-start.17 = (bf16[32,1024]{1,0:T(8,128)(2,1)}, bf16[32,1024]{1,0:T(8,128)(2,1)}, u32[]{:S(2)}, u32[]{:S(2)}) collective-permute-start(bf16[32,1024]{1,0:T(8,128)(2,1)} %get-tuple-element.50), channel_id=1, source_target_pairs={{0,66},{2,64},{64,2},{66,0},{1,67},{3,65},{65,3},{67,1},{4,70},{6,... | collective-permute-start | bytes 196616 | tf_op jit(solution)/shard_map/ppermute | solution.py:53
  149.1 41.4 %collective-permute-start.16 = (bf16[32,1024]{1,0:T(8,128)(2,1)}, bf16[32,1024]{1,0:T(8,128)(2,1)}, u32[]{:S(2)}, u32[]{:S(2)}) collective-permute-start(bf16[32,1024]{1,0:T(8,128)(2,1)} %get-tuple-element.51), channel_id=1, source_target_pairs={{0,64},{2,66},{64,0},{66,2},{1,65},{3,67},{65,1},{67,3},{4,68},{6,... | collective-permute-start | bytes 196616 | tf_op jit(solution)/shard_map/ppermute | solution.py:53
  151.7 5.9 %collective-permute-start.35 = (bf16[32,1024]{1,0:T(8,128)(2,1)S(1)}, bf16[32,1024]{1,0:T(8,128)(2,1)S(1)}, u32[]{:S(2)}, u32[]{:S(2)}) collective-permute-start(bf16[32,1024]{1,0:T(8,128)(2,1)S(1)} %get-tuple-element.39), channel_id=1, source_target_pairs={{0,66},{2,64},{64,2},{66,0},{1,67},{3,65},{65,3},{67,1},{4,70},{6,... | collective-permute-start | bytes 196616 | tf_op jit(solution)/shard_map/ppermute | solution.py:53
  162.7 8.8 %collective-permute-start.40 = (f32[17,128]{1,0:T(8,128)S(1)}, f32[17,128]{1,0:T(8,128)S(1)}, u32[]{:S(2)}, u32[]{:S(2)}) collective-permute-start(f32[17,128]{1,0:T(8,128)S(1)} %bitcast_add_fusion), channel_id=1, source_target_pairs={{0,64},{2,66},{64,0},{66,2},{1,65},{3,67},{65,1},{67,3},{4,68},{6,... | collective-permute-start | bytes 26120 | tf_op jit(solution)/shard_map/ppermute | solution.py:53
  164.2 7.3 %collective-permute-start.41 = (f32[17,128]{1,0:T(8,128)S(1)}, f32[17,128]{1,0:T(8,128)S(1)}, u32[]{:S(2)}, u32[]{:S(2)}) collective-permute-start(f32[17,128]{1,0:T(8,128)S(1)} %bitcast_add_fusion), channel_id=1, source_target_pairs={{0,66},{2,64},{64,2},{66,0},{1,67},{3,65},{65,3},{67,1},{4,70},{6,... | collective-permute-start | bytes 26120 | tf_op jit(solution)/shard_map/ppermute | solution.py:53
  167.8 34.4 %all-to-all-start.1 = ((bf16[16,2,32,384]{3,2,1,0:T(8,128)(2,1)}), bf16[16,2,32,384]{3,2,1,0:T(8,128)(2,1)S(1)}, u32[]{:S(2)}, u32[]{:S(2)}) async-start(bf16[16,2,32,384]{3,2,1,0:T(8,128)(2,1)} %copy_bitcast_fusion), calls=%async_computation.1 | async-start | bytes 1572864 | tf_op jit(solution)/shard_map/all_to_all | solution.py:208
  171.5 11.5 %collective-permute-start.43 = (f32[17,128]{1,0:T(8,128)S(1)}, f32[17,128]{1,0:T(8,128)S(1)}, u32[]{:S(2)}, u32[]{:S(2)}) collective-permute-start(f32[17,128]{1,0:T(8,128)S(1)} %add_add_fusion.2), channel_id=1, source_target_pairs={{0,32},{16,48},{32,0},{48,16},{1,33},{17,49},{33,1},{49,17},{2,34}... | collective-permute-start | bytes 26120 | tf_op jit(solution)/shard_map/ppermute | solution.py:53
  174.9 11.0 %collective-permute-start.44 = (f32[17,128]{1,0:T(8,128)S(1)}, f32[17,128]{1,0:T(8,128)S(1)}, u32[]{:S(2)}, u32[]{:S(2)}) collective-permute-start(f32[17,128]{1,0:T(8,128)S(1)} %add_add_fusion.2), channel_id=1, source_target_pairs={{0,48},{16,32},{32,16},{48,0},{1,49},{17,33},{33,17},{49,1},{2,50}... | collective-permute-start | bytes 26120 | tf_op jit(solution)/shard_map/ppermute | solution.py:53
  176.1 9.9 %collective-permute-start.42 = (f32[17,128]{1,0:T(8,128)S(1)}, f32[17,128]{1,0:T(8,128)S(1)}, u32[]{:S(2)}, u32[]{:S(2)}) collective-permute-start(f32[17,128]{1,0:T(8,128)S(1)} %add_add_fusion.2), channel_id=1, source_target_pairs={{0,16},{16,0},{32,48},{48,32},{1,17},{17,1},{33,49},{49,33},{2,18}... | collective-permute-start | bytes 26120 | tf_op jit(solution)/shard_map/ppermute | solution.py:53
  183.0 7.5 %collective-permute-start.15 = (bf16[32,1024]{1,0:T(8,128)(2,1)S(1)}, bf16[32,1024]{1,0:T(8,128)(2,1)S(1)}, u32[]{:S(2)}, u32[]{:S(2)}) collective-permute-start(bf16[32,1024]{1,0:T(8,128)(2,1)S(1)} %copy-done.36), channel_id=1, source_target_pairs={{0,2},{2,0},{64,66},{66,64},{1,3},{3,1},{65,67},{67,65},{4,6},{6,4... | collective-permute-start | bytes 196616 | tf_op jit(solution)/shard_map/ppermute | solution.py:53
  185.9 6.3 %collective-permute-start.46 = (f32[17,128]{1,0:T(8,128)S(1)}, f32[17,128]{1,0:T(8,128)S(1)}, u32[]{:S(2)}, u32[]{:S(2)}) collective-permute-start(f32[17,128]{1,0:T(8,128)S(1)} %add_add_fusion.1), channel_id=1, source_target_pairs={{0,8},{4,12},{8,0},{12,4},{1,9},{5,13},{9,1},{13,5},{2,10},{6,14},... | collective-permute-start | bytes 26120 | tf_op jit(solution)/shard_map/ppermute | solution.py:53
  195.4 6.8 %collective-permute-start.19 = (bf16[2,32,1024]{2,1,0:T(8,128)(2,1)S(1)}, bf16[2,32,1024]{2,1,0:T(8,128)(2,1)S(1)}, u32[]{:S(2)}, u32[]{:S(2)}) collective-permute-start(bf16[2,32,1024]{2,1,0:T(8,128)(2,1)S(1)} %pad_maximum_fusion.12), channel_id=1, source_target_pairs={{0,2},{2,0},{1,3},{3,1},{4,6},{6,4},{5,7},{7,5},{8,10},{10,8},{9,1... | collective-permute-start | bytes 393224 | tf_op jit(solution)/shard_map/ppermute | solution.py:53
  197.0 6.8 %collective-permute-start.37 = (bf16[2,32,1024]{2,1,0:T(8,128)(2,1)S(1)}, bf16[2,32,1024]{2,1,0:T(8,128)(2,1)S(1)}, u32[]{:S(2)}, u32[]{:S(2)}) collective-permute-start(bf16[2,32,1024]{2,1,0:T(8,128)(2,1)S(1)} %pad_maximum_fusion.15), channel_id=1, source_target_pairs={{0,2},{2,0},{1,3},{3,1},{4,6},{6,4},{5,7},{7,5},{8,10},{10,8},{9,1... | collective-permute-start | bytes 393224 | tf_op jit(solution)/shard_map/ppermute | solution.py:53
  (83 other events, 831.3 us)
Sparse Core Ops, SparseCore 0:
  21.0 55.4 all-gather.1
  129.7 99.8 all-reduce.2

commit v2 on v1

v2 whole, which is shorter than its diff:
```python
import functools

import jax
import jax.numpy as jnp
from jax import lax
from jax.experimental import pallas as pl
from jax.experimental.pallas import tpu as pltpu
from jax.sharding import Mesh, PartitionSpec as P

EPSILON = 1e-05
ROPE_BASE = 1000000.0
AXES = ("zl", "y", "x", "zh", "c")
Z = ("zl", "zh")
PLANE = ("zl", "y", "x")
BF = jnp.bfloat16
F32 = jnp.float32
SCALE = 64 ** (-0.5)
WHOLE = pl.BlockSpec(memory_space=pltpu.VMEM)


def call(body, outs, *operands):
    return pl.pallas_call(
        body,
        out_shape=[jax.ShapeDtypeStruct(shape, kind) for shape, kind in outs],
        in_specs=[WHOLE] * len(operands),
        out_specs=[WHOLE] * len(outs),
        compiler_params=pltpu.CompilerParams(vmem_limit_bytes=40 * 2**20),
    )(*operands)


def dot(left, right):
    return jnp.dot(left, right, preferred_element_type=F32)


def left_product(left, right):
    return lax.dot_general(left, right, (((0,), (0,)), ((), ())), preferred_element_type=F32)


def right_product(left, right):
    return lax.dot_general(left, right, (((1,), (1,)), ((), ())), preferred_element_type=F32)


def row_scale(values):
    return lax.rsqrt(jnp.mean(values * values, axis=-1, keepdims=True) + EPSILON)


def row_norm_grad(grad, normal, scale):
    return scale * (grad - normal * jnp.mean(grad * normal, axis=-1, keepdims=True))


def lanes(values):
    return lax.broadcasted_iota(jnp.int32, values.shape, 1)


def head_sum(values):
    low = lanes(values) < 64
    first = jnp.sum(jnp.where(low, values, 0.0), axis=-1, keepdims=True)
    second = jnp.sum(jnp.where(low, 0.0, values), axis=-1, keepdims=True)
    return jnp.where(low, first, second)


def head_scale(values):
    return lax.rsqrt(head_sum(values * values) * (1.0 / 64) + EPSILON)


def head_norm_grad(grad, normal, scale):
    return scale * (grad - normal * (head_sum(grad * normal) * (1.0 / 64)))


def other_half(values):
    low = (lanes(values) & 63) < 32
    return jnp.where(low, pltpu.roll(values, 96, 1), pltpu.roll(values, 32, 1))


def project(own, other, w, attn_gain, qk_gain, cosine, sine, normed, qh, kv, qkv):
    x = jnp.concatenate([own[...], other[...]]).astype(F32)
    low = (x * row_scale(x) * attn_gain[...]).astype(BF)
    normed[...] = low
    out = dot(low, w[:, :256])
    qkv[...] = out
    q, k = out[:, :128], out[:, 128:]
    cos, sin = cosine[...], sine[...]
    qn = q * head_scale(q) * qk_gain[0:1]
    qh[...] = (qn * cos + other_half(qn) * sin).astype(BF)
    kn = k * head_scale(k) * qk_gain[1:2]
    kr = kn * cos + other_half(kn) * sin
    kv[...] = jnp.where(lanes(k) < 64, kr, k).astype(BF)


def weights_of(q, k, visible):
    scores = right_product(q, k) * SCALE
    return jnp.where(visible, jnp.exp(scores), 0.0)


def attend(qh, kv0, kv1, kv2, kv3, own_places, places, w, send, keep, o_out, l_out):
    sums, totals = [0.0, 0.0], [0.0, 0.0]
    mine = own_places[...]
    for i, kv in enumerate((kv0, kv1, kv2, kv3)):
        visible = places[:, i * 256 : (i + 1) * 256] <= mine
        k, v = kv[:, :64], kv[:, 64:]
        for g in range(2):
            u = weights_of(qh[:, g * 64 : (g + 1) * 64], k, visible)
            totals[g] = totals[g] + jnp.sum(u, axis=-1, keepdims=True)
            sums[g] = sums[g] + dot(u.astype(BF), v)
    o = jnp.concatenate([sums[g] / totals[g] for g in range(2)], axis=1)
    o_out[...] = o
    l_out[...] = jnp.where(lanes(o) < 64, totals[0], totals[1])
    partial = right_product(o.astype(BF), w[:, 256:]).reshape(4, 2, 32, 1024)
    send[...] = partial[:, 1].astype(BF)
    keep[...] = partial[:, 0]


def pair_add(keep, got, own, one, two, three):
    own[...] = keep[0] + got[0].astype(F32)
    for k, out in ((1, one), (2, two), (3, three)):
        out[...] = (keep[k] + got[k].astype(F32)).astype(BF)


def total_of(own, one, two, three):
    return (own[...] + one[...].astype(F32)) + (two[...].astype(F32) + three[...].astype(F32))


def hidden(own, one, two, three, x, gain, h, hn):
    rows = x[:32].astype(F32) + total_of(own, one, two, three)
    h[...] = rows
    hn[...] = (rows * row_scale(rows) * gain[...]).astype(BF)


def feed_parts(gate, up, d_act):
    sig = jax.nn.sigmoid(gate)
    silu = gate * sig
    active = silu * up
    d_gate = d_act * up * sig * (1.0 + gate * (1.0 - sig))
    return active.astype(BF), d_gate, d_act * silu


def feed(p0, p1, p2, p3, p4, p5, p6, p7, dy_own, dy_other, w, send, keep, hn, act, dgu):
    rows = jnp.concatenate([p[...] for p in (p0, p1, p2, p3, p4, p5, p6, p7)])
    hn[...] = rows
    dy = jnp.concatenate([dy_own[...], dy_other[...]])
    def both(left, at, width):
        first, second = left[:, :512], left[:, 512:]
        return dot(first, w[:, 0, :, at : at + width].reshape(512, width)) + dot(
            second, w[:, 1, :, at : at + width].reshape(512, width)
        )
    gate, up, d_act = both(rows, 0, 512), both(rows, 512, 512), both(dy, 1024, 512)
    active, d_gate, d_up = feed_parts(gate, up, d_act)
    act[:, :512] = active
    d_gate, d_up = d_gate.astype(BF), d_up.astype(BF)
    dgu[:, :512] = d_gate
    dgu[:, 512:1024] = d_up
    tail, d_tail = both(rows, 1536, 128), both(dy, 1664, 128)
    low = lanes(tail) < 64
    gate = jnp.where(low, tail, 0.0)
    up = jnp.where(low, pltpu.roll(tail, 64, 1), 0.0)
    active, dg_tail, du_tail = feed_parts(gate, up, d_tail)
    act[:, 512:] = active
    dgu_tail = jnp.where(low, dg_tail, pltpu.roll(du_tail, 64, 1)).astype(BF)
    dgu[:, 1024:] = dgu_tail
    halves = []
    for z in range(2):
        part = right_product(d_gate, w[:, z, :, :512].reshape(512, 512))
        part = part + right_product(d_up, w[:, z, :, 512:1024].reshape(512, 512))
        part = part + right_product(dgu_tail, w[:, z, :, 1536:1664].reshape(512, 128))
        halves.append(part)
    partial = jnp.concatenate(halves, axis=1).reshape(4, 2, 32, 1024)
    send[...] = partial[:, 1].astype(BF)
    keep[...] = partial[:, 0]


def feed_weights(hn, dy_own, dy_other, act, dgu, w, send, keep, dw):
    dy = jnp.concatenate([dy_own[...], dy_other[...]])
    rows, active = hn[...], act[...]
    halves = []
    for z in range(2):
        part = right_product(active[:, :512], w[:, z, :, 1024:1536].reshape(512, 512))
        halves.append(part + right_product(active[:, 512:], w[:, z, :, 1664:].reshape(512, 128)))
    partial = jnp.concatenate(halves, axis=1).reshape(4, 2, 32, 1024)
    send[...] = partial[:, 1].astype(BF)
    keep[...] = partial[:, 0]
    for z in range(2):
        left, left_dy = rows[:, z * 512 : (z + 1) * 512], dy[:, z * 512 : (z + 1) * 512]
        def put(value, at, width):
            dw[:, z, :, at : at + width] = value.astype(BF).reshape(16, 32, width)
        put(left_product(left, dgu[:, :512]), 0, 512)
        put(left_product(left, dgu[:, 512:1024]), 512, 512)
        put(left_product(left_dy, active[:, :512]), 1024, 512)
        put(left_product(left, dgu[:, 1024:]), 1536, 128)
        put(left_product(left_dy, active[:, 512:]), 1664, 128)


def block_rows(own, one, two, three, h, out):
    out[...] = (h[...] + total_of(own, one, two, three)).astype(BF)


def hidden_grad(own, one, two, three, h, dy, gain, dh, low, gain_part):
    d_hn = total_of(own, one, two, three)
    rows = h[...]
    scale = row_scale(rows)
    hat = rows * scale
    gain_part[...] = jnp.sum(d_hn * hat, axis=0, keepdims=True)
    grad = dy[:32].astype(F32) + row_norm_grad(d_hn * gain[...], hat, scale)
    dh[...] = grad
    low[...] = grad.astype(BF)


def attend_grad(
    p0, p1, p2, p3, p4, p5, p6, p7, qh, kv0, kv1, kv2, kv3, own_places, places, w, o, l,
    d_attn, d_qh, d_kv0, d_kv1, d_kv2, d_kv3,
):
    rows = jnp.concatenate([p[...] for p in (p0, p1, p2, p3, p4, p5, p6, p7)])
    d_attn[...] = rows
    d_o = dot(rows, w[:, 256:])
    denom = l[...]
    d_inner = (d_o / denom).astype(BF)
    delta = head_sum(d_o * o[...]) / denom
    mine = own_places[...]
    d_q = [0.0, 0.0]
    for i, (kv, d_kv) in enumerate(((kv0, d_kv0), (kv1, d_kv1), (kv2, d_kv2), (kv3, d_kv3))):
        visible = places[:, i * 256 : (i + 1) * 256] <= mine
        k, v = kv[:, :64], kv[:, 64:]
        d_k, d_v = 0.0, 0.0
        for g in range(2):
            at = slice(g * 64, (g + 1) * 64)
            q, di = qh[:, at], d_inner[:, at]
            u = weights_of(q, k, visible)
            ds = (u * (right_product(di, v) - delta[:, g * 64 : g * 64 + 1])).astype(BF)
            d_q[g] = d_q[g] + dot(ds, k)
            d_k = d_k + left_product(ds, q)
            d_v = d_v + left_product(u.astype(BF), di)
        d_kv[...] = jnp.concatenate([d_k * SCALE, d_v], axis=1).astype(d_kv.dtype)
    d_qh[...] = jnp.concatenate(d_q, axis=1) * SCALE


def project_grad(
    d_qh, own, one, two, three, qkv, cosine, sine, qk_gain, w, x_own, x_other,
    d_qkv, send, keep, gain_part, head_part,
):
    d_kv = total_of(own, one, two, three)
    cos, sin = cosine[...], sine[...]
    q, k = qkv[:, :128], qkv[:, 128:]
    q_scale, k_scale = head_scale(q), head_scale(k)
    q_hat, k_hat = q * q_scale, k * k_scale
    d_q = d_qh[...]
    d_qn = d_q * cos - other_half(d_q) * sin
    d_kn = d_kv * cos - other_half(d_kv) * sin
    head_part[0:1] = jnp.sum(d_qn * q_hat, axis=0, keepdims=True)
    head_part[1:2] = jnp.sum(d_kn * k_hat, axis=0, keepdims=True)
    d_q = head_norm_grad(d_qn * qk_gain[0:1], q_hat, q_scale)
    d_k = head_norm_grad(d_kn * qk_gain[1:2], k_hat, k_scale)
    d_k = jnp.where(lanes(d_k) < 64, d_k, d_kv)
    low = jnp.concatenate([d_q, d_k], axis=1).astype(BF)
    d_qkv[...] = low
    partial = right_product(low, w[:, :256])
    x = jnp.concatenate([x_own[...], x_other[...]]).astype(F32)
    gain_part[...] = jnp.sum(partial * (x * row_scale(x)), axis=0, keepdims=True)
    partial = partial.reshape(4, 2, 32, 1024)
    send[...] = partial[:, 1].astype(BF)
    keep[...] = partial[:, 0]


def attend_weights(normed, d_qkv, dw):
    dw[...] = left_product(normed[...], d_qkv[...]).astype(BF)


def out_weights(d_attn, o, dw):
    dw[...] = left_product(d_attn[...], o[...].astype(BF)).astype(BF)


def token_rows(own, one, two, three, dh, x, gain, out):
    d_xn = total_of(own, one, two, three)
    rows = x[:32].astype(F32)
    scale = row_scale(rows)
    grad = row_norm_grad(d_xn * gain[...], rows * scale, scale)
    out[...] = (dh[...] + grad).astype(BF)


def finish_attend(parts, wq, wk, wv, wo):
    low = jnp.sum(parts[0].astype(F32), axis=0)
    high = jnp.sum(parts[1].astype(F32), axis=0)
    wq[...] = jnp.concatenate([low[:, :128], high[:, :128]], axis=1)
    wk[...] = jnp.concatenate([low[:, 128:192], high[:, 128:192]], axis=1)
    wv[...] = jnp.concatenate([low[:, 192:256], high[:, 192:256]], axis=1)
    wo[...] = jnp.concatenate([low[:, 256:], high[:, 256:]], axis=1)


def swap(value, axes, size, mask):
    return lax.ppermute(value, axes, [(i, i ^ mask) for i in range(size)])


def fan(pieces, axes):
    return [swap(pieces[k], axes, 4, k) for k in (1, 2, 3)]


def sum_scatter(send, keep):
    got = swap(send, "c", 2, 1)
    small = ((32, 1024), BF)
    own, one, two, three = call(pair_add, [((32, 1024), F32), small, small, small], keep, got)
    return [own] + fan([None, one, two, three], Z)


def gather_rows(rows):
    column = [rows] + fan([rows] * 4, Z)
    pieces = []
    for piece in column:
        pieces += [piece, swap(piece, "c", 2, 1)]
    return pieces


def place_rows(head, p0, p1, p2, p3, out):
    for k, piece in enumerate((p0, p1, p2, p3)):
        out[pl.ds((head[0] ^ k) * 32, 32)] = piece[...]


def gather_head(rows, head):
    other = swap(rows, "c", 2, 1)
    pieces = [rows, other, swap(rows, "zh", 2, 1), swap(other, "zh", 2, 1)]
    return pl.pallas_call(
        place_rows,
        out_shape=jax.ShapeDtypeStruct((128, 1024), BF),
        in_specs=[pl.BlockSpec(memory_space=pltpu.SMEM)] + [WHOLE] * 4,
        out_specs=WHOLE,
    )(head.reshape(1), *pieces)[None]


def column_half(parts, zl):
    return [
        jnp.where(zl == 0, p[:, : p.shape[1] // 2], p[:, p.shape[1] // 2 :]) for p in parts
    ]


def feed_columns(gate, up, down):
    zeros = jnp.zeros_like(gate[:, :64])
    parts = [gate[:, :512], up[:, :512], down[:, :512], gate[:, 512:], up[:, 512:], down[:, 512:]]
    return jnp.concatenate(parts + [zeros], axis=1)


def local(
    tokens, positions, attn_gain, ffn_gain, query_gain, key_gain,
    w_query, w_key, w_value, w_out, w_gate, w_up, w_down, cotangent,
):
    zl, y, head = lax.axis_index("zl"), lax.axis_index("y"), lax.axis_index(("zh", "c"))
    attn_gain_row, ffn_gain_row = attn_gain[None], ffn_gain[None]

    small = [w_query, w_key, w_value, w_out]
    lows = jnp.concatenate([p[:, : p.shape[1] // 2] for p in small], axis=1)
    highs = jnp.concatenate([p[:, p.shape[1] // 2 :] for p in small], axis=1)
    blocks = jnp.broadcast_to(jnp.stack([lows, highs])[:, None], (2, 16, 32, 384))
    w_a = lax.all_to_all(blocks.reshape(1024, 384), PLANE, 0, 0, tiled=True)

    feeds = [w_gate, w_up, w_down]
    keep_f = feed_columns(*column_half(feeds, zl))
    send_f = feed_columns(*column_half(feeds, 1 - zl))
    got_f = swap(send_f, "zl", 2, 1)
    rows_f = jnp.where(zl == 0, jnp.stack([keep_f, got_f]), jnp.stack([got_f, keep_f]))
    w_f = lax.all_gather(rows_f, ("y", "x"), axis=0)

    order = head ^ jnp.arange(4)
    x_own = tokens[0].reshape(4, 32, 1024)[order].reshape(128, 1024)
    x_other = swap(x_own, "zl", 2, 1)
    dy_own = cotangent[0].reshape(4, 32, 1024)[order].reshape(128, 1024)
    dy_other = swap(dy_own, "zl", 2, 1)

    steps = jnp.array([dl * 16 + ky * 4 + d for ky in range(4) for dl in range(2) for d in range(4)])
    places = positions[0].reshape(32, 32)[steps ^ (zl * 16 + y * 4 + head)].reshape(1024)
    own_places = places[:256]
    frequency = ROPE_BASE ** (-(jnp.arange(32).astype(F32) * 2.0 / 64))
    angles = own_places.astype(F32)[:, None] * frequency
    cosine, sine = jnp.cos(angles), jnp.sin(angles)
    cosine = jnp.concatenate([cosine] * 4, axis=1)
    sine = jnp.concatenate([-sine, sine] * 2, axis=1)
    own_places, places = own_places[:, None], places[None]
    qk_gain = jnp.stack([jnp.tile(query_gain, 2), jnp.tile(key_gain, 2)])

    halves = [((4, 32, 1024), BF), ((4, 32, 1024), F32)]
    flat = ((256, 128), BF)
    normed, qh, kv, qkv = call(
        project, [((256, 1024), BF), flat, flat, ((256, 256), F32)],
        x_own, x_other, w_a, attn_gain_row, qk_gain, cosine, sine,
    )
    kvs = [kv] + fan([kv] * 4, "y")
    send, keep, o, l = call(
        attend, halves + [((256, 128), F32)] * 2, qh, *kvs, own_places, places, w_a
    )
    h, hn = call(
        hidden, [((32, 1024), F32), ((32, 1024), BF)],
        *sum_scatter(send, keep), x_own, ffn_gain_row,
    )
    send, keep, hn_all, act, dgu = call(
        feed, halves + [((256, 1024), BF), ((256, 640), BF), ((256, 1152), BF)],
        *gather_rows(hn), dy_own, dy_other, w_f,
    )
    d_hn = sum_scatter(send, keep)
    send_b, keep_b, dw_f = call(
        feed_weights, halves + [((16, 2, 32, 1792), BF)], hn_all, dy_own, dy_other, act, dgu, w_f
    )
    (rows,) = call(block_rows, [((32, 1024), BF)], *sum_scatter(send_b, keep_b), h)
    block_out = gather_head(rows, head)
    dw_f = lax.psum_scatter(
        dw_f.reshape(1024, 1792), ("y", "x"), scatter_dimension=0, tiled=True
    ).reshape(2, 32, 1792)
    dh, d_low, ffn_gain_part = call(
        hidden_grad, [((32, 1024), F32), ((32, 1024), BF), ((1, 1024), F32)],
        *d_hn, h, dy_own, ffn_gain_row,
    )
    d_attn, d_qh, *d_kvs = call(
        attend_grad,
        [((256, 1024), BF), ((256, 128), F32), ((256, 128), F32), flat, flat, flat],
        *gather_rows(d_low), qh, *kvs, own_places, places, w_a, o, l,
    )
    d_qkv, send, keep, attn_gain_part, head_part = call(
        project_grad,
        [((256, 256), BF)] + halves + [((1, 1024), F32), ((2, 128), F32)],
        d_qh, d_kvs[0], *fan(d_kvs, "y"), qkv, cosine, sine, qk_gain, w_a, x_own, x_other,
    )
    d_xn = sum_scatter(send, keep)
    (dw_qkv,) = call(attend_weights, [((1024, 256), BF)], normed, d_qkv)
    (dw_o,) = call(out_weights, [((1024, 128), BF)], d_attn, o)
    dw_a = jnp.concatenate([dw_qkv, dw_o], axis=1)
    dw_a = lax.all_to_all(dw_a, PLANE, 0, 0, tiled=True)
    (rows,) = call(token_rows, [((32, 1024), BF)], *d_xn, dh, x_own, attn_gain_row)
    tokens_grad = gather_head(rows, head)
    grad_wq, grad_wk, grad_wv, grad_wo = call(
        finish_attend, [((32, n), F32) for n in (256, 128, 128, 256)],
        dw_a.reshape(2, 16, 32, 384),
    )

    def finish(total):
        other = swap(jnp.where(zl == 0, total[1], total[0]), "zl", 2, 1)
        own = jnp.where(zl == 0, total[0], total[1])
        low, high = jnp.where(zl == 0, own, other), jnp.where(zl == 0, other, own)
        outs = []
        for i in range(3):
            wide, tail = slice(i * 512, (i + 1) * 512), slice(1536 + i * 64, 1600 + i * 64)
            pieces = [low[:, wide], low[:, tail], high[:, wide], high[:, tail]]
            outs.append(jnp.concatenate(pieces, axis=1).astype(F32))
        return outs

    grad_wg, grad_wu, grad_wd = finish(dw_f)

    head_part = head_part[:, :64] + head_part[:, 64:] * jnp.array([[1.0], [0.0]], F32)
    gains = jnp.concatenate([attn_gain_part[0], ffn_gain_part[0], head_part.reshape(-1)])
    gains = gains.reshape(17, 128)
    gains = gains + swap(gains, "c", 2, 1)
    for axes in (Z, "y", "x"):
        one, two, three = fan([gains] * 4, axes)
        gains = (gains + one) + (two + three)
    gains = gains.reshape(-1)
    return (
        block_out, tokens_grad, gains[:1024], gains[1024:2048], gains[2048:2112], gains[2112:],
        grad_wq, grad_wk, grad_wv, grad_wo, grad_wg, grad_wu, grad_wd,
    )


def solution(mesh):
    cube = Mesh(mesh.devices.reshape(2, 4, 4, 2, 2), AXES)
    rows = P("x", ("zl", "y"), None)
    weight = P(("zl", "y", "x"), ("zh", "c"))
    return jax.shard_map(
        local,
        mesh=cube,
        in_specs=(rows, P("x", None)) + (P(),) * 4 + (weight,) * 7 + (rows,),
        out_specs=(rows, rows) + (P(),) * 4 + (weight,) * 7,
        check_vma=False,
    )
```

time: 247 us -> 195 us (0.79)
  waiting for transfers between devices: 71.4 us -> 49.5 us
  matrix products: 19.3 us -> 0 us
  Pallas kernels: 0 us -> 17.6 us
  other arithmetic: 23.5 us -> 8.36 us
  local copies, waits for them, and re-layouts: 40.5 us -> 25.4 us
    unnamed x3 -> x2, waiting for transfers between devices: 20.8 us -> 0.03 us
    dot_general x21 -> x0, matrix products: 19.3 us -> none  [the longest x5 7.56 us: left_product(): lax.dot_general(left, right, (((0,), (0,)), ((), ())), preferred_element_...]
    pallas_call x0 -> x19, Pallas kernels: none -> 17.6 us  [the longest x17 14.3 us: call(): pl.pallas_call(body, out_shape=[jax.ShapeDtypeStruct(shape, kind) for sha...]
    unnamed x122 -> x119, local copies, waits for them, and re-layouts: 5.02 us -> 19 us
    concatenate x10 -> x5, local copies, waits for them, and re-layouts: 11.7 us -> 0.49 us  [the longest x3 0.3 us: finish(): outs.append(jnp.concatenate(pieces, axis=1).astype(F32))]
    convert_element_type x18 -> x3, other arithmetic: 10.3 us -> 2.03 us  [finish(): outs.append(jnp.concatenate(pieces, axis=1).astype(F32))]
    reduce_sum x11 -> x0, other arithmetic: 3.72 us -> none  [the longest x1 1.07 us: local(): attn_gain_part = jnp.sum(d_xn * own_hat, axis=0)]
    gather x4 -> x2, local copies, waits for them, and re-layouts: 5.69 us -> 2.2 us  [the longest x1 1.64 us: local(): dy_own = cotangent[0].reshape(4, 32, 1024)[order].reshape(128, 1024)]
  transfers between devices with their start and end apart: 54 -> 60, of which waited for: 22 -> 23; matrix products, arithmetic and copies ran while one was open for 29% -> 5% of each run, Pallas kernels for 0% -> 7%
where the time goes in v2:
time: 195 us; the launch traced here: 192 us
  starting transfers between devices  75.7 us (39%)
  waiting for transfers between devices  49.5 us (25%)
  local copies, waits for them, and re-layouts  25.4 us (13%)
  Pallas kernels  17.6 us (9%)
  between operations  14.9 us (8%)
  other arithmetic  8.36 us (4%)
    ppermute x56, starting transfers between devices, swap(): return lax.ppermute(value, axes, [(i, i ^ mask) for i in range(size)])  63.4 us
    ppermute x56, waiting for transfers between devices, swap(): return lax.ppermute(value, axes, [(i, i ^ mask) for i in range(size)])  36.7 us
    unnamed x119, local copies, waits for them, and re-layouts  19 us
    pallas_call x17, Pallas kernels, call(): pl.pallas_call(body, out_shape=[jax.ShapeDtypeStruct(shape, kind) for sha...  14.3 us
    all_to_all x1, waiting for transfers between devices, local(): w_a = lax.all_to_all(blocks.reshape(1024, 384), PLANE, 0, 0, tiled=True)  12.5 us
    all_to_all x1, starting transfers between devices, local(): w_a = lax.all_to_all(blocks.reshape(1024, 384), PLANE, 0, 0, tiled=True)  7.45 us
    all_to_all x1, starting transfers between devices, local(): dw_a = lax.all_to_all(dw_a, PLANE, 0, 0, tiled=True)  4.81 us
  transfers between devices with their start and end apart: 60, of which 23 were waited for; matrix products, arithmetic and copies ran while one was open for 5% of the time, Pallas kernels for 7%

profile of v2, /device:TPU:0, one launch (start us, length us, event | category | flops | bytes accessed | tf_op | source)
XLA Modules:
  0.0 191.5 jit_solution(12839949519893017890)
XLA Ops:
  9.4 2.1 %collective-permute-start.16 = (bf16[32,1792]{1,0:T(8,128)(2,1)S(1)}, bf16[32,1792]{1,0:T(8,128)(2,1)S(1)}, u32[]{:S(2)}, u32[]{:S(2)}) collective-permute-start(bf16[32,1792]{1,0:T(8,128)(2,1)S(1)} %concatenate.52), channel_id=1, source_target_pairs={{0,64},{64,0},{1,65},{65,1},{2,66},{66,2},{3,67},{67,3},{4,68},{68... | collective-permute-start | bytes 344072 | tf_op jit(solution)/shard_map/ppermute | solution.py:288
  11.6 3.0 %collective-permute-done.16 = bf16[32,1792]{1,0:T(8,128)(2,1)S(1)} collective-permute-done((bf16[32,1792]{1,0:T(8,128)(2,1)S(1)}, bf16[32,1792]{1,0:T(8,128)(2,1)S(1)}, u32[]{:S(2)}, u32[]{:S(2)}) %collective-permute-start.16) | collective-permute-done | bytes 114720 | tf_op jit(solution)/shard_map/ppermute | solution.py:288
  16.0 1.8 collective-permute-start
  19.1 7.5 %all-to-all-start = ((bf16[32,32,384]{2,1,0:T(8,128)(2,1)}), bf16[32,32,384]{2,1,0:T(8,128)(2,1)S(1)}, u32[]{:S(2)}, u32[]{:S(2)}) async-start(bf16[32,32,384]{2,1,0:T(8,128)(2,1)} %bitcast.6), calls=%async_computation | async-start | bytes 1572864 | tf_op jit(solution)/shard_map/all_to_all | solution.py:349
  29.6 12.5 %all-to-all-done = bf16[32,32,384]{2,1,0:T(8,128)(2,1)S(1)} async-done(((bf16[32,32,384]{2,1,0:T(8,128)(2,1)}), bf16[32,32,384]{2,1,0:T(8,128)(2,1)S(1)}, u32[]{:S(2)}, u32[]{:S(2)}) %all-to-all-start) | async-done | bytes 786464 | tf_op jit(solution)/shard_map/all_to_all | solution.py:349
  43.6 2.3 %collective-permute-start.3 = (bf16[256,128]{1,0:T(8,128)(2,1)S(1)}, bf16[256,128]{1,0:T(8,128)(2,1)S(1)}, u32[]{:S(2)}, u32[]{:S(2)}) collective-permute-start(bf16[256,128]{1,0:T(8,128)(2,1)S(1)} %get-tuple-element.66.kv0), channel_id=1, source_target_pairs={{0,48},{16,32},{32,16},{48,0},{1,49},{17,33},{33,17},{49,1},{2,50}... | collective-permute-start | bytes 196616 | tf_op jit(solution)/shard_map/ppermute | solution.py:288
  49.1 2.6 %collective-permute-done.2.kv2 = bf16[256,128]{1,0:T(8,128)(2,1)S(1)} collective-permute-done((bf16[256,128]{1,0:T(8,128)(2,1)S(1)}, bf16[256,128]{1,0:T(8,128)(2,1)S(1)}, u32[]{:S(2)}, u32[]{:S(2)}) %collective-permute-start.2) | collective-permute-done | bytes 65568 | tf_op jit(solution)/shard_map/ppermute | solution.py:288
  51.7 2.1 %shard_map.256 = (bf16[4,32,1024]{2,1,0:T(8,128)(2,1)}, f32[4,32,1024]{2,1,0:T(8,128)S(1)}, f32[256,128]{1,0:T(8,128)S(1)}, f32[256,128]{1,0:T(8,128)S(1)}) custom-call(bf16[256,128]{1,0:T(8,128)(2,1)S(1)} %get-tuple-element.65.qh, bf16[256,128]{1,0:T(8,128)(2,1)S(1)} %get-tuple-element.66.kv0, bf16[256,128]{1,0:T(8,128)(2,1)S(1)} %collective-permute-done.1.kv1, ...), custom_call_target="tpu_custom_call" | custom-call | tf_op jit(solution)/shard_map/pallas_call | solution.py:22
  56.9 3.6 %collective-permute-start.5 = (bf16[32,1024]{1,0:T(8,128)(2,1)S(1)}, bf16[32,1024]{1,0:T(8,128)(2,1)S(1)}, u32[]{:S(2)}, u32[]{:S(2)}) collective-permute-start(bf16[32,1024]{1,0:T(8,128)(2,1)S(1)} %get-tuple-element.70), channel_id=1, source_target_pairs={{0,2},{2,0},{64,66},{66,64},{1,3},{3,1},{65,67},{67,65},{4,6},{6,4... | collective-permute-start | bytes 196616 | tf_op jit(solution)/shard_map/ppermute | solution.py:288
  61.3 7.5 %collective-permute-done.5.one = bf16[32,1024]{1,0:T(8,128)(2,1)S(1)} collective-permute-done((bf16[32,1024]{1,0:T(8,128)(2,1)S(1)}, bf16[32,1024]{1,0:T(8,128)(2,1)S(1)}, u32[]{:S(2)}, u32[]{:S(2)}) %collective-permute-start.5) | collective-permute-done | bytes 65568 | tf_op jit(solution)/shard_map/ppermute | solution.py:288
  71.5 2.3 %collective-permute-start.9 = (bf16[32,1024]{1,0:T(8,128)(2,1)S(1)}, bf16[32,1024]{1,0:T(8,128)(2,1)S(1)}, u32[]{:S(2)}, u32[]{:S(2)}) collective-permute-start(bf16[32,1024]{1,0:T(8,128)(2,1)S(1)} %get-tuple-element.73.p0), channel_id=1, source_target_pairs={{0,2},{2,0},{64,66},{66,64},{1,3},{3,1},{65,67},{67,65},{4,6},{6,4... | collective-permute-start | bytes 196616 | tf_op jit(solution)/shard_map/ppermute | solution.py:288
  80.4 2.0 %copy-done.1 = bf16[16,2,32,1792]{3,2,1,0:T(8,128)(2,1)S(1)} copy-done((bf16[16,2,32,1792]{3,2,1,0:T(8,128)(2,1)S(1)}, bf16[16,2,32,1792]{3,2,1,0:T(8,128)(2,1)}, u32[]{:S(2)}) %copy-start.1) | copy-done | bytes 3670040
  87.5 2.1 %shard_map.259 = (bf16[4,32,1024]{2,1,0:T(8,128)(2,1)S(1)}, f32[4,32,1024]{2,1,0:T(8,128)S(1)}, bf16[256,1024]{1,0:T(8,128)(2,1)S(1)}, bf16[256,640]{1,0:T(8,128)(2,1)S(1)}, bf16[256,1152]{1,0:T(8,128)(2,1)S(1)}) custom-call(bf16[32,1024]{1,0:T(8,128)(2,1)S(1)} %get-tuple-element.73.p0, bf16[32,1024]{1,0:T(8,128)(2,1)S(1)} %copy-done.29, ...), custom_call_target="tpu_custom_call" | custom-call | tf_op jit(solution)/shard_map/pallas_call | solution.py:22
  91.9 1.9 copy-done.3
  97.4 2.4 %collective-permute-start.25 = (bf16[32,1024]{1,0:T(8,128)(2,1)S(1)}, bf16[32,1024]{1,0:T(8,128)(2,1)S(1)}, u32[]{:S(2)}, u32[]{:S(2)}) collective-permute-start(bf16[32,1024]{1,0:T(8,128)(2,1)S(1)} %get-tuple-element.87), channel_id=1, source_target_pairs={{0,2},{2,0},{64,66},{66,64},{1,3},{3,1},{65,67},{67,65},{4,6},{6,4... | collective-permute-start | bytes 196616 | tf_op jit(solution)/shard_map/ppermute | solution.py:288
  105.5 1.8 collective-permute-start.33
  107.4 2.9 %collective-permute-start.29 = (bf16[32,1024]{1,0:T(8,128)(2,1)S(1)}, bf16[32,1024]{1,0:T(8,128)(2,1)S(1)}, u32[]{:S(2)}, u32[]{:S(2)}) collective-permute-start(bf16[32,1024]{1,0:T(8,128)(2,1)S(1)} %get-tuple-element.90.p0), channel_id=1, source_target_pairs={{0,2},{2,0},{64,66},{66,64},{1,3},{3,1},{65,67},{67,65},{4,6},{6,4... | collective-permute-start | bytes 196616 | tf_op jit(solution)/shard_map/ppermute | solution.py:288
  114.5 3.1 %shard_map.266 = (bf16[256,1024]{1,0:T(8,128)(2,1)S(1)}, f32[256,128]{1,0:T(8,128)S(1)}, f32[256,128]{1,0:T(8,128)S(1)}, bf16[256,128]{1,0:T(8,128)(2,1)S(1)}, b...) custom-call(bf16[32,1024]{1,0:T(8,128)(2,1)S(1)} %get-tuple-element.90.p0, ...), custom_call_target="tpu_custom_call" | custom-call | tf_op jit(solution)/shard_map/pallas_call | solution.py:22
  119.1 2.1 %collective-permute-start.36 = (bf16[256,128]{1,0:T(8,128)(2,1)S(1)}, bf16[256,128]{1,0:T(8,128)(2,1)S(1)}, u32[]{:S(2)}, u32[]{:S(2)}) collective-permute-start(bf16[256,128]{1,0:T(8,128)(2,1)S(1)} %get-tuple-element.96), channel_id=1, source_target_pairs={{0,32},{16,48},{32,0},{48,16},{1,33},{17,49},{33,1},{49,17},{2,34}... | collective-permute-start | bytes 196616 | tf_op jit(solution)/shard_map/ppermute | solution.py:288
  123.1 2.8 %collective-permute-start.18 = (bf16[32,1024]{1,0:T(8,128)(2,1)}, bf16[32,1024]{1,0:T(8,128)(2,1)S(1)}, u32[]{:S(2)}, u32[]{:S(2)}) collective-permute-start(bf16[32,1024]{1,0:T(8,128)(2,1)} %get-tuple-element.80), channel_id=1, source_target_pairs={{0,2},{2,0},{64,66},{66,64},{1,3},{3,1},{65,67},{67,65},{4,6},{6,4... | collective-permute-start | bytes 196616 | tf_op jit(solution)/shard_map/ppermute | solution.py:288
  127.9 1.8 shard_map.267
  133.6 1.8 collective-permute-start.48
  135.9 3.0 %collective-permute-start.22 = (bf16[32,1024]{1,0:T(8,128)(2,1)S(1)}, bf16[32,1024]{1,0:T(8,128)(2,1)S(1)}, u32[]{:S(2)}, u32[]{:S(2)}) collective-permute-start(bf16[32,1024]{1,0:T(8,128)(2,1)S(1)} %shard_map.262.p0), channel_id=1, source_target_pairs={{0,2},{2,0},{1,3},{3,1},{4,6},{6,4},{5,7},{7,5},{8,10},{10,8},{9,1... | collective-permute-start | bytes 196616 | tf_op jit(solution)/shard_map/ppermute | solution.py:288
  140.6 1.8 collective-permute-start.51
  142.4 2.3 %collective-permute-start.49 = (f32[17,128]{1,0:T(8,128)S(1)}, f32[17,128]{1,0:T(8,128)S(1)}, u32[]{:S(2)}, u32[]{:S(2)}) collective-permute-start(f32[17,128]{1,0:T(8,128)S(1)} %add_add_fusion.2), channel_id=1, source_target_pairs={{0,16},{16,0},{32,48},{48,32},{1,17},{17,1},{33,49},{49,33},{2,18}... | collective-permute-start | bytes 26120 | tf_op jit(solution)/shard_map/ppermute | solution.py:288
  147.9 2.0 %collective-permute-start.54 = (f32[17,128]{1,0:T(8,128)S(1)}, f32[17,128]{1,0:T(8,128)S(1)}, u32[]{:S(2)}, u32[]{:S(2)}) collective-permute-start(f32[17,128]{1,0:T(8,128)S(1)} %add_add_fusion.1), channel_id=1, source_target_pairs={{0,12},{4,8},{8,4},{12,0},{1,13},{5,9},{9,5},{13,1},{2,14},{6,10},... | collective-permute-start | bytes 26120 | tf_op jit(solution)/shard_map/ppermute | solution.py:288
  150.1 2.0 %collective-permute-start.52 = (f32[17,128]{1,0:T(8,128)S(1)}, f32[17,128]{1,0:T(8,128)S(1)}, u32[]{:S(2)}, u32[]{:S(2)}) collective-permute-start(f32[17,128]{1,0:T(8,128)S(1)} %add_add_fusion.1), channel_id=1, source_target_pairs={{0,4},{4,0},{8,12},{12,8},{1,5},{5,1},{9,13},{13,9},{2,6},{6,2},{1... | collective-permute-start | bytes 26120 | tf_op jit(solution)/shard_map/ppermute | solution.py:288
  153.0 4.8 %all-to-all-start.1 = ((bf16[32,32,384]{2,1,0:T(8,128)(2,1)}), bf16[32,32,384]{2,1,0:T(8,128)(2,1)S(1)}, u32[]{:S(2)}, u32[]{:S(2)}) async-start(bf16[32,32,384]{2,1,0:T(8,128)(2,1)} %bitcast.22), calls=%async_computation.1 | async-start | bytes 1572864 | tf_op jit(solution)/shard_map/all_to_all | solution.py:420
  157.9 2.4 %collective-permute-start.39 = (bf16[32,1024]{1,0:T(8,128)(2,1)S(1)}, bf16[32,1024]{1,0:T(8,128)(2,1)S(1)}, u32[]{:S(2)}, u32[]{:S(2)}) collective-permute-start(bf16[32,1024]{1,0:T(8,128)(2,1)S(1)} %get-tuple-element.102), channel_id=1, source_target_pairs={{0,2},{2,0},{64,66},{66,64},{1,3},{3,1},{65,67},{67,65},{4,6},{6,4... | collective-permute-start | bytes 196616 | tf_op jit(solution)/shard_map/ppermute | solution.py:288
  162.5 4.9 %collective-permute-done.39.one = bf16[32,1024]{1,0:T(8,128)(2,1)S(1)} collective-permute-done((bf16[32,1024]{1,0:T(8,128)(2,1)S(1)}, bf16[32,1024]{1,0:T(8,128)(2,1)S(1)}, u32[]{:S(2)}, u32[]{:S(2)}) %collective-permute-start.39) | collective-permute-done | bytes 65568 | tf_op jit(solution)/shard_map/ppermute | solution.py:288
  167.4 2.9 %collective-permute-done.40.two = bf16[32,1024]{1,0:T(8,128)(2,1)S(1)} collective-permute-done((bf16[32,1024]{1,0:T(8,128)(2,1)S(1)}, bf16[32,1024]{1,0:T(8,128)(2,1)S(1)}, u32[]{:S(2)}, u32[]{:S(2)}) %collective-permute-start.40) | collective-permute-done | bytes 65568 | tf_op jit(solution)/shard_map/ppermute | solution.py:288
  171.2 2.1 %collective-permute-start.43 = (bf16[32,1024]{1,0:T(8,128)(2,1)S(1)}, bf16[32,1024]{1,0:T(8,128)(2,1)S(1)}, u32[]{:S(2)}, u32[]{:S(2)}) collective-permute-start(bf16[32,1024]{1,0:T(8,128)(2,1)S(1)} %shard_map.269.p0), channel_id=1, source_target_pairs={{0,2},{2,0},{1,3},{3,1},{4,6},{6,4},{5,7},{7,5},{8,10},{10,8},{9,1... | collective-permute-start | bytes 196616 | tf_op jit(solution)/shard_map/ppermute | solution.py:288
  (296 shorter events, 76.4 us)
Async XLA Ops:
  7.2 73.2 %all-gather.2.cloned.1.call-start = ((), (), s32[]{:S(2)}) async-start(), calls=%async_computation.3 | async-start | bytes 3899392 | tf_op jit(solution)/shard_map/all_gather | solution.py:356
  16.0 13.6 %collective-permute-start = (bf16[128,1024]{1,0:T(8,128)(2,1)S(1)}, bf16[128,1024]{1,0:T(8,128)(2,1)S(1)}, u32[]{:S(2)}, u32[]{:S(2)}) collective-permute-start(bf16[128,1024]{1,0:T(8,128)(2,1)S(1)} %bitcast.40), channel_id=1, source_target_pairs={{0,64},{64,0},{1,65},{65,1},{2,66},{66,2},{3,67},{67,3},{4,68},{68... | collective-permute-start | bytes 786440 | tf_op jit(solution)/shard_map/ppermute | solution.py:288
  19.1 23.0 %all-to-all-start = ((bf16[32,32,384]{2,1,0:T(8,128)(2,1)}), bf16[32,32,384]{2,1,0:T(8,128)(2,1)S(1)}, u32[]{:S(2)}, u32[]{:S(2)}) async-start(bf16[32,32,384]{2,1,0:T(8,128)(2,1)} %bitcast.6), calls=%async_computation | async-start | bytes 1572864 | tf_op jit(solution)/shard_map/all_to_all | solution.py:349
  26.6 148.5 %reduce-scatter.2.cloned.1.call-start = ((), (), s32[]{:S(2)}) async-start(), calls=%async_computation.4 | async-start | bytes 3899392 | tf_op jit(solution)/shard_map/reduce_scatter | solution.py:399
  56.1 21.8 %collective-permute-start.15 = (bf16[128,1024]{1,0:T(8,128)(2,1)S(1)}, bf16[128,1024]{1,0:T(8,128)(2,1)S(1)}, u32[]{:S(2)}, u32[]{:S(2)}) collective-permute-start(bf16[128,1024]{1,0:T(8,128)(2,1)S(1)} %bitcast.45), channel_id=1, source_target_pairs={{0,64},{64,0},{1,65},{65,1},{2,66},{66,2},{3,67},{67,3},{4,68},{68... | collective-permute-start | bytes 786440 | tf_op jit(solution)/shard_map/ppermute | solution.py:288
  56.9 12.0 %collective-permute-start.5 = (bf16[32,1024]{1,0:T(8,128)(2,1)S(1)}, bf16[32,1024]{1,0:T(8,128)(2,1)S(1)}, u32[]{:S(2)}, u32[]{:S(2)}) collective-permute-start(bf16[32,1024]{1,0:T(8,128)(2,1)S(1)} %get-tuple-element.70), channel_id=1, source_target_pairs={{0,2},{2,0},{64,66},{66,64},{1,3},{3,1},{65,67},{67,65},{4,6},{6,4... | collective-permute-start | bytes 196616 | tf_op jit(solution)/shard_map/ppermute | solution.py:288
  60.5 8.3 %collective-permute-start.6 = (bf16[32,1024]{1,0:T(8,128)(2,1)S(1)}, bf16[32,1024]{1,0:T(8,128)(2,1)S(1)}, u32[]{:S(2)}, u32[]{:S(2)}) collective-permute-start(bf16[32,1024]{1,0:T(8,128)(2,1)S(1)} %get-tuple-element.71), channel_id=1, source_target_pairs={{0,64},{2,66},{64,0},{66,2},{1,65},{3,67},{65,1},{67,3},{4,68},{6,... | collective-permute-start | bytes 196616 | tf_op jit(solution)/shard_map/ppermute | solution.py:288
  61.3 7.5 %collective-permute-start.7 = (bf16[32,1024]{1,0:T(8,128)(2,1)S(1)}, bf16[32,1024]{1,0:T(8,128)(2,1)S(1)}, u32[]{:S(2)}, u32[]{:S(2)}) collective-permute-start(bf16[32,1024]{1,0:T(8,128)(2,1)S(1)} %get-tuple-element.72), channel_id=1, source_target_pairs={{0,66},{2,64},{64,2},{66,0},{1,67},{3,65},{65,3},{67,1},{4,70},{6,... | collective-permute-start | bytes 196616 | tf_op jit(solution)/shard_map/ppermute | solution.py:288
  97.4 6.0 %collective-permute-start.25 = (bf16[32,1024]{1,0:T(8,128)(2,1)S(1)}, bf16[32,1024]{1,0:T(8,128)(2,1)S(1)}, u32[]{:S(2)}, u32[]{:S(2)}) collective-permute-start(bf16[32,1024]{1,0:T(8,128)(2,1)S(1)} %get-tuple-element.87), channel_id=1, source_target_pairs={{0,2},{2,0},{64,66},{66,64},{1,3},{3,1},{65,67},{67,65},{4,6},{6,4... | collective-permute-start | bytes 196616 | tf_op jit(solution)/shard_map/ppermute | solution.py:288
  101.6 20.9 %collective-permute-start.17 = (bf16[4,32,1024]{2,1,0:T(8,128)(2,1)}, bf16[4,32,1024]{2,1,0:T(8,128)(2,1)S(1)}, u32[]{:S(2)}, u32[]{:S(2)}) collective-permute-start(bf16[4,32,1024]{2,1,0:T(8,128)(2,1)} %copy-done.40), channel_id=1, source_target_pairs={{0,1},{1,0},{2,3},{3,2},{4,5},{5,4},{6,7},{7,6},{8,9},{9,8},{10,11... | collective-permute-start | bytes 786440 | tf_op jit(solution)/shard_map/ppermute | solution.py:288
  105.5 6.2 %collective-permute-start.33 = (bf16[32,1024]{1,0:T(8,128)(2,1)S(1)}, bf16[32,1024]{1,0:T(8,128)(2,1)S(1)}, u32[]{:S(2)}, u32[]{:S(2)}) collective-permute-start(bf16[32,1024]{1,0:T(8,128)(2,1)S(1)} %get-tuple-element.90.p0), channel_id=1, source_target_pairs={{0,66},{2,64},{64,2},{66,0},{1,67},{3,65},{65,3},{67,1},{4,70},{6,... | collective-permute-start | bytes 196616 | tf_op jit(solution)/shard_map/ppermute | solution.py:288
  107.4 5.8 %collective-permute-start.29 = (bf16[32,1024]{1,0:T(8,128)(2,1)S(1)}, bf16[32,1024]{1,0:T(8,128)(2,1)S(1)}, u32[]{:S(2)}, u32[]{:S(2)}) collective-permute-start(bf16[32,1024]{1,0:T(8,128)(2,1)S(1)} %get-tuple-element.90.p0), channel_id=1, source_target_pairs={{0,2},{2,0},{64,66},{66,64},{1,3},{3,1},{65,67},{67,65},{4,6},{6,4... | collective-permute-start | bytes 196616 | tf_op jit(solution)/shard_map/ppermute | solution.py:288
  117.7 8.3 %collective-permute-start.35 = (bf16[256,128]{1,0:T(8,128)(2,1)S(1)}, bf16[256,128]{1,0:T(8,128)(2,1)S(1)}, u32[]{:S(2)}, u32[]{:S(2)}) collective-permute-start(bf16[256,128]{1,0:T(8,128)(2,1)S(1)} %get-tuple-element.95), channel_id=1, source_target_pairs={{0,16},{16,0},{32,48},{48,32},{1,17},{17,1},{33,49},{49,33},{2,18}... | collective-permute-start | bytes 196616 | tf_op jit(solution)/shard_map/ppermute | solution.py:288
  119.1 8.6 %collective-permute-start.36 = (bf16[256,128]{1,0:T(8,128)(2,1)S(1)}, bf16[256,128]{1,0:T(8,128)(2,1)S(1)}, u32[]{:S(2)}, u32[]{:S(2)}) collective-permute-start(bf16[256,128]{1,0:T(8,128)(2,1)S(1)} %get-tuple-element.96), channel_id=1, source_target_pairs={{0,32},{16,48},{32,0},{48,16},{1,33},{17,49},{33,1},{49,17},{2,34}... | collective-permute-start | bytes 196616 | tf_op jit(solution)/shard_map/ppermute | solution.py:288
  121.2 6.7 %collective-permute-start.37 = (bf16[256,128]{1,0:T(8,128)(2,1)S(1)}, bf16[256,128]{1,0:T(8,128)(2,1)S(1)}, u32[]{:S(2)}, u32[]{:S(2)}) collective-permute-start(bf16[256,128]{1,0:T(8,128)(2,1)S(1)} %get-tuple-element.97), channel_id=1, source_target_pairs={{0,48},{16,32},{32,16},{48,0},{1,49},{17,33},{33,17},{49,1},{2,50}... | collective-permute-start | bytes 196616 | tf_op jit(solution)/shard_map/ppermute | solution.py:288
  123.1 7.5 %collective-permute-start.18 = (bf16[32,1024]{1,0:T(8,128)(2,1)}, bf16[32,1024]{1,0:T(8,128)(2,1)S(1)}, u32[]{:S(2)}, u32[]{:S(2)}) collective-permute-start(bf16[32,1024]{1,0:T(8,128)(2,1)} %get-tuple-element.80), channel_id=1, source_target_pairs={{0,2},{2,0},{64,66},{66,64},{1,3},{3,1},{65,67},{67,65},{4,6},{6,4... | collective-permute-start | bytes 196616 | tf_op jit(solution)/shard_map/ppermute | solution.py:288
  131.5 7.4 %collective-permute-start.21 = (bf16[32,1024]{1,0:T(8,128)(2,1)S(1)}, bf16[32,1024]{1,0:T(8,128)(2,1)S(1)}, u32[]{:S(2)}, u32[]{:S(2)}) collective-permute-start(bf16[32,1024]{1,0:T(8,128)(2,1)S(1)} %shard_map.262.p0), channel_id=1, source_target_pairs={{0,1},{1,0},{2,3},{3,2},{4,5},{5,4},{6,7},{7,6},{8,9},{9,8},{10,11... | collective-permute-start | bytes 196616 | tf_op jit(solution)/shard_map/ppermute | solution.py:288
  131.8 7.6 %collective-permute-start.47 = (f32[17,128]{1,0:T(8,128)S(1)}, f32[17,128]{1,0:T(8,128)S(1)}, u32[]{:S(2)}, u32[]{:S(2)}) collective-permute-start(f32[17,128]{1,0:T(8,128)S(1)} %fusion.2), channel_id=1, source_target_pairs={{0,64},{2,66},{64,0},{66,2},{1,65},{3,67},{65,1},{67,3},{4,68},{6,... | collective-permute-start | bytes 26120 | tf_op jit(solution)/shard_map/ppermute | solution.py:288
  133.6 5.9 %collective-permute-start.48 = (f32[17,128]{1,0:T(8,128)S(1)}, f32[17,128]{1,0:T(8,128)S(1)}, u32[]{:S(2)}, u32[]{:S(2)}) collective-permute-start(f32[17,128]{1,0:T(8,128)S(1)} %fusion.2), channel_id=1, source_target_pairs={{0,66},{2,64},{64,2},{66,0},{1,67},{3,65},{65,3},{67,1},{4,70},{6,... | collective-permute-start | bytes 26120 | tf_op jit(solution)/shard_map/ppermute | solution.py:288
  135.9 9.2 %collective-permute-start.22 = (bf16[32,1024]{1,0:T(8,128)(2,1)S(1)}, bf16[32,1024]{1,0:T(8,128)(2,1)S(1)}, u32[]{:S(2)}, u32[]{:S(2)}) collective-permute-start(bf16[32,1024]{1,0:T(8,128)(2,1)S(1)} %shard_map.262.p0), channel_id=1, source_target_pairs={{0,2},{2,0},{1,3},{3,1},{4,6},{6,4},{5,7},{7,5},{8,10},{10,8},{9,1... | collective-permute-start | bytes 196616 | tf_op jit(solution)/shard_map/ppermute | solution.py:288
  138.9 6.2 %collective-permute-start.23 = (bf16[32,1024]{1,0:T(8,128)(2,1)S(1)}, bf16[32,1024]{1,0:T(8,128)(2,1)S(1)}, u32[]{:S(2)}, u32[]{:S(2)}) collective-permute-start(bf16[32,1024]{1,0:T(8,128)(2,1)S(1)} %collective-permute-done.21.p1), channel_id=1, source_target_pairs={{0,2},{2,0},{1,3},{3,1},{4,6},{6,4},{5,7},{7,5},{8,10},{10,8},{9,1... | collective-permute-start | bytes 196616 | tf_op jit(solution)/shard_map/ppermute | solution.py:288
  140.6 7.2 %collective-permute-start.51 = (f32[17,128]{1,0:T(8,128)S(1)}, f32[17,128]{1,0:T(8,128)S(1)}, u32[]{:S(2)}, u32[]{:S(2)}) collective-permute-start(f32[17,128]{1,0:T(8,128)S(1)} %add_add_fusion.2), channel_id=1, source_target_pairs={{0,48},{16,32},{32,16},{48,0},{1,49},{17,33},{33,17},{49,1},{2,50}... | collective-permute-start | bytes 26120 | tf_op jit(solution)/shard_map/ppermute | solution.py:288
  147.5 10.4 %collective-permute-start.38 = (bf16[4,32,1024]{2,1,0:T(8,128)(2,1)}, bf16[4,32,1024]{2,1,0:T(8,128)(2,1)S(1)}, u32[]{:S(2)}, u32[]{:S(2)}) collective-permute-start(bf16[4,32,1024]{2,1,0:T(8,128)(2,1)} %get-tuple-element.100), channel_id=1, source_target_pairs={{0,1},{1,0},{2,3},{3,2},{4,5},{5,4},{6,7},{7,6},{8,9},{9,8},{10,11... | collective-permute-start | bytes 786440 | tf_op jit(solution)/shard_map/ppermute | solution.py:288
  147.9 13.6 %collective-permute-start.54 = (f32[17,128]{1,0:T(8,128)S(1)}, f32[17,128]{1,0:T(8,128)S(1)}, u32[]{:S(2)}, u32[]{:S(2)}) collective-permute-start(f32[17,128]{1,0:T(8,128)S(1)} %add_add_fusion.1), channel_id=1, source_target_pairs={{0,12},{4,8},{8,4},{12,0},{1,13},{5,9},{9,5},{13,1},{2,14},{6,10},... | collective-permute-start | bytes 26120 | tf_op jit(solution)/shard_map/ppermute | solution.py:288
  149.9 12.6 %collective-permute-start.53 = (f32[17,128]{1,0:T(8,128)S(1)}, f32[17,128]{1,0:T(8,128)S(1)}, u32[]{:S(2)}, u32[]{:S(2)}) collective-permute-start(f32[17,128]{1,0:T(8,128)S(1)} %add_add_fusion.1), channel_id=1, source_target_pairs={{0,8},{4,12},{8,0},{12,4},{1,9},{5,13},{9,1},{13,5},{2,10},{6,14},... | collective-permute-start | bytes 26120 | tf_op jit(solution)/shard_map/ppermute | solution.py:288
  150.1 12.4 %collective-permute-start.52 = (f32[17,128]{1,0:T(8,128)S(1)}, f32[17,128]{1,0:T(8,128)S(1)}, u32[]{:S(2)}, u32[]{:S(2)}) collective-permute-start(f32[17,128]{1,0:T(8,128)S(1)} %add_add_fusion.1), channel_id=1, source_target_pairs={{0,4},{4,0},{8,12},{12,8},{1,5},{5,1},{9,13},{13,9},{2,6},{6,2},{1... | collective-permute-start | bytes 26120 | tf_op jit(solution)/shard_map/ppermute | solution.py:288
  153.0 28.3 %all-to-all-start.1 = ((bf16[32,32,384]{2,1,0:T(8,128)(2,1)}), bf16[32,32,384]{2,1,0:T(8,128)(2,1)S(1)}, u32[]{:S(2)}, u32[]{:S(2)}) async-start(bf16[32,32,384]{2,1,0:T(8,128)(2,1)} %bitcast.22), calls=%async_computation.1 | async-start | bytes 1572864 | tf_op jit(solution)/shard_map/all_to_all | solution.py:420
  157.9 9.5 %collective-permute-start.39 = (bf16[32,1024]{1,0:T(8,128)(2,1)S(1)}, bf16[32,1024]{1,0:T(8,128)(2,1)S(1)}, u32[]{:S(2)}, u32[]{:S(2)}) collective-permute-start(bf16[32,1024]{1,0:T(8,128)(2,1)S(1)} %get-tuple-element.102), channel_id=1, source_target_pairs={{0,2},{2,0},{64,66},{66,64},{1,3},{3,1},{65,67},{67,65},{4,6},{6,4... | collective-permute-start | bytes 196616 | tf_op jit(solution)/shard_map/ppermute | solution.py:288
  160.3 10.0 %collective-permute-start.40 = (bf16[32,1024]{1,0:T(8,128)(2,1)S(1)}, bf16[32,1024]{1,0:T(8,128)(2,1)S(1)}, u32[]{:S(2)}, u32[]{:S(2)}) collective-permute-start(bf16[32,1024]{1,0:T(8,128)(2,1)S(1)} %get-tuple-element.103), channel_id=1, source_target_pairs={{0,64},{2,66},{64,0},{66,2},{1,65},{3,67},{65,1},{67,3},{4,68},{6,... | collective-permute-start | bytes 196616 | tf_op jit(solution)/shard_map/ppermute | solution.py:288
  161.5 8.8 %collective-permute-start.41 = (bf16[32,1024]{1,0:T(8,128)(2,1)S(1)}, bf16[32,1024]{1,0:T(8,128)(2,1)S(1)}, u32[]{:S(2)}, u32[]{:S(2)}) collective-permute-start(bf16[32,1024]{1,0:T(8,128)(2,1)S(1)} %get-tuple-element.104), channel_id=1, source_target_pairs={{0,66},{2,64},{64,2},{66,0},{1,67},{3,65},{65,3},{67,1},{4,70},{6,... | collective-permute-start | bytes 196616 | tf_op jit(solution)/shard_map/ppermute | solution.py:288
  171.2 7.0 %collective-permute-start.43 = (bf16[32,1024]{1,0:T(8,128)(2,1)S(1)}, bf16[32,1024]{1,0:T(8,128)(2,1)S(1)}, u32[]{:S(2)}, u32[]{:S(2)}) collective-permute-start(bf16[32,1024]{1,0:T(8,128)(2,1)S(1)} %shard_map.269.p0), channel_id=1, source_target_pairs={{0,2},{2,0},{1,3},{3,1},{4,6},{6,4},{5,7},{7,5},{8,10},{10,8},{9,1... | collective-permute-start | bytes 196616 | tf_op jit(solution)/shard_map/ppermute | solution.py:288
  176.1 6.0 %collective-permute-start.55 = (bf16[32,1792]{1,0:T(8,128)(2,1)S(1)}, bf16[32,1792]{1,0:T(8,128)(2,1)S(1)}, u32[]{:S(2)}, u32[]{:S(2)}) collective-permute-start(bf16[32,1792]{1,0:T(8,128)(2,1)S(1)} %broadcast_select_fusion.2), channel_id=1, source_target_pairs={{0,64},{64,0},{1,65},{65,1},{2,66},{66,2},{3,67},{67,3},{4,68},{68... | collective-permute-start | bytes 344072 | tf_op jit(solution)/shard_map/ppermute | solution.py:288
  (87 other events, 590.2 us)
Sparse Core Ops, SparseCore 0:
  15.5 55.1 all-gather.1
  95.4 79.6 reduce-scatter.1

commit v3 on v2

--- a/solution.py
+++ b/solution.py
@@ -18,13 +18,13 @@
 WHOLE = pl.BlockSpec(memory_space=pltpu.VMEM)
 
 
-def call(body, outs, *operands):
+def call(body, outs, *operands, room=12):
     return pl.pallas_call(
         body,
         out_shape=[jax.ShapeDtypeStruct(shape, kind) for shape, kind in outs],
         in_specs=[WHOLE] * len(operands),
         out_specs=[WHOLE] * len(outs),
-        compiler_params=pltpu.CompilerParams(vmem_limit_bytes=40 * 2**20),
+        compiler_params=pltpu.CompilerParams(vmem_limit_bytes=room * 2**20),
     )(*operands)
 
 
@@ -181,7 +181,9 @@
     for z in range(2):
         left, left_dy = rows[:, z * 512 : (z + 1) * 512], dy[:, z * 512 : (z + 1) * 512]
         def put(value, at, width):
-            dw[:, z, :, at : at + width] = value.astype(BF).reshape(16, 32, width)
+            blocks = value.astype(BF).reshape(4, 4, 32, width)
+            for y in range(4):
+                dw[:, z, y, :, at : at + width] = blocks[y]
         put(left_product(left, dgu[:, :512]), 0, 512)
         put(left_product(left, dgu[:, 512:1024]), 512, 512)
         put(left_product(left_dy, active[:, :512]), 1024, 512)
@@ -259,12 +261,17 @@
     keep[...] = partial[:, 0]
 
 
-def attend_weights(normed, d_qkv, dw):
-    dw[...] = left_product(normed[...], d_qkv[...]).astype(BF)
-
-
-def out_weights(d_attn, o, dw):
-    dw[...] = left_product(d_attn[...], o[...].astype(BF)).astype(BF)
+def attend_weights(normed, d_qkv, d_attn, o, attn_part, ffn_part, head_part, dw):
+    first = left_product(normed[...], d_qkv[...]).astype(BF)
+    second = left_product(d_attn[...], o[...].astype(BF)).astype(BF)
+    dw[:, :32, :256] = first.reshape(32, 32, 256)
+    dw[:, :32, 256:] = second.reshape(32, 32, 128)
+    def fold(part):
+        rows = [part[:, i * 128 : (i + 1) * 128] for i in range(8)]
+        return jnp.concatenate(rows + [jnp.zeros((8, 128), F32)])
+    heads = jnp.concatenate([head_part[...], jnp.zeros((14, 128), F32)])
+    gains = jnp.concatenate([fold(attn_part), fold(ffn_part), heads], axis=1).astype(BF)
+    dw[:, 32:, :] = jnp.broadcast_to(gains[None], (32, 16, 384))
 
 
 def token_rows(own, one, two, three, dh, x, gain, out):
@@ -275,15 +282,38 @@
     out[...] = (dh[...] + grad).astype(BF)
 
 
-def finish_attend(parts, wq, wk, wv, wo):
-    low = jnp.sum(parts[0].astype(F32), axis=0)
-    high = jnp.sum(parts[1].astype(F32), axis=0)
+def finish_attend(parts, wq, wk, wv, wo, gains):
+    sums = [jnp.sum(parts[z].astype(F32), axis=0) for z in range(2)]
+    gains[...] = sums[0][32:] + sums[1][32:]
+    low, high = sums[0][:32], sums[1][:32]
     wq[...] = jnp.concatenate([low[:, :128], high[:, :128]], axis=1)
     wk[...] = jnp.concatenate([low[:, 128:192], high[:, 128:192]], axis=1)
     wv[...] = jnp.concatenate([low[:, 192:256], high[:, 192:256]], axis=1)
     wo[...] = jnp.concatenate([low[:, 256:], high[:, 256:]], axis=1)
 
 
+def finish_feed(parts, wg, wu, wd):
+    low = jnp.sum(parts[0].astype(F32), axis=0)
+    high = jnp.sum(parts[1].astype(F32), axis=0)
+    for i, out in enumerate((wg, wu, wd)):
+        wide, tail = slice(i * 512, (i + 1) * 512), slice(1536 + i * 64, 1600 + i * 64)
+        out[...] = jnp.concatenate(
+            [low[:, wide], low[:, tail], high[:, wide], high[:, tail]], axis=1
+        )
+
+
+def finish_gains(one, two, attn, ffn, query, key):
+    total = one[...] + two[...]
+    attn[...] = total[:8, :128]
+    ffn[...] = total[:8, 128:256]
+    query[...] = total[0:1, 256:320] + total[0:1, 320:384]
+    key[...] = total[1:2, 256:320]
+
+
+def add_gains(one, two, out):
+    out[...] = one[...] + two[...]
+
+
 def swap(value, axes, size, mask):
     return lax.ppermute(value, axes, [(i, i ^ mask) for i in range(size)])
 
@@ -292,11 +322,15 @@
     return [swap(pieces[k], axes, 4, k) for k in (1, 2, 3)]
 
 
-def sum_scatter(send, keep):
+def sum_pair(send, keep):
     got = swap(send, "c", 2, 1)
     small = ((32, 1024), BF)
-    own, one, two, three = call(pair_add, [((32, 1024), F32), small, small, small], keep, got)
-    return [own] + fan([None, one, two, three], Z)
+    return list(call(pair_add, [((32, 1024), F32), small, small, small], keep, got))
+
+
+def sum_scatter(send, keep):
+    own, *rest = sum_pair(send, keep)
+    return [own] + fan([None] + rest, Z)
 
 
 def gather_rows(rows):
@@ -335,6 +369,11 @@
     return jnp.concatenate(parts + [zeros], axis=1)
 
 
+def after(values, *first):
+    out = lax.optimization_barrier(tuple(values) + tuple(first))
+    return list(out[: len(values)])
+
+
 def local(
     tokens, positions, attn_gain, ffn_gain, query_gain, key_gain,
     w_query, w_key, w_value, w_out, w_gate, w_up, w_down, cotangent,
@@ -342,27 +381,30 @@
     zl, y, head = lax.axis_index("zl"), lax.axis_index("y"), lax.axis_index(("zh", "c"))
     attn_gain_row, ffn_gain_row = attn_gain[None], ffn_gain[None]
 
+    feeds = [w_gate, w_up, w_down]
+    send_f = feed_columns(*column_half(feeds, 1 - zl))
+    got_f = swap(send_f, "zl", 2, 1)
+
     small = [w_query, w_key, w_value, w_out]
+    small = after(small, send_f)
     lows = jnp.concatenate([p[:, : p.shape[1] // 2] for p in small], axis=1)
     highs = jnp.concatenate([p[:, p.shape[1] // 2 :] for p in small], axis=1)
     blocks = jnp.broadcast_to(jnp.stack([lows, highs])[:, None], (2, 16, 32, 384))
-    w_a = lax.all_to_all(blocks.reshape(1024, 384), PLANE, 0, 0, tiled=True)
-
-    feeds = [w_gate, w_up, w_down]
-    keep_f = feed_columns(*column_half(feeds, zl))
-    send_f = feed_columns(*column_half(feeds, 1 - zl))
-    got_f = swap(send_f, "zl", 2, 1)
+    blocks = blocks.reshape(1024, 384)
+    w_a = lax.all_to_all(blocks, PLANE, 0, 0, tiled=True)
+
+    order = head ^ jnp.arange(4)
+    (late_tokens,) = after([tokens], blocks)
+    x_own = late_tokens[0].reshape(4, 32, 1024)[order].reshape(128, 1024)
+    x_other = swap(x_own, "zl", 2, 1)
+
+    keep_f = feed_columns(*column_half(after(feeds, blocks), zl))
     rows_f = jnp.where(zl == 0, jnp.stack([keep_f, got_f]), jnp.stack([got_f, keep_f]))
     w_f = lax.all_gather(rows_f, ("y", "x"), axis=0)
 
-    order = head ^ jnp.arange(4)
-    x_own = tokens[0].reshape(4, 32, 1024)[order].reshape(128, 1024)
-    x_other = swap(x_own, "zl", 2, 1)
-    dy_own = cotangent[0].reshape(4, 32, 1024)[order].reshape(128, 1024)
-    dy_other = swap(dy_own, "zl", 2, 1)
-
+    (late_positions,) = after([positions], blocks)
     steps = jnp.array([dl * 16 + ky * 4 + d for ky in range(4) for dl in range(2) for d in range(4)])
-    places = positions[0].reshape(32, 32)[steps ^ (zl * 16 + y * 4 + head)].reshape(1024)
+    places = late_positions[0].reshape(32, 32)[steps ^ (zl * 16 + y * 4 + head)].reshape(1024)
     own_places = places[:256]
     frequency = ROPE_BASE ** (-(jnp.arange(32).astype(F32) * 2.0 / 64))
     angles = own_places.astype(F32)[:, None] * frequency
@@ -379,6 +421,9 @@
         x_own, x_other, w_a, attn_gain_row, qk_gain, cosine, sine,
     )
     kvs = [kv] + fan([kv] * 4, "y")
+    (late_dy,) = after([cotangent], kv)
+    dy_own = late_dy[0].reshape(4, 32, 1024)[order].reshape(128, 1024)
+    dy_other = swap(dy_own, "zl", 2, 1)
     send, keep, o, l = call(
         attend, halves + [((256, 128), F32)] * 2, qh, *kvs, own_places, places, w_a
     )
@@ -388,17 +433,18 @@
     )
     send, keep, hn_all, act, dgu = call(
         feed, halves + [((256, 1024), BF), ((256, 640), BF), ((256, 1152), BF)],
-        *gather_rows(hn), dy_own, dy_other, w_f,
-    )
-    d_hn = sum_scatter(send, keep)
+        *gather_rows(hn), dy_own, dy_other, w_f, room=20,
+    )
+    pair = sum_pair(send, keep)
+    act, dgu = after([act, dgu], *pair)
+    d_hn = [pair[0]] + fan([None] + pair[1:], Z)
     send_b, keep_b, dw_f = call(
-        feed_weights, halves + [((16, 2, 32, 1792), BF)], hn_all, dy_own, dy_other, act, dgu, w_f
-    )
-    (rows,) = call(block_rows, [((32, 1024), BF)], *sum_scatter(send_b, keep_b), h)
-    block_out = gather_head(rows, head)
+        feed_weights, halves + [((4, 2, 4, 32, 1792), BF)],
+        hn_all, dy_own, dy_other, act, dgu, w_f, room=20,
+    )
     dw_f = lax.psum_scatter(
-        dw_f.reshape(1024, 1792), ("y", "x"), scatter_dimension=0, tiled=True
-    ).reshape(2, 32, 1792)
+        dw_f.reshape(1024, 1792), "x", scatter_dimension=0, tiled=True
+    )
     dh, d_low, ffn_gain_part = call(
         hidden_grad, [((32, 1024), F32), ((32, 1024), BF), ((1, 1024), F32)],
         *d_hn, h, dy_own, ffn_gain_row,
@@ -413,41 +459,34 @@
         [((256, 256), BF)] + halves + [((1, 1024), F32), ((2, 128), F32)],
         d_qh, d_kvs[0], *fan(d_kvs, "y"), qkv, cosine, sine, qk_gain, w_a, x_own, x_other,
     )
+    (dw_a,) = call(
+        attend_weights, [((32, 48, 384), BF)],
+        normed, d_qkv, d_attn, o, attn_gain_part, ffn_gain_part, head_part,
+    )
+    (keep,) = after([keep], dw_a)
     d_xn = sum_scatter(send, keep)
-    (dw_qkv,) = call(attend_weights, [((1024, 256), BF)], normed, d_qkv)
-    (dw_o,) = call(out_weights, [((1024, 128), BF)], d_attn, o)
-    dw_a = jnp.concatenate([dw_qkv, dw_o], axis=1)
+    (send_b,) = after([send_b], d_xn[0])
+    (rows,) = call(block_rows, [((32, 1024), BF)], *sum_scatter(send_b, keep_b), h)
     dw_a = lax.all_to_all(dw_a, PLANE, 0, 0, tiled=True)
+    block_out = gather_head(rows, head)
     (rows,) = call(token_rows, [((32, 1024), BF)], *d_xn, dh, x_own, attn_gain_row)
     tokens_grad = gather_head(rows, head)
-    grad_wq, grad_wk, grad_wv, grad_wo = call(
-        finish_attend, [((32, n), F32) for n in (256, 128, 128, 256)],
-        dw_a.reshape(2, 16, 32, 384),
-    )
-
-    def finish(total):
-        other = swap(jnp.where(zl == 0, total[1], total[0]), "zl", 2, 1)
-        own = jnp.where(zl == 0, total[0], total[1])
-        low, high = jnp.where(zl == 0, own, other), jnp.where(zl == 0, other, own)
-        outs = []
-        for i in range(3):
-            wide, tail = slice(i * 512, (i + 1) * 512), slice(1536 + i * 64, 1600 + i * 64)
-            pieces = [low[:, wide], low[:, tail], high[:, wide], high[:, tail]]
-            outs.append(jnp.concatenate(pieces, axis=1).astype(F32))
-        return outs
-
-    grad_wg, grad_wu, grad_wd = finish(dw_f)
-
-    head_part = head_part[:, :64] + head_part[:, 64:] * jnp.array([[1.0], [0.0]], F32)
-    gains = jnp.concatenate([attn_gain_part[0], ffn_gain_part[0], head_part.reshape(-1)])
-    gains = gains.reshape(17, 128)
-    gains = gains + swap(gains, "c", 2, 1)
-    for axes in (Z, "y", "x"):
-        one, two, three = fan([gains] * 4, axes)
-        gains = (gains + one) + (two + three)
-    gains = gains.reshape(-1)
+    dw_f = lax.all_to_all(dw_f, ("zl", "y"), 0, 0, tiled=True)
+    grad_wq, grad_wk, grad_wv, grad_wo, gains = call(
+        finish_attend, [((32, n), F32) for n in (256, 128, 128, 256)] + [((16, 384), F32)],
+        dw_a.reshape(2, 16, 48, 384),
+    )
+    (gains,) = call(add_gains, [((16, 384), F32)], gains, swap(gains, "c", 2, 1))
+    attn_sum, ffn_sum, query_sum, key_sum = call(
+        finish_gains, [((8, 128), F32)] * 2 + [((1, 64), F32)] * 2,
+        gains, swap(gains, "zh", 2, 1),
+    )
+    grad_wg, grad_wu, grad_wd = call(
+        finish_feed, [((32, 1152), F32)] * 3, dw_f.reshape(2, 4, 32, 1792)
+    )
     return (
-        block_out, tokens_grad, gains[:1024], gains[1024:2048], gains[2048:2112], gains[2112:],
+        block_out, tokens_grad, attn_sum.reshape(1024), ffn_sum.reshape(1024),
+        query_sum.reshape(64), key_sum.reshape(64),
         grad_wq, grad_wk, grad_wv, grad_wo, grad_wg, grad_wu, grad_wd,
     )
 

time: 195 us -> 199 us (1.021)
  blocking collectives: 0 us -> 21.6 us
  starting transfers between devices: 75.7 us -> 60.7 us
  waiting for transfers between devices: 49.5 us -> 53.1 us
  local copies, waits for them, and re-layouts: 25.4 us -> 22.5 us
    all_to_all x0 -> x1, blocking collectives: none -> 21.6 us  [local(): dw_a = lax.all_to_all(dw_a, PLANE, 0, 0, tiled=True)]
    ppermute x56 -> x47, starting transfers between devices: 63.4 us -> 48.3 us  [swap(): return lax.ppermute(value, axes, [(i, i ^ mask) for i in range(size)])]
    unnamed x119 -> x84, local copies, waits for them, and re-layouts: 19 us -> 14.4 us
    ppermute x56 -> x47, waiting for transfers between devices: 36.7 us -> 40.4 us  [swap(): return lax.ppermute(value, axes, [(i, i ^ mask) for i in range(size)])]
    slice x4, local copies, waits for them, and re-layouts: 0.16 us -> 3.12 us  [local(): lows = jnp.concatenate([p[:, :p.shape[1] // 2] for p in small], axis=1)]
    select_n x2 -> x5, other arithmetic: 1.9 us -> 4.72 us  [column_half(): jnp.where(zl == 0, p[:, :p.shape[1] // 2], p[:, p.shape[1] // 2:])]
    convert_element_type x3 -> x0, other arithmetic: 2.03 us -> none  [finish(): outs.append(jnp.concatenate(pieces, axis=1).astype(F32))]
    pallas_call x17 -> x19, Pallas kernels: 14.3 us -> 14.2 us  [call(): pl.pallas_call(body, out_shape=[jax.ShapeDtypeStruct(shape, kind) for sha...]
  transfers between devices with their start and end apart: 60 -> 51, of which waited for: 23 -> 23; matrix products, arithmetic and copies ran while one was open for 5% -> 6% of each run, Pallas kernels for 7% -> 7%
where the time goes in v3:
time: 199 us; the launch traced here: 197 us
  starting transfers between devices  60.7 us (31%)
  waiting for transfers between devices  53.1 us (27%)
  local copies, waits for them, and re-layouts  22.5 us (11%)
  blocking collectives  21.6 us (11%)
  Pallas kernels  17.6 us (9%)
  between operations  14.8 us (7%)
  other arithmetic  7.18 us (4%)
    ppermute x47, starting transfers between devices, swap(): return lax.ppermute(value, axes, [(i, i ^ mask) for i in range(size)])  48.3 us
    ppermute x47, waiting for transfers between devices, swap(): return lax.ppermute(value, axes, [(i, i ^ mask) for i in range(size)])  40.4 us
    all_to_all x1, blocking collectives, local(): dw_a = lax.all_to_all(dw_a, PLANE, 0, 0, tiled=True)  21.6 us
    unnamed x84, local copies, waits for them, and re-layouts  14.4 us
    pallas_call x19, Pallas kernels, call(): pl.pallas_call(body, out_shape=[jax.ShapeDtypeStruct(shape, kind) for sha...  14.2 us
    all_to_all x1, waiting for transfers between devices, local(): w_a = lax.all_to_all(blocks, PLANE, 0, 0, tiled=True)  12.6 us
    all_to_all x1, starting transfers between devices, local(): w_a = lax.all_to_all(blocks, PLANE, 0, 0, tiled=True)  8.76 us
    select_n x5, other arithmetic, column_half(): jnp.where(zl == 0, p[:, :p.shape[1] // 2], p[:, p.shape[1] // 2:])  4.72 us
  transfers between devices with their start and end apart: 51, of which 23 were waited for; matrix products, arithmetic and copies ran while one was open for 6% of the time, Pallas kernels for 7%

profile of v3, /device:TPU:0, one launch (start us, length us, event | category | flops | bytes accessed | tf_op | source)
XLA Modules:
  0.0 197.3 jit_solution(125456732871750074)
XLA Ops:
  9.4 2.1 %collective-permute-start.16 = (bf16[32,1792]{1,0:T(8,128)(2,1)S(1)}, bf16[32,1792]{1,0:T(8,128)(2,1)S(1)}, u32[]{:S(2)}, u32[]{:S(2)}) collective-permute-start(bf16[32,1792]{1,0:T(8,128)(2,1)S(1)} %concatenate.32), channel_id=1, source_target_pairs={{0,64},{64,0},{1,65},{65,1},{2,66},{66,2},{3,67},{67,3},{4,68},{68... | collective-permute-start | bytes 344072 | tf_op jit(solution)/shard_map/ppermute | solution.py:318
  20.2 8.8 %all-to-all-start = ((bf16[32,32,384]{2,1,0:T(8,128)(2,1)}), bf16[32,32,384]{2,1,0:T(8,128)(2,1)S(1)}, u32[]{:S(2)}, u32[]{:S(2)}) async-start(bf16[32,32,384]{2,1,0:T(8,128)(2,1)} %bitcast.7), calls=%async_computation | async-start | bytes 1572864 | tf_op jit(solution)/shard_map/all_to_all | solution.py:394
  32.1 12.6 %all-to-all-done = bf16[32,32,384]{2,1,0:T(8,128)(2,1)S(1)} async-done(((bf16[32,32,384]{2,1,0:T(8,128)(2,1)}), bf16[32,32,384]{2,1,0:T(8,128)(2,1)S(1)}, u32[]{:S(2)}, u32[]{:S(2)}) %all-to-all-start) | async-done | bytes 786464 | tf_op jit(solution)/shard_map/all_to_all | solution.py:394
  46.8 3.2 %collective-permute-start.2 = (bf16[256,128]{1,0:T(8,128)(2,1)S(1)}, bf16[256,128]{1,0:T(8,128)(2,1)S(1)}, u32[]{:S(2)}, u32[]{:S(2)}) collective-permute-start(bf16[256,128]{1,0:T(8,128)(2,1)S(1)} %get-tuple-element.94.kv0), channel_id=1, source_target_pairs={{0,32},{16,48},{32,0},{48,16},{1,33},{17,49},{33,1},{49,17},{2,34}... | collective-permute-start | bytes 196616 | tf_op jit(solution)/shard_map/ppermute | solution.py:318
  51.2 1.8 collective-permute-done.2.kv2
  52.9 2.5 %collective-permute-done.3.kv3 = bf16[256,128]{1,0:T(8,128)(2,1)S(1)} collective-permute-done((bf16[256,128]{1,0:T(8,128)(2,1)S(1)}, bf16[256,128]{1,0:T(8,128)(2,1)S(1)}, u32[]{:S(2)}, u32[]{:S(2)}) %collective-permute-start.3) | collective-permute-done | bytes 65568 | tf_op jit(solution)/shard_map/ppermute | solution.py:318
  55.5 2.1 %shard_map.247 = (bf16[4,32,1024]{2,1,0:T(8,128)(2,1)}, f32[4,32,1024]{2,1,0:T(8,128)S(1)}, f32[256,128]{1,0:T(8,128)S(1)}, f32[256,128]{1,0:T(8,128)S(1)}) custom-call(bf16[256,128]{1,0:T(8,128)(2,1)S(1)} %get-tuple-element.93.qh, bf16[256,128]{1,0:T(8,128)(2,1)S(1)} %get-tuple-element.94.kv0, bf16[256,128]{1,0:T(8,128)(2,1)S(1)} %collective-permute-done.1.kv1, ...), custom_call_target="tpu_custom_call" | custom-call | tf_op jit(solution)/shard_map/pallas_call | solution.py:22
  60.4 4.0 %collective-permute-start.5 = (bf16[32,1024]{1,0:T(8,128)(2,1)S(1)}, bf16[32,1024]{1,0:T(8,128)(2,1)S(1)}, u32[]{:S(2)}, u32[]{:S(2)}) collective-permute-start(bf16[32,1024]{1,0:T(8,128)(2,1)S(1)} %get-tuple-element.98), channel_id=1, source_target_pairs={{0,2},{2,0},{64,66},{66,64},{1,3},{3,1},{65,67},{67,65},{4,6},{6,4... | collective-permute-start | bytes 196616 | tf_op jit(solution)/shard_map/ppermute | solution.py:318
  65.2 7.5 %collective-permute-done.5.one = bf16[32,1024]{1,0:T(8,128)(2,1)S(1)} collective-permute-done((bf16[32,1024]{1,0:T(8,128)(2,1)S(1)}, bf16[32,1024]{1,0:T(8,128)(2,1)S(1)}, u32[]{:S(2)}, u32[]{:S(2)}) %collective-permute-start.5) | collective-permute-done | bytes 65568 | tf_op jit(solution)/shard_map/ppermute | solution.py:318
  72.9 2.5 %collective-permute-start.9 = (bf16[32,1024]{1,0:T(8,128)(2,1)S(1)}, bf16[32,1024]{1,0:T(8,128)(2,1)S(1)}, u32[]{:S(2)}, u32[]{:S(2)}) collective-permute-start(bf16[32,1024]{1,0:T(8,128)(2,1)S(1)} %get-tuple-element.101.p0), channel_id=1, source_target_pairs={{0,2},{2,0},{64,66},{66,64},{1,3},{3,1},{65,67},{67,65},{4,6},{6,4... | collective-permute-start | bytes 196616 | tf_op jit(solution)/shard_map/ppermute | solution.py:318
  77.0 2.1 %collective-permute-done.9.p2 = bf16[32,1024]{1,0:T(8,128)(2,1)S(1)} collective-permute-done((bf16[32,1024]{1,0:T(8,128)(2,1)S(1)}, bf16[32,1024]{1,0:T(8,128)(2,1)S(1)}, u32[]{:S(2)}, u32[]{:S(2)}) %collective-permute-start.9) | collective-permute-done | bytes 65568 | tf_op jit(solution)/shard_map/ppermute | solution.py:318
  82.1 2.0 %copy-done.1 = bf16[16,2,32,1792]{3,2,1,0:T(8,128)(2,1)S(1)} copy-done((bf16[16,2,32,1792]{3,2,1,0:T(8,128)(2,1)S(1)}, bf16[16,2,32,1792]{3,2,1,0:T(8,128)(2,1)}, u32[]{:S(2)}) %copy-start.1) | copy-done | bytes 3670040
  84.2 2.1 %shard_map.250 = (bf16[4,32,1024]{2,1,0:T(8,128)(2,1)S(1)}, f32[4,32,1024]{2,1,0:T(8,128)S(1)}, bf16[256,1024]{1,0:T(8,128)(2,1)S(1)}, bf16[256,640]{1,0:T(8,128)(2,1)S(1)}, bf16[256,1152]{1,0:T(8,128)(2,1)S(1)}) custom-call(bf16[32,1024]{1,0:T(8,128)(2,1)S(1)} %get-tuple-element.101.p0, bf16[32,1024]{1,0:T(8,128)(2,1)S(1)} %collective-permute-done.8.p1, ...), custom_call_target="tpu_custom_call" | custom-call | tf_op jit(solution)/shard_map/pallas_call | solution.py:22
  90.6 1.7 shard_map.252
  92.3 1.8 copy-done.3
  99.1 2.3 %collective-permute-done.18.one = bf16[32,1024]{1,0:T(8,128)(2,1)S(1)} collective-permute-done((bf16[32,1024]{1,0:T(8,128)(2,1)}, bf16[32,1024]{1,0:T(8,128)(2,1)S(1)}, u32[]{:S(2)}, u32[]{:S(2)}) %collective-permute-start.18) | collective-permute-done | bytes 65568 | tf_op jit(solution)/shard_map/ppermute | solution.py:318
  101.3 1.8 collective-permute-done.20.three
  108.5 1.8 collective-permute-done.22.p2
  113.6 3.1 %shard_map.254 = (bf16[256,1024]{1,0:T(8,128)(2,1)S(1)}, f32[256,128]{1,0:T(8,128)S(1)}, f32[256,128]{1,0:T(8,128)S(1)}, bf16[256,128]{1,0:T(8,128)(2,1)S(1)}, b...) custom-call(bf16[32,1024]{1,0:T(8,128)(2,1)S(1)} %get-tuple-element.120.p0, ...), custom_call_target="tpu_custom_call" | custom-call | tf_op jit(solution)/shard_map/pallas_call | solution.py:22
  116.8 3.3 %collective-permute-start.29 = (bf16[256,128]{1,0:T(8,128)(2,1)S(1)}, bf16[256,128]{1,0:T(8,128)(2,1)S(1)}, u32[]{:S(2)}, u32[]{:S(2)}) collective-permute-start(bf16[256,128]{1,0:T(8,128)(2,1)S(1)} %get-tuple-element.126), channel_id=1, source_target_pairs={{0,32},{16,48},{32,0},{48,16},{1,33},{17,49},{33,1},{49,17},{2,34}... | collective-permute-start | bytes 196616 | tf_op jit(solution)/shard_map/ppermute | solution.py:318
  121.7 1.9 collective-permute-done.29.two
  123.6 1.9 collective-permute-done.30.three
  129.1 21.6 %all_to_all.25 = bf16[32,48,384]{2,1,0:T(8,128)(2,1)S(1)} all-to-all(bf16[32,48,384]{2,1,0:T(8,128)(2,1)S(1)} %shard_map.256), channel_id=1, replica_groups=mesh['zl'=2,'y'=4,'x'=4,'zh'=2,'c'=2] {'zl','y','x'}, dimensions={0} | all-to-all | bytes 2359296 | tf_op jit(solution)/shard_map/all_to_all | solution.py:470
  150.6 3.6 %all-to-all-start.2 = ((bf16[8,32,1792]{2,1,0:T(8,128)(2,1)}), bf16[8,32,1792]{2,1,0:T(8,128)(2,1)S(1)}, u32[]{:S(2)}, u32[]{:S(2)}) async-start(bf16[8,32,1792]{2,1,0:T(8,128)(2,1)} %bitcast.49), calls=%async_computation.3 | async-start | bytes 1835008 | tf_op jit(solution)/shard_map/all_to_all | solution.py:474
  154.3 1.7 collective-permute-done.31.got
  157.3 2.6 %collective-permute-start.39 = (bf16[32,1024]{1,0:T(8,128)(2,1)S(1)}, bf16[32,1024]{1,0:T(8,128)(2,1)S(1)}, u32[]{:S(2)}, u32[]{:S(2)}) collective-permute-start(bf16[32,1024]{1,0:T(8,128)(2,1)S(1)} %get-tuple-element.144), channel_id=1, source_target_pairs={{0,2},{2,0},{64,66},{66,64},{1,3},{3,1},{65,67},{67,65},{4,6},{6,4... | collective-permute-start | bytes 196616 | tf_op jit(solution)/shard_map/ppermute | solution.py:318
  161.9 2.3 %collective-permute-start.33 = (bf16[32,1024]{1,0:T(8,128)(2,1)S(1)}, bf16[32,1024]{1,0:T(8,128)(2,1)S(1)}, u32[]{:S(2)}, u32[]{:S(2)}) collective-permute-start(bf16[32,1024]{1,0:T(8,128)(2,1)S(1)} %get-tuple-element.141), channel_id=1, source_target_pairs={{0,2},{2,0},{64,66},{66,64},{1,3},{3,1},{65,67},{67,65},{4,6},{6,4... | collective-permute-start | bytes 196616 | tf_op jit(solution)/shard_map/ppermute | solution.py:318
  165.4 3.2 %collective-permute-done.39.one = bf16[32,1024]{1,0:T(8,128)(2,1)S(1)} collective-permute-done((bf16[32,1024]{1,0:T(8,128)(2,1)S(1)}, bf16[32,1024]{1,0:T(8,128)(2,1)S(1)}, u32[]{:S(2)}, u32[]{:S(2)}) %collective-permute-start.39) | collective-permute-done | bytes 65568 | tf_op jit(solution)/shard_map/ppermute | solution.py:318
  168.6 1.8 collective-permute-start.35
  172.0 2.2 %collective-permute-done.35.three = bf16[32,1024]{1,0:T(8,128)(2,1)S(1)} collective-permute-done((bf16[32,1024]{1,0:T(8,128)(2,1)S(1)}, bf16[32,1024]{1,0:T(8,128)(2,1)S(1)}, u32[]{:S(2)}, u32[]{:S(2)}) %collective-permute-start.35) | collective-permute-done | bytes 65568 | tf_op jit(solution)/shard_map/ppermute | solution.py:318
  174.8 3.1 %collective-permute-start.44 = (bf16[32,1024]{1,0:T(8,128)(2,1)S(1)}, bf16[32,1024]{1,0:T(8,128)(2,1)S(1)}, u32[]{:S(2)}, u32[]{:S(2)}) collective-permute-start(bf16[32,1024]{1,0:T(8,128)(2,1)S(1)} %collective-permute-done.42.p1), channel_id=1, source_target_pairs={{0,2},{2,0},{1,3},{3,1},{4,6},{6,4},{5,7},{7,5},{8,10},{10,8},{9,1... | collective-permute-start | bytes 196616 | tf_op jit(solution)/shard_map/ppermute | solution.py:318
  178.3 3.1 %collective-permute-start.38 = (bf16[32,1024]{1,0:T(8,128)(2,1)S(1)}, bf16[32,1024]{1,0:T(8,128)(2,1)S(1)}, u32[]{:S(2)}, u32[]{:S(2)}) collective-permute-start(bf16[32,1024]{1,0:T(8,128)(2,1)S(1)} %collective-permute-done.36.p1), channel_id=1, source_target_pairs={{0,2},{2,0},{1,3},{3,1},{4,6},{6,4},{5,7},{7,5},{8,10},{10,8},{9,1... | collective-permute-start | bytes 196616 | tf_op jit(solution)/shard_map/ppermute | solution.py:318
  (230 shorter events, 64.5 us)
Async XLA Ops:
  7.2 74.9 %all-gather.2.cloned.1.call-start = ((), (), s32[]{:S(2)}) async-start(), calls=%async_computation.4 | async-start | bytes 3899392 | tf_op jit(solution)/shard_map/all_gather | solution.py:403
  9.4 9.3 %collective-permute-start.16 = (bf16[32,1792]{1,0:T(8,128)(2,1)S(1)}, bf16[32,1792]{1,0:T(8,128)(2,1)S(1)}, u32[]{:S(2)}, u32[]{:S(2)}) collective-permute-start(bf16[32,1792]{1,0:T(8,128)(2,1)S(1)} %concatenate.32), channel_id=1, source_target_pairs={{0,64},{64,0},{1,65},{65,1},{2,66},{66,2},{3,67},{67,3},{4,68},{68... | collective-permute-start | bytes 344072 | tf_op jit(solution)/shard_map/ppermute | solution.py:318
  20.1 12.0 %collective-permute-start = (bf16[128,1024]{1,0:T(8,128)(2,1)S(1)}, bf16[128,1024]{1,0:T(8,128)(2,1)S(1)}, u32[]{:S(2)}, u32[]{:S(2)}) collective-permute-start(bf16[128,1024]{1,0:T(8,128)(2,1)S(1)} %bitcast.33), channel_id=1, source_target_pairs={{0,64},{64,0},{1,65},{65,1},{2,66},{66,2},{3,67},{67,3},{4,68},{68... | collective-permute-start | bytes 786440 | tf_op jit(solution)/shard_map/ppermute | solution.py:318
  20.2 24.5 %all-to-all-start = ((bf16[32,32,384]{2,1,0:T(8,128)(2,1)}), bf16[32,32,384]{2,1,0:T(8,128)(2,1)S(1)}, u32[]{:S(2)}, u32[]{:S(2)}) async-start(bf16[32,32,384]{2,1,0:T(8,128)(2,1)} %bitcast.7), calls=%async_computation | async-start | bytes 1572864 | tf_op jit(solution)/shard_map/all_to_all | solution.py:394
  29.0 121.6 %reduce-scatter.2.cloned.1.call-start = ((), (), s32[]{:S(2)}) async-start(), calls=%async_computation.5 | async-start | bytes 4587520 | tf_op jit(solution)/shard_map/reduce_scatter | solution.py:445
  46.8 6.1 %collective-permute-start.2 = (bf16[256,128]{1,0:T(8,128)(2,1)S(1)}, bf16[256,128]{1,0:T(8,128)(2,1)S(1)}, u32[]{:S(2)}, u32[]{:S(2)}) collective-permute-start(bf16[256,128]{1,0:T(8,128)(2,1)S(1)} %get-tuple-element.94.kv0), channel_id=1, source_target_pairs={{0,32},{16,48},{32,0},{48,16},{1,33},{17,49},{33,1},{49,17},{2,34}... | collective-permute-start | bytes 196616 | tf_op jit(solution)/shard_map/ppermute | solution.py:318
  50.0 5.5 %collective-permute-start.3 = (bf16[256,128]{1,0:T(8,128)(2,1)S(1)}, bf16[256,128]{1,0:T(8,128)(2,1)S(1)}, u32[]{:S(2)}, u32[]{:S(2)}) collective-permute-start(bf16[256,128]{1,0:T(8,128)(2,1)S(1)} %get-tuple-element.94.kv0), channel_id=1, source_target_pairs={{0,48},{16,32},{32,16},{48,0},{1,49},{17,33},{33,17},{49,1},{2,50}... | collective-permute-start | bytes 196616 | tf_op jit(solution)/shard_map/ppermute | solution.py:318
  59.9 21.0 %collective-permute-start.15 = (bf16[128,1024]{1,0:T(8,128)(2,1)S(1)}, bf16[128,1024]{1,0:T(8,128)(2,1)S(1)}, u32[]{:S(2)}, u32[]{:S(2)}) collective-permute-start(bf16[128,1024]{1,0:T(8,128)(2,1)S(1)} %bitcast.39), channel_id=1, source_target_pairs={{0,64},{64,0},{1,65},{65,1},{2,66},{66,2},{3,67},{67,3},{4,68},{68... | collective-permute-start | bytes 786440 | tf_op jit(solution)/shard_map/ppermute | solution.py:318
  60.4 12.3 %collective-permute-start.5 = (bf16[32,1024]{1,0:T(8,128)(2,1)S(1)}, bf16[32,1024]{1,0:T(8,128)(2,1)S(1)}, u32[]{:S(2)}, u32[]{:S(2)}) collective-permute-start(bf16[32,1024]{1,0:T(8,128)(2,1)S(1)} %get-tuple-element.98), channel_id=1, source_target_pairs={{0,2},{2,0},{64,66},{66,64},{1,3},{3,1},{65,67},{67,65},{4,6},{6,4... | collective-permute-start | bytes 196616 | tf_op jit(solution)/shard_map/ppermute | solution.py:318
  64.4 8.3 %collective-permute-start.6 = (bf16[32,1024]{1,0:T(8,128)(2,1)S(1)}, bf16[32,1024]{1,0:T(8,128)(2,1)S(1)}, u32[]{:S(2)}, u32[]{:S(2)}) collective-permute-start(bf16[32,1024]{1,0:T(8,128)(2,1)S(1)} %get-tuple-element.99), channel_id=1, source_target_pairs={{0,64},{2,66},{64,0},{66,2},{1,65},{3,67},{65,1},{67,3},{4,68},{6,... | collective-permute-start | bytes 196616 | tf_op jit(solution)/shard_map/ppermute | solution.py:318
  65.2 7.5 %collective-permute-start.7 = (bf16[32,1024]{1,0:T(8,128)(2,1)S(1)}, bf16[32,1024]{1,0:T(8,128)(2,1)S(1)}, u32[]{:S(2)}, u32[]{:S(2)}) collective-permute-start(bf16[32,1024]{1,0:T(8,128)(2,1)S(1)} %get-tuple-element.100), channel_id=1, source_target_pairs={{0,66},{2,64},{64,2},{66,0},{1,67},{3,65},{65,3},{67,1},{4,70},{6,... | collective-permute-start | bytes 196616 | tf_op jit(solution)/shard_map/ppermute | solution.py:318
  72.9 6.3 %collective-permute-start.9 = (bf16[32,1024]{1,0:T(8,128)(2,1)S(1)}, bf16[32,1024]{1,0:T(8,128)(2,1)S(1)}, u32[]{:S(2)}, u32[]{:S(2)}) collective-permute-start(bf16[32,1024]{1,0:T(8,128)(2,1)S(1)} %get-tuple-element.101.p0), channel_id=1, source_target_pairs={{0,2},{2,0},{64,66},{66,64},{1,3},{3,1},{65,67},{67,65},{4,6},{6,4... | collective-permute-start | bytes 196616 | tf_op jit(solution)/shard_map/ppermute | solution.py:318
  75.4 5.5 %collective-permute-start.13 = (bf16[32,1024]{1,0:T(8,128)(2,1)S(1)}, bf16[32,1024]{1,0:T(8,128)(2,1)S(1)}, u32[]{:S(2)}, u32[]{:S(2)}) collective-permute-start(bf16[32,1024]{1,0:T(8,128)(2,1)S(1)} %get-tuple-element.101.p0), channel_id=1, source_target_pairs={{0,66},{2,64},{64,2},{66,0},{1,67},{3,65},{65,3},{67,1},{4,70},{6,... | collective-permute-start | bytes 196616 | tf_op jit(solution)/shard_map/ppermute | solution.py:318
  94.9 6.4 %collective-permute-start.18 = (bf16[32,1024]{1,0:T(8,128)(2,1)}, bf16[32,1024]{1,0:T(8,128)(2,1)S(1)}, u32[]{:S(2)}, u32[]{:S(2)}) collective-permute-start(bf16[32,1024]{1,0:T(8,128)(2,1)} %copy-done.30), channel_id=1, source_target_pairs={{0,2},{2,0},{64,66},{66,64},{1,3},{3,1},{65,67},{67,65},{4,6},{6,4... | collective-permute-start | bytes 196616 | tf_op jit(solution)/shard_map/ppermute | solution.py:318
  96.3 5.1 %collective-permute-start.19 = (bf16[32,1024]{1,0:T(8,128)(2,1)}, bf16[32,1024]{1,0:T(8,128)(2,1)S(1)}, u32[]{:S(2)}, u32[]{:S(2)}) collective-permute-start(bf16[32,1024]{1,0:T(8,128)(2,1)} %copy-done.29), channel_id=1, source_target_pairs={{0,64},{2,66},{64,0},{66,2},{1,65},{3,67},{65,1},{67,3},{4,68},{6,... | collective-permute-start | bytes 196616 | tf_op jit(solution)/shard_map/ppermute | solution.py:318
  97.5 5.7 %collective-permute-start.20 = (bf16[32,1024]{1,0:T(8,128)(2,1)}, bf16[32,1024]{1,0:T(8,128)(2,1)S(1)}, u32[]{:S(2)}, u32[]{:S(2)}) collective-permute-start(bf16[32,1024]{1,0:T(8,128)(2,1)} %copy-done.28), channel_id=1, source_target_pairs={{0,66},{2,64},{64,2},{66,0},{1,67},{3,65},{65,3},{67,1},{4,70},{6,... | collective-permute-start | bytes 196616 | tf_op jit(solution)/shard_map/ppermute | solution.py:318
  104.3 6.0 %collective-permute-start.22 = (bf16[32,1024]{1,0:T(8,128)(2,1)S(1)}, bf16[32,1024]{1,0:T(8,128)(2,1)S(1)}, u32[]{:S(2)}, u32[]{:S(2)}) collective-permute-start(bf16[32,1024]{1,0:T(8,128)(2,1)S(1)} %get-tuple-element.120.p0), channel_id=1, source_target_pairs={{0,2},{2,0},{64,66},{66,64},{1,3},{3,1},{65,67},{67,65},{4,6},{6,4... | collective-permute-start | bytes 196616 | tf_op jit(solution)/shard_map/ppermute | solution.py:318
  106.8 5.5 %collective-permute-start.26 = (bf16[32,1024]{1,0:T(8,128)(2,1)S(1)}, bf16[32,1024]{1,0:T(8,128)(2,1)S(1)}, u32[]{:S(2)}, u32[]{:S(2)}) collective-permute-start(bf16[32,1024]{1,0:T(8,128)(2,1)S(1)} %get-tuple-element.120.p0), channel_id=1, source_target_pairs={{0,66},{2,64},{64,2},{66,0},{1,67},{3,65},{65,3},{67,1},{4,70},{6,... | collective-permute-start | bytes 196616 | tf_op jit(solution)/shard_map/ppermute | solution.py:318
  116.8 6.8 %collective-permute-start.29 = (bf16[256,128]{1,0:T(8,128)(2,1)S(1)}, bf16[256,128]{1,0:T(8,128)(2,1)S(1)}, u32[]{:S(2)}, u32[]{:S(2)}) collective-permute-start(bf16[256,128]{1,0:T(8,128)(2,1)S(1)} %get-tuple-element.126), channel_id=1, source_target_pairs={{0,32},{16,48},{32,0},{48,16},{1,33},{17,49},{33,1},{49,17},{2,34}... | collective-permute-start | bytes 196616 | tf_op jit(solution)/shard_map/ppermute | solution.py:318
  120.0 5.5 %collective-permute-start.30 = (bf16[256,128]{1,0:T(8,128)(2,1)S(1)}, bf16[256,128]{1,0:T(8,128)(2,1)S(1)}, u32[]{:S(2)}, u32[]{:S(2)}) collective-permute-start(bf16[256,128]{1,0:T(8,128)(2,1)S(1)} %get-tuple-element.127), channel_id=1, source_target_pairs={{0,48},{16,32},{32,16},{48,0},{1,49},{17,33},{33,17},{49,1},{2,50}... | collective-permute-start | bytes 196616 | tf_op jit(solution)/shard_map/ppermute | solution.py:318
  150.6 39.0 %all-to-all-start.2 = ((bf16[8,32,1792]{2,1,0:T(8,128)(2,1)}), bf16[8,32,1792]{2,1,0:T(8,128)(2,1)S(1)}, u32[]{:S(2)}, u32[]{:S(2)}) async-start(bf16[8,32,1792]{2,1,0:T(8,128)(2,1)} %bitcast.49), calls=%async_computation.3 | async-start | bytes 1835008 | tf_op jit(solution)/shard_map/all_to_all | solution.py:474
  157.3 11.3 %collective-permute-start.39 = (bf16[32,1024]{1,0:T(8,128)(2,1)S(1)}, bf16[32,1024]{1,0:T(8,128)(2,1)S(1)}, u32[]{:S(2)}, u32[]{:S(2)}) collective-permute-start(bf16[32,1024]{1,0:T(8,128)(2,1)S(1)} %get-tuple-element.144), channel_id=1, source_target_pairs={{0,2},{2,0},{64,66},{66,64},{1,3},{3,1},{65,67},{67,65},{4,6},{6,4... | collective-permute-start | bytes 196616 | tf_op jit(solution)/shard_map/ppermute | solution.py:318
  160.0 10.5 %collective-permute-start.40 = (bf16[32,1024]{1,0:T(8,128)(2,1)S(1)}, bf16[32,1024]{1,0:T(8,128)(2,1)S(1)}, u32[]{:S(2)}, u32[]{:S(2)}) collective-permute-start(bf16[32,1024]{1,0:T(8,128)(2,1)S(1)} %get-tuple-element.145), channel_id=1, source_target_pairs={{0,64},{2,66},{64,0},{66,2},{1,65},{3,67},{65,1},{67,3},{4,68},{6,... | collective-permute-start | bytes 196616 | tf_op jit(solution)/shard_map/ppermute | solution.py:318
  161.2 9.3 %collective-permute-start.41 = (bf16[32,1024]{1,0:T(8,128)(2,1)S(1)}, bf16[32,1024]{1,0:T(8,128)(2,1)S(1)}, u32[]{:S(2)}, u32[]{:S(2)}) collective-permute-start(bf16[32,1024]{1,0:T(8,128)(2,1)S(1)} %get-tuple-element.146), channel_id=1, source_target_pairs={{0,66},{2,64},{64,2},{66,0},{1,67},{3,65},{65,3},{67,1},{4,70},{6,... | collective-permute-start | bytes 196616 | tf_op jit(solution)/shard_map/ppermute | solution.py:318
  161.9 9.5 %collective-permute-start.33 = (bf16[32,1024]{1,0:T(8,128)(2,1)S(1)}, bf16[32,1024]{1,0:T(8,128)(2,1)S(1)}, u32[]{:S(2)}, u32[]{:S(2)}) collective-permute-start(bf16[32,1024]{1,0:T(8,128)(2,1)S(1)} %get-tuple-element.141), channel_id=1, source_target_pairs={{0,2},{2,0},{64,66},{66,64},{1,3},{3,1},{65,67},{67,65},{4,6},{6,4... | collective-permute-start | bytes 196616 | tf_op jit(solution)/shard_map/ppermute | solution.py:318
  164.2 7.8 %collective-permute-start.34 = (bf16[32,1024]{1,0:T(8,128)(2,1)S(1)}, bf16[32,1024]{1,0:T(8,128)(2,1)S(1)}, u32[]{:S(2)}, u32[]{:S(2)}) collective-permute-start(bf16[32,1024]{1,0:T(8,128)(2,1)S(1)} %get-tuple-element.142), channel_id=1, source_target_pairs={{0,64},{2,66},{64,0},{66,2},{1,65},{3,67},{65,1},{67,3},{4,68},{6,... | collective-permute-start | bytes 196616 | tf_op jit(solution)/shard_map/ppermute | solution.py:318
  168.6 5.5 %collective-permute-start.35 = (bf16[32,1024]{1,0:T(8,128)(2,1)S(1)}, bf16[32,1024]{1,0:T(8,128)(2,1)S(1)}, u32[]{:S(2)}, u32[]{:S(2)}) collective-permute-start(bf16[32,1024]{1,0:T(8,128)(2,1)S(1)} %get-tuple-element.143), channel_id=1, source_target_pairs={{0,66},{2,64},{64,2},{66,0},{1,67},{3,65},{65,3},{67,1},{4,70},{6,... | collective-permute-start | bytes 196616 | tf_op jit(solution)/shard_map/ppermute | solution.py:318
  174.3 9.5 %collective-permute-start.43 = (bf16[32,1024]{1,0:T(8,128)(2,1)S(1)}, bf16[32,1024]{1,0:T(8,128)(2,1)S(1)}, u32[]{:S(2)}, u32[]{:S(2)}) collective-permute-start(bf16[32,1024]{1,0:T(8,128)(2,1)S(1)} %shard_map.261.p0), channel_id=1, source_target_pairs={{0,2},{2,0},{1,3},{3,1},{4,6},{6,4},{5,7},{7,5},{8,10},{10,8},{9,1... | collective-permute-start | bytes 196616 | tf_op jit(solution)/shard_map/ppermute | solution.py:318
  174.8 9.1 %collective-permute-start.44 = (bf16[32,1024]{1,0:T(8,128)(2,1)S(1)}, bf16[32,1024]{1,0:T(8,128)(2,1)S(1)}, u32[]{:S(2)}, u32[]{:S(2)}) collective-permute-start(bf16[32,1024]{1,0:T(8,128)(2,1)S(1)} %collective-permute-done.42.p1), channel_id=1, source_target_pairs={{0,2},{2,0},{1,3},{3,1},{4,6},{6,4},{5,7},{7,5},{8,10},{10,8},{9,1... | collective-permute-start | bytes 196616 | tf_op jit(solution)/shard_map/ppermute | solution.py:318
  177.9 8.2 %collective-permute-start.37 = (bf16[32,1024]{1,0:T(8,128)(2,1)S(1)}, bf16[32,1024]{1,0:T(8,128)(2,1)S(1)}, u32[]{:S(2)}, u32[]{:S(2)}) collective-permute-start(bf16[32,1024]{1,0:T(8,128)(2,1)S(1)} %shard_map.259.p0), channel_id=1, source_target_pairs={{0,2},{2,0},{1,3},{3,1},{4,6},{6,4},{5,7},{7,5},{8,10},{10,8},{9,1... | collective-permute-start | bytes 196616 | tf_op jit(solution)/shard_map/ppermute | solution.py:318
  178.3 7.8 %collective-permute-start.38 = (bf16[32,1024]{1,0:T(8,128)(2,1)S(1)}, bf16[32,1024]{1,0:T(8,128)(2,1)S(1)}, u32[]{:S(2)}, u32[]{:S(2)}) collective-permute-start(bf16[32,1024]{1,0:T(8,128)(2,1)S(1)} %collective-permute-done.36.p1), channel_id=1, source_target_pairs={{0,2},{2,0},{1,3},{3,1},{4,6},{6,4},{5,7},{7,5},{8,10},{10,8},{9,1... | collective-permute-start | bytes 196616 | tf_op jit(solution)/shard_map/ppermute | solution.py:318
  183.4 5.6 %collective-permute-start.46 = (f32[16,384]{1,0:T(8,128)S(1)}, f32[16,384]{1,0:T(8,128)S(1)}, u32[]{:S(2)}, u32[]{:S(2)}) collective-permute-start(f32[16,384]{1,0:T(8,128)S(1)} %shard_map.264.one), channel_id=1, source_target_pairs={{0,2},{2,0},{1,3},{3,1},{4,6},{6,4},{5,7},{7,5},{8,10},{10,8},{9,1... | collective-permute-start | bytes 73736 | tf_op jit(solution)/shard_map/ppermute | solution.py:318
  (61 other events, 524.9 us)
Sparse Core Ops, SparseCore 0:
  19.6 54.3 all-gather.1
  95.0 39.7 reduce-scatter.1

commit v4 on v3

--- a/solution.py
+++ b/solution.py
@@ -18,14 +18,23 @@
 WHOLE = pl.BlockSpec(memory_space=pltpu.VMEM)
 
 
-def call(body, outs, *operands, room=12):
-    return pl.pallas_call(
-        body,
-        out_shape=[jax.ShapeDtypeStruct(shape, kind) for shape, kind in outs],
-        in_specs=[WHOLE] * len(operands),
-        out_specs=[WHOLE] * len(outs),
-        compiler_params=pltpu.CompilerParams(vmem_limit_bytes=room * 2**20),
-    )(*operands)
+class Far:
+    def __init__(self, value, kind=None):
+        self.value, self.kind = value, kind
+
+
+def call(body, outs, *operands, room=16):
+    spec = lambda item: pl.BlockSpec() if isinstance(item, Far) else WHOLE
+    bare = lambda item: item.value if isinstance(item, Far) else item
+    return list(
+        pl.pallas_call(
+            body,
+            out_shape=[jax.ShapeDtypeStruct(*bare(out)) for out in outs],
+            in_specs=[spec(item) for item in operands],
+            out_specs=[spec(out) for out in outs],
+            compiler_params=pltpu.CompilerParams(vmem_limit_bytes=room * 2**20),
+        )(*[bare(item) for item in operands])
+    )
 
 
 def dot(left, right):
@@ -134,7 +143,10 @@
     return active.astype(BF), d_gate, d_act * silu
 
 
-def feed(p0, p1, p2, p3, p4, p5, p6, p7, dy_own, dy_other, w, send, keep, hn, act, dgu):
+def feed(
+    p0, p1, p2, p3, p4, p5, p6, p7, dy_own, dy_other, w,
+    send, keep, hn, act, dgu,
+):
     rows = jnp.concatenate([p[...] for p in (p0, p1, p2, p3, p4, p5, p6, p7)])
     hn[...] = rows
     dy = jnp.concatenate([dy_own[...], dy_other[...]])
@@ -164,20 +176,21 @@
         part = part + right_product(dgu_tail, w[:, z, :, 1536:1664].reshape(512, 128))
         halves.append(part)
     partial = jnp.concatenate(halves, axis=1).reshape(4, 2, 32, 1024)
-    send[...] = partial[:, 1].astype(BF)
-    keep[...] = partial[:, 0]
-
-
-def feed_weights(hn, dy_own, dy_other, act, dgu, w, send, keep, dw):
+    send[:, :32] = partial[:, 1].astype(BF)
+    keep[:, :32] = partial[:, 0]
+    low_act = act[...]
+    halves = []
+    for z in range(2):
+        part = right_product(low_act[:, :512], w[:, z, :, 1024:1536].reshape(512, 512))
+        halves.append(part + right_product(low_act[:, 512:], w[:, z, :, 1664:].reshape(512, 128)))
+    partial = jnp.concatenate(halves, axis=1).reshape(4, 2, 32, 1024)
+    send[:, 32:] = partial[:, 1].astype(BF)
+    keep[:, 32:] = partial[:, 0]
+
+
+def feed_weights(hn, dy_own, dy_other, act, dgu, dw):
     dy = jnp.concatenate([dy_own[...], dy_other[...]])
     rows, active = hn[...], act[...]
-    halves = []
-    for z in range(2):
-        part = right_product(active[:, :512], w[:, z, :, 1024:1536].reshape(512, 512))
-        halves.append(part + right_product(active[:, 512:], w[:, z, :, 1664:].reshape(512, 128)))
-    partial = jnp.concatenate(halves, axis=1).reshape(4, 2, 32, 1024)
-    send[...] = partial[:, 1].astype(BF)
-    keep[...] = partial[:, 0]
     for z in range(2):
         left, left_dy = rows[:, z * 512 : (z + 1) * 512], dy[:, z * 512 : (z + 1) * 512]
         def put(value, at, width):
@@ -191,13 +204,11 @@
         put(left_product(left_dy, active[:, 512:]), 1664, 128)
 
 
-def block_rows(own, one, two, three, h, out):
-    out[...] = (h[...] + total_of(own, one, two, three)).astype(BF)
-
-
-def hidden_grad(own, one, two, three, h, dy, gain, dh, low, gain_part):
-    d_hn = total_of(own, one, two, three)
+def hidden_grad(own, one, two, three, h, dy, gain, dh, low, gain_part, block):
+    total = total_of(own, one, two, three)
+    d_hn, branch = total[:32], total[32:]
     rows = h[...]
+    block[...] = (rows + branch).astype(BF)
     scale = row_scale(rows)
     hat = rows * scale
     gain_part[...] = jnp.sum(d_hn * hat, axis=0, keepdims=True)
@@ -235,8 +246,8 @@
 
 
 def project_grad(
-    d_qh, own, one, two, three, qkv, cosine, sine, qk_gain, w, x_own, x_other,
-    d_qkv, send, keep, gain_part, head_part,
+    d_qh, own, one, two, three, qkv, cosine, sine, qk_gain, w, x_own, x_other, ffn_part,
+    d_qkv, send, keep, gains,
 ):
     d_kv = total_of(own, one, two, three)
     cos, sin = cosine[...], sine[...]
@@ -246,8 +257,9 @@
     d_q = d_qh[...]
     d_qn = d_q * cos - other_half(d_q) * sin
     d_kn = d_kv * cos - other_half(d_kv) * sin
-    head_part[0:1] = jnp.sum(d_qn * q_hat, axis=0, keepdims=True)
-    head_part[1:2] = jnp.sum(d_kn * k_hat, axis=0, keepdims=True)
+    heads = jnp.concatenate(
+        [jnp.sum(d_qn * q_hat, axis=0, keepdims=True), jnp.sum(d_kn * k_hat, axis=0, keepdims=True)]
+    )
     d_q = head_norm_grad(d_qn * qk_gain[0:1], q_hat, q_scale)
     d_k = head_norm_grad(d_kn * qk_gain[1:2], k_hat, k_scale)
     d_k = jnp.where(lanes(d_k) < 64, d_k, d_kv)
@@ -255,31 +267,38 @@
     d_qkv[...] = low
     partial = right_product(low, w[:, :256])
     x = jnp.concatenate([x_own[...], x_other[...]]).astype(F32)
-    gain_part[...] = jnp.sum(partial * (x * row_scale(x)), axis=0, keepdims=True)
+    attn_part = jnp.sum(partial * (x * row_scale(x)), axis=0, keepdims=True)
+    def fold(part):
+        rows = [part[:, i * 128 : (i + 1) * 128] for i in range(8)]
+        return jnp.concatenate(rows + [jnp.zeros((8, 128), F32)])
+    heads = jnp.concatenate([heads, jnp.zeros((14, 128), F32)])
+    gains[...] = jnp.concatenate([fold(attn_part), fold(ffn_part), heads], axis=1).astype(BF)
     partial = partial.reshape(4, 2, 32, 1024)
     send[...] = partial[:, 1].astype(BF)
     keep[...] = partial[:, 0]
 
 
-def attend_weights(normed, d_qkv, d_attn, o, attn_part, ffn_part, head_part, dw):
-    first = left_product(normed[...], d_qkv[...]).astype(BF)
-    second = left_product(d_attn[...], o[...].astype(BF)).astype(BF)
-    dw[:, :32, :256] = first.reshape(32, 32, 256)
-    dw[:, :32, 256:] = second.reshape(32, 32, 128)
-    def fold(part):
-        rows = [part[:, i * 128 : (i + 1) * 128] for i in range(8)]
-        return jnp.concatenate(rows + [jnp.zeros((8, 128), F32)])
-    heads = jnp.concatenate([head_part[...], jnp.zeros((14, 128), F32)])
-    gains = jnp.concatenate([fold(attn_part), fold(ffn_part), heads], axis=1).astype(BF)
-    dw[:, 32:, :] = jnp.broadcast_to(gains[None], (32, 16, 384))
-
-
-def token_rows(own, one, two, three, dh, x, gain, out):
+def attend_weights(normed, d_qkv, d_attn, o, gains, dw):
+    first = left_product(normed[...], d_qkv[...]).astype(BF).reshape(8, 4, 32, 256)
+    second = left_product(d_attn[...], o[...].astype(BF)).astype(BF).reshape(8, 4, 32, 128)
+    for i in range(8):
+        dw[:, i * 32 : (i + 1) * 32, :256] = first[i]
+        dw[:, i * 32 : (i + 1) * 32, 256:] = second[i]
+    dw[:, 256:] = jnp.broadcast_to(gains[...][None], (4, 16, 384))
+
+
+def share_gains(dw, out):
+    out[:, :32] = dw[:256].reshape(8, 32, 384)
+    out[:, 32:] = jnp.broadcast_to(dw[256:][None], (8, 16, 384))
+
+
+def token_rows(own, one, two, three, dh, x, gain, block, out):
     d_xn = total_of(own, one, two, three)
     rows = x[:32].astype(F32)
     scale = row_scale(rows)
     grad = row_norm_grad(d_xn * gain[...], rows * scale, scale)
-    out[...] = (dh[...] + grad).astype(BF)
+    out[:32] = (dh[...] + grad).astype(BF)
+    out[32:] = block[...]
 
 
 def finish_attend(parts, wq, wk, wv, wo, gains):
@@ -302,6 +321,10 @@
         )
 
 
+def add_two(own, one, out):
+    out[...] = own[...] + one[...]
+
+
 def finish_gains(one, two, attn, ffn, query, key):
     total = one[...] + two[...]
     attn[...] = total[:8, :128]
@@ -310,8 +333,29 @@
     key[...] = total[1:2, 256:320]
 
 
-def add_gains(one, two, out):
-    out[...] = one[...] + two[...]
+def prepare(zl, wq, wk, wv, wo, wg, wu, wd, blocks, send_f, keep_f):
+    for z in range(2):
+        at = 0
+        for w in (wq, wk, wv, wo):
+            width = w.shape[1] // 2
+            part = w[:, z * width : (z + 1) * width]
+            blocks[z, :, :, at : at + width] = jnp.broadcast_to(part[None], (16, 32, width))
+            at += width
+    pad = jnp.zeros((32, 64), BF)
+    sides = []
+    for z in range(2):
+        parts = [w[:, z * 576 : (z + 1) * 576] for w in (wg, wu, wd)]
+        sides.append(
+            jnp.concatenate([p[:, :512] for p in parts] + [p[:, 512:] for p in parts] + [pad], axis=1)
+        )
+    first = zl[0] == 0
+    keep_f[...] = jnp.where(first, sides[0], sides[1])
+    send_f[...] = jnp.where(first, sides[1], sides[0])
+
+
+def order_rows(zl, own, got, out):
+    out[zl[0]] = own[...]
+    out[1 - zl[0]] = got[...]
 
 
 def swap(value, axes, size, mask):
@@ -324,8 +368,8 @@
 
 def sum_pair(send, keep):
     got = swap(send, "c", 2, 1)
-    small = ((32, 1024), BF)
-    return list(call(pair_add, [((32, 1024), F32), small, small, small], keep, got))
+    shape = send.shape[1:]
+    return call(pair_add, [(shape, F32)] + [(shape, BF)] * 3, keep, got)
 
 
 def sum_scatter(send, keep):
@@ -341,9 +385,11 @@
     return pieces
 
 
-def place_rows(head, p0, p1, p2, p3, out):
+def place_rows(head, p0, p1, p2, p3, tokens_grad, block_out):
     for k, piece in enumerate((p0, p1, p2, p3)):
-        out[pl.ds((head[0] ^ k) * 32, 32)] = piece[...]
+        at = pl.ds((head[0] ^ k) * 32, 32)
+        tokens_grad[at] = piece[:32]
+        block_out[at] = piece[32:]
 
 
 def gather_head(rows, head):
@@ -351,22 +397,10 @@
     pieces = [rows, other, swap(rows, "zh", 2, 1), swap(other, "zh", 2, 1)]
     return pl.pallas_call(
         place_rows,
-        out_shape=jax.ShapeDtypeStruct((128, 1024), BF),
+        out_shape=[jax.ShapeDtypeStruct((128, 1024), BF)] * 2,
         in_specs=[pl.BlockSpec(memory_space=pltpu.SMEM)] + [WHOLE] * 4,
-        out_specs=WHOLE,
-    )(head.reshape(1), *pieces)[None]
-
-
-def column_half(parts, zl):
-    return [
-        jnp.where(zl == 0, p[:, : p.shape[1] // 2], p[:, p.shape[1] // 2 :]) for p in parts
-    ]
-
-
-def feed_columns(gate, up, down):
-    zeros = jnp.zeros_like(gate[:, :64])
-    parts = [gate[:, :512], up[:, :512], down[:, :512], gate[:, 512:], up[:, 512:], down[:, 512:]]
-    return jnp.concatenate(parts + [zeros], axis=1)
+        out_specs=[pl.BlockSpec()] * 2,
+    )(head.reshape(1), *pieces)
 
 
 def after(values, *first):
@@ -381,26 +415,35 @@
     zl, y, head = lax.axis_index("zl"), lax.axis_index("y"), lax.axis_index(("zh", "c"))
     attn_gain_row, ffn_gain_row = attn_gain[None], ffn_gain[None]
 
-    feeds = [w_gate, w_up, w_down]
-    send_f = feed_columns(*column_half(feeds, 1 - zl))
+    scalar = pl.BlockSpec(memory_space=pltpu.SMEM)
+    zl_ref = zl.reshape(1)
+    blocks, send_f, keep_f = pl.pallas_call(
+        prepare,
+        out_shape=[
+            jax.ShapeDtypeStruct(shape, BF)
+            for shape in ((2, 16, 32, 384), (32, 1792), (32, 1792))
+        ],
+        in_specs=[scalar] + [pl.BlockSpec()] * 7,
+        out_specs=[WHOLE] * 3,
+    )(zl_ref, w_query, w_key, w_value, w_out, w_gate, w_up, w_down)
     got_f = swap(send_f, "zl", 2, 1)
-
-    small = [w_query, w_key, w_value, w_out]
-    small = after(small, send_f)
-    lows = jnp.concatenate([p[:, : p.shape[1] // 2] for p in small], axis=1)
-    highs = jnp.concatenate([p[:, p.shape[1] // 2 :] for p in small], axis=1)
-    blocks = jnp.broadcast_to(jnp.stack([lows, highs])[:, None], (2, 16, 32, 384))
-    blocks = blocks.reshape(1024, 384)
-    w_a = lax.all_to_all(blocks, PLANE, 0, 0, tiled=True)
+    w_a = lax.all_to_all(blocks.reshape(1024, 384), PLANE, 0, 0, tiled=True)
+    rows_f = pl.pallas_call(
+        order_rows,
+        out_shape=jax.ShapeDtypeStruct((2, 32, 1792), BF),
+        in_specs=[scalar] + [WHOLE] * 2,
+        out_specs=pl.BlockSpec(),
+    )(zl_ref, keep_f, got_f)
+    w_f = lax.all_gather(rows_f, ("y", "x"), axis=0)
 
     order = head ^ jnp.arange(4)
     (late_tokens,) = after([tokens], blocks)
     x_own = late_tokens[0].reshape(4, 32, 1024)[order].reshape(128, 1024)
     x_other = swap(x_own, "zl", 2, 1)
 
-    keep_f = feed_columns(*column_half(after(feeds, blocks), zl))
-    rows_f = jnp.where(zl == 0, jnp.stack([keep_f, got_f]), jnp.stack([got_f, keep_f]))
-    w_f = lax.all_gather(rows_f, ("y", "x"), axis=0)
+    (late_dy,) = after([cotangent], x_own)
+    dy_own = late_dy[0].reshape(4, 32, 1024)[order].reshape(128, 1024)
+    dy_other = swap(dy_own, "zl", 2, 1)
 
     (late_positions,) = after([positions], blocks)
     steps = jnp.array([dl * 16 + ky * 4 + d for ky in range(4) for dl in range(2) for d in range(4)])
@@ -415,74 +458,74 @@
     qk_gain = jnp.stack([jnp.tile(query_gain, 2), jnp.tile(key_gain, 2)])
 
     halves = [((4, 32, 1024), BF), ((4, 32, 1024), F32)]
-    flat = ((256, 128), BF)
+    flat, wide_flat = ((256, 128), BF), ((256, 128), F32)
+    rows_low, rows_high = ((32, 1024), BF), ((32, 1024), F32)
     normed, qh, kv, qkv = call(
-        project, [((256, 1024), BF), flat, flat, ((256, 256), F32)],
-        x_own, x_other, w_a, attn_gain_row, qk_gain, cosine, sine,
+        project, [Far(((256, 1024), BF)), flat, flat, Far(((256, 256), F32))],
+        x_own, x_other, Far(w_a), attn_gain_row, qk_gain, cosine, sine,
     )
     kvs = [kv] + fan([kv] * 4, "y")
-    (late_dy,) = after([cotangent], kv)
-    dy_own = late_dy[0].reshape(4, 32, 1024)[order].reshape(128, 1024)
-    dy_other = swap(dy_own, "zl", 2, 1)
     send, keep, o, l = call(
-        attend, halves + [((256, 128), F32)] * 2, qh, *kvs, own_places, places, w_a
+        attend, halves + [Far(wide_flat)] * 2, qh, *kvs, own_places, places, Far(w_a)
     )
     h, hn = call(
-        hidden, [((32, 1024), F32), ((32, 1024), BF)],
-        *sum_scatter(send, keep), x_own, ffn_gain_row,
+        hidden, [Far(rows_high), rows_low], *sum_scatter(send, keep), x_own, ffn_gain_row
     )
     send, keep, hn_all, act, dgu = call(
-        feed, halves + [((256, 1024), BF), ((256, 640), BF), ((256, 1152), BF)],
-        *gather_rows(hn), dy_own, dy_other, w_f, room=20,
+        feed,
+        [((4, 64, 1024), BF), ((4, 64, 1024), F32)]
+        + [((256, 1024), BF), ((256, 640), BF), ((256, 1152), BF)],
+        *gather_rows(hn), dy_own, dy_other, Far(w_f), room=24,
     )
     pair = sum_pair(send, keep)
     act, dgu = after([act, dgu], *pair)
     d_hn = [pair[0]] + fan([None] + pair[1:], Z)
-    send_b, keep_b, dw_f = call(
-        feed_weights, halves + [((4, 2, 4, 32, 1792), BF)],
-        hn_all, dy_own, dy_other, act, dgu, w_f, room=20,
-    )
-    dw_f = lax.psum_scatter(
-        dw_f.reshape(1024, 1792), "x", scatter_dimension=0, tiled=True
-    )
-    dh, d_low, ffn_gain_part = call(
-        hidden_grad, [((32, 1024), F32), ((32, 1024), BF), ((1, 1024), F32)],
-        *d_hn, h, dy_own, ffn_gain_row,
+    (dw_f,) = call(
+        feed_weights, [Far(((4, 2, 4, 32, 1792), BF))], hn_all, dy_own, dy_other, act, dgu, room=24
+    )
+    dw_f = lax.psum_scatter(dw_f.reshape(1024, 1792), "x", scatter_dimension=0, tiled=True)
+    dh, d_low, ffn_part, block = call(
+        hidden_grad, [Far(rows_high), rows_low, Far(((1, 1024), F32)), Far(rows_low)],
+        *d_hn, Far(h), dy_own, ffn_gain_row,
     )
     d_attn, d_qh, *d_kvs = call(
-        attend_grad,
-        [((256, 1024), BF), ((256, 128), F32), ((256, 128), F32), flat, flat, flat],
-        *gather_rows(d_low), qh, *kvs, own_places, places, w_a, o, l,
-    )
-    d_qkv, send, keep, attn_gain_part, head_part = call(
-        project_grad,
-        [((256, 256), BF)] + halves + [((1, 1024), F32), ((2, 128), F32)],
-        d_qh, d_kvs[0], *fan(d_kvs, "y"), qkv, cosine, sine, qk_gain, w_a, x_own, x_other,
+        attend_grad, [Far(((256, 1024), BF)), wide_flat, wide_flat, flat, flat, flat],
+        *gather_rows(d_low), Far(qh), *[Far(t) for t in kvs], own_places, places, Far(w_a), Far(o), Far(l),
+    )
+    d_qkv, send, keep, gains = call(
+        project_grad, [((256, 256), BF)] + halves + [((16, 384), BF)],
+        d_qh, d_kvs[0], *fan(d_kvs, "y"), Far(qkv), cosine, sine, qk_gain, Far(w_a),
+        Far(x_own), Far(x_other), Far(ffn_part),
     )
     (dw_a,) = call(
-        attend_weights, [((32, 48, 384), BF)],
-        normed, d_qkv, d_attn, o, attn_gain_part, ffn_gain_part, head_part,
+        attend_weights, [Far(((4, 272, 384), BF))], Far(normed), d_qkv, Far(d_attn), Far(o), gains
     )
     (keep,) = after([keep], dw_a)
+    dw_a = lax.psum_scatter(dw_a.reshape(1088, 384), "x", scatter_dimension=0, tiled=True)
     d_xn = sum_scatter(send, keep)
-    (send_b,) = after([send_b], d_xn[0])
-    (rows,) = call(block_rows, [((32, 1024), BF)], *sum_scatter(send_b, keep_b), h)
-    dw_a = lax.all_to_all(dw_a, PLANE, 0, 0, tiled=True)
-    block_out = gather_head(rows, head)
-    (rows,) = call(token_rows, [((32, 1024), BF)], *d_xn, dh, x_own, attn_gain_row)
-    tokens_grad = gather_head(rows, head)
+    (rows,) = call(
+        token_rows, [((64, 1024), BF)], *d_xn, Far(dh), x_own, attn_gain_row, Far(block)
+    )
+    tokens_grad, block_out = gather_head(rows, head)
+    tokens_grad, block_out = tokens_grad[None], block_out[None]
+
+    (dw_f,) = after([dw_f], rows)
     dw_f = lax.all_to_all(dw_f, ("zl", "y"), 0, 0, tiled=True)
+    grad_wg, grad_wu, grad_wd = call(
+        finish_feed, [Far(((32, 1152), F32))] * 3, dw_f.reshape(2, 4, 32, 1792)
+    )
+    (dw_a,) = after([dw_a], grad_wg)
+    (dw_a,) = call(share_gains, [((8, 48, 384), BF)], dw_a)
+    dw_a = lax.all_to_all(dw_a, ("zl", "y"), 0, 0, tiled=True)
     grad_wq, grad_wk, grad_wv, grad_wo, gains = call(
-        finish_attend, [((32, n), F32) for n in (256, 128, 128, 256)] + [((16, 384), F32)],
-        dw_a.reshape(2, 16, 48, 384),
-    )
-    (gains,) = call(add_gains, [((16, 384), F32)], gains, swap(gains, "c", 2, 1))
+        finish_attend,
+        [Far(((32, n), F32)) for n in (256, 128, 128, 256)] + [((16, 384), F32)],
+        dw_a.reshape(2, 4, 48, 384),
+    )
+    (gains,) = call(add_two, [((16, 384), F32)], gains, swap(gains, "c", 2, 1))
     attn_sum, ffn_sum, query_sum, key_sum = call(
         finish_gains, [((8, 128), F32)] * 2 + [((1, 64), F32)] * 2,
         gains, swap(gains, "zh", 2, 1),
-    )
-    grad_wg, grad_wu, grad_wd = call(
-        finish_feed, [((32, 1152), F32)] * 3, dw_f.reshape(2, 4, 32, 1792)
     )
     return (
         block_out, tokens_grad, attn_sum.reshape(1024), ffn_sum.reshape(1024),

time: 199 us -> 186 us (0.935)
  local copies, waits for them, and re-layouts: 22.5 us -> 14.6 us
  blocking collectives: 21.6 us -> 16.9 us
  other arithmetic: 7.18 us -> 2.86 us
  waiting for transfers between devices: 53.1 us -> 57.2 us
  Pallas kernels: 17.6 us -> 21.5 us
  starting transfers between devices: 60.7 us -> 57.7 us
    ppermute x47 -> x40, waiting for transfers between devices: 40.4 us -> 51 us  [swap(): return lax.ppermute(value, axes, [(i, i ^ mask) for i in range(size)])]
    all_to_all x2, waiting for transfers between devices: 12.6 us -> 3.28 us  [the longest x1 3.28 us: local(): dw_a = lax.all_to_all(dw_a, ('zl', 'y'), 0, 0, tiled=True)]
    select_n x6 -> x0, other arithmetic: 5.43 us -> none  [the longest x5 4.72 us: column_half(): jnp.where(zl == 0, p[:, :p.shape[1] // 2], p[:, p.shape[1] // 2:])]
    all_to_all x1, blocking collectives: 21.6 us -> 16.9 us  [local(): dw_f = lax.all_to_all(dw_f, ('zl', 'y'), 0, 0, tiled=True)]
    ppermute x47 -> x40, starting transfers between devices: 48.3 us -> 43.8 us  [swap(): return lax.ppermute(value, axes, [(i, i ^ mask) for i in range(size)])]
    pallas_call x21, Pallas kernels: 17.6 us -> 21.5 us  [the longest x18 15.8 us: call(): pl.pallas_call(body, out_shape=[jax.ShapeDtypeStruct(*bare(out)) for out...]
    unnamed x84 -> x64, local copies, waits for them, and re-layouts: 14.4 us -> 10.7 us
    slice x16 -> x0, local copies, waits for them, and re-layouts: 3.17 us -> none  [the longest x4 3.12 us: local(): lows = jnp.concatenate([p[:, :p.shape[1] // 2] for p in small], axis=1)]
  transfers between devices with their start and end apart: 51 -> 45, of which waited for: 23 -> 27; matrix products, arithmetic and copies ran while one was open for 6% -> 4% of each run, Pallas kernels for 7% -> 7%
where the time goes in v4:
time: 186 us; the launch traced here: 185 us
  starting transfers between devices  57.7 us (31%)
  waiting for transfers between devices  57.2 us (31%)
  Pallas kernels  21.5 us (12%)
  blocking collectives  16.9 us (9%)
  local copies, waits for them, and re-layouts  14.6 us (8%)
  between operations  14.2 us (8%)
  other arithmetic  2.86 us (2%)
    ppermute x40, waiting for transfers between devices, swap(): return lax.ppermute(value, axes, [(i, i ^ mask) for i in range(size)])  51 us
    ppermute x40, starting transfers between devices, swap(): return lax.ppermute(value, axes, [(i, i ^ mask) for i in range(size)])  43.8 us
    all_to_all x1, blocking collectives, local(): dw_f = lax.all_to_all(dw_f, ('zl', 'y'), 0, 0, tiled=True)  16.9 us
    pallas_call x18, Pallas kernels, call(): pl.pallas_call(body, out_shape=[jax.ShapeDtypeStruct(*bare(out)) for out...  15.8 us
    unnamed x64, local copies, waits for them, and re-layouts  10.7 us
    all_to_all x1, starting transfers between devices, local(): w_a = lax.all_to_all(blocks.reshape(1024, 384), PLANE, 0, 0, tiled=True)  8.51 us
    all_to_all x1, starting transfers between devices, local(): dw_a = lax.all_to_all(dw_a, ('zl', 'y'), 0, 0, tiled=True)  5.27 us
  transfers between devices with their start and end apart: 45, of which 27 were waited for; matrix products, arithmetic and copies ran while one was open for 4% of the time, Pallas kernels for 7%

profile of v4, /device:TPU:0, one launch (start us, length us, event | category | flops | bytes accessed | tf_op | source)
XLA Modules:
  0.0 185.0 jit_solution(6828493307390207134)
XLA Ops:
  7.3 2.2 %shard_map.246 = (bf16[2,16,32,384]{3,2,1,0:T(8,128)(2,1)}, bf16[32,1792]{1,0:T(8,128)(2,1)}, bf16[32,1792]{1,0:T(8,128)(2,1)}) custom-call(s32[1]{0:T(128)} %bitcast.1.zl, bf16[32,256]{1,0:T(8,128)(2,1)} %wq.1, bf16[32,128]{1,0:T(8,128)(2,1)} %wk.1, bf16[32,128]{1,0:T(8,128)(2,1)} %wv.1, bf16[32,256]{1,0:T(8,128)(2,1)} %wo.1, bf16[32,1152]{1,0:T(8,128)(2,1)} %wg.1, ...), custom_call_target="tpu_custom_call" | custom-call | tf_op jit(solution)/shard_map/pallas_call | solution.py:420
  9.5 2.0 %collective-permute-start.16 = (bf16[32,1792]{1,0:T(8,128)(2,1)}, bf16[32,1792]{1,0:T(8,128)(2,1)S(1)}, u32[]{:S(2)}, u32[]{:S(2)}) collective-permute-start(bf16[32,1792]{1,0:T(8,128)(2,1)} %get-tuple-element.93), channel_id=1, source_target_pairs={{0,64},{64,0},{1,65},{65,1},{2,66},{66,2},{3,67},{67,3},{4,68},{68... | collective-permute-start | bytes 344072 | tf_op jit(solution)/shard_map/ppermute | solution.py:362
  11.5 3.4 %collective-permute-done.16.got = bf16[32,1792]{1,0:T(8,128)(2,1)S(1)} collective-permute-done((bf16[32,1792]{1,0:T(8,128)(2,1)}, bf16[32,1792]{1,0:T(8,128)(2,1)S(1)}, u32[]{:S(2)}, u32[]{:S(2)}) %collective-permute-start.16) | collective-permute-done | bytes 114720 | tf_op jit(solution)/shard_map/ppermute | solution.py:362
  17.2 8.5 %all-to-all-start = ((bf16[32,32,384]{2,1,0:T(8,128)(2,1)}), bf16[32,32,384]{2,1,0:T(8,128)(2,1)S(1)}, u32[]{:S(2)}, u32[]{:S(2)}) async-start(bf16[32,32,384]{2,1,0:T(8,128)(2,1)} %bitcast.47), calls=%async_computation | async-start | bytes 1572864 | tf_op jit(solution)/shard_map/all_to_all | solution.py:430
  26.4 1.9 %collective-permute-start = (bf16[128,1024]{1,0:T(8,128)(2,1)S(1)}, bf16[128,1024]{1,0:T(8,128)(2,1)S(1)}, u32[]{:S(2)}, u32[]{:S(2)}) collective-permute-start(bf16[128,1024]{1,0:T(8,128)(2,1)S(1)} %bitcast.30), channel_id=1, source_target_pairs={{0,64},{64,0},{1,65},{65,1},{2,66},{66,2},{3,67},{67,3},{4,68},{68... | collective-permute-start | bytes 786440 | tf_op jit(solution)/shard_map/ppermute | solution.py:362
  32.6 9.0 %collective-permute-done.other.x_other = bf16[128,1024]{1,0:T(8,128)(2,1)S(1)} collective-permute-done((bf16[128,1024]{1,0:T(8,128)(2,1)S(1)}, bf16[128,1024]{1,0:T(8,128)(2,1)S(1)}, u32[]{:S(2)}, u32[]{:S(2)}) %collective-permute-start) | collective-permute-done | bytes 262176 | tf_op jit(solution)/shard_map/ppermute | solution.py:362
  43.1 2.4 %collective-permute-start.3 = (bf16[256,128]{1,0:T(8,128)(2,1)S(1)}, bf16[256,128]{1,0:T(8,128)(2,1)S(1)}, u32[]{:S(2)}, u32[]{:S(2)}) collective-permute-start(bf16[256,128]{1,0:T(8,128)(2,1)S(1)} %get-tuple-element.83.kv0), channel_id=1, source_target_pairs={{0,48},{16,32},{32,16},{48,0},{1,49},{17,33},{33,17},{49,1},{2,50}... | collective-permute-start | bytes 196616 | tf_op jit(solution)/shard_map/ppermute | solution.py:362
  48.5 2.7 %collective-permute-done.2.kv2 = bf16[256,128]{1,0:T(8,128)(2,1)S(1)} collective-permute-done((bf16[256,128]{1,0:T(8,128)(2,1)S(1)}, bf16[256,128]{1,0:T(8,128)(2,1)S(1)}, u32[]{:S(2)}, u32[]{:S(2)}) %collective-permute-start.2) | collective-permute-done | bytes 65568 | tf_op jit(solution)/shard_map/ppermute | solution.py:362
  51.2 2.1 %shard_map.248 = (bf16[4,32,1024]{2,1,0:T(8,128)(2,1)}, f32[4,32,1024]{2,1,0:T(8,128)S(1)}, f32[256,128]{1,0:T(8,128)S(1)}, f32[256,128]{1,0:T(8,128)S(1)}) custom-call(bf16[256,128]{1,0:T(8,128)(2,1)S(1)} %get-tuple-element.82.qh, bf16[256,128]{1,0:T(8,128)(2,1)S(1)} %get-tuple-element.83.kv0, bf16[256,128]{1,0:T(8,128)(2,1)S(1)} %collective-permute-done.1.kv1, ...), custom_call_target="tpu_custom_call" | custom-call | tf_op jit(solution)/shard_map/pallas_call | solution.py:30
  56.7 3.6 %collective-permute-start.5 = (bf16[32,1024]{1,0:T(8,128)(2,1)S(1)}, bf16[32,1024]{1,0:T(8,128)(2,1)S(1)}, u32[]{:S(2)}, u32[]{:S(2)}) collective-permute-start(bf16[32,1024]{1,0:T(8,128)(2,1)S(1)} %get-tuple-element.87), channel_id=1, source_target_pairs={{0,2},{2,0},{64,66},{66,64},{1,3},{3,1},{65,67},{67,65},{4,6},{6,4... | collective-permute-start | bytes 196616 | tf_op jit(solution)/shard_map/ppermute | solution.py:362
  61.0 7.7 %collective-permute-done.5.one = bf16[32,1024]{1,0:T(8,128)(2,1)S(1)} collective-permute-done((bf16[32,1024]{1,0:T(8,128)(2,1)S(1)}, bf16[32,1024]{1,0:T(8,128)(2,1)S(1)}, u32[]{:S(2)}, u32[]{:S(2)}) %collective-permute-start.5) | collective-permute-done | bytes 65568 | tf_op jit(solution)/shard_map/ppermute | solution.py:362
  71.0 2.6 %collective-permute-start.9 = (bf16[32,1024]{1,0:T(8,128)(2,1)S(1)}, bf16[32,1024]{1,0:T(8,128)(2,1)S(1)}, u32[]{:S(2)}, u32[]{:S(2)}) collective-permute-start(bf16[32,1024]{1,0:T(8,128)(2,1)S(1)} %get-tuple-element.90.p0), channel_id=1, source_target_pairs={{0,2},{2,0},{64,66},{66,64},{1,3},{3,1},{65,67},{67,65},{4,6},{6,4... | collective-permute-start | bytes 196616 | tf_op jit(solution)/shard_map/ppermute | solution.py:362
  74.9 1.9 %collective-permute-done.9.p2 = bf16[32,1024]{1,0:T(8,128)(2,1)S(1)} collective-permute-done((bf16[32,1024]{1,0:T(8,128)(2,1)S(1)}, bf16[32,1024]{1,0:T(8,128)(2,1)S(1)}, u32[]{:S(2)}, u32[]{:S(2)}) %collective-permute-start.9) | collective-permute-done | bytes 65568 | tf_op jit(solution)/shard_map/ppermute | solution.py:362
  78.0 2.0 %copy-done.2 = bf16[32,32,1792]{2,1,0:T(8,128)(2,1)S(1)} copy-done((bf16[32,32,1792]{2,1,0:T(8,128)(2,1)S(1)}, bf16[32,32,1792]{2,1,0:T(8,128)(2,1)}, u32[]{:S(2)}) %copy-start.2) | copy-done | bytes 3670040
  80.0 2.5 %shard_map.252 = (bf16[4,64,1024]{2,1,0:T(8,128)(2,1)S(1)}, f32[4,64,1024]{2,1,0:T(8,128)S(1)}, bf16[256,1024]{1,0:T(8,128)(2,1)S(1)}, bf16[256,640]{1,0:T(8,128)(2,1)S(1)}, bf16[256,1152]{1,0:T(8,128)(2,1)S(1)}) custom-call(bf16[32,1024]{1,0:T(8,128)(2,1)S(1)} %get-tuple-element.90.p0, bf16[32,1024]{1,0:T(8,128)(2,1)S(1)} %collective-permute-done.8.p1, ...), custom_call_target="tpu_custom_call" | custom-call | tf_op jit(solution)/shard_map/pallas_call | solution.py:30
  86.8 1.8 copy-done.1
  88.8 2.7 %collective-permute-start.18 = (bf16[64,1024]{1,0:T(8,128)(2,1)}, bf16[64,1024]{1,0:T(8,128)(2,1)S(1)}, u32[]{:S(2)}, u32[]{:S(2)}) collective-permute-start(bf16[64,1024]{1,0:T(8,128)(2,1)} %copy-done.24), channel_id=1, source_target_pairs={{0,2},{2,0},{64,66},{66,64},{1,3},{3,1},{65,67},{67,65},{4,6},{6,4... | collective-permute-start | bytes 393224 | tf_op jit(solution)/shard_map/ppermute | solution.py:362
  93.0 3.9 %collective-permute-done.18.one = bf16[64,1024]{1,0:T(8,128)(2,1)S(1)} collective-permute-done((bf16[64,1024]{1,0:T(8,128)(2,1)}, bf16[64,1024]{1,0:T(8,128)(2,1)S(1)}, u32[]{:S(2)}, u32[]{:S(2)}) %collective-permute-start.18) | collective-permute-done | bytes 131104 | tf_op jit(solution)/shard_map/ppermute | solution.py:362
  102.4 2.1 %collective-permute-start.22 = (bf16[32,1024]{1,0:T(8,128)(2,1)S(1)}, bf16[32,1024]{1,0:T(8,128)(2,1)S(1)}, u32[]{:S(2)}, u32[]{:S(2)}) collective-permute-start(bf16[32,1024]{1,0:T(8,128)(2,1)S(1)} %get-tuple-element.101.p0), channel_id=1, source_target_pairs={{0,2},{2,0},{64,66},{66,64},{1,3},{3,1},{65,67},{67,65},{4,6},{6,4... | collective-permute-start | bytes 196616 | tf_op jit(solution)/shard_map/ppermute | solution.py:362
  106.1 2.0 %collective-permute-done.22.p2 = bf16[32,1024]{1,0:T(8,128)(2,1)S(1)} collective-permute-done((bf16[32,1024]{1,0:T(8,128)(2,1)S(1)}, bf16[32,1024]{1,0:T(8,128)(2,1)S(1)}, u32[]{:S(2)}, u32[]{:S(2)}) %collective-permute-start.22) | collective-permute-done | bytes 65568 | tf_op jit(solution)/shard_map/ppermute | solution.py:362
  109.5 3.1 %shard_map.255 = (bf16[256,1024]{1,0:T(8,128)(2,1)S(1)}, f32[256,128]{1,0:T(8,128)S(1)}, f32[256,128]{1,0:T(8,128)S(1)}, bf16[256,128]{1,0:T(8,128)(2,1)S(1)}, b...) custom-call(bf16[32,1024]{1,0:T(8,128)(2,1)S(1)} %get-tuple-element.101.p0, ...), custom_call_target="tpu_custom_call" | custom-call | tf_op jit(solution)/shard_map/pallas_call | solution.py:30
  113.2 2.2 %collective-permute-start.29 = (bf16[256,128]{1,0:T(8,128)(2,1)S(1)}, bf16[256,128]{1,0:T(8,128)(2,1)S(1)}, u32[]{:S(2)}, u32[]{:S(2)}) collective-permute-start(bf16[256,128]{1,0:T(8,128)(2,1)S(1)} %get-tuple-element.107), channel_id=1, source_target_pairs={{0,32},{16,48},{32,0},{48,16},{1,33},{17,49},{33,1},{49,17},{2,34}... | collective-permute-start | bytes 196616 | tf_op jit(solution)/shard_map/ppermute | solution.py:362
  115.4 2.0 %collective-permute-start.30 = (bf16[256,128]{1,0:T(8,128)(2,1)S(1)}, bf16[256,128]{1,0:T(8,128)(2,1)S(1)}, u32[]{:S(2)}, u32[]{:S(2)}) collective-permute-start(bf16[256,128]{1,0:T(8,128)(2,1)S(1)} %get-tuple-element.108), channel_id=1, source_target_pairs={{0,48},{16,32},{32,16},{48,0},{1,49},{17,33},{33,17},{49,1},{2,50}... | collective-permute-start | bytes 196616 | tf_op jit(solution)/shard_map/ppermute | solution.py:362
  127.0 2.2 %collective-permute-start.32 = (bf16[32,1024]{1,0:T(8,128)(2,1)S(1)}, bf16[32,1024]{1,0:T(8,128)(2,1)S(1)}, u32[]{:S(2)}, u32[]{:S(2)}) collective-permute-start(bf16[32,1024]{1,0:T(8,128)(2,1)S(1)} %get-tuple-element.119), channel_id=1, source_target_pairs={{0,2},{2,0},{64,66},{66,64},{1,3},{3,1},{65,67},{67,65},{4,6},{6,4... | collective-permute-start | bytes 196616 | tf_op jit(solution)/shard_map/ppermute | solution.py:362
  131.1 2.1 %collective-permute-done.32.one = bf16[32,1024]{1,0:T(8,128)(2,1)S(1)} collective-permute-done((bf16[32,1024]{1,0:T(8,128)(2,1)S(1)}, bf16[32,1024]{1,0:T(8,128)(2,1)S(1)}, u32[]{:S(2)}, u32[]{:S(2)}) %collective-permute-start.32) | collective-permute-done | bytes 65568 | tf_op jit(solution)/shard_map/ppermute | solution.py:362
  135.2 16.9 %all_to_all.25 = bf16[8,32,1792]{2,1,0:T(8,128)(2,1)S(1)} all-to-all(bf16[8,32,1792]{2,1,0:T(8,128)(2,1)} %bitcast.46), channel_id=1, replica_groups=mesh['zl'=2,'y'=4,'x'=4,'zh'=2,'c'=2] {'zl','y'}, dimensions={0} | all-to-all | bytes 1835008 | tf_op jit(solution)/shard_map/all_to_all | solution.py:513
  152.9 2.8 %reduce-scatter.3.cloned.1.call-done.dw = bf16[272,384]{1,0:T(8,128)(2,1)} async-done(((bf16[1088,384]{1,0:T(8,128)(2,1)}), bf16[272,384]{1,0:T(8,128)(2,1)}) %reduce-scatter.3.cloned.1.call-update) | async-done | bytes 208912 | tf_op jit(solution)/shard_map/reduce_scatter | solution.py:504
  157.4 5.3 %all-to-all-start.2 = ((bf16[8,48,384]{2,1,0:T(8,128)(2,1)}), bf16[8,48,384]{2,1,0:T(8,128)(2,1)S(1)}, u32[]{:S(2)}, u32[]{:S(2)}) async-start(bf16[8,48,384]{2,1,0:T(8,128)(2,1)} %shard_map.263), calls=%async_computation.4 | async-start | bytes 589824 | tf_op jit(solution)/shard_map/all_to_all | solution.py:519
  162.7 3.0 %collective-permute-start.36 = (bf16[64,1024]{1,0:T(8,128)(2,1)S(1)}, bf16[64,1024]{1,0:T(8,128)(2,1)S(1)}, u32[]{:S(2)}, u32[]{:S(2)}) collective-permute-start(bf16[64,1024]{1,0:T(8,128)(2,1)S(1)} %shard_map.259.p0), channel_id=1, source_target_pairs={{0,2},{2,0},{1,3},{3,1},{4,6},{6,4},{5,7},{7,5},{8,10},{10,8},{9,1... | collective-permute-start | bytes 393224 | tf_op jit(solution)/shard_map/ppermute | solution.py:362
  167.0 3.3 %all-to-all-done.2 = bf16[8,48,384]{2,1,0:T(8,128)(2,1)S(1)} async-done(((bf16[8,48,384]{2,1,0:T(8,128)(2,1)}), bf16[8,48,384]{2,1,0:T(8,128)(2,1)S(1)}, u32[]{:S(2)}, u32[]{:S(2)}) %all-to-all-start.2) | async-done | bytes 294944 | tf_op jit(solution)/shard_map/all_to_all | solution.py:519
  172.1 2.9 %collective-permute-start.39 = (f32[16,384]{1,0:T(8,128)S(1)}, f32[16,384]{1,0:T(8,128)S(1)}, u32[]{:S(2)}, u32[]{:S(2)}) collective-permute-start(f32[16,384]{1,0:T(8,128)S(1)} %shard_map.265.one), channel_id=1, source_target_pairs={{0,2},{2,0},{1,3},{3,1},{4,6},{6,4},{5,7},{7,5},{8,10},{10,8},{9,1... | collective-permute-start | bytes 73736 | tf_op jit(solution)/shard_map/ppermute | solution.py:362
  175.9 1.9 %shard_map.260 = (bf16[128,1024]{1,0:T(8,128)(2,1)}, bf16[128,1024]{1,0:T(8,128)(2,1)}) custom-call(s32[1]{0:T(128)} %bitcast.head, bf16[64,1024]{1,0:T(8,128)(2,1)} %copy-done.3, bf16[64,1024]{1,0:T(8,128)(2,1)} %copy-done.25, bf16[64,1024]{1,0:T(8,128)(2,1)} %copy-done.26, bf16[64,1024]{1,0:T(8,128)(2,1)} %copy-done.27), custom_call_target="tpu_custom_call" | custom-call | tf_op jit(solution)/shard_map/pallas_call | solution.py:398
  (169 shorter events, 56.2 us)
Async XLA Ops:
  7.2 70.8 %all-gather.3.cloned.1.call-start = ((), (), s32[]{:S(2)}) async-start(), calls=%async_computation.7 | async-start | bytes 3899392 | tf_op jit(solution)/shard_map/all_gather | solution.py:437
  9.5 5.4 %collective-permute-start.16 = (bf16[32,1792]{1,0:T(8,128)(2,1)}, bf16[32,1792]{1,0:T(8,128)(2,1)S(1)}, u32[]{:S(2)}, u32[]{:S(2)}) collective-permute-start(bf16[32,1792]{1,0:T(8,128)(2,1)} %get-tuple-element.93), channel_id=1, source_target_pairs={{0,64},{64,0},{1,65},{65,1},{2,66},{66,2},{3,67},{67,3},{4,68},{68... | collective-permute-start | bytes 344072 | tf_op jit(solution)/shard_map/ppermute | solution.py:362
  17.2 24.3 %all-to-all-start = ((bf16[32,32,384]{2,1,0:T(8,128)(2,1)}), bf16[32,32,384]{2,1,0:T(8,128)(2,1)S(1)}, u32[]{:S(2)}, u32[]{:S(2)}) async-start(bf16[32,32,384]{2,1,0:T(8,128)(2,1)} %bitcast.47), calls=%async_computation | async-start | bytes 1572864 | tf_op jit(solution)/shard_map/all_to_all | solution.py:430
  25.7 109.5 %reduce-scatter.5.cloned.1.call-start = ((), (), s32[]{:S(2)}) async-start(), calls=%async_computation.6 | async-start | bytes 4587520 | tf_op jit(solution)/shard_map/reduce_scatter | solution.py:486
  26.4 15.2 %collective-permute-start = (bf16[128,1024]{1,0:T(8,128)(2,1)S(1)}, bf16[128,1024]{1,0:T(8,128)(2,1)S(1)}, u32[]{:S(2)}, u32[]{:S(2)}) collective-permute-start(bf16[128,1024]{1,0:T(8,128)(2,1)S(1)} %bitcast.30), channel_id=1, source_target_pairs={{0,64},{64,0},{1,65},{65,1},{2,66},{66,2},{3,67},{67,3},{4,68},{68... | collective-permute-start | bytes 786440 | tf_op jit(solution)/shard_map/ppermute | solution.py:362
  43.1 5.5 %collective-permute-start.3 = (bf16[256,128]{1,0:T(8,128)(2,1)S(1)}, bf16[256,128]{1,0:T(8,128)(2,1)S(1)}, u32[]{:S(2)}, u32[]{:S(2)}) collective-permute-start(bf16[256,128]{1,0:T(8,128)(2,1)S(1)} %get-tuple-element.83.kv0), channel_id=1, source_target_pairs={{0,48},{16,32},{32,16},{48,0},{1,49},{17,33},{33,17},{49,1},{2,50}... | collective-permute-start | bytes 196616 | tf_op jit(solution)/shard_map/ppermute | solution.py:362
  45.5 5.8 %collective-permute-start.2 = (bf16[256,128]{1,0:T(8,128)(2,1)S(1)}, bf16[256,128]{1,0:T(8,128)(2,1)S(1)}, u32[]{:S(2)}, u32[]{:S(2)}) collective-permute-start(bf16[256,128]{1,0:T(8,128)(2,1)S(1)} %get-tuple-element.83.kv0), channel_id=1, source_target_pairs={{0,32},{16,48},{32,0},{48,16},{1,33},{17,49},{33,1},{49,17},{2,34}... | collective-permute-start | bytes 196616 | tf_op jit(solution)/shard_map/ppermute | solution.py:362
  46.4 4.8 %collective-permute-start.1 = (bf16[256,128]{1,0:T(8,128)(2,1)S(1)}, bf16[256,128]{1,0:T(8,128)(2,1)S(1)}, u32[]{:S(2)}, u32[]{:S(2)}) collective-permute-start(bf16[256,128]{1,0:T(8,128)(2,1)S(1)} %get-tuple-element.83.kv0), channel_id=1, source_target_pairs={{0,16},{16,0},{32,48},{48,32},{1,17},{17,1},{33,49},{49,33},{2,18}... | collective-permute-start | bytes 196616 | tf_op jit(solution)/shard_map/ppermute | solution.py:362
  55.6 21.1 %collective-permute-start.15 = (bf16[128,1024]{1,0:T(8,128)(2,1)S(1)}, bf16[128,1024]{1,0:T(8,128)(2,1)S(1)}, u32[]{:S(2)}, u32[]{:S(2)}) collective-permute-start(bf16[128,1024]{1,0:T(8,128)(2,1)S(1)} %bitcast.35), channel_id=1, source_target_pairs={{0,64},{64,0},{1,65},{65,1},{2,66},{66,2},{3,67},{67,3},{4,68},{68... | collective-permute-start | bytes 786440 | tf_op jit(solution)/shard_map/ppermute | solution.py:362
  56.7 12.0 %collective-permute-start.5 = (bf16[32,1024]{1,0:T(8,128)(2,1)S(1)}, bf16[32,1024]{1,0:T(8,128)(2,1)S(1)}, u32[]{:S(2)}, u32[]{:S(2)}) collective-permute-start(bf16[32,1024]{1,0:T(8,128)(2,1)S(1)} %get-tuple-element.87), channel_id=1, source_target_pairs={{0,2},{2,0},{64,66},{66,64},{1,3},{3,1},{65,67},{67,65},{4,6},{6,4... | collective-permute-start | bytes 196616 | tf_op jit(solution)/shard_map/ppermute | solution.py:362
  60.3 8.3 %collective-permute-start.6 = (bf16[32,1024]{1,0:T(8,128)(2,1)S(1)}, bf16[32,1024]{1,0:T(8,128)(2,1)S(1)}, u32[]{:S(2)}, u32[]{:S(2)}) collective-permute-start(bf16[32,1024]{1,0:T(8,128)(2,1)S(1)} %get-tuple-element.88), channel_id=1, source_target_pairs={{0,64},{2,66},{64,0},{66,2},{1,65},{3,67},{65,1},{67,3},{4,68},{6,... | collective-permute-start | bytes 196616 | tf_op jit(solution)/shard_map/ppermute | solution.py:362
  60.8 7.8 %collective-permute-start.7 = (bf16[32,1024]{1,0:T(8,128)(2,1)S(1)}, bf16[32,1024]{1,0:T(8,128)(2,1)S(1)}, u32[]{:S(2)}, u32[]{:S(2)}) collective-permute-start(bf16[32,1024]{1,0:T(8,128)(2,1)S(1)} %get-tuple-element.89), channel_id=1, source_target_pairs={{0,66},{2,64},{64,2},{66,0},{1,67},{3,65},{65,3},{67,1},{4,70},{6,... | collective-permute-start | bytes 196616 | tf_op jit(solution)/shard_map/ppermute | solution.py:362
  68.8 5.6 %collective-permute-start.13 = (bf16[32,1024]{1,0:T(8,128)(2,1)S(1)}, bf16[32,1024]{1,0:T(8,128)(2,1)S(1)}, u32[]{:S(2)}, u32[]{:S(2)}) collective-permute-start(bf16[32,1024]{1,0:T(8,128)(2,1)S(1)} %get-tuple-element.90.p0), channel_id=1, source_target_pairs={{0,66},{2,64},{64,2},{66,0},{1,67},{3,65},{65,3},{67,1},{4,70},{6,... | collective-permute-start | bytes 196616 | tf_op jit(solution)/shard_map/ppermute | solution.py:362
  70.4 4.3 %collective-permute-start.11 = (bf16[32,1024]{1,0:T(8,128)(2,1)S(1)}, bf16[32,1024]{1,0:T(8,128)(2,1)S(1)}, u32[]{:S(2)}, u32[]{:S(2)}) collective-permute-start(bf16[32,1024]{1,0:T(8,128)(2,1)S(1)} %get-tuple-element.90.p0), channel_id=1, source_target_pairs={{0,64},{2,66},{64,0},{66,2},{1,65},{3,67},{65,1},{67,3},{4,68},{6,... | collective-permute-start | bytes 196616 | tf_op jit(solution)/shard_map/ppermute | solution.py:362
  71.0 5.8 %collective-permute-start.9 = (bf16[32,1024]{1,0:T(8,128)(2,1)S(1)}, bf16[32,1024]{1,0:T(8,128)(2,1)S(1)}, u32[]{:S(2)}, u32[]{:S(2)}) collective-permute-start(bf16[32,1024]{1,0:T(8,128)(2,1)S(1)} %get-tuple-element.90.p0), channel_id=1, source_target_pairs={{0,2},{2,0},{64,66},{66,64},{1,3},{3,1},{65,67},{67,65},{4,6},{6,4... | collective-permute-start | bytes 196616 | tf_op jit(solution)/shard_map/ppermute | solution.py:362
  88.7 67.0 %reduce-scatter.3.cloned.1.call-start = ((), (), s32[]{:S(2)}) async-start(), calls=%async_computation.5 | async-start | bytes 1044480 | tf_op jit(solution)/shard_map/reduce_scatter | solution.py:504
  88.8 8.1 %collective-permute-start.18 = (bf16[64,1024]{1,0:T(8,128)(2,1)}, bf16[64,1024]{1,0:T(8,128)(2,1)S(1)}, u32[]{:S(2)}, u32[]{:S(2)}) collective-permute-start(bf16[64,1024]{1,0:T(8,128)(2,1)} %copy-done.24), channel_id=1, source_target_pairs={{0,2},{2,0},{64,66},{66,64},{1,3},{3,1},{65,67},{67,65},{4,6},{6,4... | collective-permute-start | bytes 393224 | tf_op jit(solution)/shard_map/ppermute | solution.py:362
  91.5 6.2 %collective-permute-start.19 = (bf16[64,1024]{1,0:T(8,128)(2,1)}, bf16[64,1024]{1,0:T(8,128)(2,1)S(1)}, u32[]{:S(2)}, u32[]{:S(2)}) collective-permute-start(bf16[64,1024]{1,0:T(8,128)(2,1)} %copy-done.23), channel_id=1, source_target_pairs={{0,64},{2,66},{64,0},{66,2},{1,65},{3,67},{65,1},{67,3},{4,68},{6,... | collective-permute-start | bytes 393224 | tf_op jit(solution)/shard_map/ppermute | solution.py:362
  91.5 7.5 %collective-permute-start.20 = (bf16[64,1024]{1,0:T(8,128)(2,1)}, bf16[64,1024]{1,0:T(8,128)(2,1)S(1)}, u32[]{:S(2)}, u32[]{:S(2)}) collective-permute-start(bf16[64,1024]{1,0:T(8,128)(2,1)} %copy-done.22), channel_id=1, source_target_pairs={{0,66},{2,64},{64,2},{66,0},{1,67},{3,65},{65,3},{67,1},{4,70},{6,... | collective-permute-start | bytes 393224 | tf_op jit(solution)/shard_map/ppermute | solution.py:362
  99.8 5.5 %collective-permute-start.26 = (bf16[32,1024]{1,0:T(8,128)(2,1)S(1)}, bf16[32,1024]{1,0:T(8,128)(2,1)S(1)}, u32[]{:S(2)}, u32[]{:S(2)}) collective-permute-start(bf16[32,1024]{1,0:T(8,128)(2,1)S(1)} %get-tuple-element.101.p0), channel_id=1, source_target_pairs={{0,66},{2,64},{64,2},{66,0},{1,67},{3,65},{65,3},{67,1},{4,70},{6,... | collective-permute-start | bytes 196616 | tf_op jit(solution)/shard_map/ppermute | solution.py:362
  101.2 4.9 %collective-permute-start.24 = (bf16[32,1024]{1,0:T(8,128)(2,1)S(1)}, bf16[32,1024]{1,0:T(8,128)(2,1)S(1)}, u32[]{:S(2)}, u32[]{:S(2)}) collective-permute-start(bf16[32,1024]{1,0:T(8,128)(2,1)S(1)} %get-tuple-element.101.p0), channel_id=1, source_target_pairs={{0,64},{2,66},{64,0},{66,2},{1,65},{3,67},{65,1},{67,3},{4,68},{6,... | collective-permute-start | bytes 196616 | tf_op jit(solution)/shard_map/ppermute | solution.py:362
  102.4 5.8 %collective-permute-start.22 = (bf16[32,1024]{1,0:T(8,128)(2,1)S(1)}, bf16[32,1024]{1,0:T(8,128)(2,1)S(1)}, u32[]{:S(2)}, u32[]{:S(2)}) collective-permute-start(bf16[32,1024]{1,0:T(8,128)(2,1)S(1)} %get-tuple-element.101.p0), channel_id=1, source_target_pairs={{0,2},{2,0},{64,66},{66,64},{1,3},{3,1},{65,67},{67,65},{4,6},{6,4... | collective-permute-start | bytes 196616 | tf_op jit(solution)/shard_map/ppermute | solution.py:362
  112.6 4.8 %collective-permute-start.28 = (bf16[256,128]{1,0:T(8,128)(2,1)S(1)}, bf16[256,128]{1,0:T(8,128)(2,1)S(1)}, u32[]{:S(2)}, u32[]{:S(2)}) collective-permute-start(bf16[256,128]{1,0:T(8,128)(2,1)S(1)} %get-tuple-element.106), channel_id=1, source_target_pairs={{0,16},{16,0},{32,48},{48,32},{1,17},{17,1},{33,49},{49,33},{2,18}... | collective-permute-start | bytes 196616 | tf_op jit(solution)/shard_map/ppermute | solution.py:362
  113.2 5.8 %collective-permute-start.29 = (bf16[256,128]{1,0:T(8,128)(2,1)S(1)}, bf16[256,128]{1,0:T(8,128)(2,1)S(1)}, u32[]{:S(2)}, u32[]{:S(2)}) collective-permute-start(bf16[256,128]{1,0:T(8,128)(2,1)S(1)} %get-tuple-element.107), channel_id=1, source_target_pairs={{0,32},{16,48},{32,0},{48,16},{1,33},{17,49},{33,1},{49,17},{2,34}... | collective-permute-start | bytes 196616 | tf_op jit(solution)/shard_map/ppermute | solution.py:362
  115.4 5.5 %collective-permute-start.30 = (bf16[256,128]{1,0:T(8,128)(2,1)S(1)}, bf16[256,128]{1,0:T(8,128)(2,1)S(1)}, u32[]{:S(2)}, u32[]{:S(2)}) collective-permute-start(bf16[256,128]{1,0:T(8,128)(2,1)S(1)} %get-tuple-element.108), channel_id=1, source_target_pairs={{0,48},{16,32},{32,16},{48,0},{1,49},{17,33},{33,17},{49,1},{2,50}... | collective-permute-start | bytes 196616 | tf_op jit(solution)/shard_map/ppermute | solution.py:362
  127.0 6.2 %collective-permute-start.32 = (bf16[32,1024]{1,0:T(8,128)(2,1)S(1)}, bf16[32,1024]{1,0:T(8,128)(2,1)S(1)}, u32[]{:S(2)}, u32[]{:S(2)}) collective-permute-start(bf16[32,1024]{1,0:T(8,128)(2,1)S(1)} %get-tuple-element.119), channel_id=1, source_target_pairs={{0,2},{2,0},{64,66},{66,64},{1,3},{3,1},{65,67},{67,65},{4,6},{6,4... | collective-permute-start | bytes 196616 | tf_op jit(solution)/shard_map/ppermute | solution.py:362
  129.2 4.3 %collective-permute-start.33 = (bf16[32,1024]{1,0:T(8,128)(2,1)S(1)}, bf16[32,1024]{1,0:T(8,128)(2,1)S(1)}, u32[]{:S(2)}, u32[]{:S(2)}) collective-permute-start(bf16[32,1024]{1,0:T(8,128)(2,1)S(1)} %get-tuple-element.120), channel_id=1, source_target_pairs={{0,64},{2,66},{64,0},{66,2},{1,65},{3,67},{65,1},{67,3},{4,68},{6,... | collective-permute-start | bytes 196616 | tf_op jit(solution)/shard_map/ppermute | solution.py:362
  129.5 5.5 %collective-permute-start.34 = (bf16[32,1024]{1,0:T(8,128)(2,1)S(1)}, bf16[32,1024]{1,0:T(8,128)(2,1)S(1)}, u32[]{:S(2)}, u32[]{:S(2)}) collective-permute-start(bf16[32,1024]{1,0:T(8,128)(2,1)S(1)} %get-tuple-element.121), channel_id=1, source_target_pairs={{0,66},{2,64},{64,2},{66,0},{1,67},{3,65},{65,3},{67,1},{4,70},{6,... | collective-permute-start | bytes 196616 | tf_op jit(solution)/shard_map/ppermute | solution.py:362
  157.4 12.8 %all-to-all-start.2 = ((bf16[8,48,384]{2,1,0:T(8,128)(2,1)}), bf16[8,48,384]{2,1,0:T(8,128)(2,1)S(1)}, u32[]{:S(2)}, u32[]{:S(2)}) async-start(bf16[8,48,384]{2,1,0:T(8,128)(2,1)} %shard_map.263), calls=%async_computation.4 | async-start | bytes 589824 | tf_op jit(solution)/shard_map/all_to_all | solution.py:519
  162.7 12.4 %collective-permute-start.36 = (bf16[64,1024]{1,0:T(8,128)(2,1)S(1)}, bf16[64,1024]{1,0:T(8,128)(2,1)S(1)}, u32[]{:S(2)}, u32[]{:S(2)}) collective-permute-start(bf16[64,1024]{1,0:T(8,128)(2,1)S(1)} %shard_map.259.p0), channel_id=1, source_target_pairs={{0,2},{2,0},{1,3},{3,1},{4,6},{6,4},{5,7},{7,5},{8,10},{10,8},{9,1... | collective-permute-start | bytes 393224 | tf_op jit(solution)/shard_map/ppermute | solution.py:362
  165.7 9.6 %collective-permute-start.37 = (bf16[64,1024]{1,0:T(8,128)(2,1)S(1)}, bf16[64,1024]{1,0:T(8,128)(2,1)S(1)}, u32[]{:S(2)}, u32[]{:S(2)}) collective-permute-start(bf16[64,1024]{1,0:T(8,128)(2,1)S(1)} %collective-permute-done.35.p1), channel_id=1, source_target_pairs={{0,2},{2,0},{1,3},{3,1},{4,6},{6,4},{5,7},{7,5},{8,10},{10,8},{9,1... | collective-permute-start | bytes 393224 | tf_op jit(solution)/shard_map/ppermute | solution.py:362
  172.1 5.7 %collective-permute-start.39 = (f32[16,384]{1,0:T(8,128)S(1)}, f32[16,384]{1,0:T(8,128)S(1)}, u32[]{:S(2)}, u32[]{:S(2)}) collective-permute-start(f32[16,384]{1,0:T(8,128)S(1)} %shard_map.265.one), channel_id=1, source_target_pairs={{0,2},{2,0},{1,3},{3,1},{4,6},{6,4},{5,7},{7,5},{8,10},{10,8},{9,1... | collective-permute-start | bytes 73736 | tf_op jit(solution)/shard_map/ppermute | solution.py:362
  (45 other events, 413.3 us)
Sparse Core Ops, SparseCore 0:
  17.3 53.6 all-gather.2
  88.9 42.0 reduce-scatter.4
  133.3 22.3 reduce-scatter.2

commit v5 on v4

--- a/solution.py
+++ b/solution.py
@@ -15,6 +15,7 @@
 BF = jnp.bfloat16
 F32 = jnp.float32
 SCALE = 64 ** (-0.5)
+GROUPS = ((0, 0, 1, 3), (0, 1, 3, 1), (1, 0, 1, 3), (1, 1, 3, 1))
 WHOLE = pl.BlockSpec(memory_space=pltpu.VMEM)
 
 
@@ -23,17 +24,19 @@
         self.value, self.kind = value, kind
 
 
-def call(body, outs, *operands, room=16):
+def call(body, outs, *operands, room=16, scalars=(), scratch=()):
     spec = lambda item: pl.BlockSpec() if isinstance(item, Far) else WHOLE
     bare = lambda item: item.value if isinstance(item, Far) else item
+    scalar = pl.BlockSpec(memory_space=pltpu.SMEM)
     return list(
         pl.pallas_call(
             body,
             out_shape=[jax.ShapeDtypeStruct(*bare(out)) for out in outs],
-            in_specs=[spec(item) for item in operands],
+            in_specs=[scalar] * len(scalars) + [spec(item) for item in operands],
             out_specs=[spec(out) for out in outs],
+            scratch_shapes=list(scratch),
             compiler_params=pltpu.CompilerParams(vmem_limit_bytes=room * 2**20),
-        )(*[bare(item) for item in operands])
+        )(*scalars, *[bare(item) for item in operands])
     )
 
 
@@ -152,8 +155,8 @@
     dy = jnp.concatenate([dy_own[...], dy_other[...]])
     def both(left, at, width):
         first, second = left[:, :512], left[:, 512:]
-        return dot(first, w[:, 0, :, at : at + width].reshape(512, width)) + dot(
-            second, w[:, 1, :, at : at + width].reshape(512, width)
+        return dot(first, w[0, :, :, at : at + width].reshape(512, width)) + dot(
+            second, w[1, :, :, at : at + width].reshape(512, width)
         )
     gate, up, d_act = both(rows, 0, 512), both(rows, 512, 512), both(dy, 1024, 512)
     active, d_gate, d_up = feed_parts(gate, up, d_act)
@@ -171,9 +174,9 @@
     dgu[:, 1024:] = dgu_tail
     halves = []
     for z in range(2):
-        part = right_product(d_gate, w[:, z, :, :512].reshape(512, 512))
-        part = part + right_product(d_up, w[:, z, :, 512:1024].reshape(512, 512))
-        part = part + right_product(dgu_tail, w[:, z, :, 1536:1664].reshape(512, 128))
+        part = right_product(d_gate, w[z, :, :, :512].reshape(512, 512))
+        part = part + right_product(d_up, w[z, :, :, 512:1024].reshape(512, 512))
+        part = part + right_product(dgu_tail, w[z, :, :, 1536:1664].reshape(512, 128))
         halves.append(part)
     partial = jnp.concatenate(halves, axis=1).reshape(4, 2, 32, 1024)
     send[:, :32] = partial[:, 1].astype(BF)
@@ -181,27 +184,61 @@
     low_act = act[...]
     halves = []
     for z in range(2):
-        part = right_product(low_act[:, :512], w[:, z, :, 1024:1536].reshape(512, 512))
-        halves.append(part + right_product(low_act[:, 512:], w[:, z, :, 1664:].reshape(512, 128)))
+        part = right_product(low_act[:, :512], w[z, :, :, 1024:1536].reshape(512, 512))
+        halves.append(part + right_product(low_act[:, 512:], w[z, :, :, 1664:].reshape(512, 128)))
     partial = jnp.concatenate(halves, axis=1).reshape(4, 2, 32, 1024)
     send[:, 32:] = partial[:, 1].astype(BF)
     keep[:, 32:] = partial[:, 0]
 
 
-def feed_weights(hn, dy_own, dy_other, act, dgu, dw):
+def feed_weights(place, hn, dy_own, dy_other, act, dgu, *outs):
+    dw = outs[8]
     dy = jnp.concatenate([dy_own[...], dy_other[...]])
     rows, active = hn[...], act[...]
     for z in range(2):
         left, left_dy = rows[:, z * 512 : (z + 1) * 512], dy[:, z * 512 : (z + 1) * 512]
         def put(value, at, width):
-            blocks = value.astype(BF).reshape(4, 4, 32, width)
-            for y in range(4):
-                dw[:, z, y, :, at : at + width] = blocks[y]
+            dw[z, :, :, at : at + width] = value.astype(BF).reshape(16, 32, width)
         put(left_product(left, dgu[:, :512]), 0, 512)
         put(left_product(left, dgu[:, 512:1024]), 512, 512)
         put(left_product(left_dy, active[:, :512]), 1024, 512)
         put(left_product(left, dgu[:, 1024:]), 1536, 128)
         put(left_product(left_dy, active[:, 512:]), 1664, 128)
+    for group, (side, z, first, second) in enumerate(GROUPS):
+        for i, (sent, kept) in enumerate(((first, 0), (2, second))):
+            for other in range(4):
+                for out, near in ((outs[group], sent), (outs[4 + group], kept)):
+                    dy_, dx_ = (other, near) if side == 0 else (near, other)
+                    at = (place[0] ^ dy_) * 4 + (place[1] ^ dx_)
+                    out[i, other] = dw[z, at, :, side * 896 : (side + 1) * 896]
+
+
+def add_first(*refs):
+    keeps, gots, sends, owns = refs[:4], refs[4:8], refs[8:12], refs[12:]
+    for keep, got, send, own in zip(keeps, gots, sends, owns):
+        own[...] = keep[0].astype(F32) + got[0].astype(F32)
+        send[...] = (keep[1].astype(F32) + got[1].astype(F32)).astype(BF)
+
+
+def add_second(*refs):
+    owns, gots, outs = refs[:4], refs[4:8], refs[8:]
+    for group, (side, z, _, _) in enumerate(GROUPS):
+        total = owns[group][...] + gots[group][...].astype(F32)
+        outs[side * 4][z] = total[0]
+        for k in range(1, 4):
+            outs[side * 4 + k][z] = total[k].astype(BF)
+
+
+def add_third(zl, *refs):
+    ins, own, send = refs[:8], refs[8], refs[9]
+    for side in range(2):
+        mine, one, two, three = ins[side * 4 : side * 4 + 4]
+        at = slice(side * 896, (side + 1) * 896)
+        def total(z):
+            first = mine[z] + one[z].astype(F32)
+            return first + (two[z].astype(F32) + three[z].astype(F32))
+        own[:, at] = total(zl[0])
+        send[:, at] = total(1 - zl[0]).astype(BF)
 
 
 def hidden_grad(own, one, two, three, h, dy, gain, dh, low, gain_part, block):
@@ -279,17 +316,11 @@
 
 
 def attend_weights(normed, d_qkv, d_attn, o, gains, dw):
-    first = left_product(normed[...], d_qkv[...]).astype(BF).reshape(8, 4, 32, 256)
-    second = left_product(d_attn[...], o[...].astype(BF)).astype(BF).reshape(8, 4, 32, 128)
-    for i in range(8):
-        dw[:, i * 32 : (i + 1) * 32, :256] = first[i]
-        dw[:, i * 32 : (i + 1) * 32, 256:] = second[i]
-    dw[:, 256:] = jnp.broadcast_to(gains[...][None], (4, 16, 384))
-
-
-def share_gains(dw, out):
-    out[:, :32] = dw[:256].reshape(8, 32, 384)
-    out[:, 32:] = jnp.broadcast_to(dw[256:][None], (8, 16, 384))
+    first = left_product(normed[...], d_qkv[...]).astype(BF)
+    second = left_product(d_attn[...], o[...].astype(BF)).astype(BF)
+    dw[:, :32, :256] = first.reshape(32, 32, 256)
+    dw[:, :32, 256:] = second.reshape(32, 32, 128)
+    dw[:, 32:] = jnp.broadcast_to(gains[...][None], (32, 16, 384))
 
 
 def token_rows(own, one, two, three, dh, x, gain, block, out):
@@ -311,9 +342,10 @@
     wo[...] = jnp.concatenate([low[:, 256:], high[:, 256:]], axis=1)
 
 
-def finish_feed(parts, wg, wu, wd):
-    low = jnp.sum(parts[0].astype(F32), axis=0)
-    high = jnp.sum(parts[1].astype(F32), axis=0)
+def finish_feed(zl, own, got, wg, wu, wd):
+    mine, its = own[...], got[...].astype(F32)
+    first = zl[0] == 0
+    low, high = jnp.where(first, mine, its), jnp.where(first, its, mine)
     for i, out in enumerate((wg, wu, wd)):
         wide, tail = slice(i * 512, (i + 1) * 512), slice(1536 + i * 64, 1600 + i * 64)
         out[...] = jnp.concatenate(
@@ -333,7 +365,7 @@
     key[...] = total[1:2, 256:320]
 
 
-def prepare(zl, wq, wk, wv, wo, wg, wu, wd, blocks, send_f, keep_f):
+def prepare(zl, head, wq, wk, wv, wo, wg, wu, wd, tokens, blocks, send_f, keep_f, x_own):
     for z in range(2):
         at = 0
         for w in (wq, wk, wv, wo):
@@ -351,11 +383,43 @@
     first = zl[0] == 0
     keep_f[...] = jnp.where(first, sides[0], sides[1])
     send_f[...] = jnp.where(first, sides[1], sides[0])
-
-
-def order_rows(zl, own, got, out):
-    out[zl[0]] = own[...]
-    out[1 - zl[0]] = got[...]
+    relative_rows(head, tokens, x_own)
+
+
+def relative_rows(head, rows, out):
+    for k in range(4):
+        out[k * 32 : (k + 1) * 32] = rows[0, pl.ds((head[0] ^ k) * 32, 32)]
+
+
+def order_rows(zl, own, got, *outs):
+    for side, out in enumerate(outs):
+        at = slice(side * 896, (side + 1) * 896)
+        out[zl[0]] = own[:, at]
+        out[1 - zl[0]] = got[:, at]
+
+
+def join_first(*refs):
+    for group, (side, z, _, _) in enumerate(GROUPS):
+        for k in range(4):
+            refs[8 + group][k] = refs[side * 4 + k][z]
+
+
+def join_second(*refs):
+    for own, got, out in zip(refs[:4], refs[4:8], refs[8:]):
+        out[0] = own[...]
+        out[1] = got[...]
+
+
+def assemble(place, *refs):
+    out = refs[8]
+    for group, (side, z, first, second) in enumerate(GROUPS):
+        held, got = refs[group], refs[4 + group]
+        for i, (near, far) in enumerate(((0, second), (first, 2))):
+            for other in range(4):
+                for blocks, step in ((held, near), (got, far)):
+                    dy_, dx_ = (other, step) if side == 0 else (step, other)
+                    at = (place[0] ^ dy_) * 4 + (place[1] ^ dx_)
+                    out[z, at, :, side * 896 : (side + 1) * 896] = blocks[i, other]
 
 
 def swap(value, axes, size, mask):
@@ -415,35 +479,33 @@
     zl, y, head = lax.axis_index("zl"), lax.axis_index("y"), lax.axis_index(("zh", "c"))
     attn_gain_row, ffn_gain_row = attn_gain[None], ffn_gain[None]
 
-    scalar = pl.BlockSpec(memory_space=pltpu.SMEM)
-    zl_ref = zl.reshape(1)
-    blocks, send_f, keep_f = pl.pallas_call(
+    zl_ref, head_ref = zl.reshape(1), head.reshape(1)
+    place = jnp.stack([y, lax.axis_index("x")])
+    side, group = ((2, 32, 896), BF), ((4, 32, 896), BF)
+    pairs = ((2, 4, 32, 896), BF)
+
+    def partner(values, turn):
+        axes = ("x", "y")
+        return [
+            swap(value, axes[g[0]], 4, g[2 + turn]) for value, g in zip(values, GROUPS)
+        ]
+
+    blocks, send_f, keep_f, x_own = call(
         prepare,
-        out_shape=[
-            jax.ShapeDtypeStruct(shape, BF)
-            for shape in ((2, 16, 32, 384), (32, 1792), (32, 1792))
-        ],
-        in_specs=[scalar] + [pl.BlockSpec()] * 7,
-        out_specs=[WHOLE] * 3,
-    )(zl_ref, w_query, w_key, w_value, w_out, w_gate, w_up, w_down)
+        [((2, 16, 32, 384), BF), ((32, 1792), BF), ((32, 1792), BF), ((128, 1024), BF)],
+        *[Far(w) for w in (w_query, w_key, w_value, w_out, w_gate, w_up, w_down, tokens)],
+        scalars=(zl_ref, head_ref),
+    )
     got_f = swap(send_f, "zl", 2, 1)
+    x_other = swap(x_own, "zl", 2, 1)
     w_a = lax.all_to_all(blocks.reshape(1024, 384), PLANE, 0, 0, tiled=True)
-    rows_f = pl.pallas_call(
-        order_rows,
-        out_shape=jax.ShapeDtypeStruct((2, 32, 1792), BF),
-        in_specs=[scalar] + [WHOLE] * 2,
-        out_specs=pl.BlockSpec(),
-    )(zl_ref, keep_f, got_f)
-    w_f = lax.all_gather(rows_f, ("y", "x"), axis=0)
-
-    order = head ^ jnp.arange(4)
-    (late_tokens,) = after([tokens], blocks)
-    x_own = late_tokens[0].reshape(4, 32, 1024)[order].reshape(128, 1024)
-    x_other = swap(x_own, "zl", 2, 1)
-
     (late_dy,) = after([cotangent], x_own)
-    dy_own = late_dy[0].reshape(4, 32, 1024)[order].reshape(128, 1024)
+    (dy_own,) = call(relative_rows, [((128, 1024), BF)], Far(late_dy), scalars=(head_ref,))
     dy_other = swap(dy_own, "zl", 2, 1)
+
+    sides = call(order_rows, [side, side], keep_f, got_f, scalars=(zl_ref,))
+    pieces = [sides[0], *fan([sides[0]] * 4, "y"), sides[1], *fan([sides[1]] * 4, "x")]
+    held = call(join_first, [group] * 4, *pieces)
 
     (late_positions,) = after([positions], blocks)
     steps = jnp.array([dl * 16 + ky * 4 + d for ky in range(4) for dl in range(2) for d in range(4)])
@@ -465,9 +527,15 @@
         x_own, x_other, Far(w_a), attn_gain_row, qk_gain, cosine, sine,
     )
     kvs = [kv] + fan([kv] * 4, "y")
+    held = after(held, kv)
+    held = call(join_second, [pairs] * 4, *held, *partner(held, 0))
     send, keep, o, l = call(
         attend, halves + [Far(wide_flat)] * 2, qh, *kvs, own_places, places, Far(w_a)
     )
+    held = after(held, send)
+    w_f = call(
+        assemble, [((2, 16, 32, 1792), BF)], *held, *partner(held, 1), scalars=(place,)
+    )[0]
     h, hn = call(
         hidden, [Far(rows_high), rows_low], *sum_scatter(send, keep), x_own, ffn_gain_row
     )
@@ -475,52 +543,61 @@
         feed,
         [((4, 64, 1024), BF), ((4, 64, 1024), F32)]
         + [((256, 1024), BF), ((256, 640), BF), ((256, 1152), BF)],
-        *gather_rows(hn), dy_own, dy_other, Far(w_f), room=24,
+        *gather_rows(hn), dy_own, dy_other, w_f, room=24,
     )
     pair = sum_pair(send, keep)
     act, dgu = after([act, dgu], *pair)
     d_hn = [pair[0]] + fan([None] + pair[1:], Z)
-    (dw_f,) = call(
-        feed_weights, [Far(((4, 2, 4, 32, 1792), BF))], hn_all, dy_own, dy_other, act, dgu, room=24
-    )
-    dw_f = lax.psum_scatter(dw_f.reshape(1024, 1792), "x", scatter_dimension=0, tiled=True)
+    groups = call(
+        feed_weights, [pairs] * 8, hn_all, dy_own, dy_other, act, dgu, room=24,
+        scalars=(place,), scratch=[pltpu.VMEM((2, 16, 32, 1792), BF)],
+    )
+    sums = call(
+        add_first, [group] * 4 + [((4, 32, 896), F32)] * 4, *groups[4:], *partner(groups[:4], 0)
+    )
     dh, d_low, ffn_part, block = call(
         hidden_grad, [Far(rows_high), rows_low, Far(((1, 1024), F32)), Far(rows_low)],
         *d_hn, Far(h), dy_own, ffn_gain_row,
     )
+    pieces_low = gather_rows(d_low)
+    pieces_low = after(pieces_low, sums[4])
     d_attn, d_qh, *d_kvs = call(
         attend_grad, [Far(((256, 1024), BF)), wide_flat, wide_flat, flat, flat, flat],
-        *gather_rows(d_low), Far(qh), *[Far(t) for t in kvs], own_places, places, Far(w_a), Far(o), Far(l),
-    )
+        *pieces_low, Far(qh), *[Far(t) for t in kvs], own_places, places, Far(w_a), Far(o), Far(l),
+    )
+    sums = call(
+        add_second, [((2, 32, 896), F32), side, side, side] * 2, *sums[4:], *partner(sums[:4], 1)
+    )
+    (d_qh,) = after([d_qh], sums[0])
     d_qkv, send, keep, gains = call(
         project_grad, [((256, 256), BF)] + halves + [((16, 384), BF)],
         d_qh, d_kvs[0], *fan(d_kvs, "y"), Far(qkv), cosine, sine, qk_gain, Far(w_a),
         Far(x_own), Far(x_other), Far(ffn_part),
     )
     (dw_a,) = call(
-        attend_weights, [Far(((4, 272, 384), BF))], Far(normed), d_qkv, Far(d_attn), Far(o), gains
-    )
-    (keep,) = after([keep], dw_a)
-    dw_a = lax.psum_scatter(dw_a.reshape(1088, 384), "x", scatter_dimension=0, tiled=True)
+        attend_weights, [((32, 48, 384), BF)], Far(normed), d_qkv, Far(d_attn), Far(o), gains
+    )
     d_xn = sum_scatter(send, keep)
+    last = [sums[0], *fan(sums[:4], "y"), sums[4], *fan(sums[4:], "x")]
+    own_f, send_f = call(
+        add_third, [((32, 1792), F32), ((32, 1792), BF)], *last, scalars=(zl_ref,)
+    )
+    grad_wg, grad_wu, grad_wd = call(
+        finish_feed, [Far(((32, 1152), F32))] * 3, own_f, swap(send_f, "zl", 2, 1),
+        scalars=(zl_ref,),
+    )
     (rows,) = call(
         token_rows, [((64, 1024), BF)], *d_xn, Far(dh), x_own, attn_gain_row, Far(block)
     )
     tokens_grad, block_out = gather_head(rows, head)
     tokens_grad, block_out = tokens_grad[None], block_out[None]
 
-    (dw_f,) = after([dw_f], rows)
-    dw_f = lax.all_to_all(dw_f, ("zl", "y"), 0, 0, tiled=True)
-    grad_wg, grad_wu, grad_wd = call(
-        finish_feed, [Far(((32, 1152), F32))] * 3, dw_f.reshape(2, 4, 32, 1792)
-    )
-    (dw_a,) = after([dw_a], grad_wg)
-    (dw_a,) = call(share_gains, [((8, 48, 384), BF)], dw_a)
-    dw_a = lax.all_to_all(dw_a, ("zl", "y"), 0, 0, tiled=True)
+    (dw_a,) = after([dw_a], d_xn[0])
+    dw_a = lax.all_to_all(dw_a, PLANE, 0, 0, tiled=True)
     grad_wq, grad_wk, grad_wv, grad_wo, gains = call(
         finish_attend,
         [Far(((32, n), F32)) for n in (256, 128, 128, 256)] + [((16, 384), F32)],
-        dw_a.reshape(2, 4, 48, 384),
+        dw_a.reshape(2, 16, 48, 384),
     )
     (gains,) = call(add_two, [((16, 384), F32)], gains, swap(gains, "c", 2, 1))
     attn_sum, ffn_sum, query_sum, key_sum = call(

time: 186 us -> 203 us (1.091)
  starting transfers between devices: 57.7 us -> 99.8 us
  blocking collectives: 16.9 us -> 0 us
  between operations: 14.2 us -> 1.23 us
  waiting for transfers between devices: 57.2 us -> 64.1 us
  local copies, waits for them, and re-layouts: 14.6 us -> 10.1 us
  Pallas kernels: 21.5 us -> 24.1 us
    ppermute x40 -> x69, starting transfers between devices: 43.8 us -> 86.6 us  [swap(): return lax.ppermute(value, axes, [(i, i ^ mask) for i in range(size)])]
    all_to_all x1 -> x0, blocking collectives: 16.9 us -> none  [local(): dw_f = lax.all_to_all(dw_f, ('zl', 'y'), 0, 0, tiled=True)]
    ppermute x40 -> x69, waiting for transfers between devices: 51 us -> 58.3 us  [swap(): return lax.ppermute(value, axes, [(i, i ^ mask) for i in range(size)])]
    pallas_call x18 -> x26, Pallas kernels: 15.8 us -> 22.2 us  [call(): pl.pallas_call(body, out_shape=[jax.ShapeDtypeStruct(*bare(out)) for out...]
    all_to_all x1, waiting for transfers between devices: 0.01 us -> 5.85 us  [local(): w_a = lax.all_to_all(blocks.reshape(1024, 384), PLANE, 0, 0, tiled=True)]
    pallas_call x2 -> x0, Pallas kernels: 3.87 us -> none  [the longest x1 2.2 us: local(): pl.pallas_call(prepare, out_shape=[jax.ShapeDtypeStruct(shape, BF) for sh...]
    all_to_all x1, waiting for transfers between devices: 3.28 us -> 0.01 us  [local(): dw_a = lax.all_to_all(dw_a, PLANE, 0, 0, tiled=True)]
    reduce_scatter x2 -> x0, waiting for transfers between devices: 2.83 us -> none  [the longest x1 2.81 us: local(): lax.psum_scatter(dw_a.reshape(1088, 384), 'x', scatter_dimension=0, tiled...]
  transfers between devices with their start and end apart: 45 -> 71, of which waited for: 27 -> 25; matrix products, arithmetic and copies ran while one was open for 4% -> 2% of each run, Pallas kernels for 7% -> 8%
where the time goes in v5:
time: 203 us; the launch traced here: 201 us
  starting transfers between devices  99.8 us (49%)
  waiting for transfers between devices  64.1 us (32%)
  Pallas kernels  24.1 us (12%)
  local copies, waits for them, and re-layouts  10.1 us (5%)
    ppermute x69, starting transfers between devices, swap(): return lax.ppermute(value, axes, [(i, i ^ mask) for i in range(size)])  86.6 us
    ppermute x69, waiting for transfers between devices, swap(): return lax.ppermute(value, axes, [(i, i ^ mask) for i in range(size)])  58.3 us
    pallas_call x26, Pallas kernels, call(): pl.pallas_call(body, out_shape=[jax.ShapeDtypeStruct(*bare(out)) for out...  22.2 us
    all_to_all x1, starting transfers between devices, local(): w_a = lax.all_to_all(blocks.reshape(1024, 384), PLANE, 0, 0, tiled=True)  8.88 us
    unnamed x78, local copies, waits for them, and re-layouts  8.48 us
    all_to_all x1, waiting for transfers between devices, local(): w_a = lax.all_to_all(blocks.reshape(1024, 384), PLANE, 0, 0, tiled=True)  5.85 us
    all_to_all x1, starting transfers between devices, local(): dw_a = lax.all_to_all(dw_a, PLANE, 0, 0, tiled=True)  4.4 us
  transfers between devices with their start and end apart: 71, of which 25 were waited for; matrix products, arithmetic and copies ran while one was open for 2% of the time, Pallas kernels for 8%

profile of v5, /device:TPU:0, one launch (start us, length us, event | category | flops | bytes accessed | tf_op | source)
XLA Modules:
  0.0 201.0 jit_solution(11234504338104170141)
XLA Ops:
  10.2 8.9 %all-to-all-start = ((bf16[32,32,384]{2,1,0:T(8,128)(2,1)}), bf16[32,32,384]{2,1,0:T(8,128)(2,1)S(1)}, u32[]{:S(2)}, u32[]{:S(2)}) async-start(bf16[32,32,384]{2,1,0:T(8,128)(2,1)} %bitcast.2), calls=%async_computation | async-start | bytes 1572864 | tf_op jit(solution)/shard_map/all_to_all | solution.py:501
  24.0 2.7 %collective-permute-start.18 = (bf16[2,32,896]{2,1,0:T(8,128)(2,1)S(1)}, bf16[2,32,896]{2,1,0:T(8,128)(2,1)S(1)}, u32[]{:S(2)}, u32[]{:S(2)}) collective-permute-start(bf16[2,32,896]{2,1,0:T(8,128)(2,1)S(1)} %get-tuple-element.145.refs_0_), channel_id=1, source_target_pairs={{0,32},{16,48},{32,0},{48,16},{1,33},{17,49},{33,1},{49,17},{2,34}... | collective-permute-start | bytes 344072 | tf_op jit(solution)/shard_map/ppermute | solution.py:426
  26.7 5.8 %all-to-all-done = bf16[32,32,384]{2,1,0:T(8,128)(2,1)S(1)} async-done(((bf16[32,32,384]{2,1,0:T(8,128)(2,1)}), bf16[32,32,384]{2,1,0:T(8,128)(2,1)S(1)}, u32[]{:S(2)}, u32[]{:S(2)}) %all-to-all-start) | async-done | bytes 786464 | tf_op jit(solution)/shard_map/all_to_all | solution.py:501
  33.8 3.0 %collective-permute-start.2 = (bf16[256,128]{1,0:T(8,128)(2,1)S(1)}, bf16[256,128]{1,0:T(8,128)(2,1)S(1)}, u32[]{:S(2)}, u32[]{:S(2)}) collective-permute-start(bf16[256,128]{1,0:T(8,128)(2,1)S(1)} %get-tuple-element.134.kv0), channel_id=1, source_target_pairs={{0,32},{16,48},{32,0},{48,16},{1,33},{17,49},{33,1},{49,17},{2,34}... | collective-permute-start | bytes 196616 | tf_op jit(solution)/shard_map/ppermute | solution.py:426
  40.0 2.9 %collective-permute-start.21 = (bf16[2,32,896]{2,1,0:T(8,128)(2,1)S(1)}, bf16[2,32,896]{2,1,0:T(8,128)(2,1)}, u32[]{:S(2)}, u32[]{:S(2)}) collective-permute-start(bf16[2,32,896]{2,1,0:T(8,128)(2,1)S(1)} %get-tuple-element.146.refs_4_), channel_id=1, source_target_pairs={{0,8},{4,12},{8,0},{12,4},{1,9},{5,13},{9,1},{13,5},{2,10},{6,14},... | collective-permute-start | bytes 344072 | tf_op jit(solution)/shard_map/ppermute | solution.py:426
  53.9 3.7 %collective-permute-start.5 = (bf16[32,1024]{1,0:T(8,128)(2,1)S(1)}, bf16[32,1024]{1,0:T(8,128)(2,1)S(1)}, u32[]{:S(2)}, u32[]{:S(2)}) collective-permute-start(bf16[32,1024]{1,0:T(8,128)(2,1)S(1)} %get-tuple-element.138), channel_id=1, source_target_pairs={{0,2},{2,0},{64,66},{66,64},{1,3},{3,1},{65,67},{67,65},{4,6},{6,4... | collective-permute-start | bytes 196616 | tf_op jit(solution)/shard_map/ppermute | solution.py:426
  64.6 3.2 %collective-permute-start.7 = (bf16[32,1024]{1,0:T(8,128)(2,1)S(1)}, bf16[32,1024]{1,0:T(8,128)(2,1)S(1)}, u32[]{:S(2)}, u32[]{:S(2)}) collective-permute-start(bf16[32,1024]{1,0:T(8,128)(2,1)S(1)} %get-tuple-element.140), channel_id=1, source_target_pairs={{0,66},{2,64},{64,2},{66,0},{1,67},{3,65},{65,3},{67,1},{4,70},{6,... | collective-permute-start | bytes 196616 | tf_op jit(solution)/shard_map/ppermute | solution.py:426
  67.8 3.0 %collective-permute-done.7.three = bf16[32,1024]{1,0:T(8,128)(2,1)S(1)} collective-permute-done((bf16[32,1024]{1,0:T(8,128)(2,1)S(1)}, bf16[32,1024]{1,0:T(8,128)(2,1)S(1)}, u32[]{:S(2)}, u32[]{:S(2)}) %collective-permute-start.7) | collective-permute-done | bytes 65568 | tf_op jit(solution)/shard_map/ppermute | solution.py:426
  73.0 3.8 %collective-permute-done.9.p2 = bf16[32,1024]{1,0:T(8,128)(2,1)S(1)} collective-permute-done((bf16[32,1024]{1,0:T(8,128)(2,1)S(1)}, bf16[32,1024]{1,0:T(8,128)(2,1)S(1)}, u32[]{:S(2)}, u32[]{:S(2)}) %collective-permute-start.9) | collective-permute-done | bytes 65568 | tf_op jit(solution)/shard_map/ppermute | solution.py:426
  77.2 3.8 %collective-permute-done.11.p4 = bf16[32,1024]{1,0:T(8,128)(2,1)S(1)} collective-permute-done((bf16[32,1024]{1,0:T(8,128)(2,1)S(1)}, bf16[32,1024]{1,0:T(8,128)(2,1)S(1)}, u32[]{:S(2)}, u32[]{:S(2)}) %collective-permute-start.11) | collective-permute-done | bytes 65568 | tf_op jit(solution)/shard_map/ppermute | solution.py:426
  81.0 3.2 %collective-permute-start.13 = (bf16[32,1024]{1,0:T(8,128)(2,1)S(1)}, bf16[32,1024]{1,0:T(8,128)(2,1)S(1)}, u32[]{:S(2)}, u32[]{:S(2)}) collective-permute-start(bf16[32,1024]{1,0:T(8,128)(2,1)S(1)} %get-tuple-element.141.p0), channel_id=1, source_target_pairs={{0,66},{2,64},{64,2},{66,0},{1,67},{3,65},{65,3},{67,1},{4,70},{6,... | collective-permute-start | bytes 196616 | tf_op jit(solution)/shard_map/ppermute | solution.py:426
  84.3 2.3 %collective-permute-done.13.p6 = bf16[32,1024]{1,0:T(8,128)(2,1)S(1)} collective-permute-done((bf16[32,1024]{1,0:T(8,128)(2,1)S(1)}, bf16[32,1024]{1,0:T(8,128)(2,1)S(1)}, u32[]{:S(2)}, u32[]{:S(2)}) %collective-permute-start.13) | collective-permute-done | bytes 65568 | tf_op jit(solution)/shard_map/ppermute | solution.py:426
  88.3 2.2 %shard_map.255.w = bf16[2,16,32,1792]{3,2,1,0:T(8,128)(2,1)S(1)} custom-call(s32[2]{0:T(128)S(1)} %pad_add_fusion.place, bf16[2,4,32,896]{3,2,1,0:T(8,128)(2,1)S(1)} %get-tuple-element.159.refs_0_, bf16[2,4,32,896]{3,2,1,0:T(8,128)(2,1)} %get-tuple-element.160.refs_1_, bf16[2,4,32,896]{3,2,1,0:T(8,128)(2,1)} %get-tuple-element.161.refs_2_, ...), custom_call_target="tpu_custom_call" | custom-call | tf_op jit(solution)/shard_map/pallas_call | solution.py:32
  90.5 3.1 %collective-permute-done.15.dy_other = bf16[128,1024]{1,0:T(8,128)(2,1)S(1)} collective-permute-done((bf16[128,1024]{1,0:T(8,128)(2,1)S(1)}, bf16[128,1024]{1,0:T(8,128)(2,1)S(1)}, u32[]{:S(2)}, u32[]{:S(2)}) %collective-permute-start.15) | collective-permute-done | bytes 262176 | tf_op jit(solution)/shard_map/ppermute | solution.py:426
  93.6 2.5 %shard_map.256 = (bf16[4,64,1024]{2,1,0:T(8,128)(2,1)S(1)}, f32[4,64,1024]{2,1,0:T(8,128)S(1)}, bf16[256,1024]{1,0:T(8,128)(2,1)S(1)}, bf16[256,640]{1,0:T(8,128)(2,1)S(1)}, bf16[256,1152]{1,0:T(8,128)(2,1)S(1)}) custom-call(bf16[32,1024]{1,0:T(8,128)(2,1)S(1)} %copy-done.19, bf16[32,1024]{1,0:T(8,128)(2,1)S(1)} %collective-permute-done.8.p1, ...), custom_call_target="tpu_custom_call" | custom-call | tf_op jit(solution)/shard_map/pallas_call | solution.py:32
  103.5 2.2 %collective-permute-start.44 = (bf16[2,4,32,896]{3,2,1,0:T(8,128)(2,1)S(1)}, bf16[2,4,32,896]{3,2,1,0:T(8,128)(2,1)S(1)}, u32[]{:S(2)}, u32[]{:S(2)}) collective-permute-start(bf16[2,4,32,896]{3,2,1,0:T(8,128)(2,1)S(1)} %get-tuple-element.182), channel_id=1, source_target_pairs={{0,16},{16,0},{32,48},{48,32},{1,17},{17,1},{33,49},{49,33},{2,18}... | collective-permute-start | bytes 1376264 | tf_op jit(solution)/shard_map/ppermute | solution.py:426
  107.5 2.2 %collective-permute-start.32 = (bf16[64,1024]{1,0:T(8,128)(2,1)S(1)}, bf16[64,1024]{1,0:T(8,128)(2,1)S(1)}, u32[]{:S(2)}, u32[]{:S(2)}) collective-permute-start(bf16[64,1024]{1,0:T(8,128)(2,1)S(1)} %get-tuple-element.166), channel_id=1, source_target_pairs={{0,2},{2,0},{64,66},{66,64},{1,3},{3,1},{65,67},{67,65},{4,6},{6,4... | collective-permute-start | bytes 393224 | tf_op jit(solution)/shard_map/ppermute | solution.py:426
  109.7 4.3 %collective-permute-done.32.one = bf16[64,1024]{1,0:T(8,128)(2,1)S(1)} collective-permute-done((bf16[64,1024]{1,0:T(8,128)(2,1)S(1)}, bf16[64,1024]{1,0:T(8,128)(2,1)S(1)}, u32[]{:S(2)}, u32[]{:S(2)}) %collective-permute-start.32) | collective-permute-done | bytes 131104 | tf_op jit(solution)/shard_map/ppermute | solution.py:426
  114.1 4.9 %collective-permute-done.33.two = bf16[64,1024]{1,0:T(8,128)(2,1)S(1)} collective-permute-done((bf16[64,1024]{1,0:T(8,128)(2,1)S(1)}, bf16[64,1024]{1,0:T(8,128)(2,1)S(1)}, u32[]{:S(2)}, u32[]{:S(2)}) %collective-permute-start.33) | collective-permute-done | bytes 131104 | tf_op jit(solution)/shard_map/ppermute | solution.py:426
  119.0 2.7 %collective-permute-start.34 = (bf16[64,1024]{1,0:T(8,128)(2,1)S(1)}, bf16[64,1024]{1,0:T(8,128)(2,1)S(1)}, u32[]{:S(2)}, u32[]{:S(2)}) collective-permute-start(bf16[64,1024]{1,0:T(8,128)(2,1)S(1)} %get-tuple-element.168), channel_id=1, source_target_pairs={{0,66},{2,64},{64,2},{66,0},{1,67},{3,65},{65,3},{67,1},{4,70},{6,... | collective-permute-start | bytes 393224 | tf_op jit(solution)/shard_map/ppermute | solution.py:426
  121.7 3.4 %collective-permute-done.34.three = bf16[64,1024]{1,0:T(8,128)(2,1)S(1)} collective-permute-done((bf16[64,1024]{1,0:T(8,128)(2,1)S(1)}, bf16[64,1024]{1,0:T(8,128)(2,1)S(1)}, u32[]{:S(2)}, u32[]{:S(2)}) %collective-permute-start.34) | collective-permute-done | bytes 131104 | tf_op jit(solution)/shard_map/ppermute | solution.py:426
  126.4 2.6 %collective-permute-start.38 = (bf16[32,1024]{1,0:T(8,128)(2,1)S(1)}, bf16[32,1024]{1,0:T(8,128)(2,1)S(1)}, u32[]{:S(2)}, u32[]{:S(2)}) collective-permute-start(bf16[32,1024]{1,0:T(8,128)(2,1)S(1)} %get-tuple-element.185.p0), channel_id=1, source_target_pairs={{0,64},{2,66},{64,0},{66,2},{1,65},{3,67},{65,1},{67,3},{4,68},{6,... | collective-permute-start | bytes 196616 | tf_op jit(solution)/shard_map/ppermute | solution.py:426
  132.0 2.5 %collective-permute-done.40.p6 = bf16[32,1024]{1,0:T(8,128)(2,1)S(1)} collective-permute-done((bf16[32,1024]{1,0:T(8,128)(2,1)S(1)}, bf16[32,1024]{1,0:T(8,128)(2,1)S(1)}, u32[]{:S(2)}, u32[]{:S(2)}) %collective-permute-start.40) | collective-permute-done | bytes 65568 | tf_op jit(solution)/shard_map/ppermute | solution.py:426
  138.9 3.1 %shard_map.261 = (bf16[256,1024]{1,0:T(8,128)(2,1)S(1)}, f32[256,128]{1,0:T(8,128)S(1)}, f32[256,128]{1,0:T(8,128)S(1)}, bf16[256,128]{1,0:T(8,128)(2,1)S(1)}, b...) custom-call(bf16[32,1024]{1,0:T(8,128)(2,1)S(1)} %get-tuple-element.185.p0, ...), custom_call_target="tpu_custom_call" | custom-call | tf_op jit(solution)/shard_map/pallas_call | solution.py:32
  147.6 2.3 %collective-permute-done.51.two = bf16[256,128]{1,0:T(8,128)(2,1)S(1)} collective-permute-done((bf16[256,128]{1,0:T(8,128)(2,1)S(1)}, bf16[256,128]{1,0:T(8,128)(2,1)S(1)}, u32[]{:S(2)}, u32[]{:S(2)}) %collective-permute-start.51) | collective-permute-done | bytes 65568 | tf_op jit(solution)/shard_map/ppermute | solution.py:426
  153.6 4.4 %all-to-all-start.1 = ((bf16[32,48,384]{2,1,0:T(8,128)(2,1)}), bf16[32,48,384]{2,1,0:T(8,128)(2,1)S(1)}, u32[]{:S(2)}, u32[]{:S(2)}) async-start(bf16[32,48,384]{2,1,0:T(8,128)(2,1)} %shard_map.267), calls=%async_computation.1 | async-start | bytes 2359296 | tf_op jit(solution)/shard_map/all_to_all | solution.py:596
  159.9 2.7 %collective-permute-start.63 = (bf16[2,32,896]{2,1,0:T(8,128)(2,1)S(1)}, bf16[2,32,896]{2,1,0:T(8,128)(2,1)S(1)}, u32[]{:S(2)}, u32[]{:S(2)}) collective-permute-start(bf16[2,32,896]{2,1,0:T(8,128)(2,1)S(1)} %copy-done.33), channel_id=1, source_target_pairs={{0,32},{16,48},{32,0},{48,16},{1,33},{17,49},{33,1},{49,17},{2,34}... | collective-permute-start | bytes 344072 | tf_op jit(solution)/shard_map/ppermute | solution.py:426
  162.6 2.6 %collective-permute-start.54 = (bf16[32,1024]{1,0:T(8,128)(2,1)S(1)}, bf16[32,1024]{1,0:T(8,128)(2,1)S(1)}, u32[]{:S(2)}, u32[]{:S(2)}) collective-permute-start(bf16[32,1024]{1,0:T(8,128)(2,1)S(1)} %get-tuple-element.214), channel_id=1, source_target_pairs={{0,2},{2,0},{64,66},{66,64},{1,3},{3,1},{65,67},{67,65},{4,6},{6,4... | collective-permute-start | bytes 196616 | tf_op jit(solution)/shard_map/ppermute | solution.py:426
  166.8 9.0 %collective-permute-done.54.one = bf16[32,1024]{1,0:T(8,128)(2,1)S(1)} collective-permute-done((bf16[32,1024]{1,0:T(8,128)(2,1)S(1)}, bf16[32,1024]{1,0:T(8,128)(2,1)S(1)}, u32[]{:S(2)}, u32[]{:S(2)}) %collective-permute-start.54) | collective-permute-done | bytes 65568 | tf_op jit(solution)/shard_map/ppermute | solution.py:426
  180.7 2.8 %collective-permute-start.66 = (bf16[2,32,896]{2,1,0:T(8,128)(2,1)S(1)}, bf16[2,32,896]{2,1,0:T(8,128)(2,1)S(1)}, u32[]{:S(2)}, u32[]{:S(2)}) collective-permute-start(bf16[2,32,896]{2,1,0:T(8,128)(2,1)S(1)} %get-tuple-element.240), channel_id=1, source_target_pairs={{0,8},{4,12},{8,0},{12,4},{1,9},{5,13},{9,1},{13,5},{2,10},{6,14},... | collective-permute-start | bytes 344072 | tf_op jit(solution)/shard_map/ppermute | solution.py:426
  184.3 2.6 %collective-permute-start.58 = (bf16[64,1024]{1,0:T(8,128)(2,1)S(1)}, bf16[64,1024]{1,0:T(8,128)(2,1)S(1)}, u32[]{:S(2)}, u32[]{:S(2)}) collective-permute-start(bf16[64,1024]{1,0:T(8,128)(2,1)S(1)} %shard_map.265.p0), channel_id=1, source_target_pairs={{0,2},{2,0},{1,3},{3,1},{4,6},{6,4},{5,7},{7,5},{8,10},{10,8},{9,1... | collective-permute-start | bytes 393224 | tf_op jit(solution)/shard_map/ppermute | solution.py:426
  194.7 2.3 %collective-permute-start.61 = (f32[16,384]{1,0:T(8,128)S(1)}, f32[16,384]{1,0:T(8,128)S(1)}, u32[]{:S(2)}, u32[]{:S(2)}) collective-permute-start(f32[16,384]{1,0:T(8,128)S(1)} %shard_map.269.one), channel_id=1, source_target_pairs={{0,2},{2,0},{1,3},{3,1},{4,6},{6,4},{5,7},{7,5},{8,10},{10,8},{9,1... | collective-permute-start | bytes 73736 | tf_op jit(solution)/shard_map/ppermute | solution.py:426
  (234 shorter events, 89.0 us)
Async XLA Ops:
  8.2 13.9 %collective-permute-start.16 = (bf16[32,1792]{1,0:T(8,128)(2,1)S(1)}, bf16[32,1792]{1,0:T(8,128)(2,1)S(1)}, u32[]{:S(2)}, u32[]{:S(2)}) collective-permute-start(bf16[32,1792]{1,0:T(8,128)(2,1)S(1)} %get-tuple-element.144), channel_id=1, source_target_pairs={{0,64},{64,0},{1,65},{65,1},{2,66},{66,2},{3,67},{67,3},{4,68},{68... | collective-permute-start | bytes 344072 | tf_op jit(solution)/shard_map/ppermute | solution.py:426
  10.2 16.5 %collective-permute-start = (bf16[128,1024]{1,0:T(8,128)(2,1)S(1)}, bf16[128,1024]{1,0:T(8,128)(2,1)S(1)}, u32[]{:S(2)}, u32[]{:S(2)}) collective-permute-start(bf16[128,1024]{1,0:T(8,128)(2,1)S(1)} %get-tuple-element.130.own.x.x_own), channel_id=1, source_target_pairs={{0,64},{64,0},{1,65},{65,1},{2,66},{66,2},{3,67},{67,3},{4,68},{68... | collective-permute-start | bytes 786440 | tf_op jit(solution)/shard_map/ppermute | solution.py:426
  10.2 22.3 %all-to-all-start = ((bf16[32,32,384]{2,1,0:T(8,128)(2,1)}), bf16[32,32,384]{2,1,0:T(8,128)(2,1)S(1)}, u32[]{:S(2)}, u32[]{:S(2)}) async-start(bf16[32,32,384]{2,1,0:T(8,128)(2,1)} %bitcast.2), calls=%async_computation | async-start | bytes 1572864 | tf_op jit(solution)/shard_map/all_to_all | solution.py:501
  22.1 15.9 %collective-permute-start.17 = (bf16[2,32,896]{2,1,0:T(8,128)(2,1)S(1)}, bf16[2,32,896]{2,1,0:T(8,128)(2,1)S(1)}, u32[]{:S(2)}, u32[]{:S(2)}) collective-permute-start(bf16[2,32,896]{2,1,0:T(8,128)(2,1)S(1)} %get-tuple-element.145.refs_0_), channel_id=1, source_target_pairs={{0,16},{16,0},{32,48},{48,32},{1,17},{17,1},{33,49},{49,33},{2,18}... | collective-permute-start | bytes 344072 | tf_op jit(solution)/shard_map/ppermute | solution.py:426
  24.0 23.0 %collective-permute-start.18 = (bf16[2,32,896]{2,1,0:T(8,128)(2,1)S(1)}, bf16[2,32,896]{2,1,0:T(8,128)(2,1)S(1)}, u32[]{:S(2)}, u32[]{:S(2)}) collective-permute-start(bf16[2,32,896]{2,1,0:T(8,128)(2,1)S(1)} %get-tuple-element.145.refs_0_), channel_id=1, source_target_pairs={{0,32},{16,48},{32,0},{48,16},{1,33},{17,49},{33,1},{49,17},{2,34}... | collective-permute-start | bytes 344072 | tf_op jit(solution)/shard_map/ppermute | solution.py:426
  38.0 9.0 %collective-permute-start.19 = (bf16[2,32,896]{2,1,0:T(8,128)(2,1)S(1)}, bf16[2,32,896]{2,1,0:T(8,128)(2,1)}, u32[]{:S(2)}, u32[]{:S(2)}) collective-permute-start(bf16[2,32,896]{2,1,0:T(8,128)(2,1)S(1)} %get-tuple-element.145.refs_0_), channel_id=1, source_target_pairs={{0,48},{16,32},{32,16},{48,0},{1,49},{17,33},{33,17},{49,1},{2,50}... | collective-permute-start | bytes 344072 | tf_op jit(solution)/shard_map/ppermute | solution.py:426
  50.3 7.8 %collective-permute-start.24 = (bf16[4,32,896]{2,1,0:T(8,128)(2,1)S(1)}, bf16[4,32,896]{2,1,0:T(8,128)(2,1)S(1)}, u32[]{:S(2)}, u32[]{:S(2)}) collective-permute-start(bf16[4,32,896]{2,1,0:T(8,128)(2,1)S(1)} %get-tuple-element.152.refs_1_), channel_id=1, source_target_pairs={{0,12},{4,8},{8,4},{12,0},{1,13},{5,9},{9,5},{13,1},{2,14},{6,10},... | collective-permute-start | bytes 688136 | tf_op jit(solution)/shard_map/ppermute | solution.py:426
  53.9 10.6 %collective-permute-start.5 = (bf16[32,1024]{1,0:T(8,128)(2,1)S(1)}, bf16[32,1024]{1,0:T(8,128)(2,1)S(1)}, u32[]{:S(2)}, u32[]{:S(2)}) collective-permute-start(bf16[32,1024]{1,0:T(8,128)(2,1)S(1)} %get-tuple-element.138), channel_id=1, source_target_pairs={{0,2},{2,0},{64,66},{66,64},{1,3},{3,1},{65,67},{67,65},{4,6},{6,4... | collective-permute-start | bytes 196616 | tf_op jit(solution)/shard_map/ppermute | solution.py:426
  61.1 26.0 %collective-permute-start.27 = (bf16[2,4,32,896]{3,2,1,0:T(8,128)(2,1)S(1)}, bf16[2,4,32,896]{3,2,1,0:T(8,128)(2,1)}, u32[]{:S(2)}, u32[]{:S(2)}) collective-permute-start(bf16[2,4,32,896]{3,2,1,0:T(8,128)(2,1)S(1)} %get-tuple-element.159.refs_0_), channel_id=1, source_target_pairs={{0,12},{4,8},{8,4},{12,0},{1,13},{5,9},{9,5},{13,1},{2,14},{6,10},... | collective-permute-start | bytes 1376264 | tf_op jit(solution)/shard_map/ppermute | solution.py:426
  62.6 24.6 %collective-permute-start.28 = (bf16[2,4,32,896]{3,2,1,0:T(8,128)(2,1)}, bf16[2,4,32,896]{3,2,1,0:T(8,128)(2,1)}, u32[]{:S(2)}, u32[]{:S(2)}) collective-permute-start(bf16[2,4,32,896]{3,2,1,0:T(8,128)(2,1)} %get-tuple-element.160.refs_1_), channel_id=1, source_target_pairs={{0,4},{4,0},{8,12},{12,8},{1,5},{5,1},{9,13},{13,9},{2,6},{6,2},{1... | collective-permute-start | bytes 1376264 | tf_op jit(solution)/shard_map/ppermute | solution.py:426
  63.3 24.4 %collective-permute-start.29 = (bf16[2,4,32,896]{3,2,1,0:T(8,128)(2,1)}, bf16[2,4,32,896]{3,2,1,0:T(8,128)(2,1)}, u32[]{:S(2)}, u32[]{:S(2)}) collective-permute-start(bf16[2,4,32,896]{3,2,1,0:T(8,128)(2,1)} %get-tuple-element.161.refs_2_), channel_id=1, source_target_pairs={{0,48},{16,32},{32,16},{48,0},{1,49},{17,33},{33,17},{49,1},{2,50}... | collective-permute-start | bytes 1376264 | tf_op jit(solution)/shard_map/ppermute | solution.py:426
  64.5 23.3 %collective-permute-start.30 = (bf16[2,4,32,896]{3,2,1,0:T(8,128)(2,1)}, bf16[2,4,32,896]{3,2,1,0:T(8,128)(2,1)}, u32[]{:S(2)}, u32[]{:S(2)}) collective-permute-start(bf16[2,4,32,896]{3,2,1,0:T(8,128)(2,1)} %get-tuple-element.162.refs_3_), channel_id=1, source_target_pairs={{0,16},{16,0},{32,48},{48,32},{1,17},{17,1},{33,49},{49,33},{2,18}... | collective-permute-start | bytes 1376264 | tf_op jit(solution)/shard_map/ppermute | solution.py:426
  100.3 26.1 %collective-permute-start.42 = (bf16[2,4,32,896]{3,2,1,0:T(8,128)(2,1)S(1)}, bf16[2,4,32,896]{3,2,1,0:T(8,128)(2,1)S(1)}, u32[]{:S(2)}, u32[]{:S(2)}) collective-permute-start(bf16[2,4,32,896]{3,2,1,0:T(8,128)(2,1)S(1)} %get-tuple-element.180), channel_id=1, source_target_pairs={{0,4},{4,0},{8,12},{12,8},{1,5},{5,1},{9,13},{13,9},{2,6},{6,2},{1... | collective-permute-start | bytes 1376264 | tf_op jit(solution)/shard_map/ppermute | solution.py:426
  101.9 27.2 %collective-permute-start.43 = (bf16[2,4,32,896]{3,2,1,0:T(8,128)(2,1)S(1)}, bf16[2,4,32,896]{3,2,1,0:T(8,128)(2,1)S(1)}, u32[]{:S(2)}, u32[]{:S(2)}) collective-permute-start(bf16[2,4,32,896]{3,2,1,0:T(8,128)(2,1)S(1)} %get-tuple-element.181), channel_id=1, source_target_pairs={{0,12},{4,8},{8,4},{12,0},{1,13},{5,9},{9,5},{13,1},{2,14},{6,10},... | collective-permute-start | bytes 1376264 | tf_op jit(solution)/shard_map/ppermute | solution.py:426
  103.5 26.0 %collective-permute-start.44 = (bf16[2,4,32,896]{3,2,1,0:T(8,128)(2,1)S(1)}, bf16[2,4,32,896]{3,2,1,0:T(8,128)(2,1)S(1)}, u32[]{:S(2)}, u32[]{:S(2)}) collective-permute-start(bf16[2,4,32,896]{3,2,1,0:T(8,128)(2,1)S(1)} %get-tuple-element.182), channel_id=1, source_target_pairs={{0,16},{16,0},{32,48},{48,32},{1,17},{17,1},{33,49},{49,33},{2,18}... | collective-permute-start | bytes 1376264 | tf_op jit(solution)/shard_map/ppermute | solution.py:426
  105.7 23.8 %collective-permute-start.45 = (bf16[2,4,32,896]{3,2,1,0:T(8,128)(2,1)S(1)}, bf16[2,4,32,896]{3,2,1,0:T(8,128)(2,1)S(1)}, u32[]{:S(2)}, u32[]{:S(2)}) collective-permute-start(bf16[2,4,32,896]{3,2,1,0:T(8,128)(2,1)S(1)} %get-tuple-element.183), channel_id=1, source_target_pairs={{0,48},{16,32},{32,16},{48,0},{1,49},{17,33},{33,17},{49,1},{2,50}... | collective-permute-start | bytes 1376264 | tf_op jit(solution)/shard_map/ppermute | solution.py:426
  130.0 14.1 %collective-permute-start.46 = (bf16[4,32,896]{2,1,0:T(8,128)(2,1)S(1)}, bf16[4,32,896]{2,1,0:T(8,128)(2,1)S(1)}, u32[]{:S(2)}, u32[]{:S(2)}) collective-permute-start(bf16[4,32,896]{2,1,0:T(8,128)(2,1)S(1)} %get-tuple-element.199), channel_id=1, source_target_pairs={{0,12},{4,8},{8,4},{12,0},{1,13},{5,9},{9,5},{13,1},{2,14},{6,10},... | collective-permute-start | bytes 688136 | tf_op jit(solution)/shard_map/ppermute | solution.py:426
  131.6 13.5 %collective-permute-start.47 = (bf16[4,32,896]{2,1,0:T(8,128)(2,1)S(1)}, bf16[4,32,896]{2,1,0:T(8,128)(2,1)S(1)}, u32[]{:S(2)}, u32[]{:S(2)}) collective-permute-start(bf16[4,32,896]{2,1,0:T(8,128)(2,1)S(1)} %get-tuple-element.200), channel_id=1, source_target_pairs={{0,4},{4,0},{8,12},{12,8},{1,5},{5,1},{9,13},{13,9},{2,6},{6,2},{1... | collective-permute-start | bytes 688136 | tf_op jit(solution)/shard_map/ppermute | solution.py:426
  134.5 12.3 %collective-permute-start.48 = (bf16[4,32,896]{2,1,0:T(8,128)(2,1)S(1)}, bf16[4,32,896]{2,1,0:T(8,128)(2,1)S(1)}, u32[]{:S(2)}, u32[]{:S(2)}) collective-permute-start(bf16[4,32,896]{2,1,0:T(8,128)(2,1)S(1)} %get-tuple-element.201), channel_id=1, source_target_pairs={{0,48},{16,32},{32,16},{48,0},{1,49},{17,33},{33,17},{49,1},{2,50}... | collective-permute-start | bytes 688136 | tf_op jit(solution)/shard_map/ppermute | solution.py:426
  136.3 10.6 %collective-permute-start.49 = (bf16[4,32,896]{2,1,0:T(8,128)(2,1)S(1)}, bf16[4,32,896]{2,1,0:T(8,128)(2,1)S(1)}, u32[]{:S(2)}, u32[]{:S(2)}) collective-permute-start(bf16[4,32,896]{2,1,0:T(8,128)(2,1)S(1)} %get-tuple-element.202), channel_id=1, source_target_pairs={{0,16},{16,0},{32,48},{48,32},{1,17},{17,1},{33,49},{49,33},{2,18}... | collective-permute-start | bytes 688136 | tf_op jit(solution)/shard_map/ppermute | solution.py:426
  153.6 39.0 %all-to-all-start.1 = ((bf16[32,48,384]{2,1,0:T(8,128)(2,1)}), bf16[32,48,384]{2,1,0:T(8,128)(2,1)S(1)}, u32[]{:S(2)}, u32[]{:S(2)}) async-start(bf16[32,48,384]{2,1,0:T(8,128)(2,1)} %shard_map.267), calls=%async_computation.1 | async-start | bytes 2359296 | tf_op jit(solution)/shard_map/all_to_all | solution.py:596
  158.0 22.7 %collective-permute-start.62 = (bf16[2,32,896]{2,1,0:T(8,128)(2,1)}, bf16[2,32,896]{2,1,0:T(8,128)(2,1)S(1)}, u32[]{:S(2)}, u32[]{:S(2)}) collective-permute-start(bf16[2,32,896]{2,1,0:T(8,128)(2,1)} %get-tuple-element.235), channel_id=1, source_target_pairs={{0,16},{16,0},{32,48},{48,32},{1,17},{17,1},{33,49},{49,33},{2,18}... | collective-permute-start | bytes 344072 | tf_op jit(solution)/shard_map/ppermute | solution.py:426
  159.9 23.6 %collective-permute-start.63 = (bf16[2,32,896]{2,1,0:T(8,128)(2,1)S(1)}, bf16[2,32,896]{2,1,0:T(8,128)(2,1)S(1)}, u32[]{:S(2)}, u32[]{:S(2)}) collective-permute-start(bf16[2,32,896]{2,1,0:T(8,128)(2,1)S(1)} %copy-done.33), channel_id=1, source_target_pairs={{0,32},{16,48},{32,0},{48,16},{1,33},{17,49},{33,1},{49,17},{2,34}... | collective-permute-start | bytes 344072 | tf_op jit(solution)/shard_map/ppermute | solution.py:426
  162.6 13.2 %collective-permute-start.54 = (bf16[32,1024]{1,0:T(8,128)(2,1)S(1)}, bf16[32,1024]{1,0:T(8,128)(2,1)S(1)}, u32[]{:S(2)}, u32[]{:S(2)}) collective-permute-start(bf16[32,1024]{1,0:T(8,128)(2,1)S(1)} %get-tuple-element.214), channel_id=1, source_target_pairs={{0,2},{2,0},{64,66},{66,64},{1,3},{3,1},{65,67},{67,65},{4,6},{6,4... | collective-permute-start | bytes 196616 | tf_op jit(solution)/shard_map/ppermute | solution.py:426
  165.2 12.0 %collective-permute-start.55 = (bf16[32,1024]{1,0:T(8,128)(2,1)S(1)}, bf16[32,1024]{1,0:T(8,128)(2,1)S(1)}, u32[]{:S(2)}, u32[]{:S(2)}) collective-permute-start(bf16[32,1024]{1,0:T(8,128)(2,1)S(1)} %get-tuple-element.215), channel_id=1, source_target_pairs={{0,64},{2,66},{64,0},{66,2},{1,65},{3,67},{65,1},{67,3},{4,68},{6,... | collective-permute-start | bytes 196616 | tf_op jit(solution)/shard_map/ppermute | solution.py:426
  166.1 11.1 %collective-permute-start.56 = (bf16[32,1024]{1,0:T(8,128)(2,1)S(1)}, bf16[32,1024]{1,0:T(8,128)(2,1)S(1)}, u32[]{:S(2)}, u32[]{:S(2)}) collective-permute-start(bf16[32,1024]{1,0:T(8,128)(2,1)S(1)} %get-tuple-element.216), channel_id=1, source_target_pairs={{0,66},{2,64},{64,2},{66,0},{1,67},{3,65},{65,3},{67,1},{4,70},{6,... | collective-permute-start | bytes 196616 | tf_op jit(solution)/shard_map/ppermute | solution.py:426
  177.4 9.5 %collective-permute-start.57 = (bf16[64,1024]{1,0:T(8,128)(2,1)S(1)}, bf16[64,1024]{1,0:T(8,128)(2,1)}, u32[]{:S(2)}, u32[]{:S(2)}) collective-permute-start(bf16[64,1024]{1,0:T(8,128)(2,1)S(1)} %shard_map.265.p0), channel_id=1, source_target_pairs={{0,1},{1,0},{2,3},{3,2},{4,5},{5,4},{6,7},{7,6},{8,9},{9,8},{10,11... | collective-permute-start | bytes 393224 | tf_op jit(solution)/shard_map/ppermute | solution.py:426
  179.3 8.5 %collective-permute-start.65 = (bf16[2,32,896]{2,1,0:T(8,128)(2,1)S(1)}, bf16[2,32,896]{2,1,0:T(8,128)(2,1)S(1)}, u32[]{:S(2)}, u32[]{:S(2)}) collective-permute-start(bf16[2,32,896]{2,1,0:T(8,128)(2,1)S(1)} %get-tuple-element.239), channel_id=1, source_target_pairs={{0,4},{4,0},{8,12},{12,8},{1,5},{5,1},{9,13},{13,9},{2,6},{6,2},{1... | collective-permute-start | bytes 344072 | tf_op jit(solution)/shard_map/ppermute | solution.py:426
  180.7 8.6 %collective-permute-start.66 = (bf16[2,32,896]{2,1,0:T(8,128)(2,1)S(1)}, bf16[2,32,896]{2,1,0:T(8,128)(2,1)S(1)}, u32[]{:S(2)}, u32[]{:S(2)}) collective-permute-start(bf16[2,32,896]{2,1,0:T(8,128)(2,1)S(1)} %get-tuple-element.240), channel_id=1, source_target_pairs={{0,8},{4,12},{8,0},{12,4},{1,9},{5,13},{9,1},{13,5},{2,10},{6,14},... | collective-permute-start | bytes 344072 | tf_op jit(solution)/shard_map/ppermute | solution.py:426
  183.6 7.8 %collective-permute-start.67 = (bf16[2,32,896]{2,1,0:T(8,128)(2,1)S(1)}, bf16[2,32,896]{2,1,0:T(8,128)(2,1)S(1)}, u32[]{:S(2)}, u32[]{:S(2)}) collective-permute-start(bf16[2,32,896]{2,1,0:T(8,128)(2,1)S(1)} %get-tuple-element.241), channel_id=1, source_target_pairs={{0,12},{4,8},{8,4},{12,0},{1,13},{5,9},{9,5},{13,1},{2,14},{6,10},... | collective-permute-start | bytes 344072 | tf_op jit(solution)/shard_map/ppermute | solution.py:426
  184.3 13.6 %collective-permute-start.58 = (bf16[64,1024]{1,0:T(8,128)(2,1)S(1)}, bf16[64,1024]{1,0:T(8,128)(2,1)S(1)}, u32[]{:S(2)}, u32[]{:S(2)}) collective-permute-start(bf16[64,1024]{1,0:T(8,128)(2,1)S(1)} %shard_map.265.p0), channel_id=1, source_target_pairs={{0,2},{2,0},{1,3},{3,1},{4,6},{6,4},{5,7},{7,5},{8,10},{10,8},{9,1... | collective-permute-start | bytes 393224 | tf_op jit(solution)/shard_map/ppermute | solution.py:426
  186.9 11.0 %collective-permute-start.59 = (bf16[64,1024]{1,0:T(8,128)(2,1)}, bf16[64,1024]{1,0:T(8,128)(2,1)}, u32[]{:S(2)}, u32[]{:S(2)}) collective-permute-start(bf16[64,1024]{1,0:T(8,128)(2,1)} %collective-permute-done.57.p1), channel_id=1, source_target_pairs={{0,2},{2,0},{1,3},{3,1},{4,6},{6,4},{5,7},{7,5},{8,10},{10,8},{9,1... | collective-permute-start | bytes 393224 | tf_op jit(solution)/shard_map/ppermute | solution.py:426
  (78 other events, 563.2 us)

commit v6 on v4

--- a/solution.py
+++ b/solution.py
@@ -19,21 +19,36 @@
 
 
 class Far:
-    def __init__(self, value, kind=None):
-        self.value, self.kind = value, kind
-
-
-def call(body, outs, *operands, room=16):
-    spec = lambda item: pl.BlockSpec() if isinstance(item, Far) else WHOLE
-    bare = lambda item: item.value if isinstance(item, Far) else item
+    def __init__(self, value):
+        self.value = value
+
+
+class Held:
+    def __init__(self, value):
+        self.value = value
+
+
+def spec(item):
+    if isinstance(item, Held):
+        return pl.BlockSpec(memory_space=pltpu.HBM)
+    return pl.BlockSpec() if isinstance(item, Far) else WHOLE
+
+
+def bare(item):
+    return item.value if isinstance(item, (Far, Held)) else item
+
+
+def call(body, outs, *operands, room=16, scalars=(), scratch=()):
+    scalar = pl.BlockSpec(memory_space=pltpu.SMEM)
     return list(
         pl.pallas_call(
             body,
             out_shape=[jax.ShapeDtypeStruct(*bare(out)) for out in outs],
-            in_specs=[spec(item) for item in operands],
+            in_specs=[scalar] * len(scalars) + [spec(item) for item in operands],
             out_specs=[spec(out) for out in outs],
+            scratch_shapes=list(scratch),
             compiler_params=pltpu.CompilerParams(vmem_limit_bytes=room * 2**20),
-        )(*[bare(item) for item in operands])
+        )(*scalars, *[bare(item) for item in operands])
     )
 
 
@@ -81,10 +96,9 @@
     return jnp.where(low, pltpu.roll(values, 96, 1), pltpu.roll(values, 32, 1))
 
 
-def project(own, other, w, attn_gain, qk_gain, cosine, sine, normed, qh, kv, qkv):
+def project(own, other, w, attn_gain, qk_gain, cosine, sine, qh, kv, qkv):
     x = jnp.concatenate([own[...], other[...]]).astype(F32)
     low = (x * row_scale(x) * attn_gain[...]).astype(BF)
-    normed[...] = low
     out = dot(low, w[:, :256])
     qkv[...] = out
     q, k = out[:, :128], out[:, 128:]
@@ -144,9 +158,14 @@
 
 
 def feed(
-    p0, p1, p2, p3, p4, p5, p6, p7, dy_own, dy_other, w,
-    send, keep, hn, act, dgu,
+    p0, p1, p2, p3, p4, p5, p6, p7, dy_own, dy_other, w_far,
+    send, keep, hn, act, dgu, w, arrived,
 ):
+    copies = []
+    for i, (at, width) in enumerate(((0, 1024), (1024, 768))):
+        part = (slice(None), slice(None), slice(None), pl.ds(at, width))
+        copies.append(pltpu.make_async_copy(w_far.at[part], w.at[part], arrived.at[i]))
+        copies[i].start()
     rows = jnp.concatenate([p[...] for p in (p0, p1, p2, p3, p4, p5, p6, p7)])
     hn[...] = rows
     dy = jnp.concatenate([dy_own[...], dy_other[...]])
@@ -155,7 +174,10 @@
         return dot(first, w[:, 0, :, at : at + width].reshape(512, width)) + dot(
             second, w[:, 1, :, at : at + width].reshape(512, width)
         )
-    gate, up, d_act = both(rows, 0, 512), both(rows, 512, 512), both(dy, 1024, 512)
+    copies[0].wait()
+    gate, up = both(rows, 0, 512), both(rows, 512, 512)
+    copies[1].wait()
+    d_act = both(dy, 1024, 512)
     active, d_gate, d_up = feed_parts(gate, up, d_act)
     act[:, :512] = active
     d_gate, d_up = d_gate.astype(BF), d_up.astype(BF)
@@ -188,20 +210,31 @@
     keep[:, 32:] = partial[:, 0]
 
 
-def feed_weights(hn, dy_own, dy_other, act, dgu, dw):
+def feed_weights(hn, dy_own, dy_other, act, dgu, out, dw, sent):
     dy = jnp.concatenate([dy_own[...], dy_other[...]])
     rows, active = hn[...], act[...]
-    for z in range(2):
-        left, left_dy = rows[:, z * 512 : (z + 1) * 512], dy[:, z * 512 : (z + 1) * 512]
-        def put(value, at, width):
+    copies = []
+    def put(left, right, at, width):
+        for z in range(2):
+            value = left_product(left[:, z * 512 : (z + 1) * 512], right)
             blocks = value.astype(BF).reshape(4, 4, 32, width)
             for y in range(4):
-                dw[:, z, y, :, at : at + width] = blocks[y]
-        put(left_product(left, dgu[:, :512]), 0, 512)
-        put(left_product(left, dgu[:, 512:1024]), 512, 512)
-        put(left_product(left_dy, active[:, :512]), 1024, 512)
-        put(left_product(left, dgu[:, 1024:]), 1536, 128)
-        put(left_product(left_dy, active[:, 512:]), 1664, 128)
+                dw[:, y, z, :, at : at + width] = blocks[y]
+    def leave(at, width):
+        part = (slice(None), slice(None), slice(None), slice(None), pl.ds(at, width))
+        copies.append(pltpu.make_async_copy(dw.at[part], out.at[part], sent.at[len(copies)]))
+        copies[-1].start()
+    put(rows, dgu[:, :512], 0, 512)
+    leave(0, 512)
+    put(rows, dgu[:, 512:1024], 512, 512)
+    leave(512, 512)
+    put(dy, active[:, :512], 1024, 512)
+    leave(1024, 512)
+    put(rows, dgu[:, 1024:], 1536, 128)
+    put(dy, active[:, 512:], 1664, 128)
+    leave(1536, 256)
+    for copy in copies:
+        copy.wait()
 
 
 def hidden_grad(own, one, two, three, h, dy, gain, dh, low, gain_part, block):
@@ -278,18 +311,14 @@
     keep[...] = partial[:, 0]
 
 
-def attend_weights(normed, d_qkv, d_attn, o, gains, dw):
-    first = left_product(normed[...], d_qkv[...]).astype(BF).reshape(8, 4, 32, 256)
-    second = left_product(d_attn[...], o[...].astype(BF)).astype(BF).reshape(8, 4, 32, 128)
-    for i in range(8):
-        dw[:, i * 32 : (i + 1) * 32, :256] = first[i]
-        dw[:, i * 32 : (i + 1) * 32, 256:] = second[i]
-    dw[:, 256:] = jnp.broadcast_to(gains[...][None], (4, 16, 384))
-
-
-def share_gains(dw, out):
-    out[:, :32] = dw[:256].reshape(8, 32, 384)
-    out[:, 32:] = jnp.broadcast_to(dw[256:][None], (8, 16, 384))
+def attend_weights(x_own, x_other, attn_gain, d_qkv, d_attn, o, gains, dw):
+    x = jnp.concatenate([x_own[...], x_other[...]]).astype(F32)
+    normed = (x * row_scale(x) * attn_gain[...]).astype(BF)
+    first = left_product(normed, d_qkv[...]).astype(BF)
+    second = left_product(d_attn[...], o[...].astype(BF)).astype(BF)
+    dw[:, :32, :256] = first.reshape(32, 32, 256)
+    dw[:, :32, 256:] = second.reshape(32, 32, 128)
+    dw[:, 32:] = jnp.broadcast_to(gains[...][None], (32, 16, 384))
 
 
 def token_rows(own, one, two, three, dh, x, gain, block, out):
@@ -311,9 +340,15 @@
     wo[...] = jnp.concatenate([low[:, 256:], high[:, 256:]], axis=1)
 
 
-def finish_feed(parts, wg, wu, wd):
-    low = jnp.sum(parts[0].astype(F32), axis=0)
-    high = jnp.sum(parts[1].astype(F32), axis=0)
+def split_feed(zl, parts, own, send):
+    own[...] = parts[pl.ds(zl[0] * 32, 32)]
+    send[...] = parts[pl.ds((1 - zl[0]) * 32, 32)]
+
+
+def finish_feed(zl, own, got, wg, wu, wd):
+    mine, its = own[...].astype(F32), got[...].astype(F32)
+    first = zl[0] == 0
+    low, high = jnp.where(first, mine, its), jnp.where(first, its, mine)
     for i, out in enumerate((wg, wu, wd)):
         wide, tail = slice(i * 512, (i + 1) * 512), slice(1536 + i * 64, 1600 + i * 64)
         out[...] = jnp.concatenate(
@@ -333,7 +368,7 @@
     key[...] = total[1:2, 256:320]
 
 
-def prepare(zl, wq, wk, wv, wo, wg, wu, wd, blocks, send_f, keep_f):
+def prepare(zl, head, wq, wk, wv, wo, wg, wu, wd, tokens, blocks, send_f, keep_f, x_own):
     for z in range(2):
         at = 0
         for w in (wq, wk, wv, wo):
@@ -351,6 +386,12 @@
     first = zl[0] == 0
     keep_f[...] = jnp.where(first, sides[0], sides[1])
     send_f[...] = jnp.where(first, sides[1], sides[0])
+    relative_rows(head, tokens, x_own)
+
+
+def relative_rows(head, rows, out):
+    for k in range(4):
+        out[k * 32 : (k + 1) * 32] = rows[0, pl.ds((head[0] ^ k) * 32, 32)]
 
 
 def order_rows(zl, own, got, out):
@@ -415,35 +456,23 @@
     zl, y, head = lax.axis_index("zl"), lax.axis_index("y"), lax.axis_index(("zh", "c"))
     attn_gain_row, ffn_gain_row = attn_gain[None], ffn_gain[None]
 
-    scalar = pl.BlockSpec(memory_space=pltpu.SMEM)
-    zl_ref = zl.reshape(1)
-    blocks, send_f, keep_f = pl.pallas_call(
+    zl_ref, head_ref = zl.reshape(1), head.reshape(1)
+    blocks, send_f, keep_f, x_own = call(
         prepare,
-        out_shape=[
-            jax.ShapeDtypeStruct(shape, BF)
-            for shape in ((2, 16, 32, 384), (32, 1792), (32, 1792))
-        ],
-        in_specs=[scalar] + [pl.BlockSpec()] * 7,
-        out_specs=[WHOLE] * 3,
-    )(zl_ref, w_query, w_key, w_value, w_out, w_gate, w_up, w_down)
+        [((2, 16, 32, 384), BF), ((32, 1792), BF), ((32, 1792), BF), ((128, 1024), BF)],
+        *[Far(w) for w in (w_query, w_key, w_value, w_out, w_gate, w_up, w_down, tokens)],
+        scalars=(zl_ref, head_ref),
+    )
     got_f = swap(send_f, "zl", 2, 1)
+    x_other = swap(x_own, "zl", 2, 1)
     w_a = lax.all_to_all(blocks.reshape(1024, 384), PLANE, 0, 0, tiled=True)
-    rows_f = pl.pallas_call(
-        order_rows,
-        out_shape=jax.ShapeDtypeStruct((2, 32, 1792), BF),
-        in_specs=[scalar] + [WHOLE] * 2,
-        out_specs=pl.BlockSpec(),
-    )(zl_ref, keep_f, got_f)
+    (rows_f,) = call(order_rows, [Far(((2, 32, 1792), BF))], keep_f, got_f, scalars=(zl_ref,))
     w_f = lax.all_gather(rows_f, ("y", "x"), axis=0)
 
-    order = head ^ jnp.arange(4)
-    (late_tokens,) = after([tokens], blocks)
-    x_own = late_tokens[0].reshape(4, 32, 1024)[order].reshape(128, 1024)
-    x_other = swap(x_own, "zl", 2, 1)
-
     (late_dy,) = after([cotangent], x_own)
-    dy_own = late_dy[0].reshape(4, 32, 1024)[order].reshape(128, 1024)
+    (dy_own,) = call(relative_rows, [((128, 1024), BF)], Far(late_dy), scalars=(head_ref,))
     dy_other = swap(dy_own, "zl", 2, 1)
+    (x_late,) = after([x_own], dy_other)
 
     (late_positions,) = after([positions], blocks)
     steps = jnp.array([dl * 16 + ky * 4 + d for ky in range(4) for dl in range(2) for d in range(4)])
@@ -460,9 +489,9 @@
     halves = [((4, 32, 1024), BF), ((4, 32, 1024), F32)]
     flat, wide_flat = ((256, 128), BF), ((256, 128), F32)
     rows_low, rows_high = ((32, 1024), BF), ((32, 1024), F32)
-    normed, qh, kv, qkv = call(
-        project, [Far(((256, 1024), BF)), flat, flat, Far(((256, 256), F32))],
-        x_own, x_other, Far(w_a), attn_gain_row, qk_gain, cosine, sine,
+    qh, kv, qkv = call(
+        project, [flat, flat, Far(((256, 256), F32))],
+        x_late, x_other, Far(w_a), attn_gain_row, qk_gain, cosine, sine,
     )
     kvs = [kv] + fan([kv] * 4, "y")
     send, keep, o, l = call(
@@ -475,13 +504,15 @@
         feed,
         [((4, 64, 1024), BF), ((4, 64, 1024), F32)]
         + [((256, 1024), BF), ((256, 640), BF), ((256, 1152), BF)],
-        *gather_rows(hn), dy_own, dy_other, Far(w_f), room=24,
+        *gather_rows(hn), dy_own, dy_other, Held(w_f), room=24,
+        scratch=[pltpu.VMEM((16, 2, 32, 1792), BF), pltpu.SemaphoreType.DMA((2,))],
     )
     pair = sum_pair(send, keep)
     act, dgu = after([act, dgu], *pair)
     d_hn = [pair[0]] + fan([None] + pair[1:], Z)
     (dw_f,) = call(
-        feed_weights, [Far(((4, 2, 4, 32, 1792), BF))], hn_all, dy_own, dy_other, act, dgu, room=24
+        feed_weights, [Held(((4, 4, 2, 32, 1792), BF))], hn_all, dy_own, dy_other, act, dgu, room=24,
+        scratch=[pltpu.VMEM((4, 4, 2, 32, 1792), BF), pltpu.SemaphoreType.DMA((4,))],
     )
     dw_f = lax.psum_scatter(dw_f.reshape(1024, 1792), "x", scatter_dimension=0, tiled=True)
     dh, d_low, ffn_part, block = call(
@@ -498,34 +529,39 @@
         Far(x_own), Far(x_other), Far(ffn_part),
     )
     (dw_a,) = call(
-        attend_weights, [Far(((4, 272, 384), BF))], Far(normed), d_qkv, Far(d_attn), Far(o), gains
-    )
-    (keep,) = after([keep], dw_a)
-    dw_a = lax.psum_scatter(dw_a.reshape(1088, 384), "x", scatter_dimension=0, tiled=True)
-    d_xn = sum_scatter(send, keep)
+        attend_weights, [((32, 48, 384), BF)],
+        Far(x_own), Far(x_other), attn_gain_row, d_qkv, Far(d_attn), Far(o), gains,
+    )
+    own, *rest = sum_pair(send, keep)
+    dw_a, dw_f = after([dw_a, dw_f], own)
+    dw_half = dw_f
+    dw_f = lax.psum_scatter(dw_f, "y", scatter_dimension=0, tiled=True)
+    dw_a = lax.all_to_all(dw_a, PLANE, 0, 0, tiled=True)
+    d_xn = after([own] + fan([None] + rest, Z), dw_half)
     (rows,) = call(
         token_rows, [((64, 1024), BF)], *d_xn, Far(dh), x_own, attn_gain_row, Far(block)
     )
     tokens_grad, block_out = gather_head(rows, head)
     tokens_grad, block_out = tokens_grad[None], block_out[None]
 
-    (dw_f,) = after([dw_f], rows)
-    dw_f = lax.all_to_all(dw_f, ("zl", "y"), 0, 0, tiled=True)
-    grad_wg, grad_wu, grad_wd = call(
-        finish_feed, [Far(((32, 1152), F32))] * 3, dw_f.reshape(2, 4, 32, 1792)
-    )
-    (dw_a,) = after([dw_a], grad_wg)
-    (dw_a,) = call(share_gains, [((8, 48, 384), BF)], dw_a)
-    dw_a = lax.all_to_all(dw_a, ("zl", "y"), 0, 0, tiled=True)
+    (dw_a,) = after([dw_a], rows)
     grad_wq, grad_wk, grad_wv, grad_wo, gains = call(
         finish_attend,
         [Far(((32, n), F32)) for n in (256, 128, 128, 256)] + [((16, 384), F32)],
-        dw_a.reshape(2, 4, 48, 384),
-    )
+        dw_a.reshape(2, 16, 48, 384),
+    )
+    (dw_f,) = after([dw_f], gains)
     (gains,) = call(add_two, [((16, 384), F32)], gains, swap(gains, "c", 2, 1))
     attn_sum, ffn_sum, query_sum, key_sum = call(
         finish_gains, [((8, 128), F32)] * 2 + [((1, 64), F32)] * 2,
         gains, swap(gains, "zh", 2, 1),
+    )
+    own_f, send_f = call(
+        split_feed, [((32, 1792), BF)] * 2, Far(dw_f), scalars=(zl_ref,)
+    )
+    grad_wg, grad_wu, grad_wd = call(
+        finish_feed, [Far(((32, 1152), F32))] * 3, own_f, swap(send_f, "zl", 2, 1),
+        scalars=(zl_ref,),
     )
     return (
         block_out, tokens_grad, attn_sum.reshape(1024), ffn_sum.reshape(1024),

time: 186 us -> 194 us (1.043)
  waiting for transfers between devices: 57.2 us -> 74.2 us
  blocking collectives: 16.9 us -> 0 us
  local copies, waits for them, and re-layouts: 14.6 us -> 19.5 us
  starting transfers between devices: 57.7 us -> 60.9 us
    all_to_all x1 -> x0, blocking collectives: 16.9 us -> none  [local(): dw_f = lax.all_to_all(dw_f, ('zl', 'y'), 0, 0, tiled=True)]
    ppermute x40 -> x41, waiting for transfers between devices: 51 us -> 63.2 us  [swap(): return lax.ppermute(value, axes, [(i, i ^ mask) for i in range(size)])]
    unnamed x64 -> x58, local copies, waits for them, and re-layouts: 10.7 us -> 17.9 us
    reduce_scatter x1, waiting for transfers between devices: 0.02 us -> 7.05 us  [local(): lax.psum_scatter(dw_f.reshape(1024, 1792), 'x', scatter_dimension=0, tile...]
    pallas_call x2 -> x0, Pallas kernels: 3.87 us -> none  [the longest x1 2.2 us: local(): pl.pallas_call(prepare, out_shape=[jax.ShapeDtypeStruct(shape, BF) for sh...]
    all_to_all x1, waiting for transfers between devices: 3.28 us -> 0.01 us  [local(): dw_a = lax.all_to_all(dw_a, PLANE, 0, 0, tiled=True)]
    pallas_call x18 -> x21, Pallas kernels: 15.8 us -> 18.5 us  [call(): pl.pallas_call(body, out_shape=[jax.ShapeDtypeStruct(*bare(out)) for out...]
    gather x2 -> x0, local copies, waits for them, and re-layouts: 2.2 us -> none  [the longest x1 1.64 us: local(): dy_own = late_dy[0].reshape(4, 32, 1024)[order].reshape(128, 1024)]
  transfers between devices with their start and end apart: 45 -> 46, of which waited for: 27 -> 25; matrix products, arithmetic and copies ran while one was open for 4% -> 2% of each run, Pallas kernels for 7% -> 6%
where the time goes in v6:
time: 194 us; the launch traced here: 192 us
  waiting for transfers between devices  74.2 us (38%)
  starting transfers between devices  60.9 us (31%)
  Pallas kernels  20.4 us (11%)
  local copies, waits for them, and re-layouts  19.5 us (10%)
  between operations  14.1 us (7%)
  other arithmetic  2.85 us (1%)
    ppermute x41, waiting for transfers between devices, swap(): return lax.ppermute(value, axes, [(i, i ^ mask) for i in range(size)])  63.2 us
    ppermute x41, starting transfers between devices, swap(): return lax.ppermute(value, axes, [(i, i ^ mask) for i in range(size)])  45.7 us
    pallas_call x21, Pallas kernels, call(): pl.pallas_call(body, out_shape=[jax.ShapeDtypeStruct(*bare(out)) for out...  18.5 us
    unnamed x58, local copies, waits for them, and re-layouts  17.9 us
    all_to_all x1, starting transfers between devices, local(): w_a = lax.all_to_all(blocks.reshape(1024, 384), PLANE, 0, 0, tiled=True)  8.51 us
    reduce_scatter x1, waiting for transfers between devices, local(): lax.psum_scatter(dw_f.reshape(1024, 1792), 'x', scatter_dimension=0, tile...  7.05 us
    all_to_all x1, starting transfers between devices, local(): dw_a = lax.all_to_all(dw_a, PLANE, 0, 0, tiled=True)  6.6 us
    reduce_scatter x1, waiting for transfers between devices, local(): dw_f = lax.psum_scatter(dw_f, 'y', scatter_dimension=0, tiled=True)  3.94 us
  transfers between devices with their start and end apart: 46, of which 25 were waited for; matrix products, arithmetic and copies ran while one was open for 2% of the time, Pallas kernels for 6%

profile of v6, /device:TPU:0, one launch (start us, length us, event | category | flops | bytes accessed | tf_op | source)
XLA Modules:
  0.0 192.0 jit_solution(8892794356202450071)
XLA Ops:
  14.8 2.0 %collective-permute-start.16 = (bf16[32,1792]{1,0:T(8,128)(2,1)S(1)}, bf16[32,1792]{1,0:T(8,128)(2,1)S(1)}, u32[]{:S(2)}, u32[]{:S(2)}) collective-permute-start(bf16[32,1792]{1,0:T(8,128)(2,1)S(1)} %get-tuple-element.101), channel_id=1, source_target_pairs={{0,64},{64,0},{1,65},{65,1},{2,66},{66,2},{3,67},{67,3},{4,68},{68... | collective-permute-start | bytes 344072 | tf_op jit(solution)/shard_map/ppermute | solution.py:403
  16.8 3.1 %collective-permute-done.16.got = bf16[32,1792]{1,0:T(8,128)(2,1)S(1)} collective-permute-done((bf16[32,1792]{1,0:T(8,128)(2,1)S(1)}, bf16[32,1792]{1,0:T(8,128)(2,1)S(1)}, u32[]{:S(2)}, u32[]{:S(2)}) %collective-permute-start.16) | collective-permute-done | bytes 114720 | tf_op jit(solution)/shard_map/ppermute | solution.py:403
  20.7 8.5 %all-to-all-start = ((bf16[32,32,384]{2,1,0:T(8,128)(2,1)}), bf16[32,32,384]{2,1,0:T(8,128)(2,1)S(1)}, u32[]{:S(2)}, u32[]{:S(2)}) async-start(bf16[32,32,384]{2,1,0:T(8,128)(2,1)} %bitcast.2), calls=%async_computation | async-start | bytes 1572864 | tf_op jit(solution)/shard_map/all_to_all | solution.py:468
  29.3 1.9 collective-permute-start.1
  36.7 13.4 %collective-permute-done.dy_other = bf16[128,1024]{1,0:T(8,128)(2,1)S(1)} collective-permute-done((bf16[128,1024]{1,0:T(8,128)(2,1)S(1)}, bf16[128,1024]{1,0:T(8,128)(2,1)S(1)}, u32[]{:S(2)}, u32[]{:S(2)}) %collective-permute-start) | collective-permute-done | bytes 262176 | tf_op jit(solution)/shard_map/ppermute | solution.py:403
  50.9 2.8 %collective-permute-start.4 = (bf16[256,128]{1,0:T(8,128)(2,1)S(1)}, bf16[256,128]{1,0:T(8,128)(2,1)S(1)}, u32[]{:S(2)}, u32[]{:S(2)}) collective-permute-start(bf16[256,128]{1,0:T(8,128)(2,1)S(1)} %get-tuple-element.92.kv0), channel_id=1, source_target_pairs={{0,48},{16,32},{32,16},{48,0},{1,49},{17,33},{33,17},{49,1},{2,50}... | collective-permute-start | bytes 196616 | tf_op jit(solution)/shard_map/ppermute | solution.py:403
  56.4 3.9 %collective-permute-done.3.kv2 = bf16[256,128]{1,0:T(8,128)(2,1)S(1)} collective-permute-done((bf16[256,128]{1,0:T(8,128)(2,1)S(1)}, bf16[256,128]{1,0:T(8,128)(2,1)S(1)}, u32[]{:S(2)}, u32[]{:S(2)}) %collective-permute-start.3) | collective-permute-done | bytes 65568 | tf_op jit(solution)/shard_map/ppermute | solution.py:403
  63.4 4.0 %collective-permute-start.6 = (bf16[32,1024]{1,0:T(8,128)(2,1)S(1)}, bf16[32,1024]{1,0:T(8,128)(2,1)S(1)}, u32[]{:S(2)}, u32[]{:S(2)}) collective-permute-start(bf16[32,1024]{1,0:T(8,128)(2,1)S(1)} %get-tuple-element.96), channel_id=1, source_target_pairs={{0,2},{2,0},{64,66},{66,64},{1,3},{3,1},{65,67},{67,65},{4,6},{6,4... | collective-permute-start | bytes 196616 | tf_op jit(solution)/shard_map/ppermute | solution.py:403
  68.0 2.2 %collective-permute-done.6.one = bf16[32,1024]{1,0:T(8,128)(2,1)S(1)} collective-permute-done((bf16[32,1024]{1,0:T(8,128)(2,1)S(1)}, bf16[32,1024]{1,0:T(8,128)(2,1)S(1)}, u32[]{:S(2)}, u32[]{:S(2)}) %collective-permute-start.6) | collective-permute-done | bytes 65568 | tf_op jit(solution)/shard_map/ppermute | solution.py:403
  74.6 3.4 %collective-permute-start.10 = (bf16[32,1024]{1,0:T(8,128)(2,1)S(1)}, bf16[32,1024]{1,0:T(8,128)(2,1)S(1)}, u32[]{:S(2)}, u32[]{:S(2)}) collective-permute-start(bf16[32,1024]{1,0:T(8,128)(2,1)S(1)} %get-tuple-element.99.p0), channel_id=1, source_target_pairs={{0,2},{2,0},{64,66},{66,64},{1,3},{3,1},{65,67},{67,65},{4,6},{6,4... | collective-permute-start | bytes 196616 | tf_op jit(solution)/shard_map/ppermute | solution.py:403
  82.8 2.0 %copy-done.1 = bf16[32,32,1792]{2,1,0:T(8,128)(2,1)S(1)} copy-done((bf16[32,32,1792]{2,1,0:T(8,128)(2,1)S(1)}, bf16[32,32,1792]{2,1,0:T(8,128)(2,1)}, u32[]{:S(2)}) %copy-start.1) | copy-done | bytes 3670040
  87.4 3.0 %shard_map.253 = (bf16[4,64,1024]{2,1,0:T(8,128)(2,1)S(1)}, f32[4,64,1024]{2,1,0:T(8,128)S(1)}, bf16[256,1024]{1,0:T(8,128)(2,1)S(1)}, bf16[256,640]{1,0:T(8,128)(2,1)S(1)}, bf16[256,1152]{1,0:T(8,128)(2,1)S(1)}) custom-call(bf16[32,1024]{1,0:T(8,128)(2,1)S(1)} %get-tuple-element.99.p0, bf16[32,1024]{1,0:T(8,128)(2,1)S(1)} %collective-permute-done.9.p1, ...), custom_call_target="tpu_custom_call" | custom-call | tf_op jit(solution)/shard_map/pallas_call | solution.py:44
  93.4 2.1 %shard_map.260 = bf16[4,4,2,32,1792]{4,3,2,1,0:T(8,128)(2,1)S(1)} custom-call(bf16[256,1024]{1,0:T(8,128)(2,1)S(1)} %get-tuple-element.128.hn, bf16[128,1024]{1,0:T(8,128)(2,1)S(1)} %shard_map.247.dy_own.dy, bf16[128,1024]{1,0:T(8,128)(2,1)S(1)} %collective-permute-done.dy_other, bf16[256,640]{1,0:T(8,128)(2,1)S(1)} %get-tuple-element.131.act, ...), custom_call_target="tpu_custom_call" | custom-call | tf_op jit(solution)/shard_map/pallas_call | solution.py:44
  95.5 1.8 copy-done
  97.4 2.9 %collective-permute-start.18 = (bf16[64,1024]{1,0:T(8,128)(2,1)}, bf16[64,1024]{1,0:T(8,128)(2,1)S(1)}, u32[]{:S(2)}, u32[]{:S(2)}) collective-permute-start(bf16[64,1024]{1,0:T(8,128)(2,1)} %get-tuple-element.105), channel_id=1, source_target_pairs={{0,2},{2,0},{64,66},{66,64},{1,3},{3,1},{65,67},{67,65},{4,6},{6,4... | collective-permute-start | bytes 393224 | tf_op jit(solution)/shard_map/ppermute | solution.py:403
  101.6 3.9 %collective-permute-done.18.one = bf16[64,1024]{1,0:T(8,128)(2,1)S(1)} collective-permute-done((bf16[64,1024]{1,0:T(8,128)(2,1)}, bf16[64,1024]{1,0:T(8,128)(2,1)S(1)}, u32[]{:S(2)}, u32[]{:S(2)}) %collective-permute-start.18) | collective-permute-done | bytes 131104 | tf_op jit(solution)/shard_map/ppermute | solution.py:403
  110.9 1.9 collective-permute-start.22
  114.2 2.5 %collective-permute-done.22.p2 = bf16[32,1024]{1,0:T(8,128)(2,1)S(1)} collective-permute-done((bf16[32,1024]{1,0:T(8,128)(2,1)S(1)}, bf16[32,1024]{1,0:T(8,128)(2,1)S(1)}, u32[]{:S(2)}, u32[]{:S(2)}) %collective-permute-start.22) | collective-permute-done | bytes 65568 | tf_op jit(solution)/shard_map/ppermute | solution.py:403
  117.9 3.1 %shard_map.256 = (bf16[256,1024]{1,0:T(8,128)(2,1)S(1)}, f32[256,128]{1,0:T(8,128)S(1)}, f32[256,128]{1,0:T(8,128)S(1)}, bf16[256,128]{1,0:T(8,128)(2,1)S(1)}, b...) custom-call(bf16[32,1024]{1,0:T(8,128)(2,1)S(1)} %get-tuple-element.109.p0, ...), custom_call_target="tpu_custom_call" | custom-call | tf_op jit(solution)/shard_map/pallas_call | solution.py:44
  122.7 2.4 %collective-permute-start.29 = (bf16[256,128]{1,0:T(8,128)(2,1)S(1)}, bf16[256,128]{1,0:T(8,128)(2,1)S(1)}, u32[]{:S(2)}, u32[]{:S(2)}) collective-permute-start(bf16[256,128]{1,0:T(8,128)(2,1)S(1)} %get-tuple-element.115), channel_id=1, source_target_pairs={{0,32},{16,48},{32,0},{48,16},{1,33},{17,49},{33,1},{49,17},{2,34}... | collective-permute-start | bytes 196616 | tf_op jit(solution)/shard_map/ppermute | solution.py:403
  125.8 2.9 %collective-permute-done.29.two = bf16[256,128]{1,0:T(8,128)(2,1)S(1)} collective-permute-done((bf16[256,128]{1,0:T(8,128)(2,1)S(1)}, bf16[256,128]{1,0:T(8,128)(2,1)S(1)}, u32[]{:S(2)}, u32[]{:S(2)}) %collective-permute-start.29) | collective-permute-done | bytes 65568 | tf_op jit(solution)/shard_map/ppermute | solution.py:403
  128.7 1.8 collective-permute-done.30.three
  131.7 1.7 shard_map.259
  133.4 7.1 %reduce-scatter.3.cloned.1.call-done = bf16[256,1792]{1,0:T(8,128)(2,1)} async-done(((bf16[1024,1792]{1,0:T(8,128)(2,1)}), bf16[256,1792]{1,0:T(8,128)(2,1)}) %reduce-scatter.3.cloned.1.call-update) | async-done | bytes 917520 | tf_op jit(solution)/shard_map/reduce_scatter | solution.py:517
  140.5 6.6 %all-to-all-start.1 = ((bf16[32,48,384]{2,1,0:T(8,128)(2,1)}), bf16[32,48,384]{2,1,0:T(8,128)(2,1)S(1)}, u32[]{:S(2)}, u32[]{:S(2)}) async-start(bf16[32,48,384]{2,1,0:T(8,128)(2,1)} %shard_map.259), calls=%async_computation.2 | async-start | bytes 2359296 | tf_op jit(solution)/shard_map/all_to_all | solution.py:539
  147.1 2.9 %collective-permute-start.32 = (bf16[32,1024]{1,0:T(8,128)(2,1)S(1)}, bf16[32,1024]{1,0:T(8,128)(2,1)S(1)}, u32[]{:S(2)}, u32[]{:S(2)}) collective-permute-start(bf16[32,1024]{1,0:T(8,128)(2,1)S(1)} %get-tuple-element.122), channel_id=1, source_target_pairs={{0,2},{2,0},{64,66},{66,64},{1,3},{3,1},{65,67},{67,65},{4,6},{6,4... | collective-permute-start | bytes 196616 | tf_op jit(solution)/shard_map/ppermute | solution.py:403
  151.7 11.3 %collective-permute-done.32.one = bf16[32,1024]{1,0:T(8,128)(2,1)S(1)} collective-permute-done((bf16[32,1024]{1,0:T(8,128)(2,1)S(1)}, bf16[32,1024]{1,0:T(8,128)(2,1)S(1)}, u32[]{:S(2)}, u32[]{:S(2)}) %collective-permute-start.32) | collective-permute-done | bytes 65568 | tf_op jit(solution)/shard_map/ppermute | solution.py:403
  163.0 2.5 %collective-permute-done.33.two = bf16[32,1024]{1,0:T(8,128)(2,1)S(1)} collective-permute-done((bf16[32,1024]{1,0:T(8,128)(2,1)S(1)}, bf16[32,1024]{1,0:T(8,128)(2,1)S(1)}, u32[]{:S(2)}, u32[]{:S(2)}) %collective-permute-start.33) | collective-permute-done | bytes 65568 | tf_op jit(solution)/shard_map/ppermute | solution.py:403
  165.8 2.1 %collective-permute-start.36 = (bf16[64,1024]{1,0:T(8,128)(2,1)S(1)}, bf16[64,1024]{1,0:T(8,128)(2,1)S(1)}, u32[]{:S(2)}, u32[]{:S(2)}) collective-permute-start(bf16[64,1024]{1,0:T(8,128)(2,1)S(1)} %shard_map.261.p0), channel_id=1, source_target_pairs={{0,2},{2,0},{1,3},{3,1},{4,6},{6,4},{5,7},{7,5},{8,10},{10,8},{9,1... | collective-permute-start | bytes 393224 | tf_op jit(solution)/shard_map/ppermute | solution.py:403
  170.2 3.9 %reduce-scatter.5.cloned.1.call-done.parts = bf16[64,1792]{1,0:T(8,128)(2,1)} async-done(((bf16[256,1792]{1,0:T(8,128)(2,1)}), bf16[64,1792]{1,0:T(8,128)(2,1)}) %reduce-scatter.5.cloned.1.call-update) | async-done | bytes 229392 | tf_op jit(solution)/shard_map/reduce_scatter | solution.py:538
  178.0 2.8 %collective-permute-start.39 = (f32[16,384]{1,0:T(8,128)S(1)}, f32[16,384]{1,0:T(8,128)S(1)}, u32[]{:S(2)}, u32[]{:S(2)}) collective-permute-start(f32[16,384]{1,0:T(8,128)S(1)} %shard_map.264.one), channel_id=1, source_target_pairs={{0,2},{2,0},{1,3},{3,1},{4,6},{6,4},{5,7},{7,5},{8,10},{10,8},{9,1... | collective-permute-start | bytes 73736 | tf_op jit(solution)/shard_map/ppermute | solution.py:403
  182.1 1.9 shard_map.262
  (161 shorter events, 59.3 us)
Async XLA Ops:
  7.2 75.6 %all-gather.3.cloned.1.call-start = ((), (), s32[]{:S(2)}) async-start(), calls=%async_computation.6 | async-start | bytes 3899392 | tf_op jit(solution)/shard_map/all_gather | solution.py:470
  14.8 5.1 %collective-permute-start.16 = (bf16[32,1792]{1,0:T(8,128)(2,1)S(1)}, bf16[32,1792]{1,0:T(8,128)(2,1)S(1)}, u32[]{:S(2)}, u32[]{:S(2)}) collective-permute-start(bf16[32,1792]{1,0:T(8,128)(2,1)S(1)} %get-tuple-element.101), channel_id=1, source_target_pairs={{0,64},{64,0},{1,65},{65,1},{2,66},{66,2},{3,67},{67,3},{4,68},{68... | collective-permute-start | bytes 344072 | tf_op jit(solution)/shard_map/ppermute | solution.py:403
  20.7 29.5 %all-to-all-start = ((bf16[32,32,384]{2,1,0:T(8,128)(2,1)}), bf16[32,32,384]{2,1,0:T(8,128)(2,1)S(1)}, u32[]{:S(2)}, u32[]{:S(2)}) async-start(bf16[32,32,384]{2,1,0:T(8,128)(2,1)} %bitcast.2), calls=%async_computation | async-start | bytes 1572864 | tf_op jit(solution)/shard_map/all_to_all | solution.py:468
  29.2 111.3 %reduce-scatter.3.cloned.1.call-start = ((), (), s32[]{:S(2)}) async-start(), calls=%async_computation.4 | async-start | bytes 4587520 | tf_op jit(solution)/shard_map/reduce_scatter | solution.py:517
  29.3 20.9 %collective-permute-start.1 = (bf16[128,1024]{1,0:T(8,128)(2,1)S(1)}, bf16[128,1024]{1,0:T(8,128)(2,1)S(1)}, u32[]{:S(2)}, u32[]{:S(2)}) collective-permute-start(bf16[128,1024]{1,0:T(8,128)(2,1)S(1)} %get-tuple-element.88.own.x.x_own), channel_id=1, source_target_pairs={{0,64},{64,0},{1,65},{65,1},{2,66},{66,2},{3,67},{67,3},{4,68},{68... | collective-permute-start | bytes 786440 | tf_op jit(solution)/shard_map/ppermute | solution.py:403
  32.1 18.0 %collective-permute-start = (bf16[128,1024]{1,0:T(8,128)(2,1)S(1)}, bf16[128,1024]{1,0:T(8,128)(2,1)S(1)}, u32[]{:S(2)}, u32[]{:S(2)}) collective-permute-start(bf16[128,1024]{1,0:T(8,128)(2,1)S(1)} %shard_map.247.dy_own.dy), channel_id=1, source_target_pairs={{0,64},{64,0},{1,65},{65,1},{2,66},{66,2},{3,67},{67,3},{4,68},{68... | collective-permute-start | bytes 786440 | tf_op jit(solution)/shard_map/ppermute | solution.py:403
  50.9 5.6 %collective-permute-start.4 = (bf16[256,128]{1,0:T(8,128)(2,1)S(1)}, bf16[256,128]{1,0:T(8,128)(2,1)S(1)}, u32[]{:S(2)}, u32[]{:S(2)}) collective-permute-start(bf16[256,128]{1,0:T(8,128)(2,1)S(1)} %get-tuple-element.92.kv0), channel_id=1, source_target_pairs={{0,48},{16,32},{32,16},{48,0},{1,49},{17,33},{33,17},{49,1},{2,50}... | collective-permute-start | bytes 196616 | tf_op jit(solution)/shard_map/ppermute | solution.py:403
  53.7 6.6 %collective-permute-start.3 = (bf16[256,128]{1,0:T(8,128)(2,1)S(1)}, bf16[256,128]{1,0:T(8,128)(2,1)S(1)}, u32[]{:S(2)}, u32[]{:S(2)}) collective-permute-start(bf16[256,128]{1,0:T(8,128)(2,1)S(1)} %get-tuple-element.92.kv0), channel_id=1, source_target_pairs={{0,32},{16,48},{32,0},{48,16},{1,33},{17,49},{33,1},{49,17},{2,34}... | collective-permute-start | bytes 196616 | tf_op jit(solution)/shard_map/ppermute | solution.py:403
  54.5 5.8 %collective-permute-start.2 = (bf16[256,128]{1,0:T(8,128)(2,1)S(1)}, bf16[256,128]{1,0:T(8,128)(2,1)S(1)}, u32[]{:S(2)}, u32[]{:S(2)}) collective-permute-start(bf16[256,128]{1,0:T(8,128)(2,1)S(1)} %get-tuple-element.92.kv0), channel_id=1, source_target_pairs={{0,16},{16,0},{32,48},{48,32},{1,17},{17,1},{33,49},{49,33},{2,18}... | collective-permute-start | bytes 196616 | tf_op jit(solution)/shard_map/ppermute | solution.py:403
  63.4 6.9 %collective-permute-start.6 = (bf16[32,1024]{1,0:T(8,128)(2,1)S(1)}, bf16[32,1024]{1,0:T(8,128)(2,1)S(1)}, u32[]{:S(2)}, u32[]{:S(2)}) collective-permute-start(bf16[32,1024]{1,0:T(8,128)(2,1)S(1)} %get-tuple-element.96), channel_id=1, source_target_pairs={{0,2},{2,0},{64,66},{66,64},{1,3},{3,1},{65,67},{67,65},{4,6},{6,4... | collective-permute-start | bytes 196616 | tf_op jit(solution)/shard_map/ppermute | solution.py:403
  67.5 5.5 %collective-permute-start.8 = (bf16[32,1024]{1,0:T(8,128)(2,1)S(1)}, bf16[32,1024]{1,0:T(8,128)(2,1)S(1)}, u32[]{:S(2)}, u32[]{:S(2)}) collective-permute-start(bf16[32,1024]{1,0:T(8,128)(2,1)S(1)} %get-tuple-element.98), channel_id=1, source_target_pairs={{0,66},{2,64},{64,2},{66,0},{1,67},{3,65},{65,3},{67,1},{4,70},{6,... | collective-permute-start | bytes 196616 | tf_op jit(solution)/shard_map/ppermute | solution.py:403
  73.2 6.2 %collective-permute-start.14 = (bf16[32,1024]{1,0:T(8,128)(2,1)S(1)}, bf16[32,1024]{1,0:T(8,128)(2,1)S(1)}, u32[]{:S(2)}, u32[]{:S(2)}) collective-permute-start(bf16[32,1024]{1,0:T(8,128)(2,1)S(1)} %get-tuple-element.99.p0), channel_id=1, source_target_pairs={{0,66},{2,64},{64,2},{66,0},{1,67},{3,65},{65,3},{67,1},{4,70},{6,... | collective-permute-start | bytes 196616 | tf_op jit(solution)/shard_map/ppermute | solution.py:403
  74.0 5.3 %collective-permute-start.12 = (bf16[32,1024]{1,0:T(8,128)(2,1)S(1)}, bf16[32,1024]{1,0:T(8,128)(2,1)S(1)}, u32[]{:S(2)}, u32[]{:S(2)}) collective-permute-start(bf16[32,1024]{1,0:T(8,128)(2,1)S(1)} %get-tuple-element.99.p0), channel_id=1, source_target_pairs={{0,64},{2,66},{64,0},{66,2},{1,65},{3,67},{65,1},{67,3},{4,68},{6,... | collective-permute-start | bytes 196616 | tf_op jit(solution)/shard_map/ppermute | solution.py:403
  74.6 6.3 %collective-permute-start.10 = (bf16[32,1024]{1,0:T(8,128)(2,1)S(1)}, bf16[32,1024]{1,0:T(8,128)(2,1)S(1)}, u32[]{:S(2)}, u32[]{:S(2)}) collective-permute-start(bf16[32,1024]{1,0:T(8,128)(2,1)S(1)} %get-tuple-element.99.p0), channel_id=1, source_target_pairs={{0,2},{2,0},{64,66},{66,64},{1,3},{3,1},{65,67},{67,65},{4,6},{6,4... | collective-permute-start | bytes 196616 | tf_op jit(solution)/shard_map/ppermute | solution.py:403
  97.4 76.8 %reduce-scatter.5.cloned.1.call-start = ((), (), s32[]{:S(2)}) async-start(), calls=%async_computation.5 | async-start | bytes 1146880 | tf_op jit(solution)/shard_map/reduce_scatter | solution.py:538
  97.4 8.1 %collective-permute-start.18 = (bf16[64,1024]{1,0:T(8,128)(2,1)}, bf16[64,1024]{1,0:T(8,128)(2,1)S(1)}, u32[]{:S(2)}, u32[]{:S(2)}) collective-permute-start(bf16[64,1024]{1,0:T(8,128)(2,1)} %get-tuple-element.105), channel_id=1, source_target_pairs={{0,2},{2,0},{64,66},{66,64},{1,3},{3,1},{65,67},{67,65},{4,6},{6,4... | collective-permute-start | bytes 393224 | tf_op jit(solution)/shard_map/ppermute | solution.py:403
  100.4 6.5 %collective-permute-start.19 = (bf16[64,1024]{1,0:T(8,128)(2,1)}, bf16[64,1024]{1,0:T(8,128)(2,1)S(1)}, u32[]{:S(2)}, u32[]{:S(2)}) collective-permute-start(bf16[64,1024]{1,0:T(8,128)(2,1)} %copy-done.23), channel_id=1, source_target_pairs={{0,64},{2,66},{64,0},{66,2},{1,65},{3,67},{65,1},{67,3},{4,68},{6,... | collective-permute-start | bytes 393224 | tf_op jit(solution)/shard_map/ppermute | solution.py:403
  100.4 7.5 %collective-permute-start.20 = (bf16[64,1024]{1,0:T(8,128)(2,1)S(1)}, bf16[64,1024]{1,0:T(8,128)(2,1)S(1)}, u32[]{:S(2)}, u32[]{:S(2)}) collective-permute-start(bf16[64,1024]{1,0:T(8,128)(2,1)S(1)} %get-tuple-element.107), channel_id=1, source_target_pairs={{0,66},{2,64},{64,2},{66,0},{1,67},{3,65},{65,3},{67,1},{4,70},{6,... | collective-permute-start | bytes 393224 | tf_op jit(solution)/shard_map/ppermute | solution.py:403
  108.0 5.6 %collective-permute-start.26 = (bf16[32,1024]{1,0:T(8,128)(2,1)S(1)}, bf16[32,1024]{1,0:T(8,128)(2,1)S(1)}, u32[]{:S(2)}, u32[]{:S(2)}) collective-permute-start(bf16[32,1024]{1,0:T(8,128)(2,1)S(1)} %get-tuple-element.109.p0), channel_id=1, source_target_pairs={{0,66},{2,64},{64,2},{66,0},{1,67},{3,65},{65,3},{67,1},{4,70},{6,... | collective-permute-start | bytes 196616 | tf_op jit(solution)/shard_map/ppermute | solution.py:403
  109.5 4.7 %collective-permute-start.24 = (bf16[32,1024]{1,0:T(8,128)(2,1)S(1)}, bf16[32,1024]{1,0:T(8,128)(2,1)S(1)}, u32[]{:S(2)}, u32[]{:S(2)}) collective-permute-start(bf16[32,1024]{1,0:T(8,128)(2,1)S(1)} %get-tuple-element.109.p0), channel_id=1, source_target_pairs={{0,64},{2,66},{64,0},{66,2},{1,65},{3,67},{65,1},{67,3},{4,68},{6,... | collective-permute-start | bytes 196616 | tf_op jit(solution)/shard_map/ppermute | solution.py:403
  110.9 5.8 %collective-permute-start.22 = (bf16[32,1024]{1,0:T(8,128)(2,1)S(1)}, bf16[32,1024]{1,0:T(8,128)(2,1)S(1)}, u32[]{:S(2)}, u32[]{:S(2)}) collective-permute-start(bf16[32,1024]{1,0:T(8,128)(2,1)S(1)} %get-tuple-element.109.p0), channel_id=1, source_target_pairs={{0,2},{2,0},{64,66},{66,64},{1,3},{3,1},{65,67},{67,65},{4,6},{6,4... | collective-permute-start | bytes 196616 | tf_op jit(solution)/shard_map/ppermute | solution.py:403
  121.0 4.8 %collective-permute-start.28 = (bf16[256,128]{1,0:T(8,128)(2,1)S(1)}, bf16[256,128]{1,0:T(8,128)(2,1)S(1)}, u32[]{:S(2)}, u32[]{:S(2)}) collective-permute-start(bf16[256,128]{1,0:T(8,128)(2,1)S(1)} %get-tuple-element.114), channel_id=1, source_target_pairs={{0,16},{16,0},{32,48},{48,32},{1,17},{17,1},{33,49},{49,33},{2,18}... | collective-permute-start | bytes 196616 | tf_op jit(solution)/shard_map/ppermute | solution.py:403
  122.7 6.0 %collective-permute-start.29 = (bf16[256,128]{1,0:T(8,128)(2,1)S(1)}, bf16[256,128]{1,0:T(8,128)(2,1)S(1)}, u32[]{:S(2)}, u32[]{:S(2)}) collective-permute-start(bf16[256,128]{1,0:T(8,128)(2,1)S(1)} %get-tuple-element.115), channel_id=1, source_target_pairs={{0,32},{16,48},{32,0},{48,16},{1,33},{17,49},{33,1},{49,17},{2,34}... | collective-permute-start | bytes 196616 | tf_op jit(solution)/shard_map/ppermute | solution.py:403
  125.1 5.5 %collective-permute-start.30 = (bf16[256,128]{1,0:T(8,128)(2,1)S(1)}, bf16[256,128]{1,0:T(8,128)(2,1)S(1)}, u32[]{:S(2)}, u32[]{:S(2)}) collective-permute-start(bf16[256,128]{1,0:T(8,128)(2,1)S(1)} %get-tuple-element.116), channel_id=1, source_target_pairs={{0,48},{16,32},{32,16},{48,0},{1,49},{17,33},{33,17},{49,1},{2,50}... | collective-permute-start | bytes 196616 | tf_op jit(solution)/shard_map/ppermute | solution.py:403
  140.5 29.0 %all-to-all-start.1 = ((bf16[32,48,384]{2,1,0:T(8,128)(2,1)}), bf16[32,48,384]{2,1,0:T(8,128)(2,1)S(1)}, u32[]{:S(2)}, u32[]{:S(2)}) async-start(bf16[32,48,384]{2,1,0:T(8,128)(2,1)} %shard_map.259), calls=%async_computation.2 | async-start | bytes 2359296 | tf_op jit(solution)/shard_map/all_to_all | solution.py:539
  147.1 15.9 %collective-permute-start.32 = (bf16[32,1024]{1,0:T(8,128)(2,1)S(1)}, bf16[32,1024]{1,0:T(8,128)(2,1)S(1)}, u32[]{:S(2)}, u32[]{:S(2)}) collective-permute-start(bf16[32,1024]{1,0:T(8,128)(2,1)S(1)} %get-tuple-element.122), channel_id=1, source_target_pairs={{0,2},{2,0},{64,66},{66,64},{1,3},{3,1},{65,67},{67,65},{4,6},{6,4... | collective-permute-start | bytes 196616 | tf_op jit(solution)/shard_map/ppermute | solution.py:403
  150.0 15.5 %collective-permute-start.33 = (bf16[32,1024]{1,0:T(8,128)(2,1)S(1)}, bf16[32,1024]{1,0:T(8,128)(2,1)S(1)}, u32[]{:S(2)}, u32[]{:S(2)}) collective-permute-start(bf16[32,1024]{1,0:T(8,128)(2,1)S(1)} %get-tuple-element.123), channel_id=1, source_target_pairs={{0,64},{2,66},{64,0},{66,2},{1,65},{3,67},{65,1},{67,3},{4,68},{6,... | collective-permute-start | bytes 196616 | tf_op jit(solution)/shard_map/ppermute | solution.py:403
  151.2 14.3 %collective-permute-start.34 = (bf16[32,1024]{1,0:T(8,128)(2,1)S(1)}, bf16[32,1024]{1,0:T(8,128)(2,1)S(1)}, u32[]{:S(2)}, u32[]{:S(2)}) collective-permute-start(bf16[32,1024]{1,0:T(8,128)(2,1)S(1)} %get-tuple-element.124), channel_id=1, source_target_pairs={{0,66},{2,64},{64,2},{66,0},{1,67},{3,65},{65,3},{67,1},{4,70},{6,... | collective-permute-start | bytes 196616 | tf_op jit(solution)/shard_map/ppermute | solution.py:403
  165.8 14.9 %collective-permute-start.36 = (bf16[64,1024]{1,0:T(8,128)(2,1)S(1)}, bf16[64,1024]{1,0:T(8,128)(2,1)S(1)}, u32[]{:S(2)}, u32[]{:S(2)}) collective-permute-start(bf16[64,1024]{1,0:T(8,128)(2,1)S(1)} %shard_map.261.p0), channel_id=1, source_target_pairs={{0,2},{2,0},{1,3},{3,1},{4,6},{6,4},{5,7},{7,5},{8,10},{10,8},{9,1... | collective-permute-start | bytes 393224 | tf_op jit(solution)/shard_map/ppermute | solution.py:403
  167.9 12.9 %collective-permute-start.37 = (bf16[64,1024]{1,0:T(8,128)(2,1)S(1)}, bf16[64,1024]{1,0:T(8,128)(2,1)S(1)}, u32[]{:S(2)}, u32[]{:S(2)}) collective-permute-start(bf16[64,1024]{1,0:T(8,128)(2,1)S(1)} %collective-permute-done.35.p1), channel_id=1, source_target_pairs={{0,2},{2,0},{1,3},{3,1},{4,6},{6,4},{5,7},{7,5},{8,10},{10,8},{9,1... | collective-permute-start | bytes 393224 | tf_op jit(solution)/shard_map/ppermute | solution.py:403
  175.1 9.5 %collective-permute-start.40 = (bf16[32,1792]{1,0:T(8,128)(2,1)S(1)}, bf16[32,1792]{1,0:T(8,128)(2,1)S(1)}, u32[]{:S(2)}, u32[]{:S(2)}) collective-permute-start(bf16[32,1792]{1,0:T(8,128)(2,1)S(1)} %get-tuple-element.155), channel_id=1, source_target_pairs={{0,64},{64,0},{1,65},{65,1},{2,66},{66,2},{3,67},{67,3},{4,68},{68... | collective-permute-start | bytes 344072 | tf_op jit(solution)/shard_map/ppermute | solution.py:403
  178.0 6.0 %collective-permute-start.39 = (f32[16,384]{1,0:T(8,128)S(1)}, f32[16,384]{1,0:T(8,128)S(1)}, u32[]{:S(2)}, u32[]{:S(2)}) collective-permute-start(f32[16,384]{1,0:T(8,128)S(1)} %shard_map.264.one), channel_id=1, source_target_pairs={{0,2},{2,0},{1,3},{3,1},{4,6},{6,4},{5,7},{7,5},{8,10},{10,8},{9,1... | collective-permute-start | bytes 73736 | tf_op jit(solution)/shard_map/ppermute | solution.py:403
  (43 other events, 263.5 us)
Sparse Core Ops, SparseCore 0:
  20.8 54.1 all-gather.2
  97.5 42.9 reduce-scatter.2
  142.9 31.2 reduce-scatter.4

commit v7 on v6

--- a/solution.py
+++ b/solution.py
@@ -23,22 +23,15 @@
         self.value = value
 
 
-class Held:
-    def __init__(self, value):
-        self.value = value
-
-
 def spec(item):
-    if isinstance(item, Held):
-        return pl.BlockSpec(memory_space=pltpu.HBM)
     return pl.BlockSpec() if isinstance(item, Far) else WHOLE
 
 
 def bare(item):
-    return item.value if isinstance(item, (Far, Held)) else item
-
-
-def call(body, outs, *operands, room=16, scalars=(), scratch=()):
+    return item.value if isinstance(item, Far) else item
+
+
+def call(body, outs, *operands, room=8, scalars=(), scratch=()):
     scalar = pl.BlockSpec(memory_space=pltpu.SMEM)
     return list(
         pl.pallas_call(
@@ -47,7 +40,7 @@
             in_specs=[scalar] * len(scalars) + [spec(item) for item in operands],
             out_specs=[spec(out) for out in outs],
             scratch_shapes=list(scratch),
-            compiler_params=pltpu.CompilerParams(vmem_limit_bytes=room * 2**20),
+            compiler_params=pltpu.CompilerParams(vmem_limit_bytes=room * 2**20 if room else None),
         )(*scalars, *[bare(item) for item in operands])
     )
 
@@ -158,14 +151,9 @@
 
 
 def feed(
-    p0, p1, p2, p3, p4, p5, p6, p7, dy_own, dy_other, w_far,
-    send, keep, hn, act, dgu, w, arrived,
+    p0, p1, p2, p3, p4, p5, p6, p7, dy_own, dy_other, w,
+    send, keep, hn, act, dgu,
 ):
-    copies = []
-    for i, (at, width) in enumerate(((0, 1024), (1024, 768))):
-        part = (slice(None), slice(None), slice(None), pl.ds(at, width))
-        copies.append(pltpu.make_async_copy(w_far.at[part], w.at[part], arrived.at[i]))
-        copies[i].start()
     rows = jnp.concatenate([p[...] for p in (p0, p1, p2, p3, p4, p5, p6, p7)])
     hn[...] = rows
     dy = jnp.concatenate([dy_own[...], dy_other[...]])
@@ -174,10 +162,7 @@
         return dot(first, w[:, 0, :, at : at + width].reshape(512, width)) + dot(
             second, w[:, 1, :, at : at + width].reshape(512, width)
         )
-    copies[0].wait()
-    gate, up = both(rows, 0, 512), both(rows, 512, 512)
-    copies[1].wait()
-    d_act = both(dy, 1024, 512)
+    gate, up, d_act = both(rows, 0, 512), both(rows, 512, 512), both(dy, 1024, 512)
     active, d_gate, d_up = feed_parts(gate, up, d_act)
     act[:, :512] = active
     d_gate, d_up = d_gate.astype(BF), d_up.astype(BF)
@@ -210,31 +195,20 @@
     keep[:, 32:] = partial[:, 0]
 
 
-def feed_weights(hn, dy_own, dy_other, act, dgu, out, dw, sent):
+def feed_weights(hn, dy_own, dy_other, act, dgu, dw):
     dy = jnp.concatenate([dy_own[...], dy_other[...]])
     rows, active = hn[...], act[...]
-    copies = []
     def put(left, right, at, width):
         for z in range(2):
             value = left_product(left[:, z * 512 : (z + 1) * 512], right)
             blocks = value.astype(BF).reshape(4, 4, 32, width)
             for y in range(4):
-                dw[:, y, z, :, at : at + width] = blocks[y]
-    def leave(at, width):
-        part = (slice(None), slice(None), slice(None), slice(None), pl.ds(at, width))
-        copies.append(pltpu.make_async_copy(dw.at[part], out.at[part], sent.at[len(copies)]))
-        copies[-1].start()
+                dw[:, z, y, :, at : at + width] = blocks[y]
     put(rows, dgu[:, :512], 0, 512)
-    leave(0, 512)
     put(rows, dgu[:, 512:1024], 512, 512)
-    leave(512, 512)
     put(dy, active[:, :512], 1024, 512)
-    leave(1024, 512)
     put(rows, dgu[:, 1024:], 1536, 128)
     put(dy, active[:, 512:], 1664, 128)
-    leave(1536, 256)
-    for copy in copies:
-        copy.wait()
 
 
 def hidden_grad(own, one, two, three, h, dy, gain, dh, low, gain_part, block):
@@ -340,15 +314,9 @@
     wo[...] = jnp.concatenate([low[:, 256:], high[:, 256:]], axis=1)
 
 
-def split_feed(zl, parts, own, send):
-    own[...] = parts[pl.ds(zl[0] * 32, 32)]
-    send[...] = parts[pl.ds((1 - zl[0]) * 32, 32)]
-
-
-def finish_feed(zl, own, got, wg, wu, wd):
-    mine, its = own[...].astype(F32), got[...].astype(F32)
-    first = zl[0] == 0
-    low, high = jnp.where(first, mine, its), jnp.where(first, its, mine)
+def finish_feed(parts, wg, wu, wd):
+    low = jnp.sum(parts[0].astype(F32), axis=0)
+    high = jnp.sum(parts[1].astype(F32), axis=0)
     for i, out in enumerate((wg, wu, wd)):
         wide, tail = slice(i * 512, (i + 1) * 512), slice(1536 + i * 64, 1600 + i * 64)
         out[...] = jnp.concatenate(
@@ -436,12 +404,7 @@
 def gather_head(rows, head):
     other = swap(rows, "c", 2, 1)
     pieces = [rows, other, swap(rows, "zh", 2, 1), swap(other, "zh", 2, 1)]
-    return pl.pallas_call(
-        place_rows,
-        out_shape=[jax.ShapeDtypeStruct((128, 1024), BF)] * 2,
-        in_specs=[pl.BlockSpec(memory_space=pltpu.SMEM)] + [WHOLE] * 4,
-        out_specs=[pl.BlockSpec()] * 2,
-    )(head.reshape(1), *pieces)
+    return call(place_rows, [Far(((128, 1024), BF))] * 2, *pieces, scalars=(head.reshape(1),))
 
 
 def after(values, *first):
@@ -461,18 +424,13 @@
         prepare,
         [((2, 16, 32, 384), BF), ((32, 1792), BF), ((32, 1792), BF), ((128, 1024), BF)],
         *[Far(w) for w in (w_query, w_key, w_value, w_out, w_gate, w_up, w_down, tokens)],
-        scalars=(zl_ref, head_ref),
+        scalars=(zl_ref, head_ref), room=None,
     )
     got_f = swap(send_f, "zl", 2, 1)
     x_other = swap(x_own, "zl", 2, 1)
     w_a = lax.all_to_all(blocks.reshape(1024, 384), PLANE, 0, 0, tiled=True)
     (rows_f,) = call(order_rows, [Far(((2, 32, 1792), BF))], keep_f, got_f, scalars=(zl_ref,))
     w_f = lax.all_gather(rows_f, ("y", "x"), axis=0)
-
-    (late_dy,) = after([cotangent], x_own)
-    (dy_own,) = call(relative_rows, [((128, 1024), BF)], Far(late_dy), scalars=(head_ref,))
-    dy_other = swap(dy_own, "zl", 2, 1)
-    (x_late,) = after([x_own], dy_other)
 
     (late_positions,) = after([positions], blocks)
     steps = jnp.array([dl * 16 + ky * 4 + d for ky in range(4) for dl in range(2) for d in range(4)])
@@ -491,9 +449,13 @@
     rows_low, rows_high = ((32, 1024), BF), ((32, 1024), F32)
     qh, kv, qkv = call(
         project, [flat, flat, Far(((256, 256), F32))],
-        x_late, x_other, Far(w_a), attn_gain_row, qk_gain, cosine, sine,
-    )
+        x_own, x_other, Far(w_a), attn_gain_row, qk_gain, cosine, sine,
+    )
+    (late_dy,) = after([cotangent], kv)
+    (dy_own,) = call(relative_rows, [((128, 1024), BF)], Far(late_dy), scalars=(head_ref,))
+    dy_other = swap(dy_own, "zl", 2, 1)
     kvs = [kv] + fan([kv] * 4, "y")
+    (qh,) = after([qh], dy_other)
     send, keep, o, l = call(
         attend, halves + [Far(wide_flat)] * 2, qh, *kvs, own_places, places, Far(w_a)
     )
@@ -504,15 +466,13 @@
         feed,
         [((4, 64, 1024), BF), ((4, 64, 1024), F32)]
         + [((256, 1024), BF), ((256, 640), BF), ((256, 1152), BF)],
-        *gather_rows(hn), dy_own, dy_other, Held(w_f), room=24,
-        scratch=[pltpu.VMEM((16, 2, 32, 1792), BF), pltpu.SemaphoreType.DMA((2,))],
+        *gather_rows(hn), dy_own, dy_other, w_f,
     )
     pair = sum_pair(send, keep)
     act, dgu = after([act, dgu], *pair)
     d_hn = [pair[0]] + fan([None] + pair[1:], Z)
     (dw_f,) = call(
-        feed_weights, [Held(((4, 4, 2, 32, 1792), BF))], hn_all, dy_own, dy_other, act, dgu, room=24,
-        scratch=[pltpu.VMEM((4, 4, 2, 32, 1792), BF), pltpu.SemaphoreType.DMA((4,))],
+        feed_weights, [Far(((4, 2, 4, 32, 1792), BF))], hn_all, dy_own, dy_other, act, dgu
     )
     dw_f = lax.psum_scatter(dw_f.reshape(1024, 1792), "x", scatter_dimension=0, tiled=True)
     dh, d_low, ffn_part, block = call(
@@ -533,11 +493,9 @@
         Far(x_own), Far(x_other), attn_gain_row, d_qkv, Far(d_attn), Far(o), gains,
     )
     own, *rest = sum_pair(send, keep)
-    dw_a, dw_f = after([dw_a, dw_f], own)
-    dw_half = dw_f
-    dw_f = lax.psum_scatter(dw_f, "y", scatter_dimension=0, tiled=True)
+    (dw_a,) = after([dw_a], own)
     dw_a = lax.all_to_all(dw_a, PLANE, 0, 0, tiled=True)
-    d_xn = after([own] + fan([None] + rest, Z), dw_half)
+    d_xn = [own] + fan([None] + rest, Z)
     (rows,) = call(
         token_rows, [((64, 1024), BF)], *d_xn, Far(dh), x_own, attn_gain_row, Far(block)
     )
@@ -550,18 +508,15 @@
         [Far(((32, n), F32)) for n in (256, 128, 128, 256)] + [((16, 384), F32)],
         dw_a.reshape(2, 16, 48, 384),
     )
+    (gains,) = call(add_two, [((16, 384), F32)], gains, swap(gains, "c", 2, 1))
     (dw_f,) = after([dw_f], gains)
-    (gains,) = call(add_two, [((16, 384), F32)], gains, swap(gains, "c", 2, 1))
+    dw_f = lax.all_to_all(dw_f, ("zl", "y"), 0, 0, tiled=True)
     attn_sum, ffn_sum, query_sum, key_sum = call(
         finish_gains, [((8, 128), F32)] * 2 + [((1, 64), F32)] * 2,
         gains, swap(gains, "zh", 2, 1),
     )
-    own_f, send_f = call(
-        split_feed, [((32, 1792), BF)] * 2, Far(dw_f), scalars=(zl_ref,)
-    )
     grad_wg, grad_wu, grad_wd = call(
-        finish_feed, [Far(((32, 1152), F32))] * 3, own_f, swap(send_f, "zl", 2, 1),
-        scalars=(zl_ref,),
+        finish_feed, [Far(((32, 1152), F32))] * 3, dw_f.reshape(2, 4, 32, 1792)
     )
     return (
         block_out, tokens_grad, attn_sum.reshape(1024), ffn_sum.reshape(1024),

time: 194 us -> 181 us (0.933)
  local copies, waits for them, and re-layouts: 19.5 us -> 12.1 us
  waiting for transfers between devices: 74.2 us -> 69.1 us
    unnamed x58 -> x32, local copies, waits for them, and re-layouts: 17.9 us -> 9.17 us
    reduce_scatter x1, waiting for transfers between devices: 7.05 us -> 0.01 us  [local(): lax.psum_scatter(dw_f.reshape(1024, 1792), 'x', scatter_dimension=0, tile...]
    ppermute x41 -> x40, waiting for transfers between devices: 63.2 us -> 68.5 us  [swap(): return lax.ppermute(value, axes, [(i, i ^ mask) for i in range(size)])]
    reduce_scatter x1 -> x0, waiting for transfers between devices: 3.94 us -> none  [local(): dw_f = lax.psum_scatter(dw_f, 'y', scatter_dimension=0, tiled=True)]
    all_to_all x0 -> x1, starting transfers between devices: none -> 3.69 us  [local(): dw_f = lax.all_to_all(dw_f, ('zl', 'y'), 0, 0, tiled=True)]
    ppermute x41 -> x40, starting transfers between devices: 45.7 us -> 43.9 us  [swap(): return lax.ppermute(value, axes, [(i, i ^ mask) for i in range(size)])]
  transfers between devices with their start and end apart: 46 -> 45, of which waited for: 25 -> 27; matrix products, arithmetic and copies ran while one was open for 2% -> 3% of each run, Pallas kernels for 6% -> 6%
where the time goes in v7:
time: 181 us; the launch traced here: 180 us
  waiting for transfers between devices  69.1 us (38%)
  starting transfers between devices  62.2 us (34%)
  Pallas kernels  19.2 us (11%)
  between operations  14.3 us (8%)
  local copies, waits for them, and re-layouts  12.1 us (7%)
  other arithmetic  2.85 us (2%)
    ppermute x40, waiting for transfers between devices, swap(): return lax.ppermute(value, axes, [(i, i ^ mask) for i in range(size)])  68.5 us
    ppermute x40, starting transfers between devices, swap(): return lax.ppermute(value, axes, [(i, i ^ mask) for i in range(size)])  43.9 us
    pallas_call x21, Pallas kernels, call(): pl.pallas_call(body, out_shape=[jax.ShapeDtypeStruct(*bare(out)) for out...  19.2 us
    unnamed x32, local copies, waits for them, and re-layouts  9.17 us
    all_to_all x1, starting transfers between devices, local(): w_a = lax.all_to_all(blocks.reshape(1024, 384), PLANE, 0, 0, tiled=True)  8.51 us
    all_to_all x1, starting transfers between devices, local(): dw_a = lax.all_to_all(dw_a, PLANE, 0, 0, tiled=True)  5.95 us
    all_to_all x1, starting transfers between devices, local(): dw_f = lax.all_to_all(dw_f, ('zl', 'y'), 0, 0, tiled=True)  3.69 us
  transfers between devices with their start and end apart: 45, of which 27 were waited for; matrix products, arithmetic and copies ran while one was open for 3% of the time, Pallas kernels for 6%

profile of v7, /device:TPU:0, one launch (start us, length us, event | category | flops | bytes accessed | tf_op | source)
XLA Modules:
  0.0 179.8 jit_solution(9212582957609146071)
XLA Ops:
  7.3 2.3 %shard_map.246 = (bf16[2,16,32,384]{3,2,1,0:T(8,128)(2,1)}, bf16[32,1792]{1,0:T(8,128)(2,1)}, bf16[32,1792]{1,0:T(8,128)(2,1)}, bf16[128,1024]{1,0:T(8,128)(2,1)}) custom-call(s32[1]{0:T(128)} %bitcast.1.zl, s32[1]{0:T(128)} %bitcast.head, bf16[32,256]{1,0:T(8,128)(2,1)} %wq.1, bf16[32,128]{1,0:T(8,128)(2,1)} %wk.1, bf16[32,128]{1,0:T(8,128)(2,1)} %wv.1, ...), custom_call_target="tpu_custom_call" | custom-call | tf_op jit(solution)/shard_map/pallas_call | solution.py:37
  9.6 2.1 %collective-permute-start.16 = (bf16[32,1792]{1,0:T(8,128)(2,1)}, bf16[32,1792]{1,0:T(8,128)(2,1)S(1)}, u32[]{:S(2)}, u32[]{:S(2)}) collective-permute-start(bf16[32,1792]{1,0:T(8,128)(2,1)} %get-tuple-element.94), channel_id=1, source_target_pairs={{0,64},{64,0},{1,65},{65,1},{2,66},{66,2},{3,67},{67,3},{4,68},{68... | collective-permute-start | bytes 344072 | tf_op jit(solution)/shard_map/ppermute | solution.py:371
  11.7 3.4 %collective-permute-done.16.got = bf16[32,1792]{1,0:T(8,128)(2,1)S(1)} collective-permute-done((bf16[32,1792]{1,0:T(8,128)(2,1)}, bf16[32,1792]{1,0:T(8,128)(2,1)S(1)}, u32[]{:S(2)}, u32[]{:S(2)}) %collective-permute-start.16) | collective-permute-done | bytes 114720 | tf_op jit(solution)/shard_map/ppermute | solution.py:371
  16.7 8.5 %all-to-all-start = ((bf16[32,32,384]{2,1,0:T(8,128)(2,1)}), bf16[32,32,384]{2,1,0:T(8,128)(2,1)S(1)}, u32[]{:S(2)}, u32[]{:S(2)}) async-start(bf16[32,32,384]{2,1,0:T(8,128)(2,1)} %bitcast.31), calls=%async_computation | async-start | bytes 1572864 | tf_op jit(solution)/shard_map/all_to_all | solution.py:431
  25.2 1.9 %collective-permute-start = (bf16[128,1024]{1,0:T(8,128)(2,1)}, bf16[128,1024]{1,0:T(8,128)(2,1)S(1)}, u32[]{:S(2)}, u32[]{:S(2)}) collective-permute-start(bf16[128,1024]{1,0:T(8,128)(2,1)} %get-tuple-element.79.own.x.x_own), channel_id=1, source_target_pairs={{0,64},{64,0},{1,65},{65,1},{2,66},{66,2},{3,67},{67,3},{4,68},{68... | collective-permute-start | bytes 786440 | tf_op jit(solution)/shard_map/ppermute | solution.py:371
  32.7 7.9 %collective-permute-done.other.x_other = bf16[128,1024]{1,0:T(8,128)(2,1)S(1)} collective-permute-done((bf16[128,1024]{1,0:T(8,128)(2,1)}, bf16[128,1024]{1,0:T(8,128)(2,1)S(1)}, u32[]{:S(2)}, u32[]{:S(2)}) %collective-permute-start) | collective-permute-done | bytes 262176 | tf_op jit(solution)/shard_map/ppermute | solution.py:371
  42.7 2.2 %collective-permute-start.4 = (bf16[256,128]{1,0:T(8,128)(2,1)S(1)}, bf16[256,128]{1,0:T(8,128)(2,1)S(1)}, u32[]{:S(2)}, u32[]{:S(2)}) collective-permute-start(bf16[256,128]{1,0:T(8,128)(2,1)S(1)} %get-tuple-element.83.kv0), channel_id=1, source_target_pairs={{0,48},{16,32},{32,16},{48,0},{1,49},{17,33},{33,17},{49,1},{2,50}... | collective-permute-start | bytes 196616 | tf_op jit(solution)/shard_map/ppermute | solution.py:371
  48.9 1.8 collective-permute-done.3.kv2
  53.7 3.7 %collective-permute-start.6 = (bf16[32,1024]{1,0:T(8,128)(2,1)S(1)}, bf16[32,1024]{1,0:T(8,128)(2,1)S(1)}, u32[]{:S(2)}, u32[]{:S(2)}) collective-permute-start(bf16[32,1024]{1,0:T(8,128)(2,1)S(1)} %get-tuple-element.89), channel_id=1, source_target_pairs={{0,2},{2,0},{64,66},{66,64},{1,3},{3,1},{65,67},{67,65},{4,6},{6,4... | collective-permute-start | bytes 196616 | tf_op jit(solution)/shard_map/ppermute | solution.py:371
  58.0 2.0 %collective-permute-done.6.one = bf16[32,1024]{1,0:T(8,128)(2,1)S(1)} collective-permute-done((bf16[32,1024]{1,0:T(8,128)(2,1)S(1)}, bf16[32,1024]{1,0:T(8,128)(2,1)S(1)}, u32[]{:S(2)}, u32[]{:S(2)}) %collective-permute-start.6) | collective-permute-done | bytes 65568 | tf_op jit(solution)/shard_map/ppermute | solution.py:371
  61.6 1.8 %collective-permute-done.8.three = bf16[32,1024]{1,0:T(8,128)(2,1)S(1)} collective-permute-done((bf16[32,1024]{1,0:T(8,128)(2,1)S(1)}, bf16[32,1024]{1,0:T(8,128)(2,1)S(1)}, u32[]{:S(2)}, u32[]{:S(2)}) %collective-permute-start.8) | collective-permute-done | bytes 65568 | tf_op jit(solution)/shard_map/ppermute | solution.py:371
  64.6 3.8 %collective-permute-start.10 = (bf16[32,1024]{1,0:T(8,128)(2,1)S(1)}, bf16[32,1024]{1,0:T(8,128)(2,1)S(1)}, u32[]{:S(2)}, u32[]{:S(2)}) collective-permute-start(bf16[32,1024]{1,0:T(8,128)(2,1)S(1)} %get-tuple-element.92.p0), channel_id=1, source_target_pairs={{0,2},{2,0},{64,66},{66,64},{1,3},{3,1},{65,67},{67,65},{4,6},{6,4... | collective-permute-start | bytes 196616 | tf_op jit(solution)/shard_map/ppermute | solution.py:371
  73.2 2.0 %copy-done.2 = bf16[32,32,1792]{2,1,0:T(8,128)(2,1)S(1)} copy-done((bf16[32,32,1792]{2,1,0:T(8,128)(2,1)S(1)}, bf16[32,32,1792]{2,1,0:T(8,128)(2,1)}, u32[]{:S(2)}) %copy-start.2) | copy-done | bytes 3670040
  77.8 2.5 %shard_map.253 = (bf16[4,64,1024]{2,1,0:T(8,128)(2,1)S(1)}, f32[4,64,1024]{2,1,0:T(8,128)S(1)}, bf16[256,1024]{1,0:T(8,128)(2,1)S(1)}, bf16[256,640]{1,0:T(8,128)(2,1)S(1)}, bf16[256,1152]{1,0:T(8,128)(2,1)S(1)}) custom-call(bf16[32,1024]{1,0:T(8,128)(2,1)S(1)} %get-tuple-element.92.p0, bf16[32,1024]{1,0:T(8,128)(2,1)S(1)} %collective-permute-done.9.p1, ...), custom_call_target="tpu_custom_call" | custom-call | tf_op jit(solution)/shard_map/pallas_call | solution.py:37
  84.6 1.8 copy-done
  86.4 2.9 %collective-permute-start.18 = (bf16[64,1024]{1,0:T(8,128)(2,1)}, bf16[64,1024]{1,0:T(8,128)(2,1)S(1)}, u32[]{:S(2)}, u32[]{:S(2)}) collective-permute-start(bf16[64,1024]{1,0:T(8,128)(2,1)} %get-tuple-element.98), channel_id=1, source_target_pairs={{0,2},{2,0},{64,66},{66,64},{1,3},{3,1},{65,67},{67,65},{4,6},{6,4... | collective-permute-start | bytes 393224 | tf_op jit(solution)/shard_map/ppermute | solution.py:371
  90.6 3.9 %collective-permute-done.18.one = bf16[64,1024]{1,0:T(8,128)(2,1)S(1)} collective-permute-done((bf16[64,1024]{1,0:T(8,128)(2,1)}, bf16[64,1024]{1,0:T(8,128)(2,1)S(1)}, u32[]{:S(2)}, u32[]{:S(2)}) %collective-permute-start.18) | collective-permute-done | bytes 131104 | tf_op jit(solution)/shard_map/ppermute | solution.py:371
  99.9 1.9 %collective-permute-start.22 = (bf16[32,1024]{1,0:T(8,128)(2,1)S(1)}, bf16[32,1024]{1,0:T(8,128)(2,1)S(1)}, u32[]{:S(2)}, u32[]{:S(2)}) collective-permute-start(bf16[32,1024]{1,0:T(8,128)(2,1)S(1)} %get-tuple-element.102.p0), channel_id=1, source_target_pairs={{0,2},{2,0},{64,66},{66,64},{1,3},{3,1},{65,67},{67,65},{4,6},{6,4... | collective-permute-start | bytes 196616 | tf_op jit(solution)/shard_map/ppermute | solution.py:371
  103.2 2.5 %collective-permute-done.22.p2 = bf16[32,1024]{1,0:T(8,128)(2,1)S(1)} collective-permute-done((bf16[32,1024]{1,0:T(8,128)(2,1)S(1)}, bf16[32,1024]{1,0:T(8,128)(2,1)S(1)}, u32[]{:S(2)}, u32[]{:S(2)}) %collective-permute-start.22) | collective-permute-done | bytes 65568 | tf_op jit(solution)/shard_map/ppermute | solution.py:371
  106.9 3.1 %shard_map.256 = (bf16[256,1024]{1,0:T(8,128)(2,1)S(1)}, f32[256,128]{1,0:T(8,128)S(1)}, f32[256,128]{1,0:T(8,128)S(1)}, bf16[256,128]{1,0:T(8,128)(2,1)S(1)}, b...) custom-call(bf16[32,1024]{1,0:T(8,128)(2,1)S(1)} %get-tuple-element.102.p0, ...), custom_call_target="tpu_custom_call" | custom-call | tf_op jit(solution)/shard_map/pallas_call | solution.py:37
  110.3 2.6 %collective-permute-start.29 = (bf16[256,128]{1,0:T(8,128)(2,1)S(1)}, bf16[256,128]{1,0:T(8,128)(2,1)S(1)}, u32[]{:S(2)}, u32[]{:S(2)}) collective-permute-start(bf16[256,128]{1,0:T(8,128)(2,1)S(1)} %get-tuple-element.108), channel_id=1, source_target_pairs={{0,32},{16,48},{32,0},{48,16},{1,33},{17,49},{33,1},{49,17},{2,34}... | collective-permute-start | bytes 196616 | tf_op jit(solution)/shard_map/ppermute | solution.py:371
  112.8 2.0 %collective-permute-start.30 = (bf16[256,128]{1,0:T(8,128)(2,1)S(1)}, bf16[256,128]{1,0:T(8,128)(2,1)S(1)}, u32[]{:S(2)}, u32[]{:S(2)}) collective-permute-start(bf16[256,128]{1,0:T(8,128)(2,1)S(1)} %get-tuple-element.109), channel_id=1, source_target_pairs={{0,48},{16,32},{32,16},{48,0},{1,49},{17,33},{33,17},{49,1},{2,50}... | collective-permute-start | bytes 196616 | tf_op jit(solution)/shard_map/ppermute | solution.py:371
  116.5 1.8 %collective-permute-done.30.three = bf16[256,128]{1,0:T(8,128)(2,1)S(1)} collective-permute-done((bf16[256,128]{1,0:T(8,128)(2,1)S(1)}, bf16[256,128]{1,0:T(8,128)(2,1)S(1)}, u32[]{:S(2)}, u32[]{:S(2)}) %collective-permute-start.30) | collective-permute-done | bytes 65568 | tf_op jit(solution)/shard_map/ppermute | solution.py:371
  121.2 5.9 %all-to-all-start.1 = ((bf16[32,48,384]{2,1,0:T(8,128)(2,1)}), bf16[32,48,384]{2,1,0:T(8,128)(2,1)S(1)}, u32[]{:S(2)}, u32[]{:S(2)}) async-start(bf16[32,48,384]{2,1,0:T(8,128)(2,1)} %shard_map.261), calls=%async_computation.1 | async-start | bytes 2359296 | tf_op jit(solution)/shard_map/all_to_all | solution.py:497
  127.1 2.2 %collective-permute-start.32 = (bf16[32,1024]{1,0:T(8,128)(2,1)S(1)}, bf16[32,1024]{1,0:T(8,128)(2,1)S(1)}, u32[]{:S(2)}, u32[]{:S(2)}) collective-permute-start(bf16[32,1024]{1,0:T(8,128)(2,1)S(1)} %get-tuple-element.115), channel_id=1, source_target_pairs={{0,2},{2,0},{64,66},{66,64},{1,3},{3,1},{65,67},{67,65},{4,6},{6,4... | collective-permute-start | bytes 196616 | tf_op jit(solution)/shard_map/ppermute | solution.py:371
  131.7 11.8 %collective-permute-done.32.one = bf16[32,1024]{1,0:T(8,128)(2,1)S(1)} collective-permute-done((bf16[32,1024]{1,0:T(8,128)(2,1)S(1)}, bf16[32,1024]{1,0:T(8,128)(2,1)S(1)}, u32[]{:S(2)}, u32[]{:S(2)}) %collective-permute-start.32) | collective-permute-done | bytes 65568 | tf_op jit(solution)/shard_map/ppermute | solution.py:371
  143.5 1.8 %collective-permute-done.33.two = bf16[32,1024]{1,0:T(8,128)(2,1)S(1)} collective-permute-done((bf16[32,1024]{1,0:T(8,128)(2,1)S(1)}, bf16[32,1024]{1,0:T(8,128)(2,1)S(1)}, u32[]{:S(2)}, u32[]{:S(2)}) %collective-permute-start.33) | collective-permute-done | bytes 65568 | tf_op jit(solution)/shard_map/ppermute | solution.py:371
  148.1 3.7 %all-to-all-start.2 = ((bf16[8,32,1792]{2,1,0:T(8,128)(2,1)}), bf16[8,32,1792]{2,1,0:T(8,128)(2,1)S(1)}, u32[]{:S(2)}, u32[]{:S(2)}) async-start(bf16[8,32,1792]{2,1,0:T(8,128)(2,1)} %bitcast.30), calls=%async_computation.3 | async-start | bytes 1835008 | tf_op jit(solution)/shard_map/all_to_all | solution.py:513
  151.9 2.1 %collective-permute-start.36 = (bf16[64,1024]{1,0:T(8,128)(2,1)S(1)}, bf16[64,1024]{1,0:T(8,128)(2,1)S(1)}, u32[]{:S(2)}, u32[]{:S(2)}) collective-permute-start(bf16[64,1024]{1,0:T(8,128)(2,1)S(1)} %shard_map.259.p0), channel_id=1, source_target_pairs={{0,2},{2,0},{1,3},{3,1},{4,6},{6,4},{5,7},{7,5},{8,10},{10,8},{9,1... | collective-permute-start | bytes 393224 | tf_op jit(solution)/shard_map/ppermute | solution.py:371
  155.4 2.1 %collective-permute-start.39 = (f32[16,384]{1,0:T(8,128)S(1)}, f32[16,384]{1,0:T(8,128)S(1)}, u32[]{:S(2)}, u32[]{:S(2)}) collective-permute-start(f32[16,384]{1,0:T(8,128)S(1)} %shard_map.263.one), channel_id=1, source_target_pairs={{0,2},{2,0},{1,3},{3,1},{4,6},{6,4},{5,7},{7,5},{8,10},{10,8},{9,1... | collective-permute-start | bytes 73736 | tf_op jit(solution)/shard_map/ppermute | solution.py:371
  157.5 10.7 %collective-permute-done.36.p2 = bf16[64,1024]{1,0:T(8,128)(2,1)S(1)} collective-permute-done((bf16[64,1024]{1,0:T(8,128)(2,1)S(1)}, bf16[64,1024]{1,0:T(8,128)(2,1)S(1)}, u32[]{:S(2)}, u32[]{:S(2)}) %collective-permute-start.36) | collective-permute-done | bytes 131104 | tf_op jit(solution)/shard_map/ppermute | solution.py:371
  168.2 2.5 %collective-permute-done.37.p3 = bf16[64,1024]{1,0:T(8,128)(2,1)S(1)} collective-permute-done((bf16[64,1024]{1,0:T(8,128)(2,1)S(1)}, bf16[64,1024]{1,0:T(8,128)(2,1)S(1)}, u32[]{:S(2)}, u32[]{:S(2)}) %collective-permute-start.37) | collective-permute-done | bytes 131104 | tf_op jit(solution)/shard_map/ppermute | solution.py:371
  (131 shorter events, 54.4 us)
Async XLA Ops:
  7.2 66.0 %all-gather.3.cloned.1.call-start = ((), (), s32[]{:S(2)}) async-start(), calls=%async_computation.5 | async-start | bytes 3899392 | tf_op jit(solution)/shard_map/all_gather | solution.py:433
  9.6 5.4 %collective-permute-start.16 = (bf16[32,1792]{1,0:T(8,128)(2,1)}, bf16[32,1792]{1,0:T(8,128)(2,1)S(1)}, u32[]{:S(2)}, u32[]{:S(2)}) collective-permute-start(bf16[32,1792]{1,0:T(8,128)(2,1)} %get-tuple-element.94), channel_id=1, source_target_pairs={{0,64},{64,0},{1,65},{65,1},{2,66},{66,2},{3,67},{67,3},{4,68},{68... | collective-permute-start | bytes 344072 | tf_op jit(solution)/shard_map/ppermute | solution.py:371
  16.7 23.9 %all-to-all-start = ((bf16[32,32,384]{2,1,0:T(8,128)(2,1)}), bf16[32,32,384]{2,1,0:T(8,128)(2,1)S(1)}, u32[]{:S(2)}, u32[]{:S(2)}) async-start(bf16[32,32,384]{2,1,0:T(8,128)(2,1)} %bitcast.31), calls=%async_computation | async-start | bytes 1572864 | tf_op jit(solution)/shard_map/all_to_all | solution.py:431
  25.2 122.9 %reduce-scatter.2.cloned.1.call-start = ((), (), s32[]{:S(2)}) async-start(), calls=%async_computation.4 | async-start | bytes 4587520 | tf_op jit(solution)/shard_map/reduce_scatter | solution.py:477
  25.2 15.4 %collective-permute-start = (bf16[128,1024]{1,0:T(8,128)(2,1)}, bf16[128,1024]{1,0:T(8,128)(2,1)S(1)}, u32[]{:S(2)}, u32[]{:S(2)}) collective-permute-start(bf16[128,1024]{1,0:T(8,128)(2,1)} %get-tuple-element.79.own.x.x_own), channel_id=1, source_target_pairs={{0,64},{64,0},{1,65},{65,1},{2,66},{66,2},{3,67},{67,3},{4,68},{68... | collective-permute-start | bytes 786440 | tf_op jit(solution)/shard_map/ppermute | solution.py:371
  41.3 6.9 %collective-permute-start.1 = (bf16[128,1024]{1,0:T(8,128)(2,1)S(1)}, bf16[128,1024]{1,0:T(8,128)(2,1)S(1)}, u32[]{:S(2)}, u32[]{:S(2)}) collective-permute-start(bf16[128,1024]{1,0:T(8,128)(2,1)S(1)} %shard_map.248.dy_own.dy), channel_id=1, source_target_pairs={{0,64},{64,0},{1,65},{65,1},{2,66},{66,2},{3,67},{67,3},{4,68},{68... | collective-permute-start | bytes 786440 | tf_op jit(solution)/shard_map/ppermute | solution.py:371
  42.7 6.2 %collective-permute-start.4 = (bf16[256,128]{1,0:T(8,128)(2,1)S(1)}, bf16[256,128]{1,0:T(8,128)(2,1)S(1)}, u32[]{:S(2)}, u32[]{:S(2)}) collective-permute-start(bf16[256,128]{1,0:T(8,128)(2,1)S(1)} %get-tuple-element.83.kv0), channel_id=1, source_target_pairs={{0,48},{16,32},{32,16},{48,0},{1,49},{17,33},{33,17},{49,1},{2,50}... | collective-permute-start | bytes 196616 | tf_op jit(solution)/shard_map/ppermute | solution.py:371
  44.9 5.8 %collective-permute-start.3 = (bf16[256,128]{1,0:T(8,128)(2,1)S(1)}, bf16[256,128]{1,0:T(8,128)(2,1)S(1)}, u32[]{:S(2)}, u32[]{:S(2)}) collective-permute-start(bf16[256,128]{1,0:T(8,128)(2,1)S(1)} %get-tuple-element.83.kv0), channel_id=1, source_target_pairs={{0,32},{16,48},{32,0},{48,16},{1,33},{17,49},{33,1},{49,17},{2,34}... | collective-permute-start | bytes 196616 | tf_op jit(solution)/shard_map/ppermute | solution.py:371
  45.9 4.7 %collective-permute-start.2 = (bf16[256,128]{1,0:T(8,128)(2,1)S(1)}, bf16[256,128]{1,0:T(8,128)(2,1)S(1)}, u32[]{:S(2)}, u32[]{:S(2)}) collective-permute-start(bf16[256,128]{1,0:T(8,128)(2,1)S(1)} %get-tuple-element.83.kv0), channel_id=1, source_target_pairs={{0,16},{16,0},{32,48},{48,32},{1,17},{17,1},{33,49},{49,33},{2,18}... | collective-permute-start | bytes 196616 | tf_op jit(solution)/shard_map/ppermute | solution.py:371
  53.7 6.3 %collective-permute-start.6 = (bf16[32,1024]{1,0:T(8,128)(2,1)S(1)}, bf16[32,1024]{1,0:T(8,128)(2,1)S(1)}, u32[]{:S(2)}, u32[]{:S(2)}) collective-permute-start(bf16[32,1024]{1,0:T(8,128)(2,1)S(1)} %get-tuple-element.89), channel_id=1, source_target_pairs={{0,2},{2,0},{64,66},{66,64},{1,3},{3,1},{65,67},{67,65},{4,6},{6,4... | collective-permute-start | bytes 196616 | tf_op jit(solution)/shard_map/ppermute | solution.py:371
  57.4 4.3 %collective-permute-start.7 = (bf16[32,1024]{1,0:T(8,128)(2,1)S(1)}, bf16[32,1024]{1,0:T(8,128)(2,1)S(1)}, u32[]{:S(2)}, u32[]{:S(2)}) collective-permute-start(bf16[32,1024]{1,0:T(8,128)(2,1)S(1)} %get-tuple-element.90), channel_id=1, source_target_pairs={{0,64},{2,66},{64,0},{66,2},{1,65},{3,67},{65,1},{67,3},{4,68},{6,... | collective-permute-start | bytes 196616 | tf_op jit(solution)/shard_map/ppermute | solution.py:371
  57.9 5.5 %collective-permute-start.8 = (bf16[32,1024]{1,0:T(8,128)(2,1)S(1)}, bf16[32,1024]{1,0:T(8,128)(2,1)S(1)}, u32[]{:S(2)}, u32[]{:S(2)}) collective-permute-start(bf16[32,1024]{1,0:T(8,128)(2,1)S(1)} %get-tuple-element.91), channel_id=1, source_target_pairs={{0,66},{2,64},{64,2},{66,0},{1,67},{3,65},{65,3},{67,1},{4,70},{6,... | collective-permute-start | bytes 196616 | tf_op jit(solution)/shard_map/ppermute | solution.py:371
  63.6 6.0 %collective-permute-start.14 = (bf16[32,1024]{1,0:T(8,128)(2,1)S(1)}, bf16[32,1024]{1,0:T(8,128)(2,1)S(1)}, u32[]{:S(2)}, u32[]{:S(2)}) collective-permute-start(bf16[32,1024]{1,0:T(8,128)(2,1)S(1)} %get-tuple-element.92.p0), channel_id=1, source_target_pairs={{0,66},{2,64},{64,2},{66,0},{1,67},{3,65},{65,3},{67,1},{4,70},{6,... | collective-permute-start | bytes 196616 | tf_op jit(solution)/shard_map/ppermute | solution.py:371
  64.4 5.2 %collective-permute-start.12 = (bf16[32,1024]{1,0:T(8,128)(2,1)S(1)}, bf16[32,1024]{1,0:T(8,128)(2,1)S(1)}, u32[]{:S(2)}, u32[]{:S(2)}) collective-permute-start(bf16[32,1024]{1,0:T(8,128)(2,1)S(1)} %get-tuple-element.92.p0), channel_id=1, source_target_pairs={{0,64},{2,66},{64,0},{66,2},{1,65},{3,67},{65,1},{67,3},{4,68},{6,... | collective-permute-start | bytes 196616 | tf_op jit(solution)/shard_map/ppermute | solution.py:371
  64.6 6.7 %collective-permute-start.10 = (bf16[32,1024]{1,0:T(8,128)(2,1)S(1)}, bf16[32,1024]{1,0:T(8,128)(2,1)S(1)}, u32[]{:S(2)}, u32[]{:S(2)}) collective-permute-start(bf16[32,1024]{1,0:T(8,128)(2,1)S(1)} %get-tuple-element.92.p0), channel_id=1, source_target_pairs={{0,2},{2,0},{64,66},{66,64},{1,3},{3,1},{65,67},{67,65},{4,6},{6,4... | collective-permute-start | bytes 196616 | tf_op jit(solution)/shard_map/ppermute | solution.py:371
  86.4 8.1 %collective-permute-start.18 = (bf16[64,1024]{1,0:T(8,128)(2,1)}, bf16[64,1024]{1,0:T(8,128)(2,1)S(1)}, u32[]{:S(2)}, u32[]{:S(2)}) collective-permute-start(bf16[64,1024]{1,0:T(8,128)(2,1)} %get-tuple-element.98), channel_id=1, source_target_pairs={{0,2},{2,0},{64,66},{66,64},{1,3},{3,1},{65,67},{67,65},{4,6},{6,4... | collective-permute-start | bytes 393224 | tf_op jit(solution)/shard_map/ppermute | solution.py:371
  89.4 6.4 %collective-permute-start.19 = (bf16[64,1024]{1,0:T(8,128)(2,1)}, bf16[64,1024]{1,0:T(8,128)(2,1)S(1)}, u32[]{:S(2)}, u32[]{:S(2)}) collective-permute-start(bf16[64,1024]{1,0:T(8,128)(2,1)} %copy-done.15), channel_id=1, source_target_pairs={{0,64},{2,66},{64,0},{66,2},{1,65},{3,67},{65,1},{67,3},{4,68},{6,... | collective-permute-start | bytes 393224 | tf_op jit(solution)/shard_map/ppermute | solution.py:371
  89.4 7.5 %collective-permute-start.20 = (bf16[64,1024]{1,0:T(8,128)(2,1)S(1)}, bf16[64,1024]{1,0:T(8,128)(2,1)S(1)}, u32[]{:S(2)}, u32[]{:S(2)}) collective-permute-start(bf16[64,1024]{1,0:T(8,128)(2,1)S(1)} %get-tuple-element.100), channel_id=1, source_target_pairs={{0,66},{2,64},{64,2},{66,0},{1,67},{3,65},{65,3},{67,1},{4,70},{6,... | collective-permute-start | bytes 393224 | tf_op jit(solution)/shard_map/ppermute | solution.py:371
  97.0 5.6 %collective-permute-start.26 = (bf16[32,1024]{1,0:T(8,128)(2,1)S(1)}, bf16[32,1024]{1,0:T(8,128)(2,1)S(1)}, u32[]{:S(2)}, u32[]{:S(2)}) collective-permute-start(bf16[32,1024]{1,0:T(8,128)(2,1)S(1)} %get-tuple-element.102.p0), channel_id=1, source_target_pairs={{0,66},{2,64},{64,2},{66,0},{1,67},{3,65},{65,3},{67,1},{4,70},{6,... | collective-permute-start | bytes 196616 | tf_op jit(solution)/shard_map/ppermute | solution.py:371
  98.5 4.7 %collective-permute-start.24 = (bf16[32,1024]{1,0:T(8,128)(2,1)S(1)}, bf16[32,1024]{1,0:T(8,128)(2,1)S(1)}, u32[]{:S(2)}, u32[]{:S(2)}) collective-permute-start(bf16[32,1024]{1,0:T(8,128)(2,1)S(1)} %get-tuple-element.102.p0), channel_id=1, source_target_pairs={{0,64},{2,66},{64,0},{66,2},{1,65},{3,67},{65,1},{67,3},{4,68},{6,... | collective-permute-start | bytes 196616 | tf_op jit(solution)/shard_map/ppermute | solution.py:371
  99.9 5.8 %collective-permute-start.22 = (bf16[32,1024]{1,0:T(8,128)(2,1)S(1)}, bf16[32,1024]{1,0:T(8,128)(2,1)S(1)}, u32[]{:S(2)}, u32[]{:S(2)}) collective-permute-start(bf16[32,1024]{1,0:T(8,128)(2,1)S(1)} %get-tuple-element.102.p0), channel_id=1, source_target_pairs={{0,2},{2,0},{64,66},{66,64},{1,3},{3,1},{65,67},{67,65},{4,6},{6,4... | collective-permute-start | bytes 196616 | tf_op jit(solution)/shard_map/ppermute | solution.py:371
  110.0 4.8 %collective-permute-start.28 = (bf16[256,128]{1,0:T(8,128)(2,1)S(1)}, bf16[256,128]{1,0:T(8,128)(2,1)S(1)}, u32[]{:S(2)}, u32[]{:S(2)}) collective-permute-start(bf16[256,128]{1,0:T(8,128)(2,1)S(1)} %get-tuple-element.107), channel_id=1, source_target_pairs={{0,16},{16,0},{32,48},{48,32},{1,17},{17,1},{33,49},{49,33},{2,18}... | collective-permute-start | bytes 196616 | tf_op jit(solution)/shard_map/ppermute | solution.py:371
  110.3 6.3 %collective-permute-start.29 = (bf16[256,128]{1,0:T(8,128)(2,1)S(1)}, bf16[256,128]{1,0:T(8,128)(2,1)S(1)}, u32[]{:S(2)}, u32[]{:S(2)}) collective-permute-start(bf16[256,128]{1,0:T(8,128)(2,1)S(1)} %get-tuple-element.108), channel_id=1, source_target_pairs={{0,32},{16,48},{32,0},{48,16},{1,33},{17,49},{33,1},{49,17},{2,34}... | collective-permute-start | bytes 196616 | tf_op jit(solution)/shard_map/ppermute | solution.py:371
  112.8 5.5 %collective-permute-start.30 = (bf16[256,128]{1,0:T(8,128)(2,1)S(1)}, bf16[256,128]{1,0:T(8,128)(2,1)S(1)}, u32[]{:S(2)}, u32[]{:S(2)}) collective-permute-start(bf16[256,128]{1,0:T(8,128)(2,1)S(1)} %get-tuple-element.109), channel_id=1, source_target_pairs={{0,48},{16,32},{32,16},{48,0},{1,49},{17,33},{33,17},{49,1},{2,50}... | collective-permute-start | bytes 196616 | tf_op jit(solution)/shard_map/ppermute | solution.py:371
  121.2 24.9 %all-to-all-start.1 = ((bf16[32,48,384]{2,1,0:T(8,128)(2,1)}), bf16[32,48,384]{2,1,0:T(8,128)(2,1)S(1)}, u32[]{:S(2)}, u32[]{:S(2)}) async-start(bf16[32,48,384]{2,1,0:T(8,128)(2,1)} %shard_map.261), calls=%async_computation.1 | async-start | bytes 2359296 | tf_op jit(solution)/shard_map/all_to_all | solution.py:497
  127.1 16.3 %collective-permute-start.32 = (bf16[32,1024]{1,0:T(8,128)(2,1)S(1)}, bf16[32,1024]{1,0:T(8,128)(2,1)S(1)}, u32[]{:S(2)}, u32[]{:S(2)}) collective-permute-start(bf16[32,1024]{1,0:T(8,128)(2,1)S(1)} %get-tuple-element.115), channel_id=1, source_target_pairs={{0,2},{2,0},{64,66},{66,64},{1,3},{3,1},{65,67},{67,65},{4,6},{6,4... | collective-permute-start | bytes 196616 | tf_op jit(solution)/shard_map/ppermute | solution.py:371
  129.3 16.0 %collective-permute-start.33 = (bf16[32,1024]{1,0:T(8,128)(2,1)S(1)}, bf16[32,1024]{1,0:T(8,128)(2,1)S(1)}, u32[]{:S(2)}, u32[]{:S(2)}) collective-permute-start(bf16[32,1024]{1,0:T(8,128)(2,1)S(1)} %get-tuple-element.116), channel_id=1, source_target_pairs={{0,64},{2,66},{64,0},{66,2},{1,65},{3,67},{65,1},{67,3},{4,68},{6,... | collective-permute-start | bytes 196616 | tf_op jit(solution)/shard_map/ppermute | solution.py:371
  130.5 14.8 %collective-permute-start.34 = (bf16[32,1024]{1,0:T(8,128)(2,1)S(1)}, bf16[32,1024]{1,0:T(8,128)(2,1)S(1)}, u32[]{:S(2)}, u32[]{:S(2)}) collective-permute-start(bf16[32,1024]{1,0:T(8,128)(2,1)S(1)} %get-tuple-element.117), channel_id=1, source_target_pairs={{0,66},{2,64},{64,2},{66,0},{1,67},{3,65},{65,3},{67,1},{4,70},{6,... | collective-permute-start | bytes 196616 | tf_op jit(solution)/shard_map/ppermute | solution.py:371
  148.1 24.0 %all-to-all-start.2 = ((bf16[8,32,1792]{2,1,0:T(8,128)(2,1)}), bf16[8,32,1792]{2,1,0:T(8,128)(2,1)S(1)}, u32[]{:S(2)}, u32[]{:S(2)}) async-start(bf16[8,32,1792]{2,1,0:T(8,128)(2,1)} %bitcast.30), calls=%async_computation.3 | async-start | bytes 1835008 | tf_op jit(solution)/shard_map/all_to_all | solution.py:513
  151.9 16.3 %collective-permute-start.36 = (bf16[64,1024]{1,0:T(8,128)(2,1)S(1)}, bf16[64,1024]{1,0:T(8,128)(2,1)S(1)}, u32[]{:S(2)}, u32[]{:S(2)}) collective-permute-start(bf16[64,1024]{1,0:T(8,128)(2,1)S(1)} %shard_map.259.p0), channel_id=1, source_target_pairs={{0,2},{2,0},{1,3},{3,1},{4,6},{6,4},{5,7},{7,5},{8,10},{10,8},{9,1... | collective-permute-start | bytes 393224 | tf_op jit(solution)/shard_map/ppermute | solution.py:371
  154.0 16.7 %collective-permute-start.37 = (bf16[64,1024]{1,0:T(8,128)(2,1)S(1)}, bf16[64,1024]{1,0:T(8,128)(2,1)S(1)}, u32[]{:S(2)}, u32[]{:S(2)}) collective-permute-start(bf16[64,1024]{1,0:T(8,128)(2,1)S(1)} %collective-permute-done.35.p1), channel_id=1, source_target_pairs={{0,2},{2,0},{1,3},{3,1},{4,6},{6,4},{5,7},{7,5},{8,10},{10,8},{9,1... | collective-permute-start | bytes 393224 | tf_op jit(solution)/shard_map/ppermute | solution.py:371
  155.4 16.1 %collective-permute-start.39 = (f32[16,384]{1,0:T(8,128)S(1)}, f32[16,384]{1,0:T(8,128)S(1)}, u32[]{:S(2)}, u32[]{:S(2)}) collective-permute-start(f32[16,384]{1,0:T(8,128)S(1)} %shard_map.263.one), channel_id=1, source_target_pairs={{0,2},{2,0},{1,3},{3,1},{4,6},{6,4},{5,7},{7,5},{8,10},{10,8},{9,1... | collective-permute-start | bytes 73736 | tf_op jit(solution)/shard_map/ppermute | solution.py:371
  (29 other events, 213.3 us)
Sparse Core Ops, SparseCore 0:
  16.8 53.6 all-gather.2
  86.6 42.2 reduce-scatter.1

commit v8 on v7

--- a/solution.py
+++ b/solution.py
@@ -195,20 +195,33 @@
     keep[:, 32:] = partial[:, 0]
 
 
-def feed_weights(hn, dy_own, dy_other, act, dgu, dw):
+def feed_weights(y, hn, dy_own, dy_other, act, dgu, dw):
     dy = jnp.concatenate([dy_own[...], dy_other[...]])
     rows, active = hn[...], act[...]
     def put(left, right, at, width):
         for z in range(2):
             value = left_product(left[:, z * 512 : (z + 1) * 512], right)
             blocks = value.astype(BF).reshape(4, 4, 32, width)
-            for y in range(4):
-                dw[:, z, y, :, at : at + width] = blocks[y]
+            for i in range(4):
+                dw[:, i ^ y[0], z, :, at : at + width] = blocks[i]
     put(rows, dgu[:, :512], 0, 512)
     put(rows, dgu[:, 512:1024], 512, 512)
     put(dy, active[:, :512], 1024, 512)
     put(rows, dgu[:, 1024:], 1536, 128)
     put(dy, active[:, 512:], 1664, 128)
+
+
+def split_sides(dw, own, one, two, three):
+    for k, piece in enumerate((own, one, two, three)):
+        piece[...] = dw[k * 64 : (k + 1) * 64].reshape(2, 32, 1792)
+
+
+def add_sides(zl, own, one, two, three, mine, send):
+    def total(z):
+        first = own[z].astype(F32) + one[z].astype(F32)
+        return first + (two[z].astype(F32) + three[z].astype(F32))
+    mine[...] = total(zl[0])
+    send[...] = total(1 - zl[0]).astype(BF)
 
 
 def hidden_grad(own, one, two, three, h, dy, gain, dh, low, gain_part, block):
@@ -276,9 +289,8 @@
     x = jnp.concatenate([x_own[...], x_other[...]]).astype(F32)
     attn_part = jnp.sum(partial * (x * row_scale(x)), axis=0, keepdims=True)
     def fold(part):
-        rows = [part[:, i * 128 : (i + 1) * 128] for i in range(8)]
-        return jnp.concatenate(rows + [jnp.zeros((8, 128), F32)])
-    heads = jnp.concatenate([heads, jnp.zeros((14, 128), F32)])
+        return jnp.concatenate([part[:, i * 128 : (i + 1) * 128] for i in range(8)])
+    heads = jnp.concatenate([heads, jnp.zeros((6, 128), F32)])
     gains[...] = jnp.concatenate([fold(attn_part), fold(ffn_part), heads], axis=1).astype(BF)
     partial = partial.reshape(4, 2, 32, 1024)
     send[...] = partial[:, 1].astype(BF)
@@ -292,7 +304,7 @@
     second = left_product(d_attn[...], o[...].astype(BF)).astype(BF)
     dw[:, :32, :256] = first.reshape(32, 32, 256)
     dw[:, :32, 256:] = second.reshape(32, 32, 128)
-    dw[:, 32:] = jnp.broadcast_to(gains[...][None], (32, 16, 384))
+    dw[:, 32:] = jnp.broadcast_to(gains[...][None], (32, 8, 384))
 
 
 def token_rows(own, one, two, three, dh, x, gain, block, out):
@@ -314,9 +326,10 @@
     wo[...] = jnp.concatenate([low[:, 256:], high[:, 256:]], axis=1)
 
 
-def finish_feed(parts, wg, wu, wd):
-    low = jnp.sum(parts[0].astype(F32), axis=0)
-    high = jnp.sum(parts[1].astype(F32), axis=0)
+def finish_feed(zl, own, got, wg, wu, wd):
+    mine, its = own[...], got[...].astype(F32)
+    first = zl[0] == 0
+    low, high = jnp.where(first, mine, its), jnp.where(first, its, mine)
     for i, out in enumerate((wg, wu, wd)):
         wide, tail = slice(i * 512, (i + 1) * 512), slice(1536 + i * 64, 1600 + i * 64)
         out[...] = jnp.concatenate(
@@ -469,10 +482,12 @@
         *gather_rows(hn), dy_own, dy_other, w_f,
     )
     pair = sum_pair(send, keep)
+    pair = sum_pair(send, keep)
     act, dgu = after([act, dgu], *pair)
     d_hn = [pair[0]] + fan([None] + pair[1:], Z)
     (dw_f,) = call(
-        feed_weights, [Far(((4, 2, 4, 32, 1792), BF))], hn_all, dy_own, dy_other, act, dgu
+        feed_weights, [Far(((4, 4, 2, 32, 1792), BF))], hn_all, dy_own, dy_other, act, dgu,
+        scalars=(y.reshape(1),),
     )
     dw_f = lax.psum_scatter(dw_f.reshape(1024, 1792), "x", scatter_dimension=0, tiled=True)
     dh, d_low, ffn_part, block = call(
@@ -484,39 +499,44 @@
         *gather_rows(d_low), Far(qh), *[Far(t) for t in kvs], own_places, places, Far(w_a), Far(o), Far(l),
     )
     d_qkv, send, keep, gains = call(
-        project_grad, [((256, 256), BF)] + halves + [((16, 384), BF)],
+        project_grad, [((256, 256), BF)] + halves + [((8, 384), BF)],
         d_qh, d_kvs[0], *fan(d_kvs, "y"), Far(qkv), cosine, sine, qk_gain, Far(w_a),
         Far(x_own), Far(x_other), Far(ffn_part),
     )
     (dw_a,) = call(
-        attend_weights, [((32, 48, 384), BF)],
+        attend_weights, [((32, 40, 384), BF)],
         Far(x_own), Far(x_other), attn_gain_row, d_qkv, Far(d_attn), Far(o), gains,
     )
     own, *rest = sum_pair(send, keep)
-    (dw_a,) = after([dw_a], own)
+    d_xn = [own] + fan([None] + rest, Z)
+    (dw_a,) = after([dw_a], *d_xn)
     dw_a = lax.all_to_all(dw_a, PLANE, 0, 0, tiled=True)
-    d_xn = [own] + fan([None] + rest, Z)
     (rows,) = call(
         token_rows, [((64, 1024), BF)], *d_xn, Far(dh), x_own, attn_gain_row, Far(block)
     )
     tokens_grad, block_out = gather_head(rows, head)
     tokens_grad, block_out = tokens_grad[None], block_out[None]
 
-    (dw_a,) = after([dw_a], rows)
+    (dw_a,) = after([dw_a], tokens_grad)
     grad_wq, grad_wk, grad_wv, grad_wo, gains = call(
         finish_attend,
-        [Far(((32, n), F32)) for n in (256, 128, 128, 256)] + [((16, 384), F32)],
-        dw_a.reshape(2, 16, 48, 384),
-    )
-    (gains,) = call(add_two, [((16, 384), F32)], gains, swap(gains, "c", 2, 1))
-    (dw_f,) = after([dw_f], gains)
-    dw_f = lax.all_to_all(dw_f, ("zl", "y"), 0, 0, tiled=True)
+        [Far(((32, n), F32)) for n in (256, 128, 128, 256)] + [((8, 384), F32)],
+        dw_a.reshape(2, 16, 40, 384),
+    )
+    (gains,) = call(add_two, [((8, 384), F32)], gains, swap(gains, "c", 2, 1))
     attn_sum, ffn_sum, query_sum, key_sum = call(
         finish_gains, [((8, 128), F32)] * 2 + [((1, 64), F32)] * 2,
         gains, swap(gains, "zh", 2, 1),
     )
+    sides = call(split_sides, [((2, 32, 1792), BF)] * 4, Far(dw_f))
+    others = after(fan(sides, "y"), gains)
+    own_f, send_f = call(
+        add_sides, [((32, 1792), F32), ((32, 1792), BF)], sides[0], *others,
+        scalars=(zl_ref,),
+    )
     grad_wg, grad_wu, grad_wd = call(
-        finish_feed, [Far(((32, 1152), F32))] * 3, dw_f.reshape(2, 4, 32, 1792)
+        finish_feed, [Far(((32, 1152), F32))] * 3, own_f, swap(send_f, "zl", 2, 1),
+        scalars=(zl_ref,),
     )
     return (
         block_out, tokens_grad, attn_sum.reshape(1024), ffn_sum.reshape(1024),

time: 181 us -> 175 us (0.967)
  waiting for transfers between devices: 69.1 us -> 59.1 us
  starting transfers between devices: 62.2 us -> 65.1 us
    ppermute x40 -> x44, waiting for transfers between devices: 68.5 us -> 59.1 us  [swap(): return lax.ppermute(value, axes, [(i, i ^ mask) for i in range(size)])]
    ppermute x40 -> x44, starting transfers between devices: 43.9 us -> 50.5 us  [swap(): return lax.ppermute(value, axes, [(i, i ^ mask) for i in range(size)])]
    all_to_all x1 -> x0, starting transfers between devices: 3.69 us -> none  [local(): dw_f = lax.all_to_all(dw_f, ('zl', 'y'), 0, 0, tiled=True)]
    unnamed x32 -> x38, local copies, waits for them, and re-layouts: 9.17 us -> 11 us
    pallas_call x21 -> x23, Pallas kernels: 19.2 us -> 18.8 us  [call(): pl.pallas_call(body, out_shape=[jax.ShapeDtypeStruct(*bare(out)) for out...]
  transfers between devices with their start and end apart: 45 -> 48, of which waited for: 27 -> 29; matrix products, arithmetic and copies ran while one was open for 3% -> 3% of each run, Pallas kernels for 6% -> 6%
where the time goes in v8:
time: 175 us; the launch traced here: 174 us
  starting transfers between devices  65.1 us (37%)
  waiting for transfers between devices  59.1 us (34%)
  Pallas kernels  18.8 us (11%)
  between operations  14.4 us (8%)
  local copies, waits for them, and re-layouts  13.9 us (8%)
  other arithmetic  2.85 us (2%)
    ppermute x44, waiting for transfers between devices, swap(): return lax.ppermute(value, axes, [(i, i ^ mask) for i in range(size)])  59.1 us
    ppermute x44, starting transfers between devices, swap(): return lax.ppermute(value, axes, [(i, i ^ mask) for i in range(size)])  50.5 us
    pallas_call x23, Pallas kernels, call(): pl.pallas_call(body, out_shape=[jax.ShapeDtypeStruct(*bare(out)) for out...  18.8 us
    unnamed x38, local copies, waits for them, and re-layouts  11 us
    all_to_all x1, starting transfers between devices, local(): w_a = lax.all_to_all(blocks.reshape(1024, 384), PLANE, 0, 0, tiled=True)  8.51 us
    all_to_all x1, starting transfers between devices, local(): dw_a = lax.all_to_all(dw_a, PLANE, 0, 0, tiled=True)  6 us
  transfers between devices with their start and end apart: 48, of which 29 were waited for; matrix products, arithmetic and copies ran while one was open for 3% of the time, Pallas kernels for 6%

profile of v8, /device:TPU:0, one launch (start us, length us, event | category | flops | bytes accessed | tf_op | source)
XLA Modules:
  0.0 174.1 jit_solution(9130328405826209171)
XLA Ops:
  7.3 2.3 %shard_map.246 = (bf16[2,16,32,384]{3,2,1,0:T(8,128)(2,1)}, bf16[32,1792]{1,0:T(8,128)(2,1)}, bf16[32,1792]{1,0:T(8,128)(2,1)}, bf16[128,1024]{1,0:T(8,128)(2,1)}) custom-call(s32[1]{0:T(128)} %bitcast.1.zl, s32[1]{0:T(128)} %bitcast.head, bf16[32,256]{1,0:T(8,128)(2,1)} %wq.1, bf16[32,128]{1,0:T(8,128)(2,1)} %wk.1, bf16[32,128]{1,0:T(8,128)(2,1)} %wv.1, ...), custom_call_target="tpu_custom_call" | custom-call | tf_op jit(solution)/shard_map/pallas_call | solution.py:37
  9.6 2.1 %collective-permute-start.16 = (bf16[32,1792]{1,0:T(8,128)(2,1)}, bf16[32,1792]{1,0:T(8,128)(2,1)S(1)}, u32[]{:S(2)}, u32[]{:S(2)}) collective-permute-start(bf16[32,1792]{1,0:T(8,128)(2,1)} %get-tuple-element.102), channel_id=1, source_target_pairs={{0,64},{64,0},{1,65},{65,1},{2,66},{66,2},{3,67},{67,3},{4,68},{68... | collective-permute-start | bytes 344072 | tf_op jit(solution)/shard_map/ppermute | solution.py:384
  11.7 3.4 %collective-permute-done.16.got = bf16[32,1792]{1,0:T(8,128)(2,1)S(1)} collective-permute-done((bf16[32,1792]{1,0:T(8,128)(2,1)}, bf16[32,1792]{1,0:T(8,128)(2,1)S(1)}, u32[]{:S(2)}, u32[]{:S(2)}) %collective-permute-start.16) | collective-permute-done | bytes 114720 | tf_op jit(solution)/shard_map/ppermute | solution.py:384
  16.6 8.5 %all-to-all-start = ((bf16[32,32,384]{2,1,0:T(8,128)(2,1)}), bf16[32,32,384]{2,1,0:T(8,128)(2,1)S(1)}, u32[]{:S(2)}, u32[]{:S(2)}) async-start(bf16[32,32,384]{2,1,0:T(8,128)(2,1)} %bitcast.28), calls=%async_computation | async-start | bytes 1572864 | tf_op jit(solution)/shard_map/all_to_all | solution.py:444
  25.2 1.9 %collective-permute-start = (bf16[128,1024]{1,0:T(8,128)(2,1)}, bf16[128,1024]{1,0:T(8,128)(2,1)S(1)}, u32[]{:S(2)}, u32[]{:S(2)}) collective-permute-start(bf16[128,1024]{1,0:T(8,128)(2,1)} %get-tuple-element.87.own.x.x_own), channel_id=1, source_target_pairs={{0,64},{64,0},{1,65},{65,1},{2,66},{66,2},{3,67},{67,3},{4,68},{68... | collective-permute-start | bytes 786440 | tf_op jit(solution)/shard_map/ppermute | solution.py:384
  32.7 7.9 %collective-permute-done.other.x_other = bf16[128,1024]{1,0:T(8,128)(2,1)S(1)} collective-permute-done((bf16[128,1024]{1,0:T(8,128)(2,1)}, bf16[128,1024]{1,0:T(8,128)(2,1)S(1)}, u32[]{:S(2)}, u32[]{:S(2)}) %collective-permute-start) | collective-permute-done | bytes 262176 | tf_op jit(solution)/shard_map/ppermute | solution.py:384
  42.7 2.2 %collective-permute-start.4 = (bf16[256,128]{1,0:T(8,128)(2,1)S(1)}, bf16[256,128]{1,0:T(8,128)(2,1)S(1)}, u32[]{:S(2)}, u32[]{:S(2)}) collective-permute-start(bf16[256,128]{1,0:T(8,128)(2,1)S(1)} %get-tuple-element.91.kv0), channel_id=1, source_target_pairs={{0,48},{16,32},{32,16},{48,0},{1,49},{17,33},{33,17},{49,1},{2,50}... | collective-permute-start | bytes 196616 | tf_op jit(solution)/shard_map/ppermute | solution.py:384
  48.9 1.8 %collective-permute-done.3.kv2 = bf16[256,128]{1,0:T(8,128)(2,1)S(1)} collective-permute-done((bf16[256,128]{1,0:T(8,128)(2,1)S(1)}, bf16[256,128]{1,0:T(8,128)(2,1)S(1)}, u32[]{:S(2)}, u32[]{:S(2)}) %collective-permute-start.3) | collective-permute-done | bytes 65568 | tf_op jit(solution)/shard_map/ppermute | solution.py:384
  53.7 3.6 %collective-permute-start.6 = (bf16[32,1024]{1,0:T(8,128)(2,1)S(1)}, bf16[32,1024]{1,0:T(8,128)(2,1)S(1)}, u32[]{:S(2)}, u32[]{:S(2)}) collective-permute-start(bf16[32,1024]{1,0:T(8,128)(2,1)S(1)} %get-tuple-element.97), channel_id=1, source_target_pairs={{0,2},{2,0},{64,66},{66,64},{1,3},{3,1},{65,67},{67,65},{4,6},{6,4... | collective-permute-start | bytes 196616 | tf_op jit(solution)/shard_map/ppermute | solution.py:384
  58.0 2.0 %collective-permute-done.6.one = bf16[32,1024]{1,0:T(8,128)(2,1)S(1)} collective-permute-done((bf16[32,1024]{1,0:T(8,128)(2,1)S(1)}, bf16[32,1024]{1,0:T(8,128)(2,1)S(1)}, u32[]{:S(2)}, u32[]{:S(2)}) %collective-permute-start.6) | collective-permute-done | bytes 65568 | tf_op jit(solution)/shard_map/ppermute | solution.py:384
  64.6 3.8 %collective-permute-start.10 = (bf16[32,1024]{1,0:T(8,128)(2,1)S(1)}, bf16[32,1024]{1,0:T(8,128)(2,1)S(1)}, u32[]{:S(2)}, u32[]{:S(2)}) collective-permute-start(bf16[32,1024]{1,0:T(8,128)(2,1)S(1)} %get-tuple-element.100.p0), channel_id=1, source_target_pairs={{0,2},{2,0},{64,66},{66,64},{1,3},{3,1},{65,67},{67,65},{4,6},{6,4... | collective-permute-start | bytes 196616 | tf_op jit(solution)/shard_map/ppermute | solution.py:384
  73.2 2.0 %copy-done.2 = bf16[32,32,1792]{2,1,0:T(8,128)(2,1)S(1)} copy-done((bf16[32,32,1792]{2,1,0:T(8,128)(2,1)S(1)}, bf16[32,32,1792]{2,1,0:T(8,128)(2,1)}, u32[]{:S(2)}) %copy-start.2) | copy-done | bytes 3670040
  77.7 2.6 %shard_map.253 = (bf16[4,64,1024]{2,1,0:T(8,128)(2,1)S(1)}, f32[4,64,1024]{2,1,0:T(8,128)S(1)}, bf16[256,1024]{1,0:T(8,128)(2,1)S(1)}, bf16[256,640]{1,0:T(8,128)(2,1)S(1)}, bf16[256,1152]{1,0:T(8,128)(2,1)S(1)}) custom-call(bf16[32,1024]{1,0:T(8,128)(2,1)S(1)} %get-tuple-element.100.p0, bf16[32,1024]{1,0:T(8,128)(2,1)S(1)} %collective-permute-done.9.p1, ...), custom_call_target="tpu_custom_call" | custom-call | tf_op jit(solution)/shard_map/pallas_call | solution.py:37
  84.7 1.8 %copy-done = bf16[4,4,2,32,1792]{4,3,2,1,0:T(8,128)(2,1)} copy-done((bf16[4,4,2,32,1792]{4,3,2,1,0:T(8,128)(2,1)}, bf16[4,4,2,32,1792]{4,3,2,1,0:T(8,128)(2,1)S(1)}, u32[]{:S(2)}) %copy-start) | copy-done | bytes 3670040
  86.6 2.9 %collective-permute-start.18 = (bf16[64,1024]{1,0:T(8,128)(2,1)}, bf16[64,1024]{1,0:T(8,128)(2,1)S(1)}, u32[]{:S(2)}, u32[]{:S(2)}) collective-permute-start(bf16[64,1024]{1,0:T(8,128)(2,1)} %copy-done.18), channel_id=1, source_target_pairs={{0,2},{2,0},{64,66},{66,64},{1,3},{3,1},{65,67},{67,65},{4,6},{6,4... | collective-permute-start | bytes 393224 | tf_op jit(solution)/shard_map/ppermute | solution.py:384
  90.9 3.8 %collective-permute-done.18.one = bf16[64,1024]{1,0:T(8,128)(2,1)S(1)} collective-permute-done((bf16[64,1024]{1,0:T(8,128)(2,1)}, bf16[64,1024]{1,0:T(8,128)(2,1)S(1)}, u32[]{:S(2)}, u32[]{:S(2)}) %collective-permute-start.18) | collective-permute-done | bytes 131104 | tf_op jit(solution)/shard_map/ppermute | solution.py:384
  100.0 1.9 %collective-permute-start.22 = (bf16[32,1024]{1,0:T(8,128)(2,1)S(1)}, bf16[32,1024]{1,0:T(8,128)(2,1)S(1)}, u32[]{:S(2)}, u32[]{:S(2)}) collective-permute-start(bf16[32,1024]{1,0:T(8,128)(2,1)S(1)} %get-tuple-element.110.p0), channel_id=1, source_target_pairs={{0,2},{2,0},{64,66},{66,64},{1,3},{3,1},{65,67},{67,65},{4,6},{6,4... | collective-permute-start | bytes 196616 | tf_op jit(solution)/shard_map/ppermute | solution.py:384
  103.3 2.5 %collective-permute-done.22.p2 = bf16[32,1024]{1,0:T(8,128)(2,1)S(1)} collective-permute-done((bf16[32,1024]{1,0:T(8,128)(2,1)S(1)}, bf16[32,1024]{1,0:T(8,128)(2,1)S(1)}, u32[]{:S(2)}, u32[]{:S(2)}) %collective-permute-start.22) | collective-permute-done | bytes 65568 | tf_op jit(solution)/shard_map/ppermute | solution.py:384
  107.1 3.1 %shard_map.256 = (bf16[256,1024]{1,0:T(8,128)(2,1)S(1)}, f32[256,128]{1,0:T(8,128)S(1)}, f32[256,128]{1,0:T(8,128)S(1)}, bf16[256,128]{1,0:T(8,128)(2,1)S(1)}, b...) custom-call(bf16[32,1024]{1,0:T(8,128)(2,1)S(1)} %get-tuple-element.110.p0, ...), custom_call_target="tpu_custom_call" | custom-call | tf_op jit(solution)/shard_map/pallas_call | solution.py:37
  110.4 2.6 %collective-permute-start.29 = (bf16[256,128]{1,0:T(8,128)(2,1)S(1)}, bf16[256,128]{1,0:T(8,128)(2,1)S(1)}, u32[]{:S(2)}, u32[]{:S(2)}) collective-permute-start(bf16[256,128]{1,0:T(8,128)(2,1)S(1)} %get-tuple-element.116), channel_id=1, source_target_pairs={{0,32},{16,48},{32,0},{48,16},{1,33},{17,49},{33,1},{49,17},{2,34}... | collective-permute-start | bytes 196616 | tf_op jit(solution)/shard_map/ppermute | solution.py:384
  113.0 2.0 %collective-permute-start.30 = (bf16[256,128]{1,0:T(8,128)(2,1)S(1)}, bf16[256,128]{1,0:T(8,128)(2,1)S(1)}, u32[]{:S(2)}, u32[]{:S(2)}) collective-permute-start(bf16[256,128]{1,0:T(8,128)(2,1)S(1)} %get-tuple-element.117), channel_id=1, source_target_pairs={{0,48},{16,32},{32,16},{48,0},{1,49},{17,33},{33,17},{49,1},{2,50}... | collective-permute-start | bytes 196616 | tf_op jit(solution)/shard_map/ppermute | solution.py:384
  116.7 1.8 %collective-permute-done.30.three = bf16[256,128]{1,0:T(8,128)(2,1)S(1)} collective-permute-done((bf16[256,128]{1,0:T(8,128)(2,1)S(1)}, bf16[256,128]{1,0:T(8,128)(2,1)S(1)}, u32[]{:S(2)}, u32[]{:S(2)}) %collective-permute-start.30) | collective-permute-done | bytes 65568 | tf_op jit(solution)/shard_map/ppermute | solution.py:384
  121.2 2.0 %collective-permute-start.32 = (bf16[32,1024]{1,0:T(8,128)(2,1)S(1)}, bf16[32,1024]{1,0:T(8,128)(2,1)S(1)}, u32[]{:S(2)}, u32[]{:S(2)}) collective-permute-start(bf16[32,1024]{1,0:T(8,128)(2,1)S(1)} %get-tuple-element.123), channel_id=1, source_target_pairs={{0,2},{2,0},{64,66},{66,64},{1,3},{3,1},{65,67},{67,65},{4,6},{6,4... | collective-permute-start | bytes 196616 | tf_op jit(solution)/shard_map/ppermute | solution.py:384
  123.4 2.0 %collective-permute-start.34 = (bf16[32,1024]{1,0:T(8,128)(2,1)S(1)}, bf16[32,1024]{1,0:T(8,128)(2,1)S(1)}, u32[]{:S(2)}, u32[]{:S(2)}) collective-permute-start(bf16[32,1024]{1,0:T(8,128)(2,1)S(1)} %get-tuple-element.125), channel_id=1, source_target_pairs={{0,66},{2,64},{64,2},{66,0},{1,67},{3,65},{65,3},{67,1},{4,70},{6,... | collective-permute-start | bytes 196616 | tf_op jit(solution)/shard_map/ppermute | solution.py:384
  128.8 6.0 %all-to-all-start.1 = ((bf16[32,40,384]{2,1,0:T(8,128)(2,1)}), bf16[32,40,384]{2,1,0:T(8,128)(2,1)S(1)}, u32[]{:S(2)}, u32[]{:S(2)}) async-start(bf16[32,40,384]{2,1,0:T(8,128)(2,1)} %shard_map.261), calls=%async_computation.1 | async-start | bytes 1966080 | tf_op jit(solution)/shard_map/all_to_all | solution.py:513
  136.4 1.9 %collective-permute-start.40 = (bf16[2,32,1792]{2,1,0:T(8,128)(2,1)S(1)}, bf16[2,32,1792]{2,1,0:T(8,128)(2,1)S(1)}, u32[]{:S(2)}, u32[]{:S(2)}) collective-permute-start(bf16[2,32,1792]{2,1,0:T(8,128)(2,1)S(1)} %get-tuple-element.150), channel_id=1, source_target_pairs={{0,16},{16,0},{32,48},{48,32},{1,17},{17,1},{33,49},{49,33},{2,18}... | collective-permute-start | bytes 688136 | tf_op jit(solution)/shard_map/ppermute | solution.py:384
  138.3 2.7 %collective-permute-start.41 = (bf16[2,32,1792]{2,1,0:T(8,128)(2,1)S(1)}, bf16[2,32,1792]{2,1,0:T(8,128)(2,1)S(1)}, u32[]{:S(2)}, u32[]{:S(2)}) collective-permute-start(bf16[2,32,1792]{2,1,0:T(8,128)(2,1)S(1)} %get-tuple-element.151), channel_id=1, source_target_pairs={{0,32},{16,48},{32,0},{48,16},{1,33},{17,49},{33,1},{49,17},{2,34}... | collective-permute-start | bytes 688136 | tf_op jit(solution)/shard_map/ppermute | solution.py:384
  141.2 2.8 %collective-permute-start.36 = (bf16[64,1024]{1,0:T(8,128)(2,1)S(1)}, bf16[64,1024]{1,0:T(8,128)(2,1)S(1)}, u32[]{:S(2)}, u32[]{:S(2)}) collective-permute-start(bf16[64,1024]{1,0:T(8,128)(2,1)S(1)} %shard_map.259.p0), channel_id=1, source_target_pairs={{0,2},{2,0},{1,3},{3,1},{4,6},{6,4},{5,7},{7,5},{8,10},{10,8},{9,1... | collective-permute-start | bytes 393224 | tf_op jit(solution)/shard_map/ppermute | solution.py:384
  144.7 7.8 %collective-permute-done.36.p2 = bf16[64,1024]{1,0:T(8,128)(2,1)S(1)} collective-permute-done((bf16[64,1024]{1,0:T(8,128)(2,1)S(1)}, bf16[64,1024]{1,0:T(8,128)(2,1)S(1)}, u32[]{:S(2)}, u32[]{:S(2)}) %collective-permute-start.36) | collective-permute-done | bytes 131104 | tf_op jit(solution)/shard_map/ppermute | solution.py:384
  152.6 2.7 %collective-permute-done.37.p3 = bf16[64,1024]{1,0:T(8,128)(2,1)S(1)} collective-permute-done((bf16[64,1024]{1,0:T(8,128)(2,1)S(1)}, bf16[64,1024]{1,0:T(8,128)(2,1)S(1)}, u32[]{:S(2)}, u32[]{:S(2)}) %collective-permute-start.37) | collective-permute-done | bytes 131104 | tf_op jit(solution)/shard_map/ppermute | solution.py:384
  160.3 2.6 %collective-permute-start.39 = (f32[8,384]{1,0:T(8,128)S(1)}, f32[8,384]{1,0:T(8,128)S(1)}, u32[]{:S(2)}, u32[]{:S(2)}) collective-permute-start(f32[8,384]{1,0:T(8,128)S(1)} %shard_map.263.one), channel_id=1, source_target_pairs={{0,2},{2,0},{1,3},{3,1},{4,6},{6,4},{5,7},{7,5},{8,10},{10,8},{9,1... | collective-permute-start | bytes 36872 | tf_op jit(solution)/shard_map/ppermute | solution.py:384
  162.9 2.9 %collective-permute-done.39.two = f32[8,384]{1,0:T(8,128)S(1)} collective-permute-done((f32[8,384]{1,0:T(8,128)S(1)}, f32[8,384]{1,0:T(8,128)S(1)}, u32[]{:S(2)}, u32[]{:S(2)}) %collective-permute-start.39) | collective-permute-done | bytes 12320 | tf_op jit(solution)/shard_map/ppermute | solution.py:384
  (145 shorter events, 59.8 us)
Async XLA Ops:
  7.2 66.0 %all-gather.3.cloned.1.call-start = ((), (), s32[]{:S(2)}) async-start(), calls=%async_computation.4 | async-start | bytes 3899392 | tf_op jit(solution)/shard_map/all_gather | solution.py:446
  9.6 5.4 %collective-permute-start.16 = (bf16[32,1792]{1,0:T(8,128)(2,1)}, bf16[32,1792]{1,0:T(8,128)(2,1)S(1)}, u32[]{:S(2)}, u32[]{:S(2)}) collective-permute-start(bf16[32,1792]{1,0:T(8,128)(2,1)} %get-tuple-element.102), channel_id=1, source_target_pairs={{0,64},{64,0},{1,65},{65,1},{2,66},{66,2},{3,67},{67,3},{4,68},{68... | collective-permute-start | bytes 344072 | tf_op jit(solution)/shard_map/ppermute | solution.py:384
  16.6 23.9 %all-to-all-start = ((bf16[32,32,384]{2,1,0:T(8,128)(2,1)}), bf16[32,32,384]{2,1,0:T(8,128)(2,1)S(1)}, u32[]{:S(2)}, u32[]{:S(2)}) async-start(bf16[32,32,384]{2,1,0:T(8,128)(2,1)} %bitcast.28), calls=%async_computation | async-start | bytes 1572864 | tf_op jit(solution)/shard_map/all_to_all | solution.py:444
  25.2 110.0 %reduce-scatter.2.cloned.1.call-start = ((), (), s32[]{:S(2)}) async-start(), calls=%async_computation.3 | async-start | bytes 4587520 | tf_op jit(solution)/shard_map/reduce_scatter | solution.py:492
  25.2 15.4 %collective-permute-start = (bf16[128,1024]{1,0:T(8,128)(2,1)}, bf16[128,1024]{1,0:T(8,128)(2,1)S(1)}, u32[]{:S(2)}, u32[]{:S(2)}) collective-permute-start(bf16[128,1024]{1,0:T(8,128)(2,1)} %get-tuple-element.87.own.x.x_own), channel_id=1, source_target_pairs={{0,64},{64,0},{1,65},{65,1},{2,66},{66,2},{3,67},{67,3},{4,68},{68... | collective-permute-start | bytes 786440 | tf_op jit(solution)/shard_map/ppermute | solution.py:384
  41.3 6.9 %collective-permute-start.1 = (bf16[128,1024]{1,0:T(8,128)(2,1)S(1)}, bf16[128,1024]{1,0:T(8,128)(2,1)S(1)}, u32[]{:S(2)}, u32[]{:S(2)}) collective-permute-start(bf16[128,1024]{1,0:T(8,128)(2,1)S(1)} %shard_map.248.dy_own.dy), channel_id=1, source_target_pairs={{0,64},{64,0},{1,65},{65,1},{2,66},{66,2},{3,67},{67,3},{4,68},{68... | collective-permute-start | bytes 786440 | tf_op jit(solution)/shard_map/ppermute | solution.py:384
  42.7 6.2 %collective-permute-start.4 = (bf16[256,128]{1,0:T(8,128)(2,1)S(1)}, bf16[256,128]{1,0:T(8,128)(2,1)S(1)}, u32[]{:S(2)}, u32[]{:S(2)}) collective-permute-start(bf16[256,128]{1,0:T(8,128)(2,1)S(1)} %get-tuple-element.91.kv0), channel_id=1, source_target_pairs={{0,48},{16,32},{32,16},{48,0},{1,49},{17,33},{33,17},{49,1},{2,50}... | collective-permute-start | bytes 196616 | tf_op jit(solution)/shard_map/ppermute | solution.py:384
  44.9 5.8 %collective-permute-start.3 = (bf16[256,128]{1,0:T(8,128)(2,1)S(1)}, bf16[256,128]{1,0:T(8,128)(2,1)S(1)}, u32[]{:S(2)}, u32[]{:S(2)}) collective-permute-start(bf16[256,128]{1,0:T(8,128)(2,1)S(1)} %get-tuple-element.91.kv0), channel_id=1, source_target_pairs={{0,32},{16,48},{32,0},{48,16},{1,33},{17,49},{33,1},{49,17},{2,34}... | collective-permute-start | bytes 196616 | tf_op jit(solution)/shard_map/ppermute | solution.py:384
  53.7 6.3 %collective-permute-start.6 = (bf16[32,1024]{1,0:T(8,128)(2,1)S(1)}, bf16[32,1024]{1,0:T(8,128)(2,1)S(1)}, u32[]{:S(2)}, u32[]{:S(2)}) collective-permute-start(bf16[32,1024]{1,0:T(8,128)(2,1)S(1)} %get-tuple-element.97), channel_id=1, source_target_pairs={{0,2},{2,0},{64,66},{66,64},{1,3},{3,1},{65,67},{67,65},{4,6},{6,4... | collective-permute-start | bytes 196616 | tf_op jit(solution)/shard_map/ppermute | solution.py:384
  57.9 5.5 %collective-permute-start.8 = (bf16[32,1024]{1,0:T(8,128)(2,1)S(1)}, bf16[32,1024]{1,0:T(8,128)(2,1)S(1)}, u32[]{:S(2)}, u32[]{:S(2)}) collective-permute-start(bf16[32,1024]{1,0:T(8,128)(2,1)S(1)} %get-tuple-element.99), channel_id=1, source_target_pairs={{0,66},{2,64},{64,2},{66,0},{1,67},{3,65},{65,3},{67,1},{4,70},{6,... | collective-permute-start | bytes 196616 | tf_op jit(solution)/shard_map/ppermute | solution.py:384
  63.6 6.0 %collective-permute-start.14 = (bf16[32,1024]{1,0:T(8,128)(2,1)S(1)}, bf16[32,1024]{1,0:T(8,128)(2,1)S(1)}, u32[]{:S(2)}, u32[]{:S(2)}) collective-permute-start(bf16[32,1024]{1,0:T(8,128)(2,1)S(1)} %get-tuple-element.100.p0), channel_id=1, source_target_pairs={{0,66},{2,64},{64,2},{66,0},{1,67},{3,65},{65,3},{67,1},{4,70},{6,... | collective-permute-start | bytes 196616 | tf_op jit(solution)/shard_map/ppermute | solution.py:384
  64.3 5.2 %collective-permute-start.12 = (bf16[32,1024]{1,0:T(8,128)(2,1)S(1)}, bf16[32,1024]{1,0:T(8,128)(2,1)S(1)}, u32[]{:S(2)}, u32[]{:S(2)}) collective-permute-start(bf16[32,1024]{1,0:T(8,128)(2,1)S(1)} %get-tuple-element.100.p0), channel_id=1, source_target_pairs={{0,64},{2,66},{64,0},{66,2},{1,65},{3,67},{65,1},{67,3},{4,68},{6,... | collective-permute-start | bytes 196616 | tf_op jit(solution)/shard_map/ppermute | solution.py:384
  64.6 6.7 %collective-permute-start.10 = (bf16[32,1024]{1,0:T(8,128)(2,1)S(1)}, bf16[32,1024]{1,0:T(8,128)(2,1)S(1)}, u32[]{:S(2)}, u32[]{:S(2)}) collective-permute-start(bf16[32,1024]{1,0:T(8,128)(2,1)S(1)} %get-tuple-element.100.p0), channel_id=1, source_target_pairs={{0,2},{2,0},{64,66},{66,64},{1,3},{3,1},{65,67},{67,65},{4,6},{6,4... | collective-permute-start | bytes 196616 | tf_op jit(solution)/shard_map/ppermute | solution.py:384
  86.6 8.1 %collective-permute-start.18 = (bf16[64,1024]{1,0:T(8,128)(2,1)}, bf16[64,1024]{1,0:T(8,128)(2,1)S(1)}, u32[]{:S(2)}, u32[]{:S(2)}) collective-permute-start(bf16[64,1024]{1,0:T(8,128)(2,1)} %copy-done.18), channel_id=1, source_target_pairs={{0,2},{2,0},{64,66},{66,64},{1,3},{3,1},{65,67},{67,65},{4,6},{6,4... | collective-permute-start | bytes 393224 | tf_op jit(solution)/shard_map/ppermute | solution.py:384
  89.5 6.3 %collective-permute-start.19 = (bf16[64,1024]{1,0:T(8,128)(2,1)S(1)}, bf16[64,1024]{1,0:T(8,128)(2,1)S(1)}, u32[]{:S(2)}, u32[]{:S(2)}) collective-permute-start(bf16[64,1024]{1,0:T(8,128)(2,1)S(1)} %copy-done.17), channel_id=1, source_target_pairs={{0,64},{2,66},{64,0},{66,2},{1,65},{3,67},{65,1},{67,3},{4,68},{6,... | collective-permute-start | bytes 393224 | tf_op jit(solution)/shard_map/ppermute | solution.py:384
  89.5 7.4 %collective-permute-start.20 = (bf16[64,1024]{1,0:T(8,128)(2,1)S(1)}, bf16[64,1024]{1,0:T(8,128)(2,1)S(1)}, u32[]{:S(2)}, u32[]{:S(2)}) collective-permute-start(bf16[64,1024]{1,0:T(8,128)(2,1)S(1)} %copy-done.15), channel_id=1, source_target_pairs={{0,66},{2,64},{64,2},{66,0},{1,67},{3,65},{65,3},{67,1},{4,70},{6,... | collective-permute-start | bytes 393224 | tf_op jit(solution)/shard_map/ppermute | solution.py:384
  97.2 5.6 %collective-permute-start.26 = (bf16[32,1024]{1,0:T(8,128)(2,1)S(1)}, bf16[32,1024]{1,0:T(8,128)(2,1)S(1)}, u32[]{:S(2)}, u32[]{:S(2)}) collective-permute-start(bf16[32,1024]{1,0:T(8,128)(2,1)S(1)} %get-tuple-element.110.p0), channel_id=1, source_target_pairs={{0,66},{2,64},{64,2},{66,0},{1,67},{3,65},{65,3},{67,1},{4,70},{6,... | collective-permute-start | bytes 196616 | tf_op jit(solution)/shard_map/ppermute | solution.py:384
  100.0 5.8 %collective-permute-start.22 = (bf16[32,1024]{1,0:T(8,128)(2,1)S(1)}, bf16[32,1024]{1,0:T(8,128)(2,1)S(1)}, u32[]{:S(2)}, u32[]{:S(2)}) collective-permute-start(bf16[32,1024]{1,0:T(8,128)(2,1)S(1)} %get-tuple-element.110.p0), channel_id=1, source_target_pairs={{0,2},{2,0},{64,66},{66,64},{1,3},{3,1},{65,67},{67,65},{4,6},{6,4... | collective-permute-start | bytes 196616 | tf_op jit(solution)/shard_map/ppermute | solution.py:384
  110.2 4.8 %collective-permute-start.28 = (bf16[256,128]{1,0:T(8,128)(2,1)S(1)}, bf16[256,128]{1,0:T(8,128)(2,1)S(1)}, u32[]{:S(2)}, u32[]{:S(2)}) collective-permute-start(bf16[256,128]{1,0:T(8,128)(2,1)S(1)} %get-tuple-element.115), channel_id=1, source_target_pairs={{0,16},{16,0},{32,48},{48,32},{1,17},{17,1},{33,49},{49,33},{2,18}... | collective-permute-start | bytes 196616 | tf_op jit(solution)/shard_map/ppermute | solution.py:384
  110.4 6.2 %collective-permute-start.29 = (bf16[256,128]{1,0:T(8,128)(2,1)S(1)}, bf16[256,128]{1,0:T(8,128)(2,1)S(1)}, u32[]{:S(2)}, u32[]{:S(2)}) collective-permute-start(bf16[256,128]{1,0:T(8,128)(2,1)S(1)} %get-tuple-element.116), channel_id=1, source_target_pairs={{0,32},{16,48},{32,0},{48,16},{1,33},{17,49},{33,1},{49,17},{2,34}... | collective-permute-start | bytes 196616 | tf_op jit(solution)/shard_map/ppermute | solution.py:384
  113.0 5.5 %collective-permute-start.30 = (bf16[256,128]{1,0:T(8,128)(2,1)S(1)}, bf16[256,128]{1,0:T(8,128)(2,1)S(1)}, u32[]{:S(2)}, u32[]{:S(2)}) collective-permute-start(bf16[256,128]{1,0:T(8,128)(2,1)S(1)} %get-tuple-element.117), channel_id=1, source_target_pairs={{0,48},{16,32},{32,16},{48,0},{1,49},{17,33},{33,17},{49,1},{2,50}... | collective-permute-start | bytes 196616 | tf_op jit(solution)/shard_map/ppermute | solution.py:384
  121.2 6.5 %collective-permute-start.32 = (bf16[32,1024]{1,0:T(8,128)(2,1)S(1)}, bf16[32,1024]{1,0:T(8,128)(2,1)S(1)}, u32[]{:S(2)}, u32[]{:S(2)}) collective-permute-start(bf16[32,1024]{1,0:T(8,128)(2,1)S(1)} %get-tuple-element.123), channel_id=1, source_target_pairs={{0,2},{2,0},{64,66},{66,64},{1,3},{3,1},{65,67},{67,65},{4,6},{6,4... | collective-permute-start | bytes 196616 | tf_op jit(solution)/shard_map/ppermute | solution.py:384
  123.4 5.5 %collective-permute-start.34 = (bf16[32,1024]{1,0:T(8,128)(2,1)S(1)}, bf16[32,1024]{1,0:T(8,128)(2,1)S(1)}, u32[]{:S(2)}, u32[]{:S(2)}) collective-permute-start(bf16[32,1024]{1,0:T(8,128)(2,1)S(1)} %get-tuple-element.125), channel_id=1, source_target_pairs={{0,66},{2,64},{64,2},{66,0},{1,67},{3,65},{65,3},{67,1},{4,70},{6,... | collective-permute-start | bytes 196616 | tf_op jit(solution)/shard_map/ppermute | solution.py:384
  128.8 27.3 %all-to-all-start.1 = ((bf16[32,40,384]{2,1,0:T(8,128)(2,1)}), bf16[32,40,384]{2,1,0:T(8,128)(2,1)S(1)}, u32[]{:S(2)}, u32[]{:S(2)}) async-start(bf16[32,40,384]{2,1,0:T(8,128)(2,1)} %shard_map.261), calls=%async_computation.1 | async-start | bytes 1966080 | tf_op jit(solution)/shard_map/all_to_all | solution.py:513
  135.1 9.0 %collective-permute-start.35 = (bf16[64,1024]{1,0:T(8,128)(2,1)S(1)}, bf16[64,1024]{1,0:T(8,128)(2,1)S(1)}, u32[]{:S(2)}, u32[]{:S(2)}) collective-permute-start(bf16[64,1024]{1,0:T(8,128)(2,1)S(1)} %shard_map.259.p0), channel_id=1, source_target_pairs={{0,1},{1,0},{2,3},{3,2},{4,5},{5,4},{6,7},{7,6},{8,9},{9,8},{10,11... | collective-permute-start | bytes 393224 | tf_op jit(solution)/shard_map/ppermute | solution.py:384
  136.4 21.6 %collective-permute-start.40 = (bf16[2,32,1792]{2,1,0:T(8,128)(2,1)S(1)}, bf16[2,32,1792]{2,1,0:T(8,128)(2,1)S(1)}, u32[]{:S(2)}, u32[]{:S(2)}) collective-permute-start(bf16[2,32,1792]{2,1,0:T(8,128)(2,1)S(1)} %get-tuple-element.150), channel_id=1, source_target_pairs={{0,16},{16,0},{32,48},{48,32},{1,17},{17,1},{33,49},{49,33},{2,18}... | collective-permute-start | bytes 688136 | tf_op jit(solution)/shard_map/ppermute | solution.py:384
  138.3 20.3 %collective-permute-start.41 = (bf16[2,32,1792]{2,1,0:T(8,128)(2,1)S(1)}, bf16[2,32,1792]{2,1,0:T(8,128)(2,1)S(1)}, u32[]{:S(2)}, u32[]{:S(2)}) collective-permute-start(bf16[2,32,1792]{2,1,0:T(8,128)(2,1)S(1)} %get-tuple-element.151), channel_id=1, source_target_pairs={{0,32},{16,48},{32,0},{48,16},{1,33},{17,49},{33,1},{49,17},{2,34}... | collective-permute-start | bytes 688136 | tf_op jit(solution)/shard_map/ppermute | solution.py:384
  141.0 17.7 %collective-permute-start.42 = (bf16[2,32,1792]{2,1,0:T(8,128)(2,1)S(1)}, bf16[2,32,1792]{2,1,0:T(8,128)(2,1)S(1)}, u32[]{:S(2)}, u32[]{:S(2)}) collective-permute-start(bf16[2,32,1792]{2,1,0:T(8,128)(2,1)S(1)} %get-tuple-element.152), channel_id=1, source_target_pairs={{0,48},{16,32},{32,16},{48,0},{1,49},{17,33},{33,17},{49,1},{2,50}... | collective-permute-start | bytes 688136 | tf_op jit(solution)/shard_map/ppermute | solution.py:384
  141.2 11.4 %collective-permute-start.36 = (bf16[64,1024]{1,0:T(8,128)(2,1)S(1)}, bf16[64,1024]{1,0:T(8,128)(2,1)S(1)}, u32[]{:S(2)}, u32[]{:S(2)}) collective-permute-start(bf16[64,1024]{1,0:T(8,128)(2,1)S(1)} %shard_map.259.p0), channel_id=1, source_target_pairs={{0,2},{2,0},{1,3},{3,1},{4,6},{6,4},{5,7},{7,5},{8,10},{10,8},{9,1... | collective-permute-start | bytes 393224 | tf_op jit(solution)/shard_map/ppermute | solution.py:384
  144.0 11.2 %collective-permute-start.37 = (bf16[64,1024]{1,0:T(8,128)(2,1)S(1)}, bf16[64,1024]{1,0:T(8,128)(2,1)S(1)}, u32[]{:S(2)}, u32[]{:S(2)}) collective-permute-start(bf16[64,1024]{1,0:T(8,128)(2,1)S(1)} %collective-permute-done.35.p1), channel_id=1, source_target_pairs={{0,2},{2,0},{1,3},{3,1},{4,6},{6,4},{5,7},{7,5},{8,10},{10,8},{9,1... | collective-permute-start | bytes 393224 | tf_op jit(solution)/shard_map/ppermute | solution.py:384
  158.8 7.7 %collective-permute-start.43 = (bf16[32,1792]{1,0:T(8,128)(2,1)S(1)}, bf16[32,1792]{1,0:T(8,128)(2,1)S(1)}, u32[]{:S(2)}, u32[]{:S(2)}) collective-permute-start(bf16[32,1792]{1,0:T(8,128)(2,1)S(1)} %get-tuple-element.157), channel_id=1, source_target_pairs={{0,64},{64,0},{1,65},{65,1},{2,66},{66,2},{3,67},{67,3},{4,68},{68... | collective-permute-start | bytes 344072 | tf_op jit(solution)/shard_map/ppermute | solution.py:384
  160.3 5.5 %collective-permute-start.39 = (f32[8,384]{1,0:T(8,128)S(1)}, f32[8,384]{1,0:T(8,128)S(1)}, u32[]{:S(2)}, u32[]{:S(2)}) collective-permute-start(f32[8,384]{1,0:T(8,128)S(1)} %shard_map.263.one), channel_id=1, source_target_pairs={{0,2},{2,0},{1,3},{3,1},{4,6},{6,4},{5,7},{7,5},{8,10},{10,8},{9,1... | collective-permute-start | bytes 36872 | tf_op jit(solution)/shard_map/ppermute | solution.py:384
  (35 other events, 208.8 us)
Sparse Core Ops, SparseCore 0:
  16.8 53.6 all-gather.2
  86.7 42.3 reduce-scatter.1

commit v9 on v8

--- a/solution.py
+++ b/solution.py
@@ -399,8 +399,8 @@
     return [own] + fan([None] + rest, Z)
 
 
-def gather_rows(rows):
-    column = [rows] + fan([rows] * 4, Z)
+def gather_rows(rows, *first):
+    column = [rows] + after(fan([rows] * 4, Z), *first)
     pieces = []
     for piece in column:
         pieces += [piece, swap(piece, "c", 2, 1)]
@@ -479,7 +479,7 @@
         feed,
         [((4, 64, 1024), BF), ((4, 64, 1024), F32)]
         + [((256, 1024), BF), ((256, 640), BF), ((256, 1152), BF)],
-        *gather_rows(hn), dy_own, dy_other, w_f,
+        *gather_rows(hn, w_f), dy_own, dy_other, w_f,
     )
     pair = sum_pair(send, keep)
     pair = sum_pair(send, keep)
@@ -489,11 +489,12 @@
         feed_weights, [Far(((4, 4, 2, 32, 1792), BF))], hn_all, dy_own, dy_other, act, dgu,
         scalars=(y.reshape(1),),
     )
-    dw_f = lax.psum_scatter(dw_f.reshape(1024, 1792), "x", scatter_dimension=0, tiled=True)
     dh, d_low, ffn_part, block = call(
         hidden_grad, [Far(rows_high), rows_low, Far(((1, 1024), F32)), Far(rows_low)],
         *d_hn, Far(h), dy_own, ffn_gain_row,
     )
+    (dw_f,) = after([dw_f], d_low)
+    dw_f = lax.psum_scatter(dw_f.reshape(1024, 1792), "x", scatter_dimension=0, tiled=True)
     d_attn, d_qh, *d_kvs = call(
         attend_grad, [Far(((256, 1024), BF)), wide_flat, wide_flat, flat, flat, flat],
         *gather_rows(d_low), Far(qh), *[Far(t) for t in kvs], own_places, places, Far(w_a), Far(o), Far(l),
@@ -528,6 +529,7 @@
         finish_gains, [((8, 128), F32)] * 2 + [((1, 64), F32)] * 2,
         gains, swap(gains, "zh", 2, 1),
     )
+    (dw_f,) = after([dw_f], rows)
     sides = call(split_sides, [((2, 32, 1792), BF)] * 4, Far(dw_f))
     others = after(fan(sides, "y"), gains)
     own_f, send_f = call(

time: 175 us -> 170 us (0.971)
  local copies, waits for them, and re-layouts: 13.9 us -> 8.86 us
    unnamed x38 -> x16, local copies, waits for them, and re-layouts: 11 us -> 5.93 us
    ppermute x44, waiting for transfers between devices: 59.1 us -> 55.1 us  [swap(): return lax.ppermute(value, axes, [(i, i ^ mask) for i in range(size)])]
    reduce_scatter x1, waiting for transfers between devices: 0.02 us -> 3.84 us  [local(): lax.psum_scatter(dw_f.reshape(1024, 1792), 'x', scatter_dimension=0, tile...]
  transfers between devices with their start and end apart: 48 -> 48, of which waited for: 29 -> 36; matrix products, arithmetic and copies ran while one was open for 3% -> 3% of each run, Pallas kernels for 6% -> 7%
where the time goes in v9:
time: 170 us; the launch traced here: 169 us
  starting transfers between devices  65.4 us (38%)
  waiting for transfers between devices  58.9 us (35%)
  Pallas kernels  18.8 us (11%)
  between operations  14.3 us (8%)
  local copies, waits for them, and re-layouts  8.86 us (5%)
  other arithmetic  2.85 us (2%)
    ppermute x44, waiting for transfers between devices, swap(): return lax.ppermute(value, axes, [(i, i ^ mask) for i in range(size)])  55.1 us
    ppermute x44, starting transfers between devices, swap(): return lax.ppermute(value, axes, [(i, i ^ mask) for i in range(size)])  51.8 us
    pallas_call x23, Pallas kernels, call(): pl.pallas_call(body, out_shape=[jax.ShapeDtypeStruct(*bare(out)) for out...  18.8 us
    all_to_all x1, starting transfers between devices, local(): w_a = lax.all_to_all(blocks.reshape(1024, 384), PLANE, 0, 0, tiled=True)  8.51 us
    unnamed x16, local copies, waits for them, and re-layouts  5.93 us
    all_to_all x1, starting transfers between devices, local(): dw_a = lax.all_to_all(dw_a, PLANE, 0, 0, tiled=True)  5.05 us
    reduce_scatter x1, waiting for transfers between devices, local(): lax.psum_scatter(dw_f.reshape(1024, 1792), 'x', scatter_dimension=0, tile...  3.84 us
  transfers between devices with their start and end apart: 48, of which 36 were waited for; matrix products, arithmetic and copies ran while one was open for 3% of the time, Pallas kernels for 7%

profile of v9, /device:TPU:0, one launch (start us, length us, event | category | flops | bytes accessed | tf_op | source)
XLA Modules:
  0.0 169.1 jit_solution(11040632317109905533)
XLA Ops:
  7.3 2.3 %shard_map.246 = (bf16[2,16,32,384]{3,2,1,0:T(8,128)(2,1)}, bf16[32,1792]{1,0:T(8,128)(2,1)}, bf16[32,1792]{1,0:T(8,128)(2,1)}, bf16[128,1024]{1,0:T(8,128)(2,1)}) custom-call(s32[1]{0:T(128)} %bitcast.1.zl, s32[1]{0:T(128)} %bitcast.head, bf16[32,256]{1,0:T(8,128)(2,1)} %wq.1, bf16[32,128]{1,0:T(8,128)(2,1)} %wk.1, bf16[32,128]{1,0:T(8,128)(2,1)} %wv.1, ...), custom_call_target="tpu_custom_call" | custom-call | tf_op jit(solution)/shard_map/pallas_call | solution.py:37
  9.6 2.1 %collective-permute-start.13 = (bf16[32,1792]{1,0:T(8,128)(2,1)}, bf16[32,1792]{1,0:T(8,128)(2,1)S(1)}, u32[]{:S(2)}, u32[]{:S(2)}) collective-permute-start(bf16[32,1792]{1,0:T(8,128)(2,1)} %get-tuple-element.110), channel_id=1, source_target_pairs={{0,64},{64,0},{1,65},{65,1},{2,66},{66,2},{3,67},{67,3},{4,68},{68... | collective-permute-start | bytes 344072 | tf_op jit(solution)/shard_map/ppermute | solution.py:384
  11.7 3.4 %collective-permute-done.13.got = bf16[32,1792]{1,0:T(8,128)(2,1)S(1)} collective-permute-done((bf16[32,1792]{1,0:T(8,128)(2,1)}, bf16[32,1792]{1,0:T(8,128)(2,1)S(1)}, u32[]{:S(2)}, u32[]{:S(2)}) %collective-permute-start.13) | collective-permute-done | bytes 114720 | tf_op jit(solution)/shard_map/ppermute | solution.py:384
  16.7 8.5 %all-to-all-start = ((bf16[32,32,384]{2,1,0:T(8,128)(2,1)}), bf16[32,32,384]{2,1,0:T(8,128)(2,1)S(1)}, u32[]{:S(2)}, u32[]{:S(2)}) async-start(bf16[32,32,384]{2,1,0:T(8,128)(2,1)} %bitcast.28), calls=%async_computation | async-start | bytes 1572864 | tf_op jit(solution)/shard_map/all_to_all | solution.py:444
  25.2 1.9 %collective-permute-start = (bf16[128,1024]{1,0:T(8,128)(2,1)}, bf16[128,1024]{1,0:T(8,128)(2,1)S(1)}, u32[]{:S(2)}, u32[]{:S(2)}) collective-permute-start(bf16[128,1024]{1,0:T(8,128)(2,1)} %get-tuple-element.95.own.x.x_own), channel_id=1, source_target_pairs={{0,64},{64,0},{1,65},{65,1},{2,66},{66,2},{3,67},{67,3},{4,68},{68... | collective-permute-start | bytes 786440 | tf_op jit(solution)/shard_map/ppermute | solution.py:384
  32.7 7.9 %collective-permute-done.other.x_other = bf16[128,1024]{1,0:T(8,128)(2,1)S(1)} collective-permute-done((bf16[128,1024]{1,0:T(8,128)(2,1)}, bf16[128,1024]{1,0:T(8,128)(2,1)S(1)}, u32[]{:S(2)}, u32[]{:S(2)}) %collective-permute-start) | collective-permute-done | bytes 262176 | tf_op jit(solution)/shard_map/ppermute | solution.py:384
  42.7 2.2 %collective-permute-start.4 = (bf16[256,128]{1,0:T(8,128)(2,1)S(1)}, bf16[256,128]{1,0:T(8,128)(2,1)S(1)}, u32[]{:S(2)}, u32[]{:S(2)}) collective-permute-start(bf16[256,128]{1,0:T(8,128)(2,1)S(1)} %get-tuple-element.99.kv0), channel_id=1, source_target_pairs={{0,48},{16,32},{32,16},{48,0},{1,49},{17,33},{33,17},{49,1},{2,50}... | collective-permute-start | bytes 196616 | tf_op jit(solution)/shard_map/ppermute | solution.py:384
  48.9 1.8 %collective-permute-done.3.kv2 = bf16[256,128]{1,0:T(8,128)(2,1)S(1)} collective-permute-done((bf16[256,128]{1,0:T(8,128)(2,1)S(1)}, bf16[256,128]{1,0:T(8,128)(2,1)S(1)}, u32[]{:S(2)}, u32[]{:S(2)}) %collective-permute-start.3) | collective-permute-done | bytes 65568 | tf_op jit(solution)/shard_map/ppermute | solution.py:384
  53.7 3.7 %collective-permute-start.6 = (bf16[32,1024]{1,0:T(8,128)(2,1)S(1)}, bf16[32,1024]{1,0:T(8,128)(2,1)S(1)}, u32[]{:S(2)}, u32[]{:S(2)}) collective-permute-start(bf16[32,1024]{1,0:T(8,128)(2,1)S(1)} %get-tuple-element.105), channel_id=1, source_target_pairs={{0,2},{2,0},{64,66},{66,64},{1,3},{3,1},{65,67},{67,65},{4,6},{6,4... | collective-permute-start | bytes 196616 | tf_op jit(solution)/shard_map/ppermute | solution.py:384
  58.0 2.0 %collective-permute-done.6.one = bf16[32,1024]{1,0:T(8,128)(2,1)S(1)} collective-permute-done((bf16[32,1024]{1,0:T(8,128)(2,1)S(1)}, bf16[32,1024]{1,0:T(8,128)(2,1)S(1)}, u32[]{:S(2)}, u32[]{:S(2)}) %collective-permute-start.6) | collective-permute-done | bytes 65568 | tf_op jit(solution)/shard_map/ppermute | solution.py:384
  61.7 1.8 %collective-permute-done.8.three = bf16[32,1024]{1,0:T(8,128)(2,1)S(1)} collective-permute-done((bf16[32,1024]{1,0:T(8,128)(2,1)S(1)}, bf16[32,1024]{1,0:T(8,128)(2,1)S(1)}, u32[]{:S(2)}, u32[]{:S(2)}) %collective-permute-start.8) | collective-permute-done | bytes 65568 | tf_op jit(solution)/shard_map/ppermute | solution.py:384
  64.6 3.8 %collective-permute-start.10 = (bf16[32,1024]{1,0:T(8,128)(2,1)S(1)}, bf16[32,1024]{1,0:T(8,128)(2,1)S(1)}, u32[]{:S(2)}, u32[]{:S(2)}) collective-permute-start(bf16[32,1024]{1,0:T(8,128)(2,1)S(1)} %get-tuple-element.108.p0), channel_id=1, source_target_pairs={{0,2},{2,0},{64,66},{66,64},{1,3},{3,1},{65,67},{67,65},{4,6},{6,4... | collective-permute-start | bytes 196616 | tf_op jit(solution)/shard_map/ppermute | solution.py:384
  73.1 2.0 %copy-done.2 = bf16[32,32,1792]{2,1,0:T(8,128)(2,1)S(1)} copy-done((bf16[32,32,1792]{2,1,0:T(8,128)(2,1)S(1)}, bf16[32,32,1792]{2,1,0:T(8,128)(2,1)}, u32[]{:S(2)}) %copy-start.2) | copy-done | bytes 3670040
  75.1 2.6 %shard_map.253 = (bf16[4,64,1024]{2,1,0:T(8,128)(2,1)S(1)}, f32[4,64,1024]{2,1,0:T(8,128)S(1)}, bf16[256,1024]{1,0:T(8,128)(2,1)S(1)}, bf16[256,640]{1,0:T(8,128)(2,1)S(1)}, bf16[256,1152]{1,0:T(8,128)(2,1)S(1)}) custom-call(bf16[32,1024]{1,0:T(8,128)(2,1)S(1)} %get-tuple-element.108.p0, bf16[32,1024]{1,0:T(8,128)(2,1)S(1)} %collective-permute-done.9.p1, ...), custom_call_target="tpu_custom_call" | custom-call | tf_op jit(solution)/shard_map/pallas_call | solution.py:37
  79.8 2.9 %collective-permute-start.18 = (bf16[64,1024]{1,0:T(8,128)(2,1)S(1)}, bf16[64,1024]{1,0:T(8,128)(2,1)S(1)}, u32[]{:S(2)}, u32[]{:S(2)}) collective-permute-start(bf16[64,1024]{1,0:T(8,128)(2,1)S(1)} %get-tuple-element.117), channel_id=1, source_target_pairs={{0,2},{2,0},{64,66},{66,64},{1,3},{3,1},{65,67},{67,65},{4,6},{6,4... | collective-permute-start | bytes 393224 | tf_op jit(solution)/shard_map/ppermute | solution.py:384
  90.1 2.0 %collective-permute-start.24 = (bf16[32,1024]{1,0:T(8,128)(2,1)S(1)}, bf16[32,1024]{1,0:T(8,128)(2,1)S(1)}, u32[]{:S(2)}, u32[]{:S(2)}) collective-permute-start(bf16[32,1024]{1,0:T(8,128)(2,1)S(1)} %get-tuple-element.121.p0), channel_id=1, source_target_pairs={{0,66},{2,64},{64,2},{66,0},{1,67},{3,65},{65,3},{67,1},{4,70},{6,... | collective-permute-start | bytes 196616 | tf_op jit(solution)/shard_map/ppermute | solution.py:384
  92.8 2.0 %collective-permute-start.22 = (bf16[32,1024]{1,0:T(8,128)(2,1)S(1)}, bf16[32,1024]{1,0:T(8,128)(2,1)S(1)}, u32[]{:S(2)}, u32[]{:S(2)}) collective-permute-start(bf16[32,1024]{1,0:T(8,128)(2,1)S(1)} %get-tuple-element.121.p0), channel_id=1, source_target_pairs={{0,2},{2,0},{64,66},{66,64},{1,3},{3,1},{65,67},{67,65},{4,6},{6,4... | collective-permute-start | bytes 196616 | tf_op jit(solution)/shard_map/ppermute | solution.py:384
  96.4 2.2 %collective-permute-done.22.p2 = bf16[32,1024]{1,0:T(8,128)(2,1)S(1)} collective-permute-done((bf16[32,1024]{1,0:T(8,128)(2,1)S(1)}, bf16[32,1024]{1,0:T(8,128)(2,1)S(1)}, u32[]{:S(2)}, u32[]{:S(2)}) %collective-permute-start.22) | collective-permute-done | bytes 65568 | tf_op jit(solution)/shard_map/ppermute | solution.py:384
  100.4 3.1 %shard_map.256 = (bf16[256,1024]{1,0:T(8,128)(2,1)S(1)}, f32[256,128]{1,0:T(8,128)S(1)}, f32[256,128]{1,0:T(8,128)S(1)}, bf16[256,128]{1,0:T(8,128)(2,1)S(1)}, b...) custom-call(bf16[32,1024]{1,0:T(8,128)(2,1)S(1)} %get-tuple-element.121.p0, ...), custom_call_target="tpu_custom_call" | custom-call | tf_op jit(solution)/shard_map/pallas_call | solution.py:37
  104.0 2.7 %collective-permute-start.29 = (bf16[256,128]{1,0:T(8,128)(2,1)S(1)}, bf16[256,128]{1,0:T(8,128)(2,1)S(1)}, u32[]{:S(2)}, u32[]{:S(2)}) collective-permute-start(bf16[256,128]{1,0:T(8,128)(2,1)S(1)} %get-tuple-element.130), channel_id=1, source_target_pairs={{0,32},{16,48},{32,0},{48,16},{1,33},{17,49},{33,1},{49,17},{2,34}... | collective-permute-start | bytes 196616 | tf_op jit(solution)/shard_map/ppermute | solution.py:384
  108.3 1.9 %collective-permute-done.29.two = bf16[256,128]{1,0:T(8,128)(2,1)S(1)} collective-permute-done((bf16[256,128]{1,0:T(8,128)(2,1)S(1)}, bf16[256,128]{1,0:T(8,128)(2,1)S(1)}, u32[]{:S(2)}, u32[]{:S(2)}) %collective-permute-start.29) | collective-permute-done | bytes 65568 | tf_op jit(solution)/shard_map/ppermute | solution.py:384
  110.2 1.9 %collective-permute-done.30.three = bf16[256,128]{1,0:T(8,128)(2,1)S(1)} collective-permute-done((bf16[256,128]{1,0:T(8,128)(2,1)S(1)}, bf16[256,128]{1,0:T(8,128)(2,1)S(1)}, u32[]{:S(2)}, u32[]{:S(2)}) %collective-permute-start.30) | collective-permute-done | bytes 65568 | tf_op jit(solution)/shard_map/ppermute | solution.py:384
  114.9 2.1 %collective-permute-start.32 = (bf16[32,1024]{1,0:T(8,128)(2,1)S(1)}, bf16[32,1024]{1,0:T(8,128)(2,1)S(1)}, u32[]{:S(2)}, u32[]{:S(2)}) collective-permute-start(bf16[32,1024]{1,0:T(8,128)(2,1)S(1)} %get-tuple-element.137), channel_id=1, source_target_pairs={{0,2},{2,0},{64,66},{66,64},{1,3},{3,1},{65,67},{67,65},{4,6},{6,4... | collective-permute-start | bytes 196616 | tf_op jit(solution)/shard_map/ppermute | solution.py:384
  117.7 1.8 %collective-permute-start.34 = (bf16[32,1024]{1,0:T(8,128)(2,1)S(1)}, bf16[32,1024]{1,0:T(8,128)(2,1)S(1)}, u32[]{:S(2)}, u32[]{:S(2)}) collective-permute-start(bf16[32,1024]{1,0:T(8,128)(2,1)S(1)} %get-tuple-element.139), channel_id=1, source_target_pairs={{0,66},{2,64},{64,2},{66,0},{1,67},{3,65},{65,3},{67,1},{4,70},{6,... | collective-permute-start | bytes 196616 | tf_op jit(solution)/shard_map/ppermute | solution.py:384
  121.4 1.8 %collective-permute-done.34.three = bf16[32,1024]{1,0:T(8,128)(2,1)S(1)} collective-permute-done((bf16[32,1024]{1,0:T(8,128)(2,1)S(1)}, bf16[32,1024]{1,0:T(8,128)(2,1)S(1)}, u32[]{:S(2)}, u32[]{:S(2)}) %collective-permute-start.34) | collective-permute-done | bytes 65568 | tf_op jit(solution)/shard_map/ppermute | solution.py:384
  123.2 5.0 %all-to-all-start.1 = ((bf16[32,40,384]{2,1,0:T(8,128)(2,1)}), bf16[32,40,384]{2,1,0:T(8,128)(2,1)S(1)}, u32[]{:S(2)}, u32[]{:S(2)}) async-start(bf16[32,40,384]{2,1,0:T(8,128)(2,1)} %shard_map.261), calls=%async_computation.1 | async-start | bytes 1966080 | tf_op jit(solution)/shard_map/all_to_all | solution.py:514
  128.6 3.8 %reduce-scatter.2.cloned.1.call-done.dw = bf16[256,1792]{1,0:T(8,128)(2,1)} async-done(((bf16[1024,1792]{1,0:T(8,128)(2,1)}), bf16[256,1792]{1,0:T(8,128)(2,1)}) %reduce-scatter.2.cloned.1.call-update) | async-done | bytes 917520 | tf_op jit(solution)/shard_map/reduce_scatter | solution.py:497
  135.2 2.7 %collective-permute-start.41 = (bf16[2,32,1792]{2,1,0:T(8,128)(2,1)S(1)}, bf16[2,32,1792]{2,1,0:T(8,128)(2,1)S(1)}, u32[]{:S(2)}, u32[]{:S(2)}) collective-permute-start(bf16[2,32,1792]{2,1,0:T(8,128)(2,1)S(1)} %get-tuple-element.167), channel_id=1, source_target_pairs={{0,32},{16,48},{32,0},{48,16},{1,33},{17,49},{33,1},{49,17},{2,34}... | collective-permute-start | bytes 688136 | tf_op jit(solution)/shard_map/ppermute | solution.py:384
  138.4 4.0 %collective-permute-start.36 = (bf16[64,1024]{1,0:T(8,128)(2,1)S(1)}, bf16[64,1024]{1,0:T(8,128)(2,1)S(1)}, u32[]{:S(2)}, u32[]{:S(2)}) collective-permute-start(bf16[64,1024]{1,0:T(8,128)(2,1)S(1)} %shard_map.259.p0), channel_id=1, source_target_pairs={{0,2},{2,0},{1,3},{3,1},{4,6},{6,4},{5,7},{7,5},{8,10},{10,8},{9,1... | collective-permute-start | bytes 393224 | tf_op jit(solution)/shard_map/ppermute | solution.py:384
  142.5 5.4 %collective-permute-done.36.p2 = bf16[64,1024]{1,0:T(8,128)(2,1)S(1)} collective-permute-done((bf16[64,1024]{1,0:T(8,128)(2,1)S(1)}, bf16[64,1024]{1,0:T(8,128)(2,1)S(1)}, u32[]{:S(2)}, u32[]{:S(2)}) %collective-permute-start.36) | collective-permute-done | bytes 131104 | tf_op jit(solution)/shard_map/ppermute | solution.py:384
  154.8 3.0 %collective-permute-start.39 = (f32[8,384]{1,0:T(8,128)S(1)}, f32[8,384]{1,0:T(8,128)S(1)}, u32[]{:S(2)}, u32[]{:S(2)}) collective-permute-start(f32[8,384]{1,0:T(8,128)S(1)} %shard_map.263.one), channel_id=1, source_target_pairs={{0,2},{2,0},{1,3},{3,1},{4,6},{6,4},{5,7},{7,5},{8,10},{10,8},{9,1... | collective-permute-start | bytes 36872 | tf_op jit(solution)/shard_map/ppermute | solution.py:384
  157.7 3.1 %collective-permute-done.39.two = f32[8,384]{1,0:T(8,128)S(1)} collective-permute-done((f32[8,384]{1,0:T(8,128)S(1)}, f32[8,384]{1,0:T(8,128)S(1)}, u32[]{:S(2)}, u32[]{:S(2)}) %collective-permute-start.39) | collective-permute-done | bytes 12320 | tf_op jit(solution)/shard_map/ppermute | solution.py:384
  (123 shorter events, 57.2 us)
Async XLA Ops:
  7.2 64.1 %all-gather.3.cloned.1.call-start = ((), (), s32[]{:S(2)}) async-start(), calls=%async_computation.4 | async-start | bytes 3899392 | tf_op jit(solution)/shard_map/all_gather | solution.py:446
  9.6 5.4 %collective-permute-start.13 = (bf16[32,1792]{1,0:T(8,128)(2,1)}, bf16[32,1792]{1,0:T(8,128)(2,1)S(1)}, u32[]{:S(2)}, u32[]{:S(2)}) collective-permute-start(bf16[32,1792]{1,0:T(8,128)(2,1)} %get-tuple-element.110), channel_id=1, source_target_pairs={{0,64},{64,0},{1,65},{65,1},{2,66},{66,2},{3,67},{67,3},{4,68},{68... | collective-permute-start | bytes 344072 | tf_op jit(solution)/shard_map/ppermute | solution.py:384
  16.7 23.9 %all-to-all-start = ((bf16[32,32,384]{2,1,0:T(8,128)(2,1)}), bf16[32,32,384]{2,1,0:T(8,128)(2,1)S(1)}, u32[]{:S(2)}, u32[]{:S(2)}) async-start(bf16[32,32,384]{2,1,0:T(8,128)(2,1)} %bitcast.28), calls=%async_computation | async-start | bytes 1572864 | tf_op jit(solution)/shard_map/all_to_all | solution.py:444
  25.2 107.2 %reduce-scatter.2.cloned.1.call-start = ((), (), s32[]{:S(2)}) async-start(), calls=%async_computation.3 | async-start | bytes 4587520 | tf_op jit(solution)/shard_map/reduce_scatter | solution.py:497
  25.2 15.4 %collective-permute-start = (bf16[128,1024]{1,0:T(8,128)(2,1)}, bf16[128,1024]{1,0:T(8,128)(2,1)S(1)}, u32[]{:S(2)}, u32[]{:S(2)}) collective-permute-start(bf16[128,1024]{1,0:T(8,128)(2,1)} %get-tuple-element.95.own.x.x_own), channel_id=1, source_target_pairs={{0,64},{64,0},{1,65},{65,1},{2,66},{66,2},{3,67},{67,3},{4,68},{68... | collective-permute-start | bytes 786440 | tf_op jit(solution)/shard_map/ppermute | solution.py:384
  41.4 6.9 %collective-permute-start.1 = (bf16[128,1024]{1,0:T(8,128)(2,1)S(1)}, bf16[128,1024]{1,0:T(8,128)(2,1)S(1)}, u32[]{:S(2)}, u32[]{:S(2)}) collective-permute-start(bf16[128,1024]{1,0:T(8,128)(2,1)S(1)} %shard_map.248.dy_own.dy), channel_id=1, source_target_pairs={{0,64},{64,0},{1,65},{65,1},{2,66},{66,2},{3,67},{67,3},{4,68},{68... | collective-permute-start | bytes 786440 | tf_op jit(solution)/shard_map/ppermute | solution.py:384
  42.7 6.2 %collective-permute-start.4 = (bf16[256,128]{1,0:T(8,128)(2,1)S(1)}, bf16[256,128]{1,0:T(8,128)(2,1)S(1)}, u32[]{:S(2)}, u32[]{:S(2)}) collective-permute-start(bf16[256,128]{1,0:T(8,128)(2,1)S(1)} %get-tuple-element.99.kv0), channel_id=1, source_target_pairs={{0,48},{16,32},{32,16},{48,0},{1,49},{17,33},{33,17},{49,1},{2,50}... | collective-permute-start | bytes 196616 | tf_op jit(solution)/shard_map/ppermute | solution.py:384
  44.9 5.8 %collective-permute-start.3 = (bf16[256,128]{1,0:T(8,128)(2,1)S(1)}, bf16[256,128]{1,0:T(8,128)(2,1)S(1)}, u32[]{:S(2)}, u32[]{:S(2)}) collective-permute-start(bf16[256,128]{1,0:T(8,128)(2,1)S(1)} %get-tuple-element.99.kv0), channel_id=1, source_target_pairs={{0,32},{16,48},{32,0},{48,16},{1,33},{17,49},{33,1},{49,17},{2,34}... | collective-permute-start | bytes 196616 | tf_op jit(solution)/shard_map/ppermute | solution.py:384
  53.7 6.3 %collective-permute-start.6 = (bf16[32,1024]{1,0:T(8,128)(2,1)S(1)}, bf16[32,1024]{1,0:T(8,128)(2,1)S(1)}, u32[]{:S(2)}, u32[]{:S(2)}) collective-permute-start(bf16[32,1024]{1,0:T(8,128)(2,1)S(1)} %get-tuple-element.105), channel_id=1, source_target_pairs={{0,2},{2,0},{64,66},{66,64},{1,3},{3,1},{65,67},{67,65},{4,6},{6,4... | collective-permute-start | bytes 196616 | tf_op jit(solution)/shard_map/ppermute | solution.py:384
  58.0 5.5 %collective-permute-start.8 = (bf16[32,1024]{1,0:T(8,128)(2,1)S(1)}, bf16[32,1024]{1,0:T(8,128)(2,1)S(1)}, u32[]{:S(2)}, u32[]{:S(2)}) collective-permute-start(bf16[32,1024]{1,0:T(8,128)(2,1)S(1)} %get-tuple-element.107), channel_id=1, source_target_pairs={{0,66},{2,64},{64,2},{66,0},{1,67},{3,65},{65,3},{67,1},{4,70},{6,... | collective-permute-start | bytes 196616 | tf_op jit(solution)/shard_map/ppermute | solution.py:384
  63.6 6.0 %collective-permute-start.12 = (bf16[32,1024]{1,0:T(8,128)(2,1)S(1)}, bf16[32,1024]{1,0:T(8,128)(2,1)S(1)}, u32[]{:S(2)}, u32[]{:S(2)}) collective-permute-start(bf16[32,1024]{1,0:T(8,128)(2,1)S(1)} %get-tuple-element.108.p0), channel_id=1, source_target_pairs={{0,66},{2,64},{64,2},{66,0},{1,67},{3,65},{65,3},{67,1},{4,70},{6,... | collective-permute-start | bytes 196616 | tf_op jit(solution)/shard_map/ppermute | solution.py:384
  64.4 5.2 %collective-permute-start.11 = (bf16[32,1024]{1,0:T(8,128)(2,1)S(1)}, bf16[32,1024]{1,0:T(8,128)(2,1)S(1)}, u32[]{:S(2)}, u32[]{:S(2)}) collective-permute-start(bf16[32,1024]{1,0:T(8,128)(2,1)S(1)} %get-tuple-element.108.p0), channel_id=1, source_target_pairs={{0,64},{2,66},{64,0},{66,2},{1,65},{3,67},{65,1},{67,3},{4,68},{6,... | collective-permute-start | bytes 196616 | tf_op jit(solution)/shard_map/ppermute | solution.py:384
  64.6 6.7 %collective-permute-start.10 = (bf16[32,1024]{1,0:T(8,128)(2,1)S(1)}, bf16[32,1024]{1,0:T(8,128)(2,1)S(1)}, u32[]{:S(2)}, u32[]{:S(2)}) collective-permute-start(bf16[32,1024]{1,0:T(8,128)(2,1)S(1)} %get-tuple-element.108.p0), channel_id=1, source_target_pairs={{0,2},{2,0},{64,66},{66,64},{1,3},{3,1},{65,67},{67,65},{4,6},{6,4... | collective-permute-start | bytes 196616 | tf_op jit(solution)/shard_map/ppermute | solution.py:384
  79.8 7.9 %collective-permute-start.18 = (bf16[64,1024]{1,0:T(8,128)(2,1)S(1)}, bf16[64,1024]{1,0:T(8,128)(2,1)S(1)}, u32[]{:S(2)}, u32[]{:S(2)}) collective-permute-start(bf16[64,1024]{1,0:T(8,128)(2,1)S(1)} %get-tuple-element.117), channel_id=1, source_target_pairs={{0,2},{2,0},{64,66},{66,64},{1,3},{3,1},{65,67},{67,65},{4,6},{6,4... | collective-permute-start | bytes 393224 | tf_op jit(solution)/shard_map/ppermute | solution.py:384
  82.7 6.4 %collective-permute-start.19 = (bf16[64,1024]{1,0:T(8,128)(2,1)S(1)}, bf16[64,1024]{1,0:T(8,128)(2,1)S(1)}, u32[]{:S(2)}, u32[]{:S(2)}) collective-permute-start(bf16[64,1024]{1,0:T(8,128)(2,1)S(1)} %get-tuple-element.118), channel_id=1, source_target_pairs={{0,64},{2,66},{64,0},{66,2},{1,65},{3,67},{65,1},{67,3},{4,68},{6,... | collective-permute-start | bytes 393224 | tf_op jit(solution)/shard_map/ppermute | solution.py:384
  82.8 7.1 %collective-permute-start.20 = (bf16[64,1024]{1,0:T(8,128)(2,1)S(1)}, bf16[64,1024]{1,0:T(8,128)(2,1)S(1)}, u32[]{:S(2)}, u32[]{:S(2)}) collective-permute-start(bf16[64,1024]{1,0:T(8,128)(2,1)S(1)} %get-tuple-element.119), channel_id=1, source_target_pairs={{0,66},{2,64},{64,2},{66,0},{1,67},{3,65},{65,3},{67,1},{4,70},{6,... | collective-permute-start | bytes 393224 | tf_op jit(solution)/shard_map/ppermute | solution.py:384
  90.1 5.6 %collective-permute-start.24 = (bf16[32,1024]{1,0:T(8,128)(2,1)S(1)}, bf16[32,1024]{1,0:T(8,128)(2,1)S(1)}, u32[]{:S(2)}, u32[]{:S(2)}) collective-permute-start(bf16[32,1024]{1,0:T(8,128)(2,1)S(1)} %get-tuple-element.121.p0), channel_id=1, source_target_pairs={{0,66},{2,64},{64,2},{66,0},{1,67},{3,65},{65,3},{67,1},{4,70},{6,... | collective-permute-start | bytes 196616 | tf_op jit(solution)/shard_map/ppermute | solution.py:384
  92.8 5.8 %collective-permute-start.22 = (bf16[32,1024]{1,0:T(8,128)(2,1)S(1)}, bf16[32,1024]{1,0:T(8,128)(2,1)S(1)}, u32[]{:S(2)}, u32[]{:S(2)}) collective-permute-start(bf16[32,1024]{1,0:T(8,128)(2,1)S(1)} %get-tuple-element.121.p0), channel_id=1, source_target_pairs={{0,2},{2,0},{64,66},{66,64},{1,3},{3,1},{65,67},{67,65},{4,6},{6,4... | collective-permute-start | bytes 196616 | tf_op jit(solution)/shard_map/ppermute | solution.py:384
  103.5 4.8 %collective-permute-start.28 = (bf16[256,128]{1,0:T(8,128)(2,1)S(1)}, bf16[256,128]{1,0:T(8,128)(2,1)S(1)}, u32[]{:S(2)}, u32[]{:S(2)}) collective-permute-start(bf16[256,128]{1,0:T(8,128)(2,1)S(1)} %get-tuple-element.129), channel_id=1, source_target_pairs={{0,16},{16,0},{32,48},{48,32},{1,17},{17,1},{33,49},{49,33},{2,18}... | collective-permute-start | bytes 196616 | tf_op jit(solution)/shard_map/ppermute | solution.py:384
  104.0 6.3 %collective-permute-start.29 = (bf16[256,128]{1,0:T(8,128)(2,1)S(1)}, bf16[256,128]{1,0:T(8,128)(2,1)S(1)}, u32[]{:S(2)}, u32[]{:S(2)}) collective-permute-start(bf16[256,128]{1,0:T(8,128)(2,1)S(1)} %get-tuple-element.130), channel_id=1, source_target_pairs={{0,32},{16,48},{32,0},{48,16},{1,33},{17,49},{33,1},{49,17},{2,34}... | collective-permute-start | bytes 196616 | tf_op jit(solution)/shard_map/ppermute | solution.py:384
  106.7 5.5 %collective-permute-start.30 = (bf16[256,128]{1,0:T(8,128)(2,1)S(1)}, bf16[256,128]{1,0:T(8,128)(2,1)S(1)}, u32[]{:S(2)}, u32[]{:S(2)}) collective-permute-start(bf16[256,128]{1,0:T(8,128)(2,1)S(1)} %get-tuple-element.131), channel_id=1, source_target_pairs={{0,48},{16,32},{32,16},{48,0},{1,49},{17,33},{33,17},{49,1},{2,50}... | collective-permute-start | bytes 196616 | tf_op jit(solution)/shard_map/ppermute | solution.py:384
  114.9 6.2 %collective-permute-start.32 = (bf16[32,1024]{1,0:T(8,128)(2,1)S(1)}, bf16[32,1024]{1,0:T(8,128)(2,1)S(1)}, u32[]{:S(2)}, u32[]{:S(2)}) collective-permute-start(bf16[32,1024]{1,0:T(8,128)(2,1)S(1)} %get-tuple-element.137), channel_id=1, source_target_pairs={{0,2},{2,0},{64,66},{66,64},{1,3},{3,1},{65,67},{67,65},{4,6},{6,4... | collective-permute-start | bytes 196616 | tf_op jit(solution)/shard_map/ppermute | solution.py:384
  117.7 5.5 %collective-permute-start.34 = (bf16[32,1024]{1,0:T(8,128)(2,1)S(1)}, bf16[32,1024]{1,0:T(8,128)(2,1)S(1)}, u32[]{:S(2)}, u32[]{:S(2)}) collective-permute-start(bf16[32,1024]{1,0:T(8,128)(2,1)S(1)} %get-tuple-element.139), channel_id=1, source_target_pairs={{0,66},{2,64},{64,2},{66,0},{1,67},{3,65},{65,3},{67,1},{4,70},{6,... | collective-permute-start | bytes 196616 | tf_op jit(solution)/shard_map/ppermute | solution.py:384
  123.2 27.2 %all-to-all-start.1 = ((bf16[32,40,384]{2,1,0:T(8,128)(2,1)}), bf16[32,40,384]{2,1,0:T(8,128)(2,1)S(1)}, u32[]{:S(2)}, u32[]{:S(2)}) async-start(bf16[32,40,384]{2,1,0:T(8,128)(2,1)} %shard_map.261), calls=%async_computation.1 | async-start | bytes 1966080 | tf_op jit(solution)/shard_map/all_to_all | solution.py:514
  128.5 14.0 %collective-permute-start.35 = (bf16[64,1024]{1,0:T(8,128)(2,1)S(1)}, bf16[64,1024]{1,0:T(8,128)(2,1)S(1)}, u32[]{:S(2)}, u32[]{:S(2)}) collective-permute-start(bf16[64,1024]{1,0:T(8,128)(2,1)S(1)} %shard_map.259.p0), channel_id=1, source_target_pairs={{0,1},{1,0},{2,3},{3,2},{4,5},{5,4},{6,7},{7,6},{8,9},{9,8},{10,11... | collective-permute-start | bytes 393224 | tf_op jit(solution)/shard_map/ppermute | solution.py:384
  133.7 18.7 %collective-permute-start.40 = (bf16[2,32,1792]{2,1,0:T(8,128)(2,1)S(1)}, bf16[2,32,1792]{2,1,0:T(8,128)(2,1)S(1)}, u32[]{:S(2)}, u32[]{:S(2)}) collective-permute-start(bf16[2,32,1792]{2,1,0:T(8,128)(2,1)S(1)} %get-tuple-element.166), channel_id=1, source_target_pairs={{0,16},{16,0},{32,48},{48,32},{1,17},{17,1},{33,49},{49,33},{2,18}... | collective-permute-start | bytes 688136 | tf_op jit(solution)/shard_map/ppermute | solution.py:384
  135.2 17.2 %collective-permute-start.41 = (bf16[2,32,1792]{2,1,0:T(8,128)(2,1)S(1)}, bf16[2,32,1792]{2,1,0:T(8,128)(2,1)S(1)}, u32[]{:S(2)}, u32[]{:S(2)}) collective-permute-start(bf16[2,32,1792]{2,1,0:T(8,128)(2,1)S(1)} %get-tuple-element.167), channel_id=1, source_target_pairs={{0,32},{16,48},{32,0},{48,16},{1,33},{17,49},{33,1},{49,17},{2,34}... | collective-permute-start | bytes 688136 | tf_op jit(solution)/shard_map/ppermute | solution.py:384
  137.9 15.1 %collective-permute-start.42 = (bf16[2,32,1792]{2,1,0:T(8,128)(2,1)S(1)}, bf16[2,32,1792]{2,1,0:T(8,128)(2,1)S(1)}, u32[]{:S(2)}, u32[]{:S(2)}) collective-permute-start(bf16[2,32,1792]{2,1,0:T(8,128)(2,1)S(1)} %get-tuple-element.168), channel_id=1, source_target_pairs={{0,48},{16,32},{32,16},{48,0},{1,49},{17,33},{33,17},{49,1},{2,50}... | collective-permute-start | bytes 688136 | tf_op jit(solution)/shard_map/ppermute | solution.py:384
  138.4 9.4 %collective-permute-start.36 = (bf16[64,1024]{1,0:T(8,128)(2,1)S(1)}, bf16[64,1024]{1,0:T(8,128)(2,1)S(1)}, u32[]{:S(2)}, u32[]{:S(2)}) collective-permute-start(bf16[64,1024]{1,0:T(8,128)(2,1)S(1)} %shard_map.259.p0), channel_id=1, source_target_pairs={{0,2},{2,0},{1,3},{3,1},{4,6},{6,4},{5,7},{7,5},{8,10},{10,8},{9,1... | collective-permute-start | bytes 393224 | tf_op jit(solution)/shard_map/ppermute | solution.py:384
  142.4 7.1 %collective-permute-start.37 = (bf16[64,1024]{1,0:T(8,128)(2,1)S(1)}, bf16[64,1024]{1,0:T(8,128)(2,1)S(1)}, u32[]{:S(2)}, u32[]{:S(2)}) collective-permute-start(bf16[64,1024]{1,0:T(8,128)(2,1)S(1)} %collective-permute-done.35.p1), channel_id=1, source_target_pairs={{0,2},{2,0},{1,3},{3,1},{4,6},{6,4},{5,7},{7,5},{8,10},{10,8},{9,1... | collective-permute-start | bytes 393224 | tf_op jit(solution)/shard_map/ppermute | solution.py:384
  153.1 8.3 %collective-permute-start.43 = (bf16[32,1792]{1,0:T(8,128)(2,1)S(1)}, bf16[32,1792]{1,0:T(8,128)(2,1)S(1)}, u32[]{:S(2)}, u32[]{:S(2)}) collective-permute-start(bf16[32,1792]{1,0:T(8,128)(2,1)S(1)} %get-tuple-element.173), channel_id=1, source_target_pairs={{0,64},{64,0},{1,65},{65,1},{2,66},{66,2},{3,67},{67,3},{4,68},{68... | collective-permute-start | bytes 344072 | tf_op jit(solution)/shard_map/ppermute | solution.py:384
  154.8 6.1 %collective-permute-start.39 = (f32[8,384]{1,0:T(8,128)S(1)}, f32[8,384]{1,0:T(8,128)S(1)}, u32[]{:S(2)}, u32[]{:S(2)}) collective-permute-start(f32[8,384]{1,0:T(8,128)S(1)} %shard_map.263.one), channel_id=1, source_target_pairs={{0,2},{2,0},{1,3},{3,1},{4,6},{6,4},{5,7},{7,5},{8,10},{10,8},{9,1... | collective-permute-start | bytes 36872 | tf_op jit(solution)/shard_map/ppermute | solution.py:384
  (24 other events, 190.8 us)
Sparse Core Ops, SparseCore 0:
  16.8 53.6 all-gather.2
  90.2 42.1 reduce-scatter.1

commit v10 on v9

--- a/solution.py
+++ b/solution.py
@@ -291,7 +291,7 @@
     def fold(part):
         return jnp.concatenate([part[:, i * 128 : (i + 1) * 128] for i in range(8)])
     heads = jnp.concatenate([heads, jnp.zeros((6, 128), F32)])
-    gains[...] = jnp.concatenate([fold(attn_part), fold(ffn_part), heads], axis=1).astype(BF)
+    gains[...] = jnp.concatenate([fold(attn_part), fold(ffn_part), heads], axis=1)
     partial = partial.reshape(4, 2, 32, 1024)
     send[...] = partial[:, 1].astype(BF)
     keep[...] = partial[:, 0]
@@ -304,7 +304,7 @@
     second = left_product(d_attn[...], o[...].astype(BF)).astype(BF)
     dw[:, :32, :256] = first.reshape(32, 32, 256)
     dw[:, :32, 256:] = second.reshape(32, 32, 128)
-    dw[:, 32:] = jnp.broadcast_to(gains[...][None], (32, 8, 384))
+    dw[:, 32:] = jnp.broadcast_to(gains[...].astype(BF)[None], (32, 8, 384))
 
 
 def token_rows(own, one, two, three, dh, x, gain, block, out):
@@ -316,9 +316,13 @@
     out[32:] = block[...]
 
 
-def finish_attend(parts, wq, wk, wv, wo, gains):
+def finish_attend(parts, wq, wk, wv, wo, attn, ffn, query, key):
     sums = [jnp.sum(parts[z].astype(F32), axis=0) for z in range(2)]
-    gains[...] = sums[0][32:] + sums[1][32:]
+    gains = sums[0][32:] + sums[1][32:]
+    attn[...] = gains[:, :128]
+    ffn[...] = gains[:, 128:256]
+    query[...] = gains[0:1, 256:320] + gains[0:1, 320:384]
+    key[...] = gains[1:2, 256:320]
     low, high = sums[0][:32], sums[1][:32]
     wq[...] = jnp.concatenate([low[:, :128], high[:, :128]], axis=1)
     wk[...] = jnp.concatenate([low[:, 128:192], high[:, 128:192]], axis=1)
@@ -339,14 +343,6 @@
 
 def add_two(own, one, out):
     out[...] = own[...] + one[...]
-
-
-def finish_gains(one, two, attn, ffn, query, key):
-    total = one[...] + two[...]
-    attn[...] = total[:8, :128]
-    ffn[...] = total[:8, 128:256]
-    query[...] = total[0:1, 256:320] + total[0:1, 320:384]
-    key[...] = total[1:2, 256:320]
 
 
 def prepare(zl, head, wq, wk, wv, wo, wg, wu, wd, tokens, blocks, send_f, keep_f, x_own):
@@ -500,10 +496,12 @@
         *gather_rows(d_low), Far(qh), *[Far(t) for t in kvs], own_places, places, Far(w_a), Far(o), Far(l),
     )
     d_qkv, send, keep, gains = call(
-        project_grad, [((256, 256), BF)] + halves + [((8, 384), BF)],
+        project_grad, [((256, 256), BF)] + halves + [((8, 384), F32)],
         d_qh, d_kvs[0], *fan(d_kvs, "y"), Far(qkv), cosine, sine, qk_gain, Far(w_a),
         Far(x_own), Far(x_other), Far(ffn_part),
     )
+    for axis in ("c", "zh"):
+        (gains,) = call(add_two, [((8, 384), F32)], gains, swap(gains, axis, 2, 1))
     (dw_a,) = call(
         attend_weights, [((32, 40, 384), BF)],
         Far(x_own), Far(x_other), attn_gain_row, d_qkv, Far(d_attn), Far(o), gains,
@@ -519,19 +517,15 @@
     tokens_grad, block_out = tokens_grad[None], block_out[None]
 
     (dw_a,) = after([dw_a], tokens_grad)
-    grad_wq, grad_wk, grad_wv, grad_wo, gains = call(
+    grad_wq, grad_wk, grad_wv, grad_wo, attn_sum, ffn_sum, query_sum, key_sum = call(
         finish_attend,
-        [Far(((32, n), F32)) for n in (256, 128, 128, 256)] + [((8, 384), F32)],
+        [Far(((32, n), F32)) for n in (256, 128, 128, 256)]
+        + [((8, 128), F32)] * 2 + [((1, 64), F32)] * 2,
         dw_a.reshape(2, 16, 40, 384),
-    )
-    (gains,) = call(add_two, [((8, 384), F32)], gains, swap(gains, "c", 2, 1))
-    attn_sum, ffn_sum, query_sum, key_sum = call(
-        finish_gains, [((8, 128), F32)] * 2 + [((1, 64), F32)] * 2,
-        gains, swap(gains, "zh", 2, 1),
     )
     (dw_f,) = after([dw_f], rows)
     sides = call(split_sides, [((2, 32, 1792), BF)] * 4, Far(dw_f))
-    others = after(fan(sides, "y"), gains)
+    others = after(fan(sides, "y"), attn_sum)
     own_f, send_f = call(
         add_sides, [((32, 1792), F32), ((32, 1792), BF)], sides[0], *others,
         scalars=(zl_ref,),

time: 170 us -> 170 us (level)
  waiting for transfers between devices: 58.9 us -> 61.4 us
    ppermute x44, waiting for transfers between devices: 55.1 us -> 61.4 us  [swap(): return lax.ppermute(value, axes, [(i, i ^ mask) for i in range(size)])]
    reduce_scatter x1, waiting for transfers between devices: 3.84 us -> 0.02 us  [local(): lax.psum_scatter(dw_f.reshape(1024, 1792), 'x', scatter_dimension=0, tile...]
    ppermute x44, starting transfers between devices: 51.8 us -> 49.9 us  [swap(): return lax.ppermute(value, axes, [(i, i ^ mask) for i in range(size)])]
  transfers between devices with their start and end apart: 48 -> 48, of which waited for: 36 -> 34; matrix products, arithmetic and copies ran while one was open for 3% -> 3% of each run, Pallas kernels for 7% -> 7%
where the time goes in v10:
time: 170 us
  starting transfers between devices  63.9 us (38%)
  waiting for transfers between devices  61.4 us (36%)
  Pallas kernels  18.2 us (11%)
  between operations  14.3 us (8%)
  local copies, waits for them, and re-layouts  8.86 us (5%)
  other arithmetic  2.85 us (2%)
    ppermute x44, waiting for transfers between devices, swap(): return lax.ppermute(value, axes, [(i, i ^ mask) for i in range(size)])  61.4 us
    ppermute x44, starting transfers between devices, swap(): return lax.ppermute(value, axes, [(i, i ^ mask) for i in range(size)])  49.9 us
    pallas_call x23, Pallas kernels, call(): pl.pallas_call(body, out_shape=[jax.ShapeDtypeStruct(*bare(out)) for out...  18.2 us
    all_to_all x1, starting transfers between devices, local(): w_a = lax.all_to_all(blocks.reshape(1024, 384), PLANE, 0, 0, tiled=True)  8.51 us
    unnamed x16, local copies, waits for them, and re-layouts  5.93 us
    all_to_all x1, starting transfers between devices, local(): dw_a = lax.all_to_all(dw_a, PLANE, 0, 0, tiled=True)  5.49 us
  transfers between devices with their start and end apart: 48, of which 34 were waited for; matrix products, arithmetic and copies ran while one was open for 3% of the time, Pallas kernels for 7%

profile of v10, /device:TPU:0, one launch (start us, length us, event | category | flops | bytes accessed | tf_op | source)
XLA Modules:
  0.0 169.6 jit_solution(12599354377864414536)
XLA Ops:
  7.3 2.3 %shard_map.246 = (bf16[2,16,32,384]{3,2,1,0:T(8,128)(2,1)}, bf16[32,1792]{1,0:T(8,128)(2,1)}, bf16[32,1792]{1,0:T(8,128)(2,1)}, bf16[128,1024]{1,0:T(8,128)(2,1)}) custom-call(s32[1]{0:T(128)} %bitcast.1.zl, s32[1]{0:T(128)} %bitcast.head, bf16[32,256]{1,0:T(8,128)(2,1)} %wq.1, bf16[32,128]{1,0:T(8,128)(2,1)} %wk.1, bf16[32,128]{1,0:T(8,128)(2,1)} %wv.1, ...), custom_call_target="tpu_custom_call" | custom-call | tf_op jit(solution)/shard_map/pallas_call | solution.py:37
  9.6 2.1 %collective-permute-start.13 = (bf16[32,1792]{1,0:T(8,128)(2,1)}, bf16[32,1792]{1,0:T(8,128)(2,1)S(1)}, u32[]{:S(2)}, u32[]{:S(2)}) collective-permute-start(bf16[32,1792]{1,0:T(8,128)(2,1)} %get-tuple-element.109), channel_id=1, source_target_pairs={{0,64},{64,0},{1,65},{65,1},{2,66},{66,2},{3,67},{67,3},{4,68},{68... | collective-permute-start | bytes 344072 | tf_op jit(solution)/shard_map/ppermute | solution.py:380
  11.7 3.4 %collective-permute-done.13.got = bf16[32,1792]{1,0:T(8,128)(2,1)S(1)} collective-permute-done((bf16[32,1792]{1,0:T(8,128)(2,1)}, bf16[32,1792]{1,0:T(8,128)(2,1)S(1)}, u32[]{:S(2)}, u32[]{:S(2)}) %collective-permute-start.13) | collective-permute-done | bytes 114720 | tf_op jit(solution)/shard_map/ppermute | solution.py:380
  16.7 8.5 %all-to-all-start = ((bf16[32,32,384]{2,1,0:T(8,128)(2,1)}), bf16[32,32,384]{2,1,0:T(8,128)(2,1)S(1)}, u32[]{:S(2)}, u32[]{:S(2)}) async-start(bf16[32,32,384]{2,1,0:T(8,128)(2,1)} %bitcast.28), calls=%async_computation | async-start | bytes 1572864 | tf_op jit(solution)/shard_map/all_to_all | solution.py:440
  25.2 1.9 %collective-permute-start = (bf16[128,1024]{1,0:T(8,128)(2,1)}, bf16[128,1024]{1,0:T(8,128)(2,1)S(1)}, u32[]{:S(2)}, u32[]{:S(2)}) collective-permute-start(bf16[128,1024]{1,0:T(8,128)(2,1)} %get-tuple-element.94.own.x.x_own), channel_id=1, source_target_pairs={{0,64},{64,0},{1,65},{65,1},{2,66},{66,2},{3,67},{67,3},{4,68},{68... | collective-permute-start | bytes 786440 | tf_op jit(solution)/shard_map/ppermute | solution.py:380
  32.7 7.9 %collective-permute-done.other.x_other = bf16[128,1024]{1,0:T(8,128)(2,1)S(1)} collective-permute-done((bf16[128,1024]{1,0:T(8,128)(2,1)}, bf16[128,1024]{1,0:T(8,128)(2,1)S(1)}, u32[]{:S(2)}, u32[]{:S(2)}) %collective-permute-start) | collective-permute-done | bytes 262176 | tf_op jit(solution)/shard_map/ppermute | solution.py:380
  42.7 2.2 %collective-permute-start.4 = (bf16[256,128]{1,0:T(8,128)(2,1)S(1)}, bf16[256,128]{1,0:T(8,128)(2,1)S(1)}, u32[]{:S(2)}, u32[]{:S(2)}) collective-permute-start(bf16[256,128]{1,0:T(8,128)(2,1)S(1)} %get-tuple-element.98.kv0), channel_id=1, source_target_pairs={{0,48},{16,32},{32,16},{48,0},{1,49},{17,33},{33,17},{49,1},{2,50}... | collective-permute-start | bytes 196616 | tf_op jit(solution)/shard_map/ppermute | solution.py:380
  48.9 1.8 %collective-permute-done.3.kv2 = bf16[256,128]{1,0:T(8,128)(2,1)S(1)} collective-permute-done((bf16[256,128]{1,0:T(8,128)(2,1)S(1)}, bf16[256,128]{1,0:T(8,128)(2,1)S(1)}, u32[]{:S(2)}, u32[]{:S(2)}) %collective-permute-start.3) | collective-permute-done | bytes 65568 | tf_op jit(solution)/shard_map/ppermute | solution.py:380
  53.7 3.6 %collective-permute-start.6 = (bf16[32,1024]{1,0:T(8,128)(2,1)S(1)}, bf16[32,1024]{1,0:T(8,128)(2,1)S(1)}, u32[]{:S(2)}, u32[]{:S(2)}) collective-permute-start(bf16[32,1024]{1,0:T(8,128)(2,1)S(1)} %get-tuple-element.104), channel_id=1, source_target_pairs={{0,2},{2,0},{64,66},{66,64},{1,3},{3,1},{65,67},{67,65},{4,6},{6,4... | collective-permute-start | bytes 196616 | tf_op jit(solution)/shard_map/ppermute | solution.py:380
  58.0 2.0 %collective-permute-done.6.one = bf16[32,1024]{1,0:T(8,128)(2,1)S(1)} collective-permute-done((bf16[32,1024]{1,0:T(8,128)(2,1)S(1)}, bf16[32,1024]{1,0:T(8,128)(2,1)S(1)}, u32[]{:S(2)}, u32[]{:S(2)}) %collective-permute-start.6) | collective-permute-done | bytes 65568 | tf_op jit(solution)/shard_map/ppermute | solution.py:380
  64.6 3.8 %collective-permute-start.10 = (bf16[32,1024]{1,0:T(8,128)(2,1)S(1)}, bf16[32,1024]{1,0:T(8,128)(2,1)S(1)}, u32[]{:S(2)}, u32[]{:S(2)}) collective-permute-start(bf16[32,1024]{1,0:T(8,128)(2,1)S(1)} %get-tuple-element.107.p0), channel_id=1, source_target_pairs={{0,2},{2,0},{64,66},{66,64},{1,3},{3,1},{65,67},{67,65},{4,6},{6,4... | collective-permute-start | bytes 196616 | tf_op jit(solution)/shard_map/ppermute | solution.py:380
  73.1 2.0 %copy-done.2 = bf16[32,32,1792]{2,1,0:T(8,128)(2,1)S(1)} copy-done((bf16[32,32,1792]{2,1,0:T(8,128)(2,1)S(1)}, bf16[32,32,1792]{2,1,0:T(8,128)(2,1)}, u32[]{:S(2)}) %copy-start.2) | copy-done | bytes 3670040
  75.1 2.6 %shard_map.253 = (bf16[4,64,1024]{2,1,0:T(8,128)(2,1)S(1)}, f32[4,64,1024]{2,1,0:T(8,128)S(1)}, bf16[256,1024]{1,0:T(8,128)(2,1)S(1)}, bf16[256,640]{1,0:T(8,128)(2,1)S(1)}, bf16[256,1152]{1,0:T(8,128)(2,1)S(1)}) custom-call(bf16[32,1024]{1,0:T(8,128)(2,1)S(1)} %get-tuple-element.107.p0, bf16[32,1024]{1,0:T(8,128)(2,1)S(1)} %collective-permute-done.9.p1, ...), custom_call_target="tpu_custom_call" | custom-call | tf_op jit(solution)/shard_map/pallas_call | solution.py:37
  79.8 2.9 %collective-permute-start.18 = (bf16[64,1024]{1,0:T(8,128)(2,1)S(1)}, bf16[64,1024]{1,0:T(8,128)(2,1)S(1)}, u32[]{:S(2)}, u32[]{:S(2)}) collective-permute-start(bf16[64,1024]{1,0:T(8,128)(2,1)S(1)} %get-tuple-element.116), channel_id=1, source_target_pairs={{0,2},{2,0},{64,66},{66,64},{1,3},{3,1},{65,67},{67,65},{4,6},{6,4... | collective-permute-start | bytes 393224 | tf_op jit(solution)/shard_map/ppermute | solution.py:380
  90.1 2.0 %collective-permute-start.24 = (bf16[32,1024]{1,0:T(8,128)(2,1)S(1)}, bf16[32,1024]{1,0:T(8,128)(2,1)S(1)}, u32[]{:S(2)}, u32[]{:S(2)}) collective-permute-start(bf16[32,1024]{1,0:T(8,128)(2,1)S(1)} %get-tuple-element.120.p0), channel_id=1, source_target_pairs={{0,66},{2,64},{64,2},{66,0},{1,67},{3,65},{65,3},{67,1},{4,70},{6,... | collective-permute-start | bytes 196616 | tf_op jit(solution)/shard_map/ppermute | solution.py:380
  92.8 2.0 %collective-permute-start.22 = (bf16[32,1024]{1,0:T(8,128)(2,1)S(1)}, bf16[32,1024]{1,0:T(8,128)(2,1)S(1)}, u32[]{:S(2)}, u32[]{:S(2)}) collective-permute-start(bf16[32,1024]{1,0:T(8,128)(2,1)S(1)} %get-tuple-element.120.p0), channel_id=1, source_target_pairs={{0,2},{2,0},{64,66},{66,64},{1,3},{3,1},{65,67},{67,65},{4,6},{6,4... | collective-permute-start | bytes 196616 | tf_op jit(solution)/shard_map/ppermute | solution.py:380
  96.4 2.2 %collective-permute-done.22.p2 = bf16[32,1024]{1,0:T(8,128)(2,1)S(1)} collective-permute-done((bf16[32,1024]{1,0:T(8,128)(2,1)S(1)}, bf16[32,1024]{1,0:T(8,128)(2,1)S(1)}, u32[]{:S(2)}, u32[]{:S(2)}) %collective-permute-start.22) | collective-permute-done | bytes 65568 | tf_op jit(solution)/shard_map/ppermute | solution.py:380
  100.4 3.1 %shard_map.256 = (bf16[256,1024]{1,0:T(8,128)(2,1)S(1)}, f32[256,128]{1,0:T(8,128)S(1)}, f32[256,128]{1,0:T(8,128)S(1)}, bf16[256,128]{1,0:T(8,128)(2,1)S(1)}, b...) custom-call(bf16[32,1024]{1,0:T(8,128)(2,1)S(1)} %get-tuple-element.120.p0, ...), custom_call_target="tpu_custom_call" | custom-call | tf_op jit(solution)/shard_map/pallas_call | solution.py:37
  104.0 2.7 %collective-permute-start.29 = (bf16[256,128]{1,0:T(8,128)(2,1)S(1)}, bf16[256,128]{1,0:T(8,128)(2,1)S(1)}, u32[]{:S(2)}, u32[]{:S(2)}) collective-permute-start(bf16[256,128]{1,0:T(8,128)(2,1)S(1)} %get-tuple-element.129), channel_id=1, source_target_pairs={{0,32},{16,48},{32,0},{48,16},{1,33},{17,49},{33,1},{49,17},{2,34}... | collective-permute-start | bytes 196616 | tf_op jit(solution)/shard_map/ppermute | solution.py:380
  108.3 1.9 %collective-permute-done.29.two = bf16[256,128]{1,0:T(8,128)(2,1)S(1)} collective-permute-done((bf16[256,128]{1,0:T(8,128)(2,1)S(1)}, bf16[256,128]{1,0:T(8,128)(2,1)S(1)}, u32[]{:S(2)}, u32[]{:S(2)}) %collective-permute-start.29) | collective-permute-done | bytes 65568 | tf_op jit(solution)/shard_map/ppermute | solution.py:380
  110.2 1.9 %collective-permute-done.30.three = bf16[256,128]{1,0:T(8,128)(2,1)S(1)} collective-permute-done((bf16[256,128]{1,0:T(8,128)(2,1)S(1)}, bf16[256,128]{1,0:T(8,128)(2,1)S(1)}, u32[]{:S(2)}, u32[]{:S(2)}) %collective-permute-start.30) | collective-permute-done | bytes 65568 | tf_op jit(solution)/shard_map/ppermute | solution.py:380
  114.9 2.1 %collective-permute-start.32 = (bf16[32,1024]{1,0:T(8,128)(2,1)S(1)}, bf16[32,1024]{1,0:T(8,128)(2,1)S(1)}, u32[]{:S(2)}, u32[]{:S(2)}) collective-permute-start(bf16[32,1024]{1,0:T(8,128)(2,1)S(1)} %get-tuple-element.136), channel_id=1, source_target_pairs={{0,2},{2,0},{64,66},{66,64},{1,3},{3,1},{65,67},{67,65},{4,6},{6,4... | collective-permute-start | bytes 196616 | tf_op jit(solution)/shard_map/ppermute | solution.py:380
  117.7 1.8 %collective-permute-start.34 = (bf16[32,1024]{1,0:T(8,128)(2,1)S(1)}, bf16[32,1024]{1,0:T(8,128)(2,1)S(1)}, u32[]{:S(2)}, u32[]{:S(2)}) collective-permute-start(bf16[32,1024]{1,0:T(8,128)(2,1)S(1)} %get-tuple-element.138), channel_id=1, source_target_pairs={{0,66},{2,64},{64,2},{66,0},{1,67},{3,65},{65,3},{67,1},{4,70},{6,... | collective-permute-start | bytes 196616 | tf_op jit(solution)/shard_map/ppermute | solution.py:380
  122.3 3.6 %collective-permute-done.39.one = f32[8,384]{1,0:T(8,128)S(1)} collective-permute-done((f32[8,384]{1,0:T(8,128)S(1)}, f32[8,384]{1,0:T(8,128)S(1)}, u32[]{:S(2)}, u32[]{:S(2)}) %collective-permute-start.39) | collective-permute-done | bytes 12320 | tf_op jit(solution)/shard_map/ppermute | solution.py:380
  127.5 5.5 %all-to-all-start.1 = ((bf16[32,40,384]{2,1,0:T(8,128)(2,1)}), bf16[32,40,384]{2,1,0:T(8,128)(2,1)S(1)}, u32[]{:S(2)}, u32[]{:S(2)}) async-start(bf16[32,40,384]{2,1,0:T(8,128)(2,1)} %shard_map.263), calls=%async_computation.1 | async-start | bytes 1966080 | tf_op jit(solution)/shard_map/all_to_all | solution.py:512
  134.6 1.9 %collective-permute-start.40 = (bf16[2,32,1792]{2,1,0:T(8,128)(2,1)S(1)}, bf16[2,32,1792]{2,1,0:T(8,128)(2,1)S(1)}, u32[]{:S(2)}, u32[]{:S(2)}) collective-permute-start(bf16[2,32,1792]{2,1,0:T(8,128)(2,1)S(1)} %get-tuple-element.164), channel_id=1, source_target_pairs={{0,16},{16,0},{32,48},{48,32},{1,17},{17,1},{33,49},{49,33},{2,18}... | collective-permute-start | bytes 688136 | tf_op jit(solution)/shard_map/ppermute | solution.py:380
  136.5 2.7 %collective-permute-start.41 = (bf16[2,32,1792]{2,1,0:T(8,128)(2,1)S(1)}, bf16[2,32,1792]{2,1,0:T(8,128)(2,1)S(1)}, u32[]{:S(2)}, u32[]{:S(2)}) collective-permute-start(bf16[2,32,1792]{2,1,0:T(8,128)(2,1)S(1)} %get-tuple-element.165), channel_id=1, source_target_pairs={{0,32},{16,48},{32,0},{48,16},{1,33},{17,49},{33,1},{49,17},{2,34}... | collective-permute-start | bytes 688136 | tf_op jit(solution)/shard_map/ppermute | solution.py:380
  139.4 2.2 %collective-permute-start.36 = (bf16[64,1024]{1,0:T(8,128)(2,1)S(1)}, bf16[64,1024]{1,0:T(8,128)(2,1)S(1)}, u32[]{:S(2)}, u32[]{:S(2)}) collective-permute-start(bf16[64,1024]{1,0:T(8,128)(2,1)S(1)} %shard_map.259.p0), channel_id=1, source_target_pairs={{0,2},{2,0},{1,3},{3,1},{4,6},{6,4},{5,7},{7,5},{8,10},{10,8},{9,1... | collective-permute-start | bytes 393224 | tf_op jit(solution)/shard_map/ppermute | solution.py:380
  142.9 7.3 %collective-permute-done.36.p2 = bf16[64,1024]{1,0:T(8,128)(2,1)S(1)} collective-permute-done((bf16[64,1024]{1,0:T(8,128)(2,1)S(1)}, bf16[64,1024]{1,0:T(8,128)(2,1)S(1)}, u32[]{:S(2)}, u32[]{:S(2)}) %collective-permute-start.36) | collective-permute-done | bytes 131104 | tf_op jit(solution)/shard_map/ppermute | solution.py:380
  150.2 2.7 %collective-permute-done.37.p3 = bf16[64,1024]{1,0:T(8,128)(2,1)S(1)} collective-permute-done((bf16[64,1024]{1,0:T(8,128)(2,1)S(1)}, bf16[64,1024]{1,0:T(8,128)(2,1)S(1)}, u32[]{:S(2)}, u32[]{:S(2)}) %collective-permute-start.37) | collective-permute-done | bytes 131104 | tf_op jit(solution)/shard_map/ppermute | solution.py:380
  154.5 2.3 %collective-permute-done.41.two = bf16[2,32,1792]{2,1,0:T(8,128)(2,1)S(1)} collective-permute-done((bf16[2,32,1792]{2,1,0:T(8,128)(2,1)S(1)}, bf16[2,32,1792]{2,1,0:T(8,128)(2,1)S(1)}, u32[]{:S(2)}, u32[]{:S(2)}) %collective-permute-start.41) | collective-permute-done | bytes 229408 | tf_op jit(solution)/shard_map/ppermute | solution.py:380
  158.6 3.3 %collective-permute-done.43.got = bf16[32,1792]{1,0:T(8,128)(2,1)S(1)} collective-permute-done((bf16[32,1792]{1,0:T(8,128)(2,1)S(1)}, bf16[32,1792]{1,0:T(8,128)(2,1)S(1)}, u32[]{:S(2)}, u32[]{:S(2)}) %collective-permute-start.43) | collective-permute-done | bytes 114720 | tf_op jit(solution)/shard_map/ppermute | solution.py:380
  (123 shorter events, 57.0 us)
Async XLA Ops:
  7.2 64.1 %all-gather.3.cloned.1.call-start = ((), (), s32[]{:S(2)}) async-start(), calls=%async_computation.4 | async-start | bytes 3899392 | tf_op jit(solution)/shard_map/all_gather | solution.py:442
  9.6 5.4 %collective-permute-start.13 = (bf16[32,1792]{1,0:T(8,128)(2,1)}, bf16[32,1792]{1,0:T(8,128)(2,1)S(1)}, u32[]{:S(2)}, u32[]{:S(2)}) collective-permute-start(bf16[32,1792]{1,0:T(8,128)(2,1)} %get-tuple-element.109), channel_id=1, source_target_pairs={{0,64},{64,0},{1,65},{65,1},{2,66},{66,2},{3,67},{67,3},{4,68},{68... | collective-permute-start | bytes 344072 | tf_op jit(solution)/shard_map/ppermute | solution.py:380
  16.7 23.9 %all-to-all-start = ((bf16[32,32,384]{2,1,0:T(8,128)(2,1)}), bf16[32,32,384]{2,1,0:T(8,128)(2,1)S(1)}, u32[]{:S(2)}, u32[]{:S(2)}) async-start(bf16[32,32,384]{2,1,0:T(8,128)(2,1)} %bitcast.28), calls=%async_computation | async-start | bytes 1572864 | tf_op jit(solution)/shard_map/all_to_all | solution.py:440
  25.2 108.2 %reduce-scatter.2.cloned.1.call-start = ((), (), s32[]{:S(2)}) async-start(), calls=%async_computation.3 | async-start | bytes 4587520 | tf_op jit(solution)/shard_map/reduce_scatter | solution.py:493
  25.2 15.4 %collective-permute-start = (bf16[128,1024]{1,0:T(8,128)(2,1)}, bf16[128,1024]{1,0:T(8,128)(2,1)S(1)}, u32[]{:S(2)}, u32[]{:S(2)}) collective-permute-start(bf16[128,1024]{1,0:T(8,128)(2,1)} %get-tuple-element.94.own.x.x_own), channel_id=1, source_target_pairs={{0,64},{64,0},{1,65},{65,1},{2,66},{66,2},{3,67},{67,3},{4,68},{68... | collective-permute-start | bytes 786440 | tf_op jit(solution)/shard_map/ppermute | solution.py:380
  41.4 6.9 %collective-permute-start.1 = (bf16[128,1024]{1,0:T(8,128)(2,1)S(1)}, bf16[128,1024]{1,0:T(8,128)(2,1)S(1)}, u32[]{:S(2)}, u32[]{:S(2)}) collective-permute-start(bf16[128,1024]{1,0:T(8,128)(2,1)S(1)} %shard_map.248.dy_own.dy), channel_id=1, source_target_pairs={{0,64},{64,0},{1,65},{65,1},{2,66},{66,2},{3,67},{67,3},{4,68},{68... | collective-permute-start | bytes 786440 | tf_op jit(solution)/shard_map/ppermute | solution.py:380
  42.7 6.2 %collective-permute-start.4 = (bf16[256,128]{1,0:T(8,128)(2,1)S(1)}, bf16[256,128]{1,0:T(8,128)(2,1)S(1)}, u32[]{:S(2)}, u32[]{:S(2)}) collective-permute-start(bf16[256,128]{1,0:T(8,128)(2,1)S(1)} %get-tuple-element.98.kv0), channel_id=1, source_target_pairs={{0,48},{16,32},{32,16},{48,0},{1,49},{17,33},{33,17},{49,1},{2,50}... | collective-permute-start | bytes 196616 | tf_op jit(solution)/shard_map/ppermute | solution.py:380
  44.9 5.8 %collective-permute-start.3 = (bf16[256,128]{1,0:T(8,128)(2,1)S(1)}, bf16[256,128]{1,0:T(8,128)(2,1)S(1)}, u32[]{:S(2)}, u32[]{:S(2)}) collective-permute-start(bf16[256,128]{1,0:T(8,128)(2,1)S(1)} %get-tuple-element.98.kv0), channel_id=1, source_target_pairs={{0,32},{16,48},{32,0},{48,16},{1,33},{17,49},{33,1},{49,17},{2,34}... | collective-permute-start | bytes 196616 | tf_op jit(solution)/shard_map/ppermute | solution.py:380
  53.7 6.3 %collective-permute-start.6 = (bf16[32,1024]{1,0:T(8,128)(2,1)S(1)}, bf16[32,1024]{1,0:T(8,128)(2,1)S(1)}, u32[]{:S(2)}, u32[]{:S(2)}) collective-permute-start(bf16[32,1024]{1,0:T(8,128)(2,1)S(1)} %get-tuple-element.104), channel_id=1, source_target_pairs={{0,2},{2,0},{64,66},{66,64},{1,3},{3,1},{65,67},{67,65},{4,6},{6,4... | collective-permute-start | bytes 196616 | tf_op jit(solution)/shard_map/ppermute | solution.py:380
  58.0 5.5 %collective-permute-start.8 = (bf16[32,1024]{1,0:T(8,128)(2,1)S(1)}, bf16[32,1024]{1,0:T(8,128)(2,1)S(1)}, u32[]{:S(2)}, u32[]{:S(2)}) collective-permute-start(bf16[32,1024]{1,0:T(8,128)(2,1)S(1)} %get-tuple-element.106), channel_id=1, source_target_pairs={{0,66},{2,64},{64,2},{66,0},{1,67},{3,65},{65,3},{67,1},{4,70},{6,... | collective-permute-start | bytes 196616 | tf_op jit(solution)/shard_map/ppermute | solution.py:380
  63.6 6.0 %collective-permute-start.12 = (bf16[32,1024]{1,0:T(8,128)(2,1)S(1)}, bf16[32,1024]{1,0:T(8,128)(2,1)S(1)}, u32[]{:S(2)}, u32[]{:S(2)}) collective-permute-start(bf16[32,1024]{1,0:T(8,128)(2,1)S(1)} %get-tuple-element.107.p0), channel_id=1, source_target_pairs={{0,66},{2,64},{64,2},{66,0},{1,67},{3,65},{65,3},{67,1},{4,70},{6,... | collective-permute-start | bytes 196616 | tf_op jit(solution)/shard_map/ppermute | solution.py:380
  64.4 5.2 %collective-permute-start.11 = (bf16[32,1024]{1,0:T(8,128)(2,1)S(1)}, bf16[32,1024]{1,0:T(8,128)(2,1)S(1)}, u32[]{:S(2)}, u32[]{:S(2)}) collective-permute-start(bf16[32,1024]{1,0:T(8,128)(2,1)S(1)} %get-tuple-element.107.p0), channel_id=1, source_target_pairs={{0,64},{2,66},{64,0},{66,2},{1,65},{3,67},{65,1},{67,3},{4,68},{6,... | collective-permute-start | bytes 196616 | tf_op jit(solution)/shard_map/ppermute | solution.py:380
  64.6 6.7 %collective-permute-start.10 = (bf16[32,1024]{1,0:T(8,128)(2,1)S(1)}, bf16[32,1024]{1,0:T(8,128)(2,1)S(1)}, u32[]{:S(2)}, u32[]{:S(2)}) collective-permute-start(bf16[32,1024]{1,0:T(8,128)(2,1)S(1)} %get-tuple-element.107.p0), channel_id=1, source_target_pairs={{0,2},{2,0},{64,66},{66,64},{1,3},{3,1},{65,67},{67,65},{4,6},{6,4... | collective-permute-start | bytes 196616 | tf_op jit(solution)/shard_map/ppermute | solution.py:380
  79.8 7.9 %collective-permute-start.18 = (bf16[64,1024]{1,0:T(8,128)(2,1)S(1)}, bf16[64,1024]{1,0:T(8,128)(2,1)S(1)}, u32[]{:S(2)}, u32[]{:S(2)}) collective-permute-start(bf16[64,1024]{1,0:T(8,128)(2,1)S(1)} %get-tuple-element.116), channel_id=1, source_target_pairs={{0,2},{2,0},{64,66},{66,64},{1,3},{3,1},{65,67},{67,65},{4,6},{6,4... | collective-permute-start | bytes 393224 | tf_op jit(solution)/shard_map/ppermute | solution.py:380
  82.7 6.4 %collective-permute-start.19 = (bf16[64,1024]{1,0:T(8,128)(2,1)S(1)}, bf16[64,1024]{1,0:T(8,128)(2,1)S(1)}, u32[]{:S(2)}, u32[]{:S(2)}) collective-permute-start(bf16[64,1024]{1,0:T(8,128)(2,1)S(1)} %get-tuple-element.117), channel_id=1, source_target_pairs={{0,64},{2,66},{64,0},{66,2},{1,65},{3,67},{65,1},{67,3},{4,68},{6,... | collective-permute-start | bytes 393224 | tf_op jit(solution)/shard_map/ppermute | solution.py:380
  82.8 7.1 %collective-permute-start.20 = (bf16[64,1024]{1,0:T(8,128)(2,1)S(1)}, bf16[64,1024]{1,0:T(8,128)(2,1)S(1)}, u32[]{:S(2)}, u32[]{:S(2)}) collective-permute-start(bf16[64,1024]{1,0:T(8,128)(2,1)S(1)} %get-tuple-element.118), channel_id=1, source_target_pairs={{0,66},{2,64},{64,2},{66,0},{1,67},{3,65},{65,3},{67,1},{4,70},{6,... | collective-permute-start | bytes 393224 | tf_op jit(solution)/shard_map/ppermute | solution.py:380
  90.1 5.6 %collective-permute-start.24 = (bf16[32,1024]{1,0:T(8,128)(2,1)S(1)}, bf16[32,1024]{1,0:T(8,128)(2,1)S(1)}, u32[]{:S(2)}, u32[]{:S(2)}) collective-permute-start(bf16[32,1024]{1,0:T(8,128)(2,1)S(1)} %get-tuple-element.120.p0), channel_id=1, source_target_pairs={{0,66},{2,64},{64,2},{66,0},{1,67},{3,65},{65,3},{67,1},{4,70},{6,... | collective-permute-start | bytes 196616 | tf_op jit(solution)/shard_map/ppermute | solution.py:380
  92.8 5.8 %collective-permute-start.22 = (bf16[32,1024]{1,0:T(8,128)(2,1)S(1)}, bf16[32,1024]{1,0:T(8,128)(2,1)S(1)}, u32[]{:S(2)}, u32[]{:S(2)}) collective-permute-start(bf16[32,1024]{1,0:T(8,128)(2,1)S(1)} %get-tuple-element.120.p0), channel_id=1, source_target_pairs={{0,2},{2,0},{64,66},{66,64},{1,3},{3,1},{65,67},{67,65},{4,6},{6,4... | collective-permute-start | bytes 196616 | tf_op jit(solution)/shard_map/ppermute | solution.py:380
  104.0 6.3 %collective-permute-start.29 = (bf16[256,128]{1,0:T(8,128)(2,1)S(1)}, bf16[256,128]{1,0:T(8,128)(2,1)S(1)}, u32[]{:S(2)}, u32[]{:S(2)}) collective-permute-start(bf16[256,128]{1,0:T(8,128)(2,1)S(1)} %get-tuple-element.129), channel_id=1, source_target_pairs={{0,32},{16,48},{32,0},{48,16},{1,33},{17,49},{33,1},{49,17},{2,34}... | collective-permute-start | bytes 196616 | tf_op jit(solution)/shard_map/ppermute | solution.py:380
  106.7 5.5 %collective-permute-start.30 = (bf16[256,128]{1,0:T(8,128)(2,1)S(1)}, bf16[256,128]{1,0:T(8,128)(2,1)S(1)}, u32[]{:S(2)}, u32[]{:S(2)}) collective-permute-start(bf16[256,128]{1,0:T(8,128)(2,1)S(1)} %get-tuple-element.130), channel_id=1, source_target_pairs={{0,48},{16,32},{32,16},{48,0},{1,49},{17,33},{33,17},{49,1},{2,50}... | collective-permute-start | bytes 196616 | tf_op jit(solution)/shard_map/ppermute | solution.py:380
  114.9 12.6 %collective-permute-start.32 = (bf16[32,1024]{1,0:T(8,128)(2,1)S(1)}, bf16[32,1024]{1,0:T(8,128)(2,1)S(1)}, u32[]{:S(2)}, u32[]{:S(2)}) collective-permute-start(bf16[32,1024]{1,0:T(8,128)(2,1)S(1)} %get-tuple-element.136), channel_id=1, source_target_pairs={{0,2},{2,0},{64,66},{66,64},{1,3},{3,1},{65,67},{67,65},{4,6},{6,4... | collective-permute-start | bytes 196616 | tf_op jit(solution)/shard_map/ppermute | solution.py:380
  117.0 10.5 %collective-permute-start.33 = (bf16[32,1024]{1,0:T(8,128)(2,1)S(1)}, bf16[32,1024]{1,0:T(8,128)(2,1)S(1)}, u32[]{:S(2)}, u32[]{:S(2)}) collective-permute-start(bf16[32,1024]{1,0:T(8,128)(2,1)S(1)} %get-tuple-element.137), channel_id=1, source_target_pairs={{0,64},{2,66},{64,0},{66,2},{1,65},{3,67},{65,1},{67,3},{4,68},{6,... | collective-permute-start | bytes 196616 | tf_op jit(solution)/shard_map/ppermute | solution.py:380
  117.7 9.8 %collective-permute-start.34 = (bf16[32,1024]{1,0:T(8,128)(2,1)S(1)}, bf16[32,1024]{1,0:T(8,128)(2,1)S(1)}, u32[]{:S(2)}, u32[]{:S(2)}) collective-permute-start(bf16[32,1024]{1,0:T(8,128)(2,1)S(1)} %get-tuple-element.138), channel_id=1, source_target_pairs={{0,66},{2,64},{64,2},{66,0},{1,67},{3,65},{65,3},{67,1},{4,70},{6,... | collective-permute-start | bytes 196616 | tf_op jit(solution)/shard_map/ppermute | solution.py:380
  120.7 5.2 %collective-permute-start.39 = (f32[8,384]{1,0:T(8,128)S(1)}, f32[8,384]{1,0:T(8,128)S(1)}, u32[]{:S(2)}, u32[]{:S(2)}) collective-permute-start(f32[8,384]{1,0:T(8,128)S(1)} %shard_map.261.own), channel_id=1, source_target_pairs={{0,2},{2,0},{1,3},{3,1},{4,6},{6,4},{5,7},{7,5},{8,10},{10,8},{9,1... | collective-permute-start | bytes 36872 | tf_op jit(solution)/shard_map/ppermute | solution.py:380
  127.5 26.2 %all-to-all-start.1 = ((bf16[32,40,384]{2,1,0:T(8,128)(2,1)}), bf16[32,40,384]{2,1,0:T(8,128)(2,1)S(1)}, u32[]{:S(2)}, u32[]{:S(2)}) async-start(bf16[32,40,384]{2,1,0:T(8,128)(2,1)} %shard_map.263), calls=%async_computation.1 | async-start | bytes 1966080 | tf_op jit(solution)/shard_map/all_to_all | solution.py:512
  133.2 8.3 %collective-permute-start.35 = (bf16[64,1024]{1,0:T(8,128)(2,1)S(1)}, bf16[64,1024]{1,0:T(8,128)(2,1)S(1)}, u32[]{:S(2)}, u32[]{:S(2)}) collective-permute-start(bf16[64,1024]{1,0:T(8,128)(2,1)S(1)} %shard_map.259.p0), channel_id=1, source_target_pairs={{0,1},{1,0},{2,3},{3,2},{4,5},{5,4},{6,7},{7,6},{8,9},{9,8},{10,11... | collective-permute-start | bytes 393224 | tf_op jit(solution)/shard_map/ppermute | solution.py:380
  134.6 19.9 %collective-permute-start.40 = (bf16[2,32,1792]{2,1,0:T(8,128)(2,1)S(1)}, bf16[2,32,1792]{2,1,0:T(8,128)(2,1)S(1)}, u32[]{:S(2)}, u32[]{:S(2)}) collective-permute-start(bf16[2,32,1792]{2,1,0:T(8,128)(2,1)S(1)} %get-tuple-element.164), channel_id=1, source_target_pairs={{0,16},{16,0},{32,48},{48,32},{1,17},{17,1},{33,49},{49,33},{2,18}... | collective-permute-start | bytes 688136 | tf_op jit(solution)/shard_map/ppermute | solution.py:380
  136.5 20.3 %collective-permute-start.41 = (bf16[2,32,1792]{2,1,0:T(8,128)(2,1)S(1)}, bf16[2,32,1792]{2,1,0:T(8,128)(2,1)S(1)}, u32[]{:S(2)}, u32[]{:S(2)}) collective-permute-start(bf16[2,32,1792]{2,1,0:T(8,128)(2,1)S(1)} %get-tuple-element.165), channel_id=1, source_target_pairs={{0,32},{16,48},{32,0},{48,16},{1,33},{17,49},{33,1},{49,17},{2,34}... | collective-permute-start | bytes 688136 | tf_op jit(solution)/shard_map/ppermute | solution.py:380
  139.1 17.7 %collective-permute-start.42 = (bf16[2,32,1792]{2,1,0:T(8,128)(2,1)S(1)}, bf16[2,32,1792]{2,1,0:T(8,128)(2,1)S(1)}, u32[]{:S(2)}, u32[]{:S(2)}) collective-permute-start(bf16[2,32,1792]{2,1,0:T(8,128)(2,1)S(1)} %get-tuple-element.166), channel_id=1, source_target_pairs={{0,48},{16,32},{32,16},{48,0},{1,49},{17,33},{33,17},{49,1},{2,50}... | collective-permute-start | bytes 688136 | tf_op jit(solution)/shard_map/ppermute | solution.py:380
  139.4 10.8 %collective-permute-start.36 = (bf16[64,1024]{1,0:T(8,128)(2,1)S(1)}, bf16[64,1024]{1,0:T(8,128)(2,1)S(1)}, u32[]{:S(2)}, u32[]{:S(2)}) collective-permute-start(bf16[64,1024]{1,0:T(8,128)(2,1)S(1)} %shard_map.259.p0), channel_id=1, source_target_pairs={{0,2},{2,0},{1,3},{3,1},{4,6},{6,4},{5,7},{7,5},{8,10},{10,8},{9,1... | collective-permute-start | bytes 393224 | tf_op jit(solution)/shard_map/ppermute | solution.py:380
  141.6 11.3 %collective-permute-start.37 = (bf16[64,1024]{1,0:T(8,128)(2,1)S(1)}, bf16[64,1024]{1,0:T(8,128)(2,1)S(1)}, u32[]{:S(2)}, u32[]{:S(2)}) collective-permute-start(bf16[64,1024]{1,0:T(8,128)(2,1)S(1)} %collective-permute-done.35.p1), channel_id=1, source_target_pairs={{0,2},{2,0},{1,3},{3,1},{4,6},{6,4},{5,7},{7,5},{8,10},{10,8},{9,1... | collective-permute-start | bytes 393224 | tf_op jit(solution)/shard_map/ppermute | solution.py:380
  157.0 4.9 %collective-permute-start.43 = (bf16[32,1792]{1,0:T(8,128)(2,1)S(1)}, bf16[32,1792]{1,0:T(8,128)(2,1)S(1)}, u32[]{:S(2)}, u32[]{:S(2)}) collective-permute-start(bf16[32,1792]{1,0:T(8,128)(2,1)S(1)} %get-tuple-element.171), channel_id=1, source_target_pairs={{0,64},{64,0},{1,65},{65,1},{2,66},{66,2},{3,67},{67,3},{4,68},{68... | collective-permute-start | bytes 344072 | tf_op jit(solution)/shard_map/ppermute | solution.py:380
  (24 other events, 191.3 us)
Sparse Core Ops, SparseCore 0:
  16.8 53.6 all-gather.2
  90.2 42.1 reduce-scatter.1
